TPU v7x, 32 devices: a whole 2x2x4 slice. The times are simulated.
32 devices in a mesh: slide: 4 (over x, core), gy: 2 (over y), gx: 4 (over z).
Axes of the slice: x: 2, y: 2, z: 4, core: 2. Of those that a mesh axis runs over, the one named last changes fastest.
Arguments:
- tokens: bfloat16 [4, 32, 64, 1024], P('slide', 'gy', 'gx'), may hold values from -64 to 64, as said below
- weights: bfloat16 [1024, 4096], replicated, may hold values from -5 to 5
- norm_gain: float32 [1024], replicated, may hold values from 0.25 to 1.75
- tissue: int32 [4, 32, 64], P('slide', 'gy', 'gx'), may hold values from 0 to 1, as said below
- cotangent: bfloat16 [4, 32, 64, 1024], P('slide', 'gy', 'gx'), may hold values from -6 to 6
Outputs:
- block_output: bfloat16 [4, 32, 64, 1024], P('slide', 'gy', 'gx')
- input_grad: bfloat16 [4, 32, 64, 1024], P('slide', 'gy', 'gx')
- weight_grads: float32 [1024, 4096], P(('slide', 'gy', 'gx'))
Inputs may be any that keep to these rules, and one draw needn't show every extreme that they name: `tokens`: token activations. 1 marks a tissue token, 0 background.
All inputs are finite; a program needn't handle non-finite values.
Results may differ from a plain program's by a relative error of at most 0.015.
The roundings to bfloat16 on the way count: a program that leaves them out, or rounds other values in their place, can miss the bound.
Values may be sent and summed in bfloat16 or wider, within the bound.
No kernel may reach another device: no remote copies, remote signals or barrier semaphores. Data moves between devices by JAX's collectives and lax.ppermute only.
A program may use at most 128 MiB of HBM per device.

v0:
```python
import math

import jax
import jax.numpy as jnp
from jax import lax
from jax.sharding import PartitionSpec as P

HEADS = 16
RADIUS = 6


EPSILON = 1e-06


def with_halo(block, sides, width):
    for axis, dim in sides:
        count = lax.axis_size(axis)
        forward = [(i, i + 1) for i in range(count - 1)]
        backward = [(target, source) for source, target in forward]
        low = lax.ppermute(
            lax.slice_in_dim(block, block.shape[dim] - width, None, axis=dim), axis, forward
        )
        high = lax.ppermute(lax.slice_in_dim(block, 0, width, axis=dim), axis, backward)
        block = jnp.concatenate([low, block, high], axis=dim)
    return block


def shifted(shard, axis, by):
    count = lax.axis_size(axis)
    pairs = [(i, i + by) for i in range(count) if 0 <= i + by < count]
    return lax.ppermute(shard, axis, pairs)


def contract(pattern, left_operand, second):
    return jnp.einsum(pattern, left_operand, second, preferred_element_type=jnp.float32)


def into_blocks(array, blocks_down, blocks_across, head_dim):
    shaped = array.reshape(blocks_down, 8, blocks_across, 8, HEADS, head_dim)
    return shaped.transpose(0, 2, 1, 3, 4, 5).reshape(
        blocks_down * blocks_across, 64, HEADS, head_dim
    )


def from_blocks(array, blocks_down, blocks_across):
    model_width = array.shape[2] * array.shape[3]
    shaped = array.reshape(blocks_down, blocks_across, 8, 8, model_width)
    return shaped.transpose(0, 2, 1, 3, 4).reshape(blocks_down * 8, blocks_across * 8, model_width)


def stack_windows(array, blocks_count):
    return jnp.stack([array[offset : offset + blocks_count] for offset in range(3)], axis=1)


def tile_attention(queries, key_values, grad_attn, row_valid, col_valid):
    tile_rows, tile_cols, model_width = queries.shape
    head_dim = model_width // HEADS
    blocks_down = tile_rows // 8
    blocks_across = tile_cols // 8
    block_count = blocks_down * blocks_across
    window_edge = 8 + 2 * RADIUS
    window_size = window_edge * window_edge
    extra_rows = 16 - 2 * RADIUS
    channels = key_values.shape[2]
    padded = jnp.pad(key_values, ((0, extra_rows), (0, extra_rows), (0, 0)))
    block_grid = padded.reshape(blocks_down + 2, 8, blocks_across + 2, 8, channels)
    row_stack = stack_windows(block_grid, blocks_down)
    full_stack = jnp.stack(
        [row_stack[:, :, :, offset : offset + blocks_across] for offset in range(3)], axis=4
    )
    windows = full_stack.reshape(blocks_down, 24, blocks_across, 24, channels)[
        :, :window_edge, :, :window_edge
    ]
    windows = windows.transpose(0, 2, 1, 3, 4).reshape(block_count, window_size, channels)
    row_padded = jnp.pad(row_valid, (0, extra_rows)).reshape(blocks_down + 2, 8)
    row_window = stack_windows(row_padded, blocks_down).reshape(blocks_down, 24)[:, :window_edge]
    col_padded = jnp.pad(col_valid, (0, extra_rows)).reshape(blocks_across + 2, 8)
    col_window = stack_windows(col_padded, blocks_across).reshape(blocks_across, 24)[
        :, :window_edge
    ]
    query_slot = jnp.arange(64)
    key_slot = jnp.arange(window_size)
    query_row = (query_slot // 8)[:, None]
    query_col = (query_slot % 8)[:, None]
    key_row = (key_slot // window_edge)[None, :]
    key_col = (key_slot % window_edge)[None, :]
    nearby = (key_row >= query_row) & (key_row <= query_row + 2 * RADIUS)
    nearby = nearby & (key_col >= query_col) & (key_col <= query_col + 2 * RADIUS)
    in_grid = (row_window[:, None, :, None] & col_window[None, :, None, :]).reshape(
        block_count, 1, 1, window_size
    )
    allowed = nearby[None, None] & in_grid
    query_blocks = into_blocks(queries, blocks_down, blocks_across, head_dim)
    grad_blocks = into_blocks(grad_attn, blocks_down, blocks_across, head_dim)
    key_blocks = windows[:, :, :model_width].reshape(block_count, window_size, HEADS, head_dim)
    value_blocks = windows[:, :, model_width:].reshape(block_count, window_size, HEADS, head_dim)
    scaling = 1.0 / math.sqrt(head_dim)
    scores = contract("nqhd,nkhd->nhqk", query_blocks, key_blocks) * scaling
    scores = jnp.where(allowed, scores, -1e30)
    row_max = jnp.max(scores, axis=-1, keepdims=True)
    exponent = jnp.exp(scores - row_max)
    attn_probs = exponent / jnp.sum(exponent, axis=-1, keepdims=True)
    probs_bf = attn_probs.astype(jnp.bfloat16)
    attended = contract("nhqk,nkhd->nqhd", probs_bf, value_blocks).astype(jnp.bfloat16)
    grad_probs = contract("nqhd,nkhd->nhqk", grad_blocks, value_blocks)
    centred = grad_probs - jnp.sum(attn_probs * grad_probs, axis=-1, keepdims=True)
    grad_scores = (attn_probs * centred * scaling).astype(jnp.bfloat16)
    grad_queries = contract("nhqk,nkhd->nqhd", grad_scores, key_blocks).astype(jnp.bfloat16)
    grad_keys = contract("nhqk,nqhd->nkhd", grad_scores, query_blocks)
    grad_values = contract("nhqk,nqhd->nkhd", probs_bf, grad_blocks)
    grad_windows = jnp.concatenate(
        [
            grad_keys.reshape(block_count, window_size, model_width),
            grad_values.reshape(block_count, window_size, model_width),
        ],
        axis=-1,
    )
    grad_windows = grad_windows.reshape(
        blocks_down, blocks_across, window_edge, window_edge, channels
    )
    grad_windows = jnp.pad(
        grad_windows, ((0, 0), (0, 0), (0, 24 - window_edge), (0, 24 - window_edge), (0, 0))
    )
    grad_windows = grad_windows.reshape(blocks_down, blocks_across, 3, 8, 3, 8, channels)
    accumulated = jnp.zeros((blocks_down + 2, 8, blocks_across + 2, 8, channels), jnp.float32)
    for offset_down in range(3):
        for offset_across in range(3):
            window_part = grad_windows[:, :, offset_down, :, offset_across].transpose(0, 2, 1, 3, 4)
            accumulated = accumulated.at[
                offset_down : offset_down + blocks_down,
                :,
                offset_across : offset_across + blocks_across,
            ].add(window_part)
    accumulated = accumulated.reshape(8 * (blocks_down + 2), 8 * (blocks_across + 2), channels)
    accumulated = accumulated[: tile_rows + 2 * RADIUS, : tile_cols + 2 * RADIUS]
    return (
        from_blocks(attended, blocks_down, blocks_across),
        from_blocks(grad_queries, blocks_down, blocks_across),
        accumulated,
    )


def run_strips(queries, padded_kv, grad_attn, row_valid, col_valid):
    tile_rows, tile_cols, model_width = queries.shape

    def strip_step(strip_index, carry):
        attended_all, grad_query_all, grad_padded_all = carry
        top_row = (strip_index * 8).astype(jnp.int32)
        query_strip = lax.dynamic_slice_in_dim(queries, top_row, 8, 0)
        kv_strip = lax.dynamic_slice_in_dim(padded_kv, top_row, 8 + 2 * RADIUS, 0)
        grad_strip = lax.dynamic_slice_in_dim(grad_attn, top_row, 8, 0)
        valid_strip = lax.dynamic_slice_in_dim(row_valid, top_row, 8 + 2 * RADIUS, 0)
        attended, grad_queries, grad_padded = tile_attention(
            query_strip, kv_strip, grad_strip, valid_strip, col_valid
        )
        attended_all = lax.dynamic_update_slice_in_dim(attended_all, attended, top_row, 0)
        grad_query_all = lax.dynamic_update_slice_in_dim(grad_query_all, grad_queries, top_row, 0)
        previous = lax.dynamic_slice_in_dim(grad_padded_all, top_row, 8 + 2 * RADIUS, 0)
        grad_padded_all = lax.dynamic_update_slice_in_dim(
            grad_padded_all, previous + grad_padded, top_row, 0
        )
        return (attended_all, grad_query_all, grad_padded_all)

    start_carry = (
        jnp.zeros((tile_rows, tile_cols, model_width), jnp.bfloat16),
        jnp.zeros((tile_rows, tile_cols, model_width), jnp.bfloat16),
        jnp.zeros((tile_rows + 2 * RADIUS, tile_cols + 2 * RADIUS, 2 * model_width), jnp.float32),
    )
    return lax.fori_loop(0, tile_rows // 8, strip_step, start_carry)


def local(tokens, weights, norm_gain, tissue, cotangent):
    tile_tokens = tokens[0]
    tile_rows, tile_cols, model_width = tile_tokens.shape
    token_count = tile_rows * tile_cols
    group_count = lax.axis_size("slide") * lax.axis_size("gy") * lax.axis_size("gx")
    weight_in = weights[:, : 3 * model_width]
    weight_out = weights[:, 3 * model_width :]
    tokens_float = tile_tokens.astype(jnp.float32)
    row_mean = jnp.mean(tokens_float, axis=-1, keepdims=True)
    centered = tokens_float - row_mean
    variance = jnp.mean(centered * centered, axis=-1, keepdims=True)
    inverse = lax.rsqrt(variance + EPSILON)
    normalized = centered * inverse
    normed = (normalized * norm_gain).astype(jnp.bfloat16)
    normed_flat = normed.reshape(token_count, model_width)
    projected = jnp.dot(normed_flat, weight_in, preferred_element_type=jnp.float32).astype(
        jnp.bfloat16
    )
    projected = projected.reshape(tile_rows, tile_cols, 3 * model_width)
    queries = projected[:, :, :model_width]
    key_values = projected[:, :, model_width:]
    tissue_tile = tissue[0]
    tissue_mask = tissue_tile.astype(jnp.float32)[:, :, None]
    upstream = cotangent[0].astype(jnp.float32)
    branch_grad = (tissue_mask * upstream).astype(jnp.bfloat16)
    branch_flat = branch_grad.reshape(token_count, model_width)
    grad_attn = jnp.dot(branch_flat, weight_out.T, preferred_element_type=jnp.float32).astype(
        jnp.bfloat16
    )
    grad_attn = grad_attn.reshape(tile_rows, tile_cols, model_width)
    padded_kv = with_halo(key_values, (("gy", 0), ("gx", 1)), RADIUS)
    row_coord = jnp.arange(tile_rows + 2 * RADIUS) + lax.axis_index("gy") * tile_rows - RADIUS
    row_valid = (row_coord >= 0) & (row_coord < tile_rows * lax.axis_size("gy"))
    col_coord = jnp.arange(tile_cols + 2 * RADIUS) + lax.axis_index("gx") * tile_cols - RADIUS
    col_valid = (col_coord >= 0) & (col_coord < tile_cols * lax.axis_size("gx"))
    operands = (queries, padded_kv, grad_attn, row_valid, col_valid)
    attended, grad_queries, grad_padded = run_strips(*operands)
    attended_flat = attended.reshape(token_count, model_width)
    inv_root = 1.0 / math.sqrt(group_count * token_count)
    part_rows = attended_flat
    out_part = lax.psum_scatter(
        lax.dot_general(
            part_rows, branch_flat, (((0,), (0,)), ((), ())), preferred_element_type=jnp.float32
        )
        * inv_root,
        ("slide", "gy", "gx"),
        scatter_dimension=0,
        tiled=True,
    )
    projection = jnp.dot(attended_flat, weight_out, preferred_element_type=jnp.float32)
    block_output = (
        tokens_float + tissue_mask * projection.reshape(tile_rows, tile_cols, model_width)
    ).astype(jnp.bfloat16)
    column_fold = grad_padded[:, RADIUS : RADIUS + tile_cols]
    for shift_by, rim_part in (
        (-1, grad_padded[:, :RADIUS]),
        (1, grad_padded[:, RADIUS + tile_cols :]),
    ):
        arrived = shifted(rim_part.astype(jnp.bfloat16), "gx", shift_by).astype(rim_part.dtype)
        if shift_by < 0:
            column_fold = column_fold.at[:, tile_cols - RADIUS :].add(arrived)
        else:
            column_fold = column_fold.at[:, :RADIUS].add(arrived)
    row_fold = column_fold[RADIUS : RADIUS + tile_rows]
    for shift_by, rim_part in ((-1, column_fold[:RADIUS]), (1, column_fold[RADIUS + tile_rows :])):
        arrived = shifted(rim_part.astype(jnp.bfloat16), "gy", shift_by).astype(rim_part.dtype)
        if shift_by < 0:
            row_fold = row_fold.at[tile_rows - RADIUS :].add(arrived)
        else:
            row_fold = row_fold.at[:RADIUS].add(arrived)
    grad_kv = row_fold.astype(jnp.bfloat16)
    grad_projected = jnp.concatenate([grad_queries, grad_kv], axis=-1).reshape(
        token_count, 3 * model_width
    )
    grad_normed = jnp.dot(grad_projected, weight_in.T, preferred_element_type=jnp.float32)
    grad_normed = grad_normed.reshape(tile_rows, tile_cols, model_width)
    scaled = grad_normed * norm_gain
    first_mean = jnp.mean(scaled, axis=-1, keepdims=True)
    second_mean = jnp.mean(scaled * normalized, axis=-1, keepdims=True)
    input_grad = (upstream + inverse * (scaled - first_mean - normalized * second_mean)).astype(
        jnp.bfloat16
    )
    part_rows = normed_flat
    in_part = lax.psum_scatter(
        lax.dot_general(
            part_rows, grad_projected, (((0,), (0,)), ((), ())), preferred_element_type=jnp.float32
        )
        * inv_root,
        ("slide", "gy", "gx"),
        scatter_dimension=0,
        tiled=True,
    )
    weight_grads = jnp.concatenate([in_part, out_part], axis=1)
    return (block_output[None], input_grad[None], weight_grads)


def solution(mesh):
    in_specs = (
        P("slide", "gy", "gx", None),
        P(),
        P(),
        P("slide", "gy", "gx"),
        P("slide", "gy", "gx", None),
    )
    out_specs = (
        P("slide", "gy", "gx", None),
        P("slide", "gy", "gx", None),
        P(("slide", "gy", "gx"), None),
    )
    return jax.shard_map(local, mesh=mesh, in_specs=in_specs, out_specs=out_specs, check_vma=False)
```

profile of v0, /device:TPU:0, one launch (start us, length us, event | category | flops | bytes accessed | tf_op | source)
XLA Modules:
  0.0 711.5 jit_solution(8018855402564643929)
XLA Ops:
  11.3 4.6 fusion.75
  17.7 5.1 collective-permute-start
  23.5 8.9 %collective-permute-done.1 = bf16[6,16,2048]{2,0,1:T(8,128)(2,1)S(1)} collective-permute-done((bf16[6,16,2048]{2,0,1:T(8,128)(2,1)S(1)}, bf16[6,16,2048]{2,0,1:T(8,128)(2,1)S(1)}, u32[]{:S(2)}, u32[]{:S(2)}) %collective-permute-start.1) | collective-permute-done | bytes 393248 | tf_op jit(solution)/shard_map/ppermute | solution.py:23
  35.7 5.2 collective-permute-start.2
  43.1 2.3 fusion.95
  45.5 10.5 %collective-permute-done.2 = bf16[28,6,2048]{2,0,1:T(8,128)(2,1)} collective-permute-done((bf16[28,6,2048]{2,0,1:T(8,128)(2,1)}, bf16[28,6,2048]{2,0,1:T(8,128)(2,1)}, u32[]{:S(2)}, u32[]{:S(2)}) %collective-permute-start.2) | collective-permute-done | bytes 688160 | tf_op jit(solution)/shard_map/ppermute | solution.py:20
  56.0 5.0 collective-permute-done.3
  61.0 2.4 pad_maximum_fusion.3
  63.3 3.7 copy.100
  68.7 3.9 broadcast_in_dim.81
  72.6 310.0 %while.33 = (s32[]{:T(128)}, bf16[16,16,1024]{2,1,0:T(8,128)(2,1)}, bf16[16,16,1024]{2,1,0:T(8,128)(2,1)}, f32[28,28,2048]{2,1,0:T(8,128)}, bf16[28,28,2048]{2,1...) while((s32[]{:T(128)}, bf16[16,16,1024]{2,1,0:T(8,128)(2,1)}, ...), condition=%wide.region_8.9_spmd, body=%wide.region_2.8_spmd.sunk | while | flops 662583808 | bytes 314590624 | solution.py:169
  101.9 2.1 constant_dynamic-slice_fusion.6
  106.1 3.4 copy.160
  109.5 3.6 fusion.196
  113.1 4.6 copy.161
  117.7 6.0 copy.162
  123.8 2.7 fusion.202
  127.2 3.6 fusion.200
  130.7 18.6 %fusion.203 = bf16[2,64,16,64]{1,3,2,0:T(8,128)(2,1)} fusion(bf16[2,400,16,64]{1,3,2,0:T(8,128)(2,1)} %bitcast.352, f32[2,16,64,400]{3,2,1,0:T(8,128)} %fusion.202, f32[2,16,64,400]{3,2,1,0:T(8,128)} %get-tuple-element.709, f32[2,16,64]{2,1,0:T(8,128)S(1)} %get-tuple-element.710), kind=kOutput, calls=%fused_computation.36.clone.1 | convolution fusion | flops 110725520 | bytes 8462336 | tf_op jit(solution)/shard_map/while/body/eval_jaxpr/nhqk,nkhd->nqhd/dot_general | solution.py:35
  149.3 3.8 fusion.201
  153.1 18.6 %fusion.204 = f32[2,400,16,64]{1,3,2,0:T(8,128)} fusion(f32[2,16,64,400]{3,2,1,0:T(8,128)} %fusion.202, bf16[1,2,8,8,16,64]{5,4,3,1,2,0:T(8,128)(2,1)S(1)} %bitcast.357, f32[2,16,64,400]{3,2,1,0:T(8,128)} %get-tuple-element.709, f32[2,16,64]{2,1,0:T(8,128)S(1)} %get-tuple-element.710), kind=kOutput, calls=%fused_computation.20.clone.1 | convolution fusion | flops 110594448 | bytes 10100736 | tf_op jit(solution)/shard_map/while/body/eval_jaxpr/nhqk,nqhd->nkhd/dot_general | solution.py:35
  171.8 5.1 convolution_bitcast_fusion.2
  180.0 6.4 copy.166
  186.4 5.8 concatenate.124
  192.3 6.4 copy.167
  198.7 7.1 %concatenate.125 = f32[1,2,20,20,1024]{4,1,3,2,0:T(2,128)} reshape(f32[2,400,16,64]{3,2,0,1:T(8,128)} %copy.167) | data formatting | bytes 6553600 | tf_op jit(solution)/shard_map/while/body/eval_jaxpr/concatenate | solution.py:111
  205.8 8.9 %pad_maximum_fusion.16 = f32[1,2,20,20,2048]{4,1,3,2,0:T(2,128)} fusion(f32[1,2,20,20,1024]{4,1,3,2,0:T(2,128)S(1)} %concatenate.124, f32[1,2,20,20,1024]{4,1,3,2,0:T(2,128)} %concatenate.125), kind=kLoop, calls=%fused_computation.2.clone.1 | loop fusion | flops 1638400 | bytes 13107200 | tf_op jit(solution)/shard_map/while/body/eval_jaxpr/concatenate | solution.py:111
  214.7 6.7 copy.168
  225.4 2.1 fusion.207
  233.5 2.9 copy-done
  246.8 3.4 copy.160
  250.2 3.6 fusion.196
  253.8 4.6 copy.161
  258.4 6.0 copy.162
  264.4 2.7 fusion.202
  267.8 3.6 fusion.200
  271.4 18.6 %fusion.203 = bf16[2,64,16,64]{1,3,2,0:T(8,128)(2,1)} fusion(bf16[2,400,16,64]{1,3,2,0:T(8,128)(2,1)} %bitcast.352, f32[2,16,64,400]{3,2,1,0:T(8,128)} %fusion.202, f32[2,16,64,400]{3,2,1,0:T(8,128)} %get-tuple-element.709, f32[2,16,64]{2,1,0:T(8,128)S(1)} %get-tuple-element.710), kind=kOutput, calls=%fused_computation.36.clone.1 | convolution fusion | flops 110725520 | bytes 8462336 | tf_op jit(solution)/shard_map/while/body/eval_jaxpr/nhqk,nkhd->nqhd/dot_general | solution.py:35
  290.0 3.8 fusion.201
  293.7 18.6 %fusion.204 = f32[2,400,16,64]{1,3,2,0:T(8,128)} fusion(f32[2,16,64,400]{3,2,1,0:T(8,128)} %fusion.202, bf16[1,2,8,8,16,64]{5,4,3,1,2,0:T(8,128)(2,1)S(1)} %bitcast.357, f32[2,16,64,400]{3,2,1,0:T(8,128)} %get-tuple-element.709, f32[2,16,64]{2,1,0:T(8,128)S(1)} %get-tuple-element.710), kind=kOutput, calls=%fused_computation.20.clone.1 | convolution fusion | flops 110594448 | bytes 10100736 | tf_op jit(solution)/shard_map/while/body/eval_jaxpr/nhqk,nqhd->nkhd/dot_general | solution.py:35
  312.4 5.1 convolution_bitcast_fusion.2
  320.7 6.4 copy.166
  327.1 5.8 concatenate.124
  332.9 6.4 copy.167
  339.3 7.1 %concatenate.125 = f32[1,2,20,20,1024]{4,1,3,2,0:T(2,128)} reshape(f32[2,400,16,64]{3,2,0,1:T(8,128)} %copy.167) | data formatting | bytes 6553600 | tf_op jit(solution)/shard_map/while/body/eval_jaxpr/concatenate | solution.py:111
  346.4 8.9 %pad_maximum_fusion.16 = f32[1,2,20,20,2048]{4,1,3,2,0:T(2,128)} fusion(f32[1,2,20,20,1024]{4,1,3,2,0:T(2,128)S(1)} %concatenate.124, f32[1,2,20,20,1024]{4,1,3,2,0:T(2,128)} %concatenate.125), kind=kLoop, calls=%fused_computation.2.clone.1 | loop fusion | flops 1638400 | bytes 13107200 | tf_op jit(solution)/shard_map/while/body/eval_jaxpr/concatenate | solution.py:111
  355.4 6.7 copy.168
  366.0 2.1 fusion.207
  374.1 2.9 copy-done
  382.6 4.0 bitcast_multiply_fusion.1
  386.7 6.7 copy.139
  395.7 5.5 collective-permute-start.5
  401.3 2.3 slice.1180
  403.6 27.2 %collective-permute-done.4 = bf16[28,6,2048]{2,0,1:T(8,128)(2,1)S(1)} collective-permute-done((bf16[28,6,2048]{2,0,1:T(8,128)(2,1)S(1)}, bf16[28,6,2048]{2,0,1:T(8,128)(2,1)S(1)}, u32[]{:S(2)}, u32[]{:S(2)}) %collective-permute-start.4) | collective-permute-done | bytes 688160 | tf_op jit(solution)/shard_map/ppermute | solution.py:31
  432.5 9.1 %scatter-add.44 = f32[28,16,2048]{2,1,0:T(8,128)} dynamic-update-slice(f32[28,16,2048]{2,1,0:T(8,128)} %slice.1180, f32[28,6,2048]{2,1,0:T(8,128)} %convert_add_fusion, s32[]{:T(128)} %constant.781.clone.1, s32[]{:T(128)} %constant.793.clone.1, s32[]{:T(128)} %constant.781.clone.1) | dynamic-update-slice | bytes 2752516 | tf_op jit(solution)/shard_map/scatter-add | solution.py:232
  441.6 2.2 slice_add_fusion.1
  443.8 9.3 %scatter-add.54 = f32[28,16,2048]{2,1,0:T(8,128)} dynamic-update-slice(f32[28,16,2048]{2,1,0:T(8,128)} %scatter-add.44, f32[28,6,2048]{2,1,0:T(8,128)S(1)} %slice_add_fusion.1, s32[]{:T(128)} %constant.781.clone.1, s32[]{:T(128)} %constant.781.clone.1, s32[]{:T(128)} %constant.781.clone.1) | dynamic-update-slice | bytes 2752516 | tf_op jit(solution)/shard_map/scatter-add | solution.py:234
  453.1 2.5 convert.12
  457.1 6.5 collective-permute-start.7
  463.6 8.6 %collective-permute-done.6 = bf16[6,16,2048]{2,1,0:T(8,128)(2,1)S(1)} collective-permute-done((bf16[6,16,2048]{2,1,0:T(8,128)(2,1)S(1)}, bf16[6,16,2048]{2,1,0:T(8,128)(2,1)S(1)}, u32[]{:S(2)}, u32[]{:S(2)}) %collective-permute-start.6) | collective-permute-done | bytes 393248 | tf_op jit(solution)/shard_map/ppermute | solution.py:31
  473.7 6.5 bitcast_multiply_fusion
  481.2 3.1 fusion.98
  484.3 4.8 fusion.129
  490.4 52.5 %reduce-scatter.5.cloned.1.call-done = f32[32,1024]{1,0:T(8,128)} async-done(((f32[1024,1024]{1,0:T(8,128)}), f32[32,1024]{1,0:T(8,128)}) %reduce-scatter.5.cloned.1.call-update) | async-done | bytes 131088 | tf_op jit(solution)/shard_map/reduce_scatter | solution.py:212
  542.9 159.6 %reduce-scatter.3.cloned.1.call-done = f32[32,3072]{1,0:T(8,128)} async-done(((f32[1024,3072]{1,0:T(8,128)}), f32[32,3072]{1,0:T(8,128)}) %reduce-scatter.3.cloned.1.call-update) | async-done | bytes 393232 | tf_op jit(solution)/shard_map/reduce_scatter | solution.py:255
  (244 shorter events, 70.6 us)
Async XLA Ops:
  7.2 535.7 %reduce-scatter.5.cloned.1.call-start = ((), (), s32[]{:S(2)}) async-start(), calls=%async_computation.3 | async-start | bytes 4325376 | tf_op jit(solution)/shard_map/reduce_scatter | solution.py:212
  8.4 7.4 %copy-start.16 = (f32[16,16]{1,0:T(8,128)}, f32[16,16]{1,0:T(8,128)S(1)}, u32[]{:S(2)}) copy-start(f32[16,16]{1,0:T(8,128)S(1)} %broadcast_multiply_fusion.2) | copy-start | bytes 3076
  9.8 6.0 copy-start.18
  16.2 16.2 %collective-permute-start.1 = (bf16[6,16,2048]{2,0,1:T(8,128)(2,1)S(1)}, bf16[6,16,2048]{2,0,1:T(8,128)(2,1)S(1)}, u32[]{:S(2)}, u32[]{:S(2)}) collective-permute-start(bf16[6,16,2048]{2,0,1:T(8,128)(2,1)S(1)} %copy.117), channel_id=1, source_target_pairs={{4,0},{5,1},{6,2},{7,3},{12,8},{13,9},{14,10},{15,11},{20,16},{21,... | collective-permute-start | bytes 1179656 | tf_op jit(solution)/shard_map/ppermute | solution.py:23
  17.5 24.8 %copy-start.21 = (s32[1,16,16]{2,1,0:T(8,128)S(1)}, s32[1,16,16]{2,1,0:T(8,128)}, u32[]{:S(2)}) copy-start(s32[1,16,16]{2,1,0:T(8,128)} %param.36) | copy-start | bytes 3076
  17.7 25.3 %copy-start.10 = (bf16[1,16,16,1024]{3,2,1,0:T(8,128)(2,1)S(1)}, bf16[1,16,16,1024]{3,2,1,0:T(8,128)(2,1)}, u32[]{:S(2)}) copy-start(bf16[1,16,16,1024]{3,2,1,0:T(8,128)(2,1)} %param.37) | copy-start | bytes 1572868
  17.7 16.2 %collective-permute-start = (bf16[6,16,2048]{2,0,1:T(8,128)(2,1)S(1)}, bf16[6,16,2048]{2,0,1:T(8,128)(2,1)S(1)}, u32[]{:S(2)}, u32[]{:S(2)}) collective-permute-start(bf16[6,16,2048]{2,0,1:T(8,128)(2,1)S(1)} %copy.115), channel_id=1, source_target_pairs={{0,4},{1,5},{2,6},{3,7},{8,12},{9,13},{10,14},{11,15},{16,20},{17,... | collective-permute-start | bytes 1179656 | tf_op jit(solution)/shard_map/ppermute | solution.py:20
  35.7 20.2 %collective-permute-start.2 = (bf16[28,6,2048]{2,0,1:T(8,128)(2,1)}, bf16[28,6,2048]{2,0,1:T(8,128)(2,1)}, u32[]{:S(2)}, u32[]{:S(2)}) collective-permute-start(bf16[28,6,2048]{2,0,1:T(8,128)(2,1)} %get-tuple-element.607), channel_id=1, source_target_pairs={{0,1},{1,2},{2,3},{4,5},{5,6},{6,7},{8,9},{9,10},{10,11},{12,13},{... | collective-permute-start | bytes 2064392 | tf_op jit(solution)/shard_map/ppermute | solution.py:20
  41.0 20.0 %collective-permute-start.3 = (bf16[28,6,2048]{2,0,1:T(8,128)(2,1)}, bf16[28,6,2048]{2,0,1:T(8,128)(2,1)}, u32[]{:S(2)}, u32[]{:S(2)}) collective-permute-start(bf16[28,6,2048]{2,0,1:T(8,128)(2,1)} %get-tuple-element.608), channel_id=1, source_target_pairs={{1,0},{2,1},{3,2},{5,4},{6,5},{7,6},{9,8},{10,9},{11,10},{13,12},{... | collective-permute-start | bytes 2064392 | tf_op jit(solution)/shard_map/ppermute | solution.py:23
  67.0 5.6 copy-start.20
  72.6 310.0 %copy-start.22 = (f32[16,16]{1,0:T(8,128)S(1)}, f32[16,16]{1,0:T(8,128)}, u32[]{:S(2)}) copy-start(f32[16,16]{1,0:T(8,128)} %get-tuple-element.613) | copy-start | bytes 3076
  95.7 8.6 %copy-start.6 = (bf16[16,16,1024]{2,1,0:T(8,128)(2,1)}, bf16[16,16,1024]{2,1,0:T(8,128)(2,1)S(1)}, u32[]{:S(2)}) copy-start(bf16[16,16,1024]{2,1,0:T(8,128)(2,1)S(1)} %get-tuple-element.758) | copy-start | bytes 1572868 | tf_op jit(solution)/shard_map/while
  95.7 8.6 %copy-start.8 = (bf16[16,16,1024]{2,1,0:T(8,128)(2,1)}, bf16[16,16,1024]{2,1,0:T(8,128)(2,1)S(1)}, u32[]{:S(2)}) copy-start(bf16[16,16,1024]{2,1,0:T(8,128)(2,1)S(1)} %get-tuple-element.759) | copy-start | bytes 1572868 | tf_op jit(solution)/shard_map/while
  123.8 2.7 copy-start.1
  171.7 5.2 copy-start.4
  171.7 5.9 copy-start.3
  171.7 6.7 copy-start.12
  179.2 0.8 copy-start.13
  228.8 1.9 slice-start
  229.1 2.9 slice-start.1
  232.0 4.4 copy-start.7
  232.0 4.4 copy-start.9
  233.4 2.9 copy-start
  236.4 8.6 %copy-start.6 = (bf16[16,16,1024]{2,1,0:T(8,128)(2,1)}, bf16[16,16,1024]{2,1,0:T(8,128)(2,1)S(1)}, u32[]{:S(2)}) copy-start(bf16[16,16,1024]{2,1,0:T(8,128)(2,1)S(1)} %get-tuple-element.758) | copy-start | bytes 1572868 | tf_op jit(solution)/shard_map/while
  236.4 8.6 %copy-start.8 = (bf16[16,16,1024]{2,1,0:T(8,128)(2,1)}, bf16[16,16,1024]{2,1,0:T(8,128)(2,1)S(1)}, u32[]{:S(2)}) copy-start(bf16[16,16,1024]{2,1,0:T(8,128)(2,1)S(1)} %get-tuple-element.759) | copy-start | bytes 1572868 | tf_op jit(solution)/shard_map/while
  264.4 2.7 copy-start.1
  312.4 5.2 copy-start.4
  312.4 5.9 copy-start.3
  312.4 6.7 copy-start.12
  319.9 0.8 copy-start.13
  369.4 1.9 slice-start
  369.7 2.9 slice-start.1
  372.7 4.4 copy-start.7
  372.7 4.4 copy-start.9
  374.1 2.9 copy-start
  386.6 14.7 %slice-start.2 = ((s8[7340032]{0:T(1024)(128)(4,1)}), s8[3145728]{0:T(1024)(128)(4,1)S(1)}, s32[]{:S(2)}) async-start(s8[7340032]{0:T(1024)(128)(4,1)} %bitcast.348), calls=%async_computation.6 | async-start | bytes 6291456
  386.6 315.9 %reduce-scatter.3.cloned.1.call-start = ((), (), s32[]{:S(2)}) async-start(), calls=%async_computation.2 | async-start | bytes 12976128 | tf_op jit(solution)/shard_map/reduce_scatter | solution.py:255
  386.7 14.6 %slice-start.3 = ((s8[7340032]{0:T(1024)(128)(4,1)}), s8[4194304]{0:T(1024)(128)(4,1)S(1)}, s32[]{:S(2)}) async-start(s8[7340032]{0:T(1024)(128)(4,1)} %bitcast.348), calls=%async_computation.7 | async-start | bytes 8388608
  394.4 36.3 %collective-permute-start.4 = (bf16[28,6,2048]{2,0,1:T(8,128)(2,1)S(1)}, bf16[28,6,2048]{2,0,1:T(8,128)(2,1)S(1)}, u32[]{:S(2)}, u32[]{:S(2)}) collective-permute-start(bf16[28,6,2048]{2,0,1:T(8,128)(2,1)S(1)} %get-tuple-element.606), channel_id=1, source_target_pairs={{1,0},{2,1},{3,2},{5,4},{6,5},{7,6},{9,8},{10,9},{11,10},{13,12},{... | collective-permute-start | bytes 2064392 | tf_op jit(solution)/shard_map/ppermute | solution.py:31
  395.7 45.9 %collective-permute-start.5 = (bf16[28,6,2048]{2,0,1:T(8,128)(2,1)}, bf16[28,6,2048]{2,0,1:T(8,128)(2,1)}, u32[]{:S(2)}, u32[]{:S(2)}) collective-permute-start(bf16[28,6,2048]{2,0,1:T(8,128)(2,1)} %get-tuple-element.605), channel_id=1, source_target_pairs={{0,1},{1,2},{2,3},{4,5},{5,6},{6,7},{8,9},{9,10},{10,11},{12,13},{... | collective-permute-start | bytes 2064392 | tf_op jit(solution)/shard_map/ppermute | solution.py:31
  453.1 3.8 copy-start.2
  455.6 16.6 %collective-permute-start.6 = (bf16[6,16,2048]{2,1,0:T(8,128)(2,1)S(1)}, bf16[6,16,2048]{2,1,0:T(8,128)(2,1)S(1)}, u32[]{:S(2)}, u32[]{:S(2)}) collective-permute-start(bf16[6,16,2048]{2,1,0:T(8,128)(2,1)S(1)} %get-tuple-element.610), channel_id=1, source_target_pairs={{4,0},{5,1},{6,2},{7,3},{12,8},{13,9},{14,10},{15,11},{20,16},{21,... | collective-permute-start | bytes 1179656 | tf_op jit(solution)/shard_map/ppermute | solution.py:31
  457.1 16.5 %copy-start.5 = (bf16[1,16,16,1024]{3,2,1,0:T(8,128)(2,1)S(1)}, bf16[1,16,16,1024]{3,2,1,0:T(8,128)(2,1)}, u32[]{:S(2)}) copy-start(bf16[1,16,16,1024]{3,2,1,0:T(8,128)(2,1)} %param.33) | copy-start | bytes 1572868
  457.1 16.5 %copy-start.14 = (bf16[16,16,1024]{2,1,0:T(8,128)(2,1)S(1)}, bf16[16,16,1024]{2,1,0:T(8,128)(2,1)}, u32[]{:S(2)}) copy-start(bf16[16,16,1024]{2,1,0:T(8,128)(2,1)} %get-tuple-element.552) | copy-start | bytes 1572868
  457.1 16.5 %copy-start.17 = (f32[16,16]{1,0:T(8,128)S(1)}, f32[16,16]{1,0:T(8,128)}, u32[]{:S(2)}) copy-start(f32[16,16]{1,0:T(8,128)} %copy-done.16) | copy-start | bytes 3076
  457.1 16.5 %copy-start.19 = (f32[16,16]{1,0:T(8,128)S(1)}, f32[16,16]{1,0:T(8,128)}, u32[]{:S(2)}) copy-start(f32[16,16]{1,0:T(8,128)} %copy-done.18) | copy-start | bytes 3076
  457.1 16.5 %copy-start.23 = (f32[1024]{0:T(1024)S(1)}, f32[1024]{0:T(1024)}, u32[]{:S(2)}) copy-start(f32[1024]{0:T(1024)} %param.35) | copy-start | bytes 12292
  457.1 16.2 %collective-permute-start.7 = (bf16[6,16,2048]{2,1,0:T(8,128)(2,1)S(1)}, bf16[6,16,2048]{2,1,0:T(8,128)(2,1)S(1)}, u32[]{:S(2)}, u32[]{:S(2)}) collective-permute-start(bf16[6,16,2048]{2,1,0:T(8,128)(2,1)S(1)} %get-tuple-element.609), channel_id=1, source_target_pairs={{0,4},{1,5},{2,6},{3,7},{8,12},{9,13},{10,14},{11,15},{16,20},{17,... | collective-permute-start | bytes 1179656 | tf_op jit(solution)/shard_map/ppermute | solution.py:31
  480.2 1.0 copy-start.15
  484.3 4.8 copy-start.11
Sparse Core Ops, SparseCore 0:
  386.7 156.0 reduce-scatter.4
  548.9 153.5 reduce-scatter.2
where the time goes:
time: 720 us; the launch traced here: 711 us
  waiting for transfers between devices  275 us (38%)
  local copies, waits for them, and re-layouts  180 us (25%)
  matrix products  124 us (17%)
  other arithmetic  60.2 us (8%)
  loops' own time  29.5 us (4%)
  starting transfers between devices  27.5 us (4%)
  between operations  14.7 us (2%)
    reduce_scatter x1, waiting for transfers between devices, local(): lax.psum_scatter(lax.dot_general(part_rows, grad_projected, (((0,), (0,))...  160 us
    dot_general x12, matrix products, contract(): jnp.einsum(pattern, left_operand, second, preferred_element_type=jnp.floa...  99 us
    reduce_scatter x1, waiting for transfers between devices, local(): lax.psum_scatter(lax.dot_general(part_rows, branch_flat, (((0,), (0,)), (...  52.5 us
    ppermute x4, waiting for transfers between devices, shifted(): return lax.ppermute(shard, axis, pairs)  36.8 us
    another operation x1, loops' own time, run_strips(): return lax.fori_loop(0, tile_rows // 8, strip_step, start_carry)  29.5 us
    while x50, local copies, waits for them, and re-layouts  26 us
    concatenate x4, local copies, waits for them, and re-layouts, tile_attention(): jnp.concatenate([grad_keys.reshape(block_count, window_size, model_width)...  25.9 us
    transpose x4, local copies, waits for them, and re-layouts, contract(): jnp.einsum(pattern, left_operand, second, preferred_element_type=jnp.floa...  25.6 us
  transfers between devices with their start and end apart: 10, of which 9 were waited for; matrix products, arithmetic and copies ran while one was open for 8% of the time, Pallas kernels for 0%

commit v1 on v0

v1 whole, which is shorter than its diff:
```python
import functools
import math

import jax
import jax.numpy as jnp
from jax import lax
from jax.experimental import pallas as pl
from jax.experimental.pallas import tpu as pltpu
from jax.sharding import PartitionSpec as P

HEADS = 16
RADIUS = 6
EPSILON = 1e-06
STRIP = 4
GROUP = 4
SIDE = 8
BF = jnp.bfloat16
F32 = jnp.float32


def swapped(array, axis, by):
    count = lax.axis_size(axis)
    return lax.ppermute(array, axis, [(i, i ^ by) for i in range(count)])


def moved(array, axis, by):
    count = lax.axis_size(axis)
    pairs = [(i, i + by) for i in range(count) if 0 <= i + by < count]
    return lax.ppermute(array, axis, pairs)


def row_halo(block, mine):
    rows_count = lax.axis_size("gy")
    if rows_count == 2:
        at_top = lax.axis_index("gy") == 0
        other = swapped(jnp.where(at_top, block[-RADIUS:], block[:RADIUS]), "gy", 1)
        zero = jnp.zeros((), block.dtype)
        top, bottom = jnp.where(at_top, zero, other), jnp.where(at_top, other, zero)
    else:
        top = moved(block[-RADIUS:], "gy", 1)
        bottom = moved(block[:RADIUS], "gy", -1)
    return jnp.concatenate([top, mine, bottom], axis=0)


def column_halo(block):
    right = moved(block[:, :SIDE], "gx", -1)
    left = moved(block[:, -SIDE:], "gx", 1)
    return jnp.concatenate([block, right, left], axis=1)


def spread_heads(block, head_dim):
    lane_head = lax.broadcasted_iota(jnp.int32, block.shape, 1) // head_dim
    zero = jnp.zeros_like(block)
    return jnp.concatenate(
        [jnp.where(lane_head == head, block, zero) for head in range(GROUP)], axis=0
    )


def gather_heads(full, count, head_dim):
    lane_head = lax.broadcasted_iota(jnp.int32, (count, full.shape[1]), 1) // head_dim
    result = full[:count]
    for head in range(1, GROUP):
        result = jnp.where(lane_head == head, full[head * count : (head + 1) * count], result)
    return result


def times(left, right):
    return jnp.dot(left, right, preferred_element_type=F32)


def times_t(left, right):
    return lax.dot_general(left, right, (((1,), (1,)), ((), ())), preferred_element_type=F32)


def fill_bias(place_ref, bias_ref, tile_rows, tile_cols):
    strips, count, window = bias_ref.shape
    slots = tile_cols + 2 * SIDE
    own = lax.broadcasted_iota(jnp.int32, (count, window), 0)
    near = lax.broadcasted_iota(jnp.int32, (count, window), 1)
    own_row, own_col = own // tile_cols, own % tile_cols
    near_row, slot = near // slots, near % slots
    near_col = jnp.where(slot < tile_cols + SIDE, slot, slot - slots)
    row_gap = near_row - RADIUS - own_row
    col_gap = near_col - own_col
    col = place_ref[1] + near_col
    allowed = (jnp.abs(row_gap) <= RADIUS) & (jnp.abs(col_gap) <= RADIUS)
    allowed = allowed & (col >= 0) & (col < place_ref[3])
    for strip in range(strips):
        row = place_ref[0] + strip * STRIP + near_row - RADIUS
        kept = allowed & (row >= 0) & (row < place_ref[2])
        bias_ref[strip] = jnp.where(kept, 0.0, -1e30).astype(F32)


def query_pass(
    head_dim, tile, place_ref, q_ref, g_ref, k_ref, v_ref, out_ref, dq_ref, stat_ref, bias_ref
):
    scaling = 1.0 / math.sqrt(head_dim)
    strips, count, window = bias_ref.shape
    step = (tile[1] + 2 * SIDE) * STRIP
    group = pl.program_id(0)

    @pl.when(group == 0)
    def _():
        fill_bias(place_ref, bias_ref, *tile)
        stat_ref[...] = jnp.zeros_like(stat_ref)

    lane = lax.broadcasted_iota(jnp.int32, (count, 128), 1) - group * (2 * GROUP)
    for strip in range(strips):
        own = pl.ds(strip * count, count)
        near = pl.ds(strip * step, window)
        queries = spread_heads(q_ref[own, :] * jnp.asarray(scaling, BF), head_dim)
        grads = spread_heads(g_ref[own, :], head_dim)
        keys = k_ref[near, :]
        values = v_ref[near, :]
        scores = times_t(queries, keys)
        grad_probs = times_t(grads, values)
        stats = stat_ref[own, :]
        probs_parts, grad_parts = [], []
        for head in range(GROUP):
            part = slice(head * count, (head + 1) * count)
            masked = scores[part] + bias_ref[strip]
            row_max = jnp.max(masked, axis=1, keepdims=True)
            exponent = jnp.exp(masked - row_max)
            grad_part = grad_probs[part]
            total = jnp.sum(exponent, axis=1, keepdims=True)
            share = 1.0 / total
            delta = jnp.sum(exponent * grad_part, axis=1, keepdims=True) * share
            probs = exponent * share
            probs_parts.append(probs.astype(BF))
            grad_parts.append((probs * (grad_part - delta)).astype(BF))
            stats = jnp.where(lane == 2 * head, row_max + jnp.log(total), stats)
            stats = jnp.where(lane == 2 * head + 1, delta, stats)
        attended = times(jnp.concatenate(probs_parts, axis=0), values)
        grad_queries = times(jnp.concatenate(grad_parts, axis=0), keys)
        out_ref[own, :] = gather_heads(attended, count, head_dim).astype(BF)
        dq_ref[own, :] = (gather_heads(grad_queries, count, head_dim) * scaling).astype(BF)
        stat_ref[own, :] = stats


def key_pass(
    head_dim,
    tile,
    first,
    place_ref,
    k_ref,
    v_ref,
    q_ref,
    g_ref,
    stat_ref,
    dk_ref,
    dv_ref,
    bias_ref,
    turned,
):
    scaling = 1.0 / math.sqrt(head_dim)
    strips, count, window = bias_ref.shape
    slots = tile[1] + 2 * SIDE
    step = slots * STRIP
    group = pl.program_id(0)

    @pl.when(group == 0)
    def _():
        fill_bias(place_ref, bias_ref, *tile)
        turned[...] = stat_ref[...].T

    rows = pl.ds(pl.multiple_of((group + first) * (2 * GROUP), 2 * GROUP), 2 * GROUP)

    def own_tokens(ref, strip):
        starts = [(RADIUS + strip * STRIP + row) * slots for row in range(STRIP)]
        return jnp.concatenate([ref[pl.ds(start, tile[1]), :] for start in starts], axis=0)

    for strip in range(strips):
        own = pl.ds(strip * count, count)
        near = pl.ds(strip * step, window)
        keys = spread_heads(own_tokens(k_ref, strip) * jnp.asarray(scaling, BF), head_dim)
        values = spread_heads(own_tokens(v_ref, strip), head_dim)
        queries = q_ref[near, :]
        grads = g_ref[near, :]
        scores = times_t(keys, queries)
        grad_probs = times_t(values, grads)
        stats = turned[rows, near]
        probs_parts, grad_parts = [], []
        for head in range(GROUP):
            part = slice(head * count, (head + 1) * count)
            masked = scores[part] + bias_ref[strip]
            probs = jnp.exp(masked - stats[2 * head : 2 * head + 1])
            centred = grad_probs[part] - stats[2 * head + 1 : 2 * head + 2]
            probs_parts.append(probs.astype(BF))
            grad_parts.append((probs * centred).astype(BF))
        grad_values = times(jnp.concatenate(probs_parts, axis=0), grads)
        grad_keys = times(jnp.concatenate(grad_parts, axis=0), queries)
        dv_ref[own, :] = gather_heads(grad_values, count, head_dim).astype(BF)
        dk_ref[own, :] = (gather_heads(grad_keys, count, head_dim) * scaling).astype(BF)


def whole(shape):
    return pl.BlockSpec(shape, lambda group: (0,) * len(shape))


def columns(rows, width, first=0):
    return pl.BlockSpec((rows, width), lambda group: (0, first + group))


PARAMS = dict(vmem_limit_bytes=24 * 1024 * 1024)


def window_shape(tile):
    return (tile[0] // STRIP, STRIP * tile[1], (STRIP + 2 * RADIUS) * (tile[1] + 2 * SIDE))


def attention_cost(tile, groups, part):
    strips, count, window = window_shape(tile)
    flops = 4 * 2 * groups * strips * GROUP * count * window * part
    return pl.CostEstimate(flops=flops, bytes_accessed=4 * 1024 * 1024, transcendentals=0)


SCALARS = pl.BlockSpec(memory_space=pltpu.SMEM)


def run_queries(place, queries, grads, keys, values, head_dim, tile):
    tokens, width = queries.shape
    ext = keys.shape[0]
    part = GROUP * head_dim
    groups = width // part
    return pl.pallas_call(
        functools.partial(query_pass, head_dim, tile),
        grid=(groups,),
        in_specs=[
            SCALARS,
            columns(tokens, part),
            columns(tokens, part),
            columns(ext, part),
            columns(ext, part),
        ],
        out_specs=[columns(tokens, part), columns(tokens, part), whole((tokens, 128))],
        out_shape=[
            jax.ShapeDtypeStruct((tokens, width), BF),
            jax.ShapeDtypeStruct((tokens, width), BF),
            jax.ShapeDtypeStruct((tokens, 128), F32),
        ],
        scratch_shapes=[pltpu.VMEM(window_shape(tile), F32)],
        compiler_params=pltpu.CompilerParams(**PARAMS),
        cost_estimate=attention_cost(tile, groups, part),
        name="query_pass",
    )(place, queries, grads, keys, values)


def run_keys(place, keys, values, queries, grads, stats, head_dim, tile, first, groups):
    tokens = tile[0] * tile[1]
    ext = queries.shape[0]
    part = GROUP * head_dim
    return pl.pallas_call(
        functools.partial(key_pass, head_dim, tile, first),
        grid=(groups,),
        in_specs=[SCALARS] + [columns(ext, part, first)] * 4 + [whole(stats.shape)],
        out_specs=[columns(tokens, part), columns(tokens, part)],
        out_shape=[
            jax.ShapeDtypeStruct((tokens, groups * part), BF),
            jax.ShapeDtypeStruct((tokens, groups * part), BF),
        ],
        scratch_shapes=[pltpu.VMEM(window_shape(tile), F32), pltpu.VMEM((128, ext), F32)],
        compiler_params=pltpu.CompilerParams(**PARAMS),
        cost_estimate=attention_cost(tile, groups, part),
        name="key_pass",
    )(place, keys, values, queries, grads, stats)


def own_part(array, index, axis):
    return lax.dynamic_index_in_dim(array, index, axis, keepdims=False)


def product_t(left, right):
    return lax.dot_general(left, right, (((0,), (0,)), ((), ())), preferred_element_type=F32)


def slide_swap(array, high):
    return swapped(array, "slide", lax.axis_size("slide") // 2 if high else 1)


def partners(across_slides):
    if across_slides:
        index = lax.axis_index("slide") // 2
        return index, [(1, 1 - index)]
    index = lax.axis_index("gy")
    return index, [(by, index ^ by) for by in range(1, lax.axis_size("gy"))]


def sent(block, across_slides, by):
    return slide_swap(block, True) if across_slides else swapped(block, "gy", by)


def pick_rows(left, index, across_slides):
    half = left.shape[1] // 2
    if across_slides:
        return lax.dynamic_slice_in_dim(left, index * half, half, axis=1)
    rest = half // lax.axis_size("gy")
    parts = [
        lax.dynamic_slice_in_dim(left, high * half + index * rest, rest, axis=1)
        for high in range(2)
    ]
    return jnp.concatenate(parts, axis=1)


def first_halving(left, right, across_slides):
    index, others = partners(across_slides)
    arrived = []
    for by, target in others:
        block = product_t(pick_rows(left, target, across_slides), right).astype(BF)
        arrived.append(sent(block, across_slides, by))
    mine = product_t(pick_rows(left, index, across_slides), right)
    for block in arrived:
        mine = mine + block.astype(F32)
    return mine


def second_halving(part, across_slides):
    index, others = partners(across_slides)
    rows = part.shape[0] // (len(others) + 1)
    mine = lax.dynamic_slice_in_dim(part, index * rows, rows, axis=0)
    for by, target in others:
        block = lax.dynamic_slice_in_dim(part, target * rows, rows, axis=0).astype(BF)
        mine = mine + sent(block, across_slides, by).astype(F32)
    return mine


def reduce_columns(part):
    count = lax.axis_size("gx")
    index = lax.axis_index("gx")
    rows = part.shape[0] // count
    mine = lax.dynamic_slice_in_dim(part, index * rows, rows, axis=0)
    arrived = []
    for by in range(count - 1, 0, -1):
        block = lax.dynamic_slice_in_dim(part, (index ^ by) * rows, rows, axis=0)
        arrived.append(swapped(block.astype(BF), "gx", by))
    for block in arrived:
        mine = mine + block.astype(F32)
    return mine


def later_halvings(one, two):
    one = second_halving(one, False)
    two = second_halving(two, True)
    return reduce_columns(jnp.concatenate([one, two], axis=1))


def after(array, *earlier):
    return lax.optimization_barrier((array, *earlier))[0]


def local(tokens, weights, norm_gain, tissue, cotangent):
    tile_tokens = tokens[0]
    tile_rows, tile_cols, model_width = tile_tokens.shape
    tile = (tile_rows, tile_cols)
    head_dim = model_width // HEADS
    token_count = tile_rows * tile_cols
    slides = lax.axis_size("slide")
    rows_count = lax.axis_size("gy")
    cols_count = lax.axis_size("gx")
    weight_in = weights[:, : 3 * model_width]
    weight_out = weights[:, 3 * model_width :]
    place = jnp.stack(
        [
            lax.axis_index("gy") * tile_rows,
            lax.axis_index("gx") * tile_cols,
            jnp.int32(tile_rows * rows_count),
            jnp.int32(tile_cols * cols_count),
        ]
    ).astype(jnp.int32)

    token_rows = row_halo(tile_tokens, tile_tokens)
    tissue_mask = tissue[0].astype(F32)[:, :, None]
    upstream = cotangent[0].astype(F32)
    branch_grad = (tissue_mask * upstream).astype(BF)
    branch_flat = branch_grad.reshape(token_count, model_width)

    def normalize(array):
        array = array.astype(F32)
        centered = array - jnp.mean(array, axis=-1, keepdims=True)
        variance = jnp.mean(centered * centered, axis=-1, keepdims=True)
        inverse = lax.rsqrt(variance + EPSILON)
        return centered * inverse, inverse

    normalized, inverse = normalize(tile_tokens.reshape(token_count, model_width))
    normed = (normalized * norm_gain).astype(BF)
    grad_attn = times_t(branch_flat, weight_out).astype(BF)
    queries = times(normed, weight_in[:, :model_width]).astype(BF)

    core = lax.axis_index("slide") % 2

    def half_swap(array):
        rows = model_width // slides

        def half(which):
            parts = [
                lax.dynamic_slice_in_dim(array, (2 * high + which) * rows, rows, axis=1)
                for high in range(slides // 2)
            ]
            return jnp.concatenate(parts, axis=1)

        return jnp.concatenate([half(core), slide_swap(half(1 - core), False)], axis=0)

    def whole_swap(array):
        return jnp.concatenate([array, slide_swap(array, False)], axis=0)

    token_ext = column_halo(token_rows)
    ext_rows, ext_cols = token_ext.shape[:2]
    branch_first = after(branch_grad, token_rows)
    branch_rows = row_halo(branch_first, branch_grad)
    token_ext = token_ext.reshape(ext_rows * ext_cols, model_width)
    normed_ext = (normalize(token_ext)[0] * norm_gain).astype(BF)
    key_ext = times(normed_ext, weight_in[:, model_width : 2 * model_width]).astype(BF)
    value_ext = times(normed_ext, weight_in[:, 2 * model_width :]).astype(BF)
    branch_ext = column_halo(branch_rows).reshape(ext_rows * ext_cols, model_width)

    attended, grad_queries, stats = run_queries(
        place, queries, grad_attn, key_ext, value_ext, head_dim, tile
    )

    stats_tile = stats.reshape(tile_rows, tile_cols, -1)
    stats_ext = column_halo(row_halo(stats_tile, stats_tile))
    stats_ext = stats_ext.reshape(ext_rows * ext_cols, -1)

    normed_pair = half_swap(normed)
    branch_pair = whole_swap(branch_flat)
    one = first_halving(normed_pair, whole_swap(grad_queries), True)
    two = first_halving(half_swap(attended), branch_pair, False)

    normed_late, branch_late = lax.optimization_barrier((normed_ext, branch_ext, stats))[:2]
    query_ext = times(normed_late, weight_in[:, :model_width]).astype(BF)
    grad_ext = times_t(branch_late, weight_out).astype(BF)

    projection = times(attended, weight_out).reshape(tile_tokens.shape)
    block_output = (tile_tokens.astype(F32) + tissue_mask * projection).astype(BF)

    stats_ext, one, two = lax.optimization_barrier((stats_ext, one, two))
    groups = HEADS // GROUP
    grad_keys, grad_values = run_keys(
        place, key_ext, value_ext, query_ext, grad_ext, stats_ext, head_dim, tile, 0, groups
    )
    first_sums = later_halvings(one, two)
    second_sums = later_halvings(
        first_halving(normed_pair, whole_swap(grad_keys), True),
        first_halving(normed_pair, whole_swap(grad_values), False),
    )

    grad_projected = jnp.concatenate([grad_queries, grad_keys, grad_values], axis=-1)
    scaled = times_t(grad_projected, weight_in) * norm_gain
    first_mean = jnp.mean(scaled, axis=-1, keepdims=True)
    second_mean = jnp.mean(scaled * normalized, axis=-1, keepdims=True)
    input_grad = inverse * (scaled - first_mean - normalized * second_mean)
    input_grad = (upstream + input_grad.reshape(tile_tokens.shape)).astype(BF)

    inv_root = 1.0 / math.sqrt(slides * rows_count * cols_count * token_count)
    width = model_width
    weight_grads = jnp.concatenate(
        [first_sums[:, :width], second_sums, first_sums[:, width:]], axis=1
    )
    return (block_output[None], input_grad[None], weight_grads * inv_root)


def solution(mesh):
    tile = P("slide", "gy", "gx", None)
    return jax.shard_map(
        local,
        mesh=mesh,
        in_specs=(tile, P(), P(), P("slide", "gy", "gx"), tile),
        out_specs=(tile, tile, P(("slide", "gy", "gx"), None)),
        check_vma=False,
    )
```

time: 720 us -> 158 us (0.22); the launches traced: 711 us -> 157 us
  waiting for transfers between devices: 275 us -> 44.7 us
  local copies, waits for them, and re-layouts: 180 us -> 8.27 us
  matrix products: 124 us -> 23.9 us
  other arithmetic: 60.2 us -> 19.2 us
  loops' own time: 29.5 us -> 0 us
  Pallas kernels: 0 us -> 17.8 us
  starting transfers between devices: 27.5 us -> 41.4 us
  between operations: 14.7 us -> 1.55 us
    reduce_scatter x2 -> x0, waiting for transfers between devices: 212 us -> none  [the longest x1 160 us: local(): lax.psum_scatter(lax.dot_general(part_rows, grad_projected, (((0,), (0,))...]
    dot_general x18 -> x16, matrix products: 124 us -> 23.9 us  [the longest x5 11.1 us: times(): return jnp.dot(left, right, preferred_element_type=F32)]
    while x52 -> x0, local copies, waits for them, and re-layouts: 36.3 us -> none
    transpose x8 -> x0, local copies, waits for them, and re-layouts: 33 us -> none  [the longest x4 25.6 us: contract(): jnp.einsum(pattern, left_operand, second, preferred_element_type=jnp.floa...]
    slice x15 -> x4, local copies, waits for them, and re-layouts: 32.4 us -> 1.1 us  [the longest x3 1.09 us: column_halo(): right = moved(block[:, :SIDE], 'gx', -1)]
    another operation x1 -> x0, loops' own time: 29.5 us -> none  [run_strips(): return lax.fori_loop(0, tile_rows // 8, strip_step, start_carry)]
    concatenate x4 -> x3, local copies, waits for them, and re-layouts: 25.9 us -> 0.11 us  [whole_swap(): return jnp.concatenate([array, slide_swap(array, False)], axis=0)]
    scatter-add x6 -> x0, local copies, waits for them, and re-layouts: 20.8 us -> none  [the longest x1 9.29 us: local(): column_fold = column_fold.at[:, :RADIUS].add(arrived)]
  transfers between devices with their start and end apart: 10 -> 29, of which waited for: 9 -> 13; matrix products, arithmetic and copies ran while one was open for 8% -> 30% of each run, Pallas kernels for 0% -> 7%
where the time goes in v1:
time: 158 us; the launch traced here: 157 us
  waiting for transfers between devices  44.7 us (28%)
  starting transfers between devices  41.4 us (26%)
  matrix products  23.9 us (15%)
  other arithmetic  19.2 us (12%)
  Pallas kernels  17.8 us (11%)
  local copies, waits for them, and re-layouts  8.27 us (5%)
    ppermute x23, waiting for transfers between devices, swapped(): return lax.ppermute(array, axis, [(i, i ^ by) for i in range(count)])  39.6 us
    ppermute x23, starting transfers between devices, swapped(): return lax.ppermute(array, axis, [(i, i ^ by) for i in range(count)])  24.1 us
    ppermute x6, starting transfers between devices, moved(): return lax.ppermute(array, axis, pairs)  17.4 us
    dot_general x5, matrix products, times(): return jnp.dot(left, right, preferred_element_type=F32)  11.1 us
    pallas_call x1, Pallas kernels, run_queries(): pl.pallas_call(functools.partial(query_pass, head_dim, tile), grid=(group...  10.3 us
    pallas_call x1, Pallas kernels, run_keys(): pl.pallas_call(functools.partial(key_pass, head_dim, tile, first), grid=(...  7.51 us
    dot_general x3, matrix products, times_t(): lax.dot_general(left, right, (((1,), (1,)), ((), ())), preferred_element_...  6.7 us
    dot_general x8, matrix products, product_t(): lax.dot_general(left, right, (((0,), (0,)), ((), ())), preferred_element_...  6.12 us
  transfers between devices with their start and end apart: 29, of which 13 were waited for; matrix products, arithmetic and copies ran while one was open for 30% of the time, Pallas kernels for 7%

profile of v1, /device:TPU:0, one launch (start us, length us, event | category | flops | bytes accessed | tf_op | source)
XLA Modules:
  0.0 156.9 jit_solution(16393631894415622573)
XLA Ops:
  0.7 1.1 select_bitcast_fusion
  1.8 3.0 %collective-permute-start = (bf16[6,16,1024]{2,1,0:T(8,128)(2,1)S(1)}, bf16[6,16,1024]{2,1,0:T(8,128)(2,1)}, u32[]{:S(2)}, u32[]{:S(2)}) collective-permute-start(bf16[6,16,1024]{2,1,0:T(8,128)(2,1)S(1)} %select_bitcast_fusion), channel_id=1, source_target_pairs={{0,4},{4,0},{1,5},{5,1},{2,6},{6,2},{3,7},{7,3},{8,12},{12,8},{9,1... | collective-permute-start | bytes 589832 | tf_op jit(solution)/shard_map/ppermute | solution.py:23
  4.8 1.2 convert_reduce_fusion
  6.0 1.3 multiply_reduce_fusion.2
  7.5 1.3 multiply_convert_fusion
  8.8 0.8 constant_dynamic-slice_fusion.15
  9.8 0.9 fusion.44
  11.3 2.3 %fusion.40.q_ref = bf16[256,1024]{1,0:T(8,128)(2,1)S(1)} fusion(bf16[256,1024]{1,0:T(8,128)(2,1)S(1)} %multiply_convert_fusion, bf16[1024,4096]{1,0:T(8,128)(2,1)} %param.6), kind=kOutput, calls=%fused_computation.57 | convolution fusion | flops 537133056 | bytes 3145728 | tf_op jit(solution)/shard_map/dot_general | solution.py:68
  13.6 2.6 %fusion.37.g_ref = bf16[256,1024]{1,0:T(8,128)(2,1)S(1)} fusion(bf16[256,1024]{1,0:T(8,128)(2,1)} %fusion.44, bf16[1024,4096]{1,0:T(8,128)(2,1)} %param.6), kind=kOutput, calls=%fused_computation.56 | convolution fusion | flops 537133056 | bytes 3145728 | tf_op jit(solution)/shard_map/dot_general | solution.py:72
  16.4 1.0 broadcast_select_fusion.3
  17.6 3.5 %collective-permute-start.2 = (bf16[28,8,1024]{2,1,0:T(8,128)(2,1)S(1)}, bf16[28,8,1024]{2,1,0:T(8,128)(2,1)S(1)}, u32[]{:S(2)}, u32[]{:S(2)}) collective-permute-start(bf16[28,8,1024]{2,1,0:T(8,128)(2,1)S(1)} %get-tuple-element.36), channel_id=1, source_target_pairs={{0,1},{1,2},{2,3},{4,5},{5,6},{6,7},{8,9},{9,10},{10,11},{12,13},{... | collective-permute-start | bytes 1376264 | tf_op jit(solution)/shard_map/ppermute | solution.py:29
  21.1 1.3 collective-permute-start.1
  23.0 0.7 copy-done.10
  23.7 1.1 pad_maximum_fusion.6
  24.8 0.9 constant_dynamic-slice_fusion.3
  25.7 3.4 %collective-permute-done.3 = bf16[6,16,1024]{2,1,0:T(8,128)(2,1)S(1)} collective-permute-done((bf16[6,16,1024]{2,1,0:T(8,128)(2,1)S(1)}, bf16[6,16,1024]{2,1,0:T(8,128)(2,1)S(1)}, u32[]{:S(2)}, u32[]{:S(2)}) %collective-permute-start.3) | collective-permute-done | bytes 196640 | tf_op jit(solution)/shard_map/ppermute | solution.py:23
  29.3 1.0 fusion.93
  30.3 5.0 %collective-permute-start.5 = (bf16[28,8,1024]{2,1,0:T(8,128)(2,1)}, bf16[28,8,1024]{2,1,0:T(8,128)(2,1)}, u32[]{:S(2)}, u32[]{:S(2)}) collective-permute-start(bf16[28,8,1024]{2,1,0:T(8,128)(2,1)} %get-tuple-element.34), channel_id=1, source_target_pairs={{0,1},{1,2},{2,3},{4,5},{5,6},{6,7},{8,9},{9,10},{10,11},{12,13},{... | collective-permute-start | bytes 1376264 | tf_op jit(solution)/shard_map/ppermute | solution.py:29
  35.3 1.5 collective-permute-start.4
  36.8 0.7 copy-done.2
  38.9 1.4 div.37
  40.3 2.1 %multiply_reduce_fusion = f32[28,32]{1,0:T(8,128)S(1)} fusion(f32[28,32]{1,0:T(8,128)} %broadcast_multiply_fusion, bf16[28,8,1024]{2,1,0:T(8,128)(2,1)} %copy-done.2, bf16[28,8,1024]{2,1,0:T(8,128)(2,1)} %copy-done.3, bf16[6,16,1024]{2,1,0:T(8,128)(2,1)S(1)} %get-tuple-element.60, bf16[16,16,1024]{2,1,0:T(8,128)(2,1)S(1)} %bitcast.57, ...), kind=kLoop, calls=%fused_computation.6 | loop fusion | flops 11926656 | bytes 1842176 | tf_op jit(solution)/shard_map/reduce_sum | solution.py:379
  43.0 1.4 rsqrt.25
  44.4 1.6 maximum_convert_fusion
  46.6 3.9 %fusion.16.k_ref = bf16[896,1024]{1,0:T(8,128)(2,1)S(1)} fusion(bf16[896,1024]{1,0:T(8,128)(2,1)S(1)} %fusion.4, bf16[1024,4096]{1,0:T(8,128)(2,1)} %param.6), kind=kOutput, calls=%fused_computation.18 | convolution fusion | flops 1879965696 | bytes 5767168 | tf_op jit(solution)/shard_map/dot_general | solution.py:68
  50.5 2.1 %fusion.19.v_ref = bf16[896,1024]{1,0:T(8,128)(2,1)S(1)} fusion(bf16[896,1024]{1,0:T(8,128)(2,1)S(1)} %fusion.4, bf16[1024,4096]{1,0:T(8,128)(2,1)S(1)} %bitcast.64), kind=kOutput, calls=%fused_computation.19 | convolution fusion | flops 1879965696 | bytes 5767168 | tf_op jit(solution)/shard_map/dot_general | solution.py:68
  52.6 10.3 %query_pass.1 = (bf16[256,1024]{1,0:T(8,128)(2,1)S(1)}, bf16[256,1024]{1,0:T(8,128)(2,1)S(1)}, f32[256,128]{1,0:T(8,128)S(1)}) custom-call(s32[4]{0:T(128)S(1)} %pad_add_fusion.place_ref, bf16[256,1024]{1,0:T(8,128)(2,1)S(1)} %fusion.40.q_ref, bf16[256,1024]{1,0:T(8,128)(2,1)S(1)} %fusion.37.g_ref, bf16[896,1024]{1,0:T(8,128)(2,1)S(1)} %fusion.16.k_ref, ...), custom_call_target="tpu_custom_call" | custom-call | flops 4294967296 | bytes 4194304 | tf_op jit(solution)/shard_map/query_pass/pallas_call | solution.py:225
  63.0 0.7 fusion.23
  63.8 1.0 add_convert_fusion.1
  65.3 3.6 %collective-permute-done.6 = f32[6,16,128]{2,1,0:T(8,128)S(1)} collective-permute-done((f32[6,16,128]{2,1,0:T(8,128)S(1)}, f32[6,16,128]{2,1,0:T(8,128)S(1)}, u32[]{:S(2)}, u32[]{:S(2)}) %collective-permute-start.6) | collective-permute-done | bytes 49184 | tf_op jit(solution)/shard_map/ppermute | solution.py:23
  69.0 4.6 %collective-permute-start.8 = (f32[28,8,128]{2,1,0:T(8,128)S(1)}, f32[28,8,128]{2,1,0:T(8,128)S(1)}, u32[]{:S(2)}, u32[]{:S(2)}) collective-permute-start(f32[28,8,128]{2,1,0:T(8,128)S(1)} %get-tuple-element.56), channel_id=1, source_target_pairs={{0,1},{1,2},{2,3},{4,5},{5,6},{6,7},{8,9},{9,10},{10,11},{12,13},{... | collective-permute-start | bytes 344072 | tf_op jit(solution)/shard_map/ppermute | solution.py:29
  73.5 1.5 collective-permute-start.7
  75.1 0.8 collective-permute-done.8
  75.9 4.3 %collective-permute-done.7 = f32[28,8,128]{2,1,0:T(8,128)S(1)} collective-permute-done((f32[28,8,128]{2,1,0:T(8,128)S(1)}, f32[28,8,128]{2,1,0:T(8,128)S(1)}, u32[]{:S(2)}, u32[]{:S(2)}) %collective-permute-start.7) | collective-permute-done | bytes 114720 | tf_op jit(solution)/shard_map/ppermute | solution.py:29
  80.3 1.3 pad_maximum_fusion
  81.6 2.1 %fusion.13.q_ref = bf16[896,1024]{1,0:T(8,128)(2,1)S(1)} fusion(bf16[896,1024]{1,0:T(8,128)(2,1)S(1)} %fusion.4, bf16[1024,4096]{1,0:T(8,128)(2,1)S(1)} %bitcast.64), kind=kOutput, calls=%fused_computation.17 | convolution fusion | flops 1879965696 | bytes 5767168 | tf_op jit(solution)/shard_map/dot_general | solution.py:68
  83.9 1.7 %convolution_convert_fusion.3 = bf16[256,1024]{1,0:T(8,128)(2,1)S(1)} fusion(bf16[256,1024]{1,0:T(8,128)(2,1)} %collective-permute-done.13, bf16[256,1024]{1,0:T(8,128)(2,1)} %fusion.44, bf16[512,128]{1,0:T(8,128)(2,1)S(1)} %get-tuple-element.42, bf16[512,128]{1,0:T(8,128)(2,1)S(1)} %get-tuple-element.43), kind=kOutput, calls=%fused_computation.54 | convolution fusion | flops 271319040 | bytes 1835008 | tf_op jit(solution)/shard_map/dot_general | solution.py:273
  86.7 1.5 collective-permute-start.11
  88.2 2.1 %convolution_convert_fusion.g_ref = bf16[896,1024]{1,0:T(8,128)(2,1)S(1)} fusion(bf16[896,1024]{1,0:T(8,128)(2,1)S(1)} %bitcast.60, bf16[1024,4096]{1,0:T(8,128)(2,1)S(1)} %bitcast.64), kind=kOutput, calls=%fused_computation.20 | convolution fusion | flops 1879965696 | bytes 5767168 | tf_op jit(solution)/shard_map/dot_general | solution.py:72
  90.3 9.7 %collective-permute-done.14 = bf16[256,1024]{1,0:T(8,128)(2,1)S(1)} collective-permute-done((bf16[256,1024]{1,0:T(8,128)(2,1)S(1)}, bf16[256,1024]{1,0:T(8,128)(2,1)S(1)}, u32[]{:S(2)}, u32[]{:S(2)}) %collective-permute-start.14) | collective-permute-done | bytes 524320 | tf_op jit(solution)/shard_map/ppermute | solution.py:23
  100.0 1.7 %convolution_add_fusion.2 = f32[256,1024]{1,0:T(8,128)S(1)} fusion(bf16[256,1024]{1,0:T(8,128)(2,1)S(1)} %collective-permute-done.14, bf16[256,1024]{1,0:T(8,128)(2,1)} %collective-permute-done.13, bf16[256,1024]{1,0:T(8,128)(2,1)} %fusion.44, bf16[512,128]{1,0:T(8,128)(2,1)S(1)} %get-tuple-element.44, bf16[512,128]{1,0:T(8,128)(2,1)S(1)} %get-tuple-element.41), kind=kOutput, calls=%fused_computation.49 | convolution fusion | flops 271581184 | bytes 2883584 | tf_op jit(solution)/shard_map/dot_general | solution.py:273
  102.2 7.5 %key_pass.1 = (bf16[256,1024]{1,0:T(8,128)(2,1)S(1)}, bf16[256,1024]{1,0:T(8,128)(2,1)S(1)}) custom-call(s32[4]{0:T(128)S(1)} %pad_add_fusion.place_ref, bf16[896,1024]{1,0:T(8,128)(2,1)S(1)} %fusion.16.k_ref, bf16[896,1024]{1,0:T(8,128)(2,1)S(1)} %fusion.19.v_ref, bf16[896,1024]{1,0:T(8,128)(2,1)S(1)} %fusion.13.q_ref, ...), custom_call_target="tpu_custom_call" | custom-call | flops 4294967296 | bytes 4194304 | tf_op jit(solution)/shard_map/key_pass/pallas_call | solution.py:252
  109.8 2.0 %fusion.92 = (f32[256]{0:T(256)S(1)}, f32[256]{0:T(256)S(1)}, f32[256,1024]{1,0:T(8,128)S(1)}) fusion(f32[256]{0:T(256)S(1)} %copy-done.19, f32[256]{0:T(256)S(1)} %copy-done.17, bf16[1,16,16,1024]{3,2,1,0:T(8,128)(2,1)S(1)} %copy-done, f32[1024]{0:T(1024)S(1)} %copy-done.13, bf16[1024,4096]{1,0:T(8,128)(2,1)S(1)} %bitcast.64, ...), kind=kOutput, calls=%fused_computation.174 | convolution fusion | flops 1617165824 | bytes 9445376 | tf_op jit(solution)/shard_map/dot_general | solution.py:72
  112.4 0.7 collective-permute-start.15
  113.5 0.9 add_convert_fusion
  114.4 1.5 collective-permute-start.16
  116.1 4.6 %collective-permute-done.15 = bf16[128,1024]{1,0:T(8,128)(2,1)S(1)} collective-permute-done((bf16[128,1024]{1,0:T(8,128)(2,1)S(1)}, bf16[128,1024]{1,0:T(8,128)(2,1)S(1)}, u32[]{:S(2)}, u32[]{:S(2)}) %collective-permute-start.15) | collective-permute-done | bytes 262176 | tf_op jit(solution)/shard_map/ppermute | solution.py:23
  120.8 1.7 %collective-permute-done.16 = bf16[128,1024]{1,0:T(8,128)(2,1)S(1)} collective-permute-done((bf16[128,1024]{1,0:T(8,128)(2,1)S(1)}, bf16[128,1024]{1,0:T(8,128)(2,1)S(1)}, u32[]{:S(2)}, u32[]{:S(2)}) %collective-permute-start.16) | collective-permute-done | bytes 262176 | tf_op jit(solution)/shard_map/ppermute | solution.py:23
  123.1 1.5 collective-permute-start.21
  125.2 1.4 collective-permute-start.24
  126.6 1.0 collective-permute-start.19
  127.7 1.5 collective-permute-start.18
  129.2 1.9 %collective-permute-start.17 = (bf16[32,2048]{1,0:T(8,128)(2,1)S(1)}, bf16[32,2048]{1,0:T(8,128)(2,1)S(1)}, u32[]{:S(2)}, u32[]{:S(2)}) collective-permute-start(bf16[32,2048]{1,0:T(8,128)(2,1)S(1)} %get-tuple-element.30), channel_id=1, source_target_pairs={{0,3},{1,2},{2,1},{3,0},{4,7},{5,6},{6,5},{7,4},{8,11},{9,10},{10,... | collective-permute-start | bytes 393224 | tf_op jit(solution)/shard_map/ppermute | solution.py:23
  131.1 4.7 %collective-permute-done.21 = bf16[256,1024]{1,0:T(8,128)(2,1)S(1)} collective-permute-done((bf16[256,1024]{1,0:T(8,128)(2,1)S(1)}, bf16[256,1024]{1,0:T(8,128)(2,1)S(1)}, u32[]{:S(2)}, u32[]{:S(2)}) %collective-permute-start.21) | collective-permute-done | bytes 524320 | tf_op jit(solution)/shard_map/ppermute | solution.py:23
  136.4 1.4 collective-permute-start.22
  138.8 1.1 collective-permute-start.25
  140.0 3.3 %collective-permute-done.22 = bf16[128,1024]{1,0:T(8,128)(2,1)S(1)} collective-permute-done((bf16[128,1024]{1,0:T(8,128)(2,1)S(1)}, bf16[128,1024]{1,0:T(8,128)(2,1)S(1)}, u32[]{:S(2)}, u32[]{:S(2)}) %collective-permute-start.22) | collective-permute-done | bytes 262176 | tf_op jit(solution)/shard_map/ppermute | solution.py:23
  143.3 1.9 %collective-permute-done.25 = bf16[128,1024]{1,0:T(8,128)(2,1)S(1)} collective-permute-done((bf16[128,1024]{1,0:T(8,128)(2,1)S(1)}, bf16[128,1024]{1,0:T(8,128)(2,1)S(1)}, u32[]{:S(2)}, u32[]{:S(2)}) %collective-permute-start.25) | collective-permute-done | bytes 262176 | tf_op jit(solution)/shard_map/ppermute | solution.py:23
  145.3 1.0 collective-permute-start.28
  146.3 1.5 collective-permute-start.27
  147.9 1.9 %collective-permute-start.26 = (bf16[32,2048]{1,0:T(8,128)(2,1)S(1)}, bf16[32,2048]{1,0:T(8,128)(2,1)S(1)}, u32[]{:S(2)}, u32[]{:S(2)}) collective-permute-start(bf16[32,2048]{1,0:T(8,128)(2,1)S(1)} %get-tuple-element.27), channel_id=1, source_target_pairs={{0,3},{1,2},{2,1},{3,0},{4,7},{5,6},{6,5},{7,4},{8,11},{9,10},{10,... | collective-permute-start | bytes 393224 | tf_op jit(solution)/shard_map/ppermute | solution.py:23
  149.8 2.7 %collective-permute-done.28 = bf16[32,2048]{1,0:T(8,128)(2,1)S(1)} collective-permute-done((bf16[32,2048]{1,0:T(8,128)(2,1)S(1)}, bf16[32,2048]{1,0:T(8,128)(2,1)S(1)}, u32[]{:S(2)}, u32[]{:S(2)}) %collective-permute-start.28) | collective-permute-done | bytes 131104 | tf_op jit(solution)/shard_map/ppermute | solution.py:23
  152.5 3.5 %collective-permute-done.27 = bf16[32,2048]{1,0:T(8,128)(2,1)S(1)} collective-permute-done((bf16[32,2048]{1,0:T(8,128)(2,1)S(1)}, bf16[32,2048]{1,0:T(8,128)(2,1)S(1)}, u32[]{:S(2)}, u32[]{:S(2)}) %collective-permute-start.27) | collective-permute-done | bytes 131104 | tf_op jit(solution)/shard_map/ppermute | solution.py:23
  156.1 0.8 maximum_multiply_fusion
  (124 shorter events, 11.0 us)
Async XLA Ops:
  0.6 9.1 %copy-start.20 = (s32[1,16,16]{2,1,0:T(8,128)S(1)}, s32[1,16,16]{2,1,0:T(8,128)}, u32[]{:S(2)}) copy-start(s32[1,16,16]{2,1,0:T(8,128)} %param.8) | copy-start | bytes 3076
  0.6 9.2 %copy-start.1 = (bf16[1,16,16,1024]{3,2,1,0:T(8,128)(2,1)S(1)}, bf16[1,16,16,1024]{3,2,1,0:T(8,128)(2,1)}, u32[]{:S(2)}) copy-start(bf16[1,16,16,1024]{3,2,1,0:T(8,128)(2,1)} %param.9) | copy-start | bytes 1572868
  1.8 14.7 %collective-permute-start = (bf16[6,16,1024]{2,1,0:T(8,128)(2,1)S(1)}, bf16[6,16,1024]{2,1,0:T(8,128)(2,1)}, u32[]{:S(2)}, u32[]{:S(2)}) collective-permute-start(bf16[6,16,1024]{2,1,0:T(8,128)(2,1)S(1)} %select_bitcast_fusion), channel_id=1, source_target_pairs={{0,4},{4,0},{1,5},{5,1},{2,6},{6,2},{3,7},{7,3},{8,12},{12,8},{9,1... | collective-permute-start | bytes 589832 | tf_op jit(solution)/shard_map/ppermute | solution.py:23
  7.4 2.2 %copy-start.16 = (f32[256]{0:T(256)}, f32[256]{0:T(256)S(1)}, u32[]{:S(2)}) copy-start(f32[256]{0:T(256)S(1)} %div.34) | copy-start | bytes 3076
  7.5 2.1 %copy-start.18 = (f32[256]{0:T(256)}, f32[256]{0:T(256)S(1)}, u32[]{:S(2)}) copy-start(f32[256]{0:T(256)S(1)} %rsqrt.23) | copy-start | bytes 3076
  9.6 13.4 %collective-permute-start.9 = (bf16[256,512]{1,0:T(8,128)(2,1)S(1)}, bf16[256,512]{1,0:T(8,128)(2,1)S(1)}, u32[]{:S(2)}, u32[]{:S(2)}) collective-permute-start(bf16[256,512]{1,0:T(8,128)(2,1)S(1)} %pad_maximum_fusion.9), channel_id=1, source_target_pairs={{0,8},{8,0},{16,24},{24,16},{1,9},{9,1},{17,25},{25,17},{2,10},{10... | collective-permute-start | bytes 786440 | tf_op jit(solution)/shard_map/ppermute | solution.py:23
  10.8 73.1 %collective-permute-start.13 = (bf16[256,1024]{1,0:T(8,128)(2,1)}, bf16[256,1024]{1,0:T(8,128)(2,1)}, u32[]{:S(2)}, u32[]{:S(2)}) collective-permute-start(bf16[256,1024]{1,0:T(8,128)(2,1)} %fusion.44), channel_id=1, source_target_pairs={{0,8},{8,0},{16,24},{24,16},{1,9},{9,1},{17,25},{25,17},{2,10},{10... | collective-permute-start | bytes 1572872 | tf_op jit(solution)/shard_map/ppermute | solution.py:23
  13.6 3.9 %copy-start = (bf16[1,16,16,1024]{3,2,1,0:T(8,128)(2,1)S(1)}, bf16[1,16,16,1024]{3,2,1,0:T(8,128)(2,1)}, u32[]{:S(2)}) copy-start(bf16[1,16,16,1024]{3,2,1,0:T(8,128)(2,1)} %param.5) | copy-start | bytes 1572868
  17.6 19.2 %collective-permute-start.2 = (bf16[28,8,1024]{2,1,0:T(8,128)(2,1)S(1)}, bf16[28,8,1024]{2,1,0:T(8,128)(2,1)S(1)}, u32[]{:S(2)}, u32[]{:S(2)}) collective-permute-start(bf16[28,8,1024]{2,1,0:T(8,128)(2,1)S(1)} %get-tuple-element.36), channel_id=1, source_target_pairs={{0,1},{1,2},{2,3},{4,5},{5,6},{6,7},{8,9},{9,10},{10,11},{12,13},{... | collective-permute-start | bytes 1376264 | tf_op jit(solution)/shard_map/ppermute | solution.py:29
  21.1 15.7 %collective-permute-start.1 = (bf16[28,8,1024]{2,1,0:T(8,128)(2,1)S(1)}, bf16[28,8,1024]{2,1,0:T(8,128)(2,1)S(1)}, u32[]{:S(2)}, u32[]{:S(2)}) collective-permute-start(bf16[28,8,1024]{2,1,0:T(8,128)(2,1)S(1)} %get-tuple-element.35), channel_id=1, source_target_pairs={{1,0},{2,1},{3,2},{5,4},{6,5},{7,6},{9,8},{10,9},{11,10},{13,12},{... | collective-permute-start | bytes 1376264 | tf_op jit(solution)/shard_map/ppermute | solution.py:29
  22.5 6.6 %collective-permute-start.3 = (bf16[6,16,1024]{2,1,0:T(8,128)(2,1)S(1)}, bf16[6,16,1024]{2,1,0:T(8,128)(2,1)S(1)}, u32[]{:S(2)}, u32[]{:S(2)}) collective-permute-start(bf16[6,16,1024]{2,1,0:T(8,128)(2,1)S(1)} %slice_select_fusion), channel_id=1, source_target_pairs={{0,4},{4,0},{1,5},{5,1},{2,6},{6,2},{3,7},{7,3},{8,12},{12,8},{9,1... | collective-permute-start | bytes 589832 | tf_op jit(solution)/shard_map/ppermute | solution.py:23
  23.0 0.7 copy-start.10
  29.1 7.7 %copy-start.4 = (bf16[6,16,1024]{2,1,0:T(8,128)(2,1)}, bf16[6,16,1024]{2,1,0:T(8,128)(2,1)S(1)}, u32[]{:S(2)}) copy-start(bf16[6,16,1024]{2,1,0:T(8,128)(2,1)S(1)} %get-tuple-element.57) | copy-start | bytes 589828
  29.1 7.7 %copy-start.6 = (bf16[6,16,1024]{2,1,0:T(8,128)(2,1)}, bf16[6,16,1024]{2,1,0:T(8,128)(2,1)S(1)}, u32[]{:S(2)}) copy-start(bf16[6,16,1024]{2,1,0:T(8,128)(2,1)S(1)} %get-tuple-element.58) | copy-start | bytes 589828
  30.3 50.0 %collective-permute-start.5 = (bf16[28,8,1024]{2,1,0:T(8,128)(2,1)}, bf16[28,8,1024]{2,1,0:T(8,128)(2,1)}, u32[]{:S(2)}, u32[]{:S(2)}) collective-permute-start(bf16[28,8,1024]{2,1,0:T(8,128)(2,1)} %get-tuple-element.34), channel_id=1, source_target_pairs={{0,1},{1,2},{2,3},{4,5},{5,6},{6,7},{8,9},{9,10},{10,11},{12,13},{... | collective-permute-start | bytes 1376264 | tf_op jit(solution)/shard_map/ppermute | solution.py:29
  35.3 45.0 %collective-permute-start.4 = (bf16[28,8,1024]{2,1,0:T(8,128)(2,1)}, bf16[28,8,1024]{2,1,0:T(8,128)(2,1)}, u32[]{:S(2)}, u32[]{:S(2)}) collective-permute-start(bf16[28,8,1024]{2,1,0:T(8,128)(2,1)} %get-tuple-element.33), channel_id=1, source_target_pairs={{1,0},{2,1},{3,2},{5,4},{6,5},{7,6},{9,8},{10,9},{11,10},{13,12},{... | collective-permute-start | bytes 1376264 | tf_op jit(solution)/shard_map/ppermute | solution.py:29
  36.8 0.8 copy-start.2
  37.6 0.8 copy-start.3
  42.4 3.6 %copy-start.13 = (f32[1024]{0:T(1024)S(1)}, f32[1024]{0:T(1024)}, u32[]{:S(2)}) copy-start(f32[1024]{0:T(1024)} %param.7) | copy-start | bytes 12292
  44.4 1.6 %copy-start.14 = (f32[896]{0:T(1024)S(1)}, f32[896]{0:T(1024)}, u32[]{:S(2)}) copy-start(f32[896]{0:T(1024)} %div.37) | copy-start | bytes 10756
  44.4 1.6 %copy-start.15 = (f32[896]{0:T(1024)S(1)}, f32[896]{0:T(1024)}, u32[]{:S(2)}) copy-start(f32[896]{0:T(1024)} %rsqrt.25) | copy-start | bytes 10756
  46.0 4.5 %slice-start = ((s8[8388608]{0:T(1024)(128)(4,1)}), s8[4194304]{0:T(1024)(128)(4,1)S(1)}, s32[]{:S(2)}) async-start(s8[8388608]{0:T(1024)(128)(4,1)} %bitcast.63), calls=%async_computation | async-start | bytes 8388608
  46.6 3.9 %slice-start.1 = ((s8[8388608]{0:T(1024)(128)(4,1)}), s8[4194304]{0:T(1024)(128)(4,1)S(1)}, s32[]{:S(2)}) async-start(s8[8388608]{0:T(1024)(128)(4,1)} %bitcast.63), calls=%async_computation.1 | async-start | bytes 8388608
  63.8 16.5 %copy-start.5 = (bf16[6,16,1024]{2,1,0:T(8,128)(2,1)S(1)}, bf16[6,16,1024]{2,1,0:T(8,128)(2,1)}, u32[]{:S(2)}) copy-start(bf16[6,16,1024]{2,1,0:T(8,128)(2,1)} %copy-done.4) | copy-start | bytes 589828
  63.8 16.5 %copy-start.7 = (bf16[6,16,1024]{2,1,0:T(8,128)(2,1)S(1)}, bf16[6,16,1024]{2,1,0:T(8,128)(2,1)}, u32[]{:S(2)}) copy-start(bf16[6,16,1024]{2,1,0:T(8,128)(2,1)} %copy-done.6) | copy-start | bytes 589828
  64.8 4.1 %collective-permute-start.6 = (f32[6,16,128]{2,1,0:T(8,128)S(1)}, f32[6,16,128]{2,1,0:T(8,128)S(1)}, u32[]{:S(2)}, u32[]{:S(2)}) collective-permute-start(f32[6,16,128]{2,1,0:T(8,128)S(1)} %bitcast.62), channel_id=1, source_target_pairs={{0,4},{4,0},{1,5},{5,1},{2,6},{6,2},{3,7},{7,3},{8,12},{12,8},{9,1... | collective-permute-start | bytes 147464 | tf_op jit(solution)/shard_map/ppermute | solution.py:23
  69.0 6.9 %collective-permute-start.8 = (f32[28,8,128]{2,1,0:T(8,128)S(1)}, f32[28,8,128]{2,1,0:T(8,128)S(1)}, u32[]{:S(2)}, u32[]{:S(2)}) collective-permute-start(f32[28,8,128]{2,1,0:T(8,128)S(1)} %get-tuple-element.56), channel_id=1, source_target_pairs={{0,1},{1,2},{2,3},{4,5},{5,6},{6,7},{8,9},{9,10},{10,11},{12,13},{... | collective-permute-start | bytes 344072 | tf_op jit(solution)/shard_map/ppermute | solution.py:29
  73.5 6.7 %collective-permute-start.7 = (f32[28,8,128]{2,1,0:T(8,128)S(1)}, f32[28,8,128]{2,1,0:T(8,128)S(1)}, u32[]{:S(2)}, u32[]{:S(2)}) collective-permute-start(f32[28,8,128]{2,1,0:T(8,128)S(1)} %get-tuple-element.55), channel_id=1, source_target_pairs={{1,0},{2,1},{3,2},{5,4},{6,5},{7,6},{9,8},{10,9},{11,10},{13,12},{... | collective-permute-start | bytes 344072 | tf_op jit(solution)/shard_map/ppermute | solution.py:29
  75.9 10.3 %collective-permute-start.10 = (bf16[256,1024]{1,0:T(8,128)(2,1)S(1)}, bf16[256,1024]{1,0:T(8,128)(2,1)S(1)}, u32[]{:S(2)}, u32[]{:S(2)}) collective-permute-start(bf16[256,1024]{1,0:T(8,128)(2,1)S(1)} %get-tuple-element.15), channel_id=1, source_target_pairs={{0,8},{8,0},{16,24},{24,16},{1,9},{9,1},{17,25},{25,17},{2,10},{10... | collective-permute-start | bytes 1572872 | tf_op jit(solution)/shard_map/ppermute | solution.py:23
  80.2 3.5 %collective-permute-start.12 = (bf16[256,512]{1,0:T(8,128)(2,1)S(1)}, bf16[256,512]{1,0:T(8,128)(2,1)S(1)}, u32[]{:S(2)}, u32[]{:S(2)}) collective-permute-start(bf16[256,512]{1,0:T(8,128)(2,1)S(1)} %pad_maximum_fusion.10), channel_id=1, source_target_pairs={{0,8},{8,0},{16,24},{24,16},{1,9},{9,1},{17,25},{25,17},{2,10},{10... | collective-permute-start | bytes 786440 | tf_op jit(solution)/shard_map/ppermute | solution.py:23
  85.6 14.4 %collective-permute-start.14 = (bf16[256,1024]{1,0:T(8,128)(2,1)S(1)}, bf16[256,1024]{1,0:T(8,128)(2,1)S(1)}, u32[]{:S(2)}, u32[]{:S(2)}) collective-permute-start(bf16[256,1024]{1,0:T(8,128)(2,1)S(1)} %convolution_convert_fusion.3), channel_id=1, source_target_pairs={{0,4},{4,0},{1,5},{5,1},{2,6},{6,2},{3,7},{7,3},{8,12},{12,8},{9,1... | collective-permute-start | bytes 1572872 | tf_op jit(solution)/shard_map/ppermute | solution.py:23
  86.7 15.0 %collective-permute-start.11 = (bf16[256,1024]{1,0:T(8,128)(2,1)S(1)}, bf16[256,1024]{1,0:T(8,128)(2,1)S(1)}, u32[]{:S(2)}, u32[]{:S(2)}) collective-permute-start(bf16[256,1024]{1,0:T(8,128)(2,1)S(1)} %convolution_convert_fusion.4), channel_id=1, source_target_pairs={{0,16},{8,24},{16,0},{24,8},{1,17},{9,25},{17,1},{25,9},{2,18},{10... | collective-permute-start | bytes 1572872 | tf_op jit(solution)/shard_map/ppermute | solution.py:23
  102.1 7.6 %copy-start.17 = (f32[256]{0:T(256)S(1)}, f32[256]{0:T(256)}, u32[]{:S(2)}) copy-start(f32[256]{0:T(256)} %copy-done.16) | copy-start | bytes 3076
  102.1 7.6 %copy-start.19 = (f32[256]{0:T(256)S(1)}, f32[256]{0:T(256)}, u32[]{:S(2)}) copy-start(f32[256]{0:T(256)} %copy-done.18) | copy-start | bytes 3076
  109.7 12.9 %collective-permute-start.20 = (bf16[256,1024]{1,0:T(8,128)(2,1)S(1)}, bf16[256,1024]{1,0:T(8,128)(2,1)S(1)}, u32[]{:S(2)}, u32[]{:S(2)}) collective-permute-start(bf16[256,1024]{1,0:T(8,128)(2,1)S(1)} %get-tuple-element.21), channel_id=1, source_target_pairs={{0,8},{8,0},{16,24},{24,16},{1,9},{9,1},{17,25},{25,17},{2,10},{10... | collective-permute-start | bytes 1572872 | tf_op jit(solution)/shard_map/ppermute | solution.py:23
  111.8 12.8 %collective-permute-start.23 = (bf16[256,1024]{1,0:T(8,128)(2,1)S(1)}, bf16[256,1024]{1,0:T(8,128)(2,1)S(1)}, u32[]{:S(2)}, u32[]{:S(2)}) collective-permute-start(bf16[256,1024]{1,0:T(8,128)(2,1)S(1)} %get-tuple-element.22), channel_id=1, source_target_pairs={{0,8},{8,0},{16,24},{24,16},{1,9},{9,1},{17,25},{25,17},{2,10},{10... | collective-permute-start | bytes 1572872 | tf_op jit(solution)/shard_map/ppermute | solution.py:23
  112.4 8.3 %collective-permute-start.15 = (bf16[128,1024]{1,0:T(8,128)(2,1)S(1)}, bf16[128,1024]{1,0:T(8,128)(2,1)S(1)}, u32[]{:S(2)}, u32[]{:S(2)}) collective-permute-start(bf16[128,1024]{1,0:T(8,128)(2,1)S(1)} %dynamic-slice_convert_fusion.3), channel_id=1, source_target_pairs={{0,4},{4,0},{1,5},{5,1},{2,6},{6,2},{3,7},{7,3},{8,12},{12,8},{9,1... | collective-permute-start | bytes 786440 | tf_op jit(solution)/shard_map/ppermute | solution.py:23
  114.4 8.0 %collective-permute-start.16 = (bf16[128,1024]{1,0:T(8,128)(2,1)S(1)}, bf16[128,1024]{1,0:T(8,128)(2,1)S(1)}, u32[]{:S(2)}, u32[]{:S(2)}) collective-permute-start(bf16[128,1024]{1,0:T(8,128)(2,1)S(1)} %dynamic-slice_convert_fusion.2), channel_id=1, source_target_pairs={{0,16},{8,24},{16,0},{24,8},{1,17},{9,25},{17,1},{25,9},{2,18},{10... | collective-permute-start | bytes 786440 | tf_op jit(solution)/shard_map/ppermute | solution.py:23
  116.1 8.6 %copy-start.11 = (bf16[512,128]{1,0:T(8,128)(2,1)S(1)}, bf16[512,128]{1,0:T(8,128)(2,1)}, u32[]{:S(2)}) copy-start(bf16[512,128]{1,0:T(8,128)(2,1)} %get-tuple-element.38) | copy-start | bytes 393220
  116.1 8.6 %copy-start.12 = (bf16[512,128]{1,0:T(8,128)(2,1)S(1)}, bf16[512,128]{1,0:T(8,128)(2,1)}, u32[]{:S(2)}) copy-start(bf16[512,128]{1,0:T(8,128)(2,1)} %get-tuple-element.39) | copy-start | bytes 393220
  123.1 12.8 %collective-permute-start.21 = (bf16[256,1024]{1,0:T(8,128)(2,1)S(1)}, bf16[256,1024]{1,0:T(8,128)(2,1)S(1)}, u32[]{:S(2)}, u32[]{:S(2)}) collective-permute-start(bf16[256,1024]{1,0:T(8,128)(2,1)S(1)} %convolution_convert_fusion.2), channel_id=1, source_target_pairs={{0,16},{8,24},{16,0},{24,8},{1,17},{9,25},{17,1},{25,9},{2,18},{10... | collective-permute-start | bytes 1572872 | tf_op jit(solution)/shard_map/ppermute | solution.py:23
  124.7 13.6 %copy-start.8 = (bf16[512,128]{1,0:T(8,128)(2,1)S(1)}, bf16[512,128]{1,0:T(8,128)(2,1)}, u32[]{:S(2)}) copy-start(bf16[512,128]{1,0:T(8,128)(2,1)} %get-tuple-element.37) | copy-start | bytes 393220
  124.7 13.6 %copy-start.9 = (bf16[512,128]{1,0:T(8,128)(2,1)S(1)}, bf16[512,128]{1,0:T(8,128)(2,1)}, u32[]{:S(2)}) copy-start(bf16[512,128]{1,0:T(8,128)(2,1)} %get-tuple-element.40) | copy-start | bytes 393220
  125.2 13.1 %collective-permute-start.24 = (bf16[256,1024]{1,0:T(8,128)(2,1)S(1)}, bf16[256,1024]{1,0:T(8,128)(2,1)S(1)}, u32[]{:S(2)}, u32[]{:S(2)}) collective-permute-start(bf16[256,1024]{1,0:T(8,128)(2,1)S(1)} %convolution_convert_fusion.1), channel_id=1, source_target_pairs={{0,4},{4,0},{1,5},{5,1},{2,6},{6,2},{3,7},{7,3},{8,12},{12,8},{9,1... | collective-permute-start | bytes 1572872 | tf_op jit(solution)/shard_map/ppermute | solution.py:23
  126.6 13.2 %collective-permute-start.19 = (bf16[32,2048]{1,0:T(8,128)(2,1)S(1)}, bf16[32,2048]{1,0:T(8,128)(2,1)S(1)}, u32[]{:S(2)}, u32[]{:S(2)}) collective-permute-start(bf16[32,2048]{1,0:T(8,128)(2,1)S(1)} %get-tuple-element.32), channel_id=1, source_target_pairs={{0,1},{1,0},{2,3},{3,2},{4,5},{5,4},{6,7},{7,6},{8,9},{9,8},{10,11... | collective-permute-start | bytes 393224 | tf_op jit(solution)/shard_map/ppermute | solution.py:23
  127.7 12.2 %collective-permute-start.18 = (bf16[32,2048]{1,0:T(8,128)(2,1)S(1)}, bf16[32,2048]{1,0:T(8,128)(2,1)S(1)}, u32[]{:S(2)}, u32[]{:S(2)}) collective-permute-start(bf16[32,2048]{1,0:T(8,128)(2,1)S(1)} %get-tuple-element.31), channel_id=1, source_target_pairs={{0,2},{1,3},{2,0},{3,1},{4,6},{5,7},{6,4},{7,5},{8,10},{9,11},{10,... | collective-permute-start | bytes 393224 | tf_op jit(solution)/shard_map/ppermute | solution.py:23
  129.2 10.7 %collective-permute-start.17 = (bf16[32,2048]{1,0:T(8,128)(2,1)S(1)}, bf16[32,2048]{1,0:T(8,128)(2,1)S(1)}, u32[]{:S(2)}, u32[]{:S(2)}) collective-permute-start(bf16[32,2048]{1,0:T(8,128)(2,1)S(1)} %get-tuple-element.30), channel_id=1, source_target_pairs={{0,3},{1,2},{2,1},{3,0},{4,7},{5,6},{6,5},{7,4},{8,11},{9,10},{10,... | collective-permute-start | bytes 393224 | tf_op jit(solution)/shard_map/ppermute | solution.py:23
  136.4 6.9 %collective-permute-start.22 = (bf16[128,1024]{1,0:T(8,128)(2,1)S(1)}, bf16[128,1024]{1,0:T(8,128)(2,1)S(1)}, u32[]{:S(2)}, u32[]{:S(2)}) collective-permute-start(bf16[128,1024]{1,0:T(8,128)(2,1)S(1)} %dynamic-slice_convert_fusion.1), channel_id=1, source_target_pairs={{0,4},{4,0},{1,5},{5,1},{2,6},{6,2},{3,7},{7,3},{8,12},{12,8},{9,1... | collective-permute-start | bytes 786440 | tf_op jit(solution)/shard_map/ppermute | solution.py:23
  138.8 6.4 %collective-permute-start.25 = (bf16[128,1024]{1,0:T(8,128)(2,1)S(1)}, bf16[128,1024]{1,0:T(8,128)(2,1)S(1)}, u32[]{:S(2)}, u32[]{:S(2)}) collective-permute-start(bf16[128,1024]{1,0:T(8,128)(2,1)S(1)} %dynamic-slice_convert_fusion), channel_id=1, source_target_pairs={{0,16},{8,24},{16,0},{24,8},{1,17},{9,25},{17,1},{25,9},{2,18},{10... | collective-permute-start | bytes 786440 | tf_op jit(solution)/shard_map/ppermute | solution.py:23
  145.3 7.2 %collective-permute-start.28 = (bf16[32,2048]{1,0:T(8,128)(2,1)S(1)}, bf16[32,2048]{1,0:T(8,128)(2,1)S(1)}, u32[]{:S(2)}, u32[]{:S(2)}) collective-permute-start(bf16[32,2048]{1,0:T(8,128)(2,1)S(1)} %get-tuple-element.29), channel_id=1, source_target_pairs={{0,1},{1,0},{2,3},{3,2},{4,5},{5,4},{6,7},{7,6},{8,9},{9,8},{10,11... | collective-permute-start | bytes 393224 | tf_op jit(solution)/shard_map/ppermute | solution.py:23
  146.3 9.7 %collective-permute-start.27 = (bf16[32,2048]{1,0:T(8,128)(2,1)S(1)}, bf16[32,2048]{1,0:T(8,128)(2,1)S(1)}, u32[]{:S(2)}, u32[]{:S(2)}) collective-permute-start(bf16[32,2048]{1,0:T(8,128)(2,1)S(1)} %get-tuple-element.28), channel_id=1, source_target_pairs={{0,2},{1,3},{2,0},{3,1},{4,6},{5,7},{6,4},{7,5},{8,10},{9,11},{10,... | collective-permute-start | bytes 393224 | tf_op jit(solution)/shard_map/ppermute | solution.py:23
  147.9 8.2 %collective-permute-start.26 = (bf16[32,2048]{1,0:T(8,128)(2,1)S(1)}, bf16[32,2048]{1,0:T(8,128)(2,1)S(1)}, u32[]{:S(2)}, u32[]{:S(2)}) collective-permute-start(bf16[32,2048]{1,0:T(8,128)(2,1)S(1)} %get-tuple-element.27), channel_id=1, source_target_pairs={{0,3},{1,2},{2,1},{3,0},{4,7},{5,6},{6,5},{7,4},{8,11},{9,10},{10,... | collective-permute-start | bytes 393224 | tf_op jit(solution)/shard_map/ppermute | solution.py:23

commit v2 on v1

--- a/solution.py
+++ b/solution.py
@@ -29,23 +29,68 @@
     return lax.ppermute(array, axis, pairs)
 
 
-def row_halo(block, mine):
+def rows_around(block, facing=None):
     rows_count = lax.axis_size("gy")
     if rows_count == 2:
         at_top = lax.axis_index("gy") == 0
-        other = swapped(jnp.where(at_top, block[-RADIUS:], block[:RADIUS]), "gy", 1)
+        if facing is None:
+            facing = jnp.where(at_top, block[-RADIUS:], block[:RADIUS])
+        return (swapped(facing, "gy", 1),)
+    return (moved(block[-RADIUS:], "gy", 1), moved(block[:RADIUS], "gy", -1))
+
+
+def with_rows(block, rows):
+    if len(rows) == 1:
+        at_top = lax.axis_index("gy") == 0
         zero = jnp.zeros((), block.dtype)
-        top, bottom = jnp.where(at_top, zero, other), jnp.where(at_top, other, zero)
-    else:
-        top = moved(block[-RADIUS:], "gy", 1)
-        bottom = moved(block[:RADIUS], "gy", -1)
-    return jnp.concatenate([top, mine, bottom], axis=0)
+        rows = (jnp.where(at_top, zero, rows[0]), jnp.where(at_top, rows[0], zero))
+    return jnp.concatenate([rows[0], block, rows[1]], axis=0)
 
 
 def column_halo(block):
     right = moved(block[:, :SIDE], "gx", -1)
     left = moved(block[:, -SIDE:], "gx", 1)
     return jnp.concatenate([block, right, left], axis=1)
+
+
+def prepare(place_ref, x_ref, c_ref, t_ref, gain_ref, both_ref, face_ref, moment_ref):
+    block, width = x_ref.shape
+    step = pl.program_id(0)
+    rows = pl.ds(pl.multiple_of(step * block, block), block)
+    x = x_ref[...].astype(F32)
+    mean = jnp.sum(x, axis=1, keepdims=True) * (1.0 / width)
+    centered = x - mean
+    variance = jnp.sum(centered * centered, axis=1, keepdims=True) * (1.0 / width)
+    inverse = lax.rsqrt(variance + EPSILON)
+    both_ref[rows, :width] = (centered * inverse * gain_ref[...]).astype(BF)
+    both_ref[rows, width:] = (c_ref[...].astype(F32) * t_ref[...]).astype(BF)
+    lane = lax.broadcasted_iota(jnp.int32, moment_ref.shape, 1)
+    moment_ref[...] = jnp.where(lane == 0, mean, inverse)
+
+    @pl.when(step == pl.num_programs(0) - 1)
+    def _():
+        first = pl.multiple_of(place_ref[4], 16)
+        face_ref[...] = both_ref[pl.ds(first, face_ref.shape[0]), :]
+
+
+def run_prepare(place, tokens, cotangent, tissue, gain, face):
+    count, width = tokens.shape
+    block = min(count, 64)
+    part = lambda columns: pl.BlockSpec((block, columns), lambda step: (step, 0))
+    return pl.pallas_call(
+        prepare,
+        grid=(count // block,),
+        in_specs=[SCALARS, part(width), part(width), part(1), whole((1, width))],
+        out_specs=[whole((count, 2 * width)), whole((face, 2 * width)), part(128)],
+        out_shape=[
+            jax.ShapeDtypeStruct((count, 2 * width), BF),
+            jax.ShapeDtypeStruct((face, 2 * width), BF),
+            jax.ShapeDtypeStruct((count, 128), F32),
+        ],
+        compiler_params=pltpu.CompilerParams(**PARAMS),
+        cost_estimate=pl.CostEstimate(flops=0, bytes_accessed=3 * 1024 * 1024, transcendentals=0),
+        name="prepare",
+    )(place, tokens, cotangent, tissue, gain)
 
 
 def spread_heads(block, head_dim):
@@ -92,7 +137,7 @@
 
 
 def query_pass(
-    head_dim, tile, place_ref, q_ref, g_ref, k_ref, v_ref, out_ref, dq_ref, stat_ref, bias_ref
+    head_dim, tile, place_ref, q_ref, g_ref, k_ref, v_ref, out_ref, stat_ref, bias_ref
 ):
     scaling = 1.0 / math.sqrt(head_dim)
     strips, count, window = bias_ref.shape
@@ -132,8 +177,8 @@
             stats = jnp.where(lane == 2 * head + 1, delta, stats)
         attended = times(jnp.concatenate(probs_parts, axis=0), values)
         grad_queries = times(jnp.concatenate(grad_parts, axis=0), keys)
-        out_ref[own, :] = gather_heads(attended, count, head_dim).astype(BF)
-        dq_ref[own, :] = (gather_heads(grad_queries, count, head_dim) * scaling).astype(BF)
+        out_ref[0, own, :] = gather_heads(attended, count, head_dim).astype(BF)
+        out_ref[1, own, :] = (gather_heads(grad_queries, count, head_dim) * scaling).astype(BF)
         stat_ref[own, :] = stats
 
 
@@ -147,8 +192,7 @@
     q_ref,
     g_ref,
     stat_ref,
-    dk_ref,
-    dv_ref,
+    out_ref,
     bias_ref,
     turned,
 ):
@@ -189,8 +233,8 @@
             grad_parts.append((probs * centred).astype(BF))
         grad_values = times(jnp.concatenate(probs_parts, axis=0), grads)
         grad_keys = times(jnp.concatenate(grad_parts, axis=0), queries)
-        dv_ref[own, :] = gather_heads(grad_values, count, head_dim).astype(BF)
-        dk_ref[own, :] = (gather_heads(grad_keys, count, head_dim) * scaling).astype(BF)
+        out_ref[1, own, :] = gather_heads(grad_values, count, head_dim).astype(BF)
+        out_ref[0, own, :] = (gather_heads(grad_keys, count, head_dim) * scaling).astype(BF)
 
 
 def whole(shape):
@@ -201,6 +245,11 @@
     return pl.BlockSpec((rows, width), lambda group: (0, first + group))
 
 
+def pair_columns(rows, width):
+    return pl.BlockSpec((2, rows, width), lambda group: (0, 0, group))
+
+
+SCALARS = pl.BlockSpec(memory_space=pltpu.SMEM)
 PARAMS = dict(vmem_limit_bytes=24 * 1024 * 1024)
 
 
@@ -212,9 +261,6 @@
     strips, count, window = window_shape(tile)
     flops = 4 * 2 * groups * strips * GROUP * count * window * part
     return pl.CostEstimate(flops=flops, bytes_accessed=4 * 1024 * 1024, transcendentals=0)
-
-
-SCALARS = pl.BlockSpec(memory_space=pltpu.SMEM)
 
 
 def run_queries(place, queries, grads, keys, values, head_dim, tile):
@@ -232,10 +278,9 @@
             columns(ext, part),
             columns(ext, part),
         ],
-        out_specs=[columns(tokens, part), columns(tokens, part), whole((tokens, 128))],
+        out_specs=[pair_columns(tokens, part), whole((tokens, 128))],
         out_shape=[
-            jax.ShapeDtypeStruct((tokens, width), BF),
-            jax.ShapeDtypeStruct((tokens, width), BF),
+            jax.ShapeDtypeStruct((2, tokens, width), BF),
             jax.ShapeDtypeStruct((tokens, 128), F32),
         ],
         scratch_shapes=[pltpu.VMEM(window_shape(tile), F32)],
@@ -253,11 +298,8 @@
         functools.partial(key_pass, head_dim, tile, first),
         grid=(groups,),
         in_specs=[SCALARS] + [columns(ext, part, first)] * 4 + [whole(stats.shape)],
-        out_specs=[columns(tokens, part), columns(tokens, part)],
-        out_shape=[
-            jax.ShapeDtypeStruct((tokens, groups * part), BF),
-            jax.ShapeDtypeStruct((tokens, groups * part), BF),
-        ],
+        out_specs=pair_columns(tokens, part),
+        out_shape=jax.ShapeDtypeStruct((2, tokens, groups * part), BF),
         scratch_shapes=[pltpu.VMEM(window_shape(tile), F32), pltpu.VMEM((128, ext), F32)],
         compiler_params=pltpu.CompilerParams(**PARAMS),
         cost_estimate=attention_cost(tile, groups, part),
@@ -289,25 +331,38 @@
     return slide_swap(block, True) if across_slides else swapped(block, "gy", by)
 
 
-def pick_rows(left, index, across_slides):
-    half = left.shape[1] // 2
+def pick_rows(array, index, across_slides):
+    rows = array.shape[1] // lax.axis_size("slide")
+    core = lax.axis_index("slide") % 2
     if across_slides:
-        return lax.dynamic_slice_in_dim(left, index * half, half, axis=1)
-    rest = half // lax.axis_size("gy")
+        return lax.dynamic_slice_in_dim(array, (2 * index + core) * rows, rows, axis=1)
+    rest = rows // lax.axis_size("gy")
     parts = [
-        lax.dynamic_slice_in_dim(left, high * half + index * rest, rest, axis=1)
-        for high in range(2)
+        lax.dynamic_slice_in_dim(array, (2 * high + core) * rows + index * rest, rest, axis=1)
+        for high in range(lax.axis_size("slide") // 2)
     ]
     return jnp.concatenate(parts, axis=1)
 
 
-def first_halving(left, right, across_slides):
+def pair_product(lefts, rights, index, across_slides):
+    total = None
+    for left, right in zip(lefts, rights):
+        term = product_t(pick_rows(left, index, across_slides), right)
+        total = term if total is None else total + term
+    return total
+
+
+def first_blocks(lefts, rights, across_slides):
+    return [
+        pair_product(lefts, rights, target, across_slides).astype(BF)
+        for _, target in partners(across_slides)[1]
+    ]
+
+
+def first_halving(blocks, lefts, rights, across_slides):
     index, others = partners(across_slides)
-    arrived = []
-    for by, target in others:
-        block = product_t(pick_rows(left, target, across_slides), right).astype(BF)
-        arrived.append(sent(block, across_slides, by))
-    mine = product_t(pick_rows(left, index, across_slides), right)
+    arrived = [sent(block, across_slides, by) for block, (by, _) in zip(blocks, others)]
+    mine = pair_product(lefts, rights, index, across_slides)
     for block in arrived:
         mine = mine + block.astype(F32)
     return mine
@@ -337,10 +392,8 @@
     return mine
 
 
-def later_halvings(one, two):
-    one = second_halving(one, False)
-    two = second_halving(two, True)
-    return reduce_columns(jnp.concatenate([one, two], axis=1))
+def second_halvings(one, two):
+    return jnp.concatenate([second_halving(one, False), second_halving(two, True)], axis=1)
 
 
 def after(array, *earlier):
@@ -358,104 +411,105 @@
     cols_count = lax.axis_size("gx")
     weight_in = weights[:, : 3 * model_width]
     weight_out = weights[:, 3 * model_width :]
+    face = RADIUS * tile_cols
+    at_top = lax.axis_index("gy") == 0
     place = jnp.stack(
         [
             lax.axis_index("gy") * tile_rows,
             lax.axis_index("gx") * tile_cols,
             jnp.int32(tile_rows * rows_count),
             jnp.int32(tile_cols * cols_count),
+            jnp.where(at_top, token_count - face, 0),
         ]
     ).astype(jnp.int32)
 
-    token_rows = row_halo(tile_tokens, tile_tokens)
-    tissue_mask = tissue[0].astype(F32)[:, :, None]
-    upstream = cotangent[0].astype(F32)
-    branch_grad = (tissue_mask * upstream).astype(BF)
-    branch_flat = branch_grad.reshape(token_count, model_width)
-
-    def normalize(array):
-        array = array.astype(F32)
-        centered = array - jnp.mean(array, axis=-1, keepdims=True)
-        variance = jnp.mean(centered * centered, axis=-1, keepdims=True)
-        inverse = lax.rsqrt(variance + EPSILON)
-        return centered * inverse, inverse
-
-    normalized, inverse = normalize(tile_tokens.reshape(token_count, model_width))
-    normed = (normalized * norm_gain).astype(BF)
+    flat = (token_count, model_width)
+    grid = (tile_rows, tile_cols, model_width)
+    tissue_mask = tissue[0].astype(F32).reshape(token_count, 1)
+    tokens_flat = tile_tokens.reshape(flat)
+    cot_flat = cotangent[0].reshape(flat)
+    both, facing, moments = run_prepare(
+        place, tokens_flat, cot_flat, tissue_mask, norm_gain.reshape(1, model_width), face
+    )
+    both_tile = both.reshape(tile_rows, tile_cols, 2 * model_width)
+    rows = rows_around(both_tile, facing.reshape(RADIUS, tile_cols, 2 * model_width))
+    middle = column_halo(both_tile)
+    both_ext = with_rows(middle, [column_halo(row) for row in rows])
+    ext_rows, ext_cols = both_ext.shape[:2]
+    ext = (ext_rows * ext_cols, -1)
+    normed_ext = both_ext[:, :, :model_width].reshape(ext)
+    branch_ext = both_ext[:, :, model_width:].reshape(ext)
+
+    normed, branch_flat = both[:, :model_width], both[:, model_width:]
+    both_other = slide_swap(both, False)
+    normed_pair = (normed, both_other[:, :model_width])
+    branch_pair = (branch_flat, both_other[:, model_width:])
     grad_attn = times_t(branch_flat, weight_out).astype(BF)
     queries = times(normed, weight_in[:, :model_width]).astype(BF)
-
-    core = lax.axis_index("slide") % 2
-
-    def half_swap(array):
-        rows = model_width // slides
-
-        def half(which):
-            parts = [
-                lax.dynamic_slice_in_dim(array, (2 * high + which) * rows, rows, axis=1)
-                for high in range(slides // 2)
-            ]
-            return jnp.concatenate(parts, axis=1)
-
-        return jnp.concatenate([half(core), slide_swap(half(1 - core), False)], axis=0)
-
-    def whole_swap(array):
-        return jnp.concatenate([array, slide_swap(array, False)], axis=0)
-
-    token_ext = column_halo(token_rows)
-    ext_rows, ext_cols = token_ext.shape[:2]
-    branch_first = after(branch_grad, token_rows)
-    branch_rows = row_halo(branch_first, branch_grad)
-    token_ext = token_ext.reshape(ext_rows * ext_cols, model_width)
-    normed_ext = (normalize(token_ext)[0] * norm_gain).astype(BF)
     key_ext = times(normed_ext, weight_in[:, model_width : 2 * model_width]).astype(BF)
     value_ext = times(normed_ext, weight_in[:, 2 * model_width :]).astype(BF)
-    branch_ext = column_halo(branch_rows).reshape(ext_rows * ext_cols, model_width)
-
-    attended, grad_queries, stats = run_queries(
-        place, queries, grad_attn, key_ext, value_ext, head_dim, tile
-    )
+
+    found, stats = run_queries(place, queries, grad_attn, key_ext, value_ext, head_dim, tile)
+    attended, grad_queries = found[0], found[1]
+
+    found_other = slide_swap(found, False)
+    attended_pair = (attended, found_other[0])
+    grad_query_pair = (grad_queries, found_other[1])
+    first_sent = first_blocks(normed_pair, grad_query_pair, True)
+    second_sent = first_blocks(attended_pair, branch_pair, False)
 
     stats_tile = stats.reshape(tile_rows, tile_cols, -1)
-    stats_ext = column_halo(row_halo(stats_tile, stats_tile))
-    stats_ext = stats_ext.reshape(ext_rows * ext_cols, -1)
-
-    normed_pair = half_swap(normed)
-    branch_pair = whole_swap(branch_flat)
-    one = first_halving(normed_pair, whole_swap(grad_queries), True)
-    two = first_halving(half_swap(attended), branch_pair, False)
-
-    normed_late, branch_late = lax.optimization_barrier((normed_ext, branch_ext, stats))[:2]
+    stats_rows = with_rows(stats_tile, rows_around(stats_tile))
+    stats_rows = after(stats_rows, *first_sent, *second_sent)
+    stats_ext = column_halo(stats_rows).reshape(ext)
+    one = first_halving(first_sent, normed_pair, grad_query_pair, True)
+    two = first_halving(second_sent, attended_pair, branch_pair, False)
+
+    normed_late, branch_late, _ = lax.optimization_barrier((normed_ext, branch_ext, stats_rows))
     query_ext = times(normed_late, weight_in[:, :model_width]).astype(BF)
     grad_ext = times_t(branch_late, weight_out).astype(BF)
 
-    projection = times(attended, weight_out).reshape(tile_tokens.shape)
-    block_output = (tile_tokens.astype(F32) + tissue_mask * projection).astype(BF)
-
     stats_ext, one, two = lax.optimization_barrier((stats_ext, one, two))
     groups = HEADS // GROUP
-    grad_keys, grad_values = run_keys(
+    owed = run_keys(
         place, key_ext, value_ext, query_ext, grad_ext, stats_ext, head_dim, tile, 0, groups
     )
-    first_sums = later_halvings(one, two)
-    second_sums = later_halvings(
-        first_halving(normed_pair, whole_swap(grad_keys), True),
-        first_halving(normed_pair, whole_swap(grad_values), False),
-    )
-
-    grad_projected = jnp.concatenate([grad_queries, grad_keys, grad_values], axis=-1)
+    grad_keys, grad_values = owed[0], owed[1]
+    owed_other = slide_swap(owed, False)
+    grad_key_pair = (grad_keys, owed_other[0])
+    grad_value_pair = (grad_values, owed_other[1])
+    third_sent = first_blocks(normed_pair, grad_key_pair, True)
+    fourth_sent = first_blocks(normed_pair, grad_value_pair, False)
+    first_part = second_halvings(one, two)
+    three = first_halving(third_sent, normed_pair, grad_key_pair, True)
+    four = first_halving(fourth_sent, normed_pair, grad_value_pair, False)
+    first_sums = reduce_columns(after(first_part, *third_sent, *fourth_sent))
+    second_sums = reduce_columns(second_halvings(three, four))
+
+    late = lax.optimization_barrier((attended, grad_keys, grad_values, third_sent, fourth_sent))
+    attended_late, keys_late, values_late = late[:3]
+    projection = times(attended_late, weight_out)
+    block_output = (tokens_flat.astype(F32) + tissue_mask * projection).astype(BF)
+
+    grad_projected = jnp.concatenate([grad_queries, keys_late, values_late], axis=-1)
     scaled = times_t(grad_projected, weight_in) * norm_gain
+    inverse = moments[:, 1:2]
+    normalized = (tokens_flat.astype(F32) - moments[:, :1]) * inverse
     first_mean = jnp.mean(scaled, axis=-1, keepdims=True)
     second_mean = jnp.mean(scaled * normalized, axis=-1, keepdims=True)
     input_grad = inverse * (scaled - first_mean - normalized * second_mean)
-    input_grad = (upstream + input_grad.reshape(tile_tokens.shape)).astype(BF)
+    input_grad = (cot_flat.astype(F32) + input_grad).astype(BF)
 
     inv_root = 1.0 / math.sqrt(slides * rows_count * cols_count * token_count)
     width = model_width
     weight_grads = jnp.concatenate(
         [first_sums[:, :width], second_sums, first_sums[:, width:]], axis=1
     )
-    return (block_output[None], input_grad[None], weight_grads * inv_root)
+    return (
+        block_output.reshape((1,) + grid),
+        input_grad.reshape((1,) + grid),
+        weight_grads * inv_root,
+    )
 
 
 def solution(mesh):

time: 158 us -> 130 us (0.82)
  waiting for transfers between devices: 44.7 us -> 27.2 us
  other arithmetic: 19.2 us -> 5.06 us
  starting transfers between devices: 41.4 us -> 44.3 us
    ppermute x23 -> x19, waiting for transfers between devices: 39.6 us -> 23.2 us  [swapped(): return lax.ppermute(array, axis, [(i, i ^ by) for i in range(count)])]
    reduce_sum x4 -> x0, other arithmetic: 4.9 us -> none  [the longest x2 3.4 us: normalize(): variance = jnp.mean(centered * centered, axis=-1, keepdims=True)]
    convert_element_type x8 -> x2, other arithmetic: 6.45 us -> 1.92 us  [the longest x1 1.22 us: local(): input_grad = (cot_flat.astype(F32) + input_grad).astype(BF)]
    unnamed x48 -> x18, local copies, waits for them, and re-layouts: 2.1 us -> 4.44 us
    select_n x6 -> x3, other arithmetic: 2.13 us -> 0.13 us  [the longest x2 0.12 us: with_rows(): rows = (jnp.where(at_top, zero, rows[0]), jnp.where(at_top, rows[0], zero))]
    slice x0 -> x6, local copies, waits for them, and re-layouts: none -> 1.83 us  [the longest x1 1.08 us: local(): normed_pair = (normed, both_other[:, :model_width])]
    pallas_call x0 -> x1, Pallas kernels: none -> 1.67 us  [run_prepare(): pl.pallas_call(prepare, grid=(count // block,), in_specs=[SCALARS, part(w...]
    ppermute x6, starting transfers between devices: 17.4 us -> 19 us  [moved(): return lax.ppermute(array, axis, pairs)]
  transfers between devices with their start and end apart: 29 -> 25, of which waited for: 13 -> 11; matrix products, arithmetic and copies ran while one was open for 30% -> 22% of each run, Pallas kernels for 7% -> 8%
where the time goes in v2:
time: 130 us; the launch traced here: 129 us
  starting transfers between devices  44.3 us (34%)
  waiting for transfers between devices  27.2 us (21%)
  matrix products  24 us (18%)
  Pallas kernels  19.2 us (15%)
  local copies, waits for them, and re-layouts  8.38 us (6%)
  other arithmetic  5.06 us (4%)
  between operations  1.32 us (1%)
    ppermute x19, starting transfers between devices, swapped(): return lax.ppermute(array, axis, [(i, i ^ by) for i in range(count)])  25.4 us
    ppermute x19, waiting for transfers between devices, swapped(): return lax.ppermute(array, axis, [(i, i ^ by) for i in range(count)])  23.2 us
    ppermute x6, starting transfers between devices, moved(): return lax.ppermute(array, axis, pairs)  19 us
    pallas_call x1, Pallas kernels, run_queries(): pl.pallas_call(functools.partial(query_pass, head_dim, tile), grid=(group...  10.3 us
    dot_general x5, matrix products, times(): return jnp.dot(left, right, preferred_element_type=F32)  10.1 us
    dot_general x16, matrix products, product_t(): lax.dot_general(left, right, (((0,), (0,)), ((), ())), preferred_element_...  7.36 us
    pallas_call x1, Pallas kernels, run_keys(): pl.pallas_call(functools.partial(key_pass, head_dim, tile, first), grid=(...  7.2 us
    dot_general x3, matrix products, times_t(): lax.dot_general(left, right, (((1,), (1,)), ((), ())), preferred_element_...  6.48 us
  transfers between devices with their start and end apart: 25, of which 11 were waited for; matrix products, arithmetic and copies ran while one was open for 22% of the time, Pallas kernels for 8%

profile of v2, /device:TPU:0, one launch (start us, length us, event | category | flops | bytes accessed | tf_op | source)
XLA Modules:
  0.0 129.5 jit_solution(9689731103218339374)
XLA Ops:
  0.6 0.7 convert_element_type.133
  1.5 1.0 copy-done
  2.6 1.0 copy-done.2
  3.6 0.7 copy-done.4
  4.3 1.7 %prepare.1 = (bf16[256,2048]{1,0:T(8,128)(2,1)S(1)}, bf16[96,2048]{1,0:T(8,128)(2,1)S(1)}, f32[256,128]{1,0:T(8,128)S(1)}) custom-call(s32[5]{0:T(128)S(1)} %stack.15.place_ref, bf16[256,1024]{1,0:T(8,128)(2,1)S(1)} %bitcast.67, bf16[256,1024]{1,0:T(8,128)(2,1)S(1)} %bitcast.69, f32[256,1]{1,0:T(8,128)S(1)} %convert_element_type.173.t_ref, ...), custom_call_target="tpu_custom_call" | custom-call | bytes 3145728 | tf_op jit(solution)/shard_map/prepare/pallas_call | solution.py:80
  6.0 3.0 %collective-permute-start = (bf16[6,16,2048]{2,1,0:T(8,128)(2,1)S(1)}, bf16[6,16,2048]{2,1,0:T(8,128)(2,1)S(1)}, u32[]{:S(2)}, u32[]{:S(2)}) collective-permute-start(bf16[6,16,2048]{2,1,0:T(8,128)(2,1)S(1)} %bitcast.73), channel_id=1, source_target_pairs={{0,4},{4,0},{1,5},{5,1},{2,6},{6,2},{3,7},{7,3},{8,12},{12,8},{9,1... | collective-permute-start | bytes 1179656 | tf_op jit(solution)/shard_map/ppermute | solution.py:23
  9.0 1.1 fusion.140
  10.1 1.3 collective-permute-start.3
  11.4 5.4 %collective-permute-start.4 = (bf16[16,8,2048]{2,1,0:T(8,128)(2,1)}, bf16[16,8,2048]{2,1,0:T(8,128)(2,1)}, u32[]{:S(2)}, u32[]{:S(2)}) collective-permute-start(bf16[16,8,2048]{2,1,0:T(8,128)(2,1)} %get-tuple-element.51), channel_id=1, source_target_pairs={{0,1},{1,2},{2,3},{4,5},{5,6},{6,7},{8,9},{9,10},{10,11},{12,13},{... | collective-permute-start | bytes 1572872 | tf_op jit(solution)/shard_map/ppermute | solution.py:29
  16.9 2.3 %fusion.44.g_ref = bf16[256,1024]{1,0:T(8,128)(2,1)S(1)} fusion(bf16[1024,4096]{1,0:T(8,128)(2,1)} %param.6, bf16[256,2048]{1,0:T(8,128)(2,1)S(1)} %get-tuple-element.18), kind=kOutput, calls=%fused_computation.49 | convolution fusion | flops 537133056 | bytes 3145728 | tf_op jit(solution)/shard_map/dot_general | solution.py:117
  19.6 2.3 %fusion.47.q_ref = bf16[256,1024]{1,0:T(8,128)(2,1)S(1)} fusion(bf16[1024,4096]{1,0:T(8,128)(2,1)} %param.6, bf16[256,2048]{1,0:T(8,128)(2,1)S(1)} %get-tuple-element.18), kind=kOutput, calls=%fused_computation.50 | convolution fusion | flops 537133056 | bytes 3145728 | tf_op jit(solution)/shard_map/dot_general | solution.py:113
  22.0 1.3 collective-permute-start.1
  23.3 4.6 %collective-permute-start.2 = (bf16[6,8,2048]{2,1,0:T(8,128)(2,1)S(1)}, bf16[6,8,2048]{2,1,0:T(8,128)(2,1)S(1)}, u32[]{:S(2)}, u32[]{:S(2)}) collective-permute-start(bf16[6,8,2048]{2,1,0:T(8,128)(2,1)S(1)} %get-tuple-element.70), channel_id=1, source_target_pairs={{0,1},{1,2},{2,3},{4,5},{5,6},{6,7},{8,9},{9,10},{10,11},{12,13},{... | collective-permute-start | bytes 589832 | tf_op jit(solution)/shard_map/ppermute | solution.py:29
  27.9 2.8 %collective-permute-done.1 = bf16[6,8,2048]{2,1,0:T(8,128)(2,1)S(1)} collective-permute-done((bf16[6,8,2048]{2,1,0:T(8,128)(2,1)S(1)}, bf16[6,8,2048]{2,1,0:T(8,128)(2,1)S(1)}, u32[]{:S(2)}, u32[]{:S(2)}) %collective-permute-start.1) | collective-permute-done | bytes 196640 | tf_op jit(solution)/shard_map/ppermute | solution.py:29
  30.8 1.2 collective-permute-done.2
  32.1 1.6 %pad_maximum_fusion = bf16[28,32,2048]{2,1,0:T(8,128)(2,1)S(1)} fusion(bf16[6,32,2048]{2,1,0:T(8,128)(2,1)S(1)} %get-tuple-element.53, bf16[16,8,2048]{2,1,0:T(8,128)(2,1)} %collective-permute-done.4, bf16[16,8,2048]{2,1,0:T(8,128)(2,1)} %collective-permute-done.3, bf16[16,16,2048]{2,1,0:T(8,128)(2,1)S(1)} %bitcast.66, ...), kind=kLoop, calls=%fused_computation.2 | loop fusion | flops 18350080 | bytes 7340032 | tf_op jit(solution)/shard_map/concatenate | solution.py:47
  33.7 0.4 fusion.139
  34.5 1.3 %slice-done.1 = s8[4194304]{0:T(1024)(128)(4,1)S(1)} async-done(((s8[8388608]{0:T(1024)(128)(4,1)}), s8[4194304]{0:T(1024)(128)(4,1)S(1)}, s32[]{:S(2)}) %slice-start.1) | async-done | bytes 4194328
  35.8 2.1 %fusion.13.k_ref = bf16[896,1024]{1,0:T(8,128)(2,1)S(1)} fusion(bf16[896,1024]{1,0:T(8,128)(2,1)S(1)} %bitcast.74, bf16[1024,4096]{1,0:T(8,128)(2,1)S(1)} %bitcast.81), kind=kOutput, calls=%fused_computation.12 | convolution fusion | flops 1879965696 | bytes 5767168 | tf_op jit(solution)/shard_map/dot_general | solution.py:113
  37.9 2.1 %fusion.16.v_ref = bf16[896,1024]{1,0:T(8,128)(2,1)S(1)} fusion(bf16[896,1024]{1,0:T(8,128)(2,1)S(1)} %bitcast.75, bf16[1024,4096]{1,0:T(8,128)(2,1)S(1)} %bitcast.81), kind=kOutput, calls=%fused_computation.13 | convolution fusion | flops 1879965696 | bytes 5767168 | tf_op jit(solution)/shard_map/dot_general | solution.py:113
  40.0 10.3 %query_pass.1 = (bf16[2,256,1024]{2,1,0:T(8,128)(2,1)S(1)}, f32[256,128]{1,0:T(8,128)S(1)}) custom-call(s32[5]{0:T(128)S(1)} %stack.15.place_ref, bf16[256,1024]{1,0:T(8,128)(2,1)S(1)} %fusion.47.q_ref, bf16[256,1024]{1,0:T(8,128)(2,1)S(1)} %fusion.44.g_ref, bf16[896,1024]{1,0:T(8,128)(2,1)S(1)} %fusion.13.k_ref, bf16[896,1024]{1,0:T(8,128)(2,1)S(1)} %fusion.16.v_ref), custom_call_target="tpu_custom_call" | custom-call | flops 4294967296 | bytes 4194304 | tf_op jit(solution)/shard_map/query_pass/pallas_call | solution.py:271
  50.5 0.3 fusion.118
  50.9 0.3 fusion.112
  51.3 0.4 collective-permute-start.5
  52.3 3.2 %collective-permute-done.5 = f32[6,16,128]{2,1,0:T(8,128)S(1)} collective-permute-done((f32[6,16,128]{2,1,0:T(8,128)S(1)}, f32[6,16,128]{2,1,0:T(8,128)S(1)}, u32[]{:S(2)}, u32[]{:S(2)}) %collective-permute-start.5) | collective-permute-done | bytes 49184 | tf_op jit(solution)/shard_map/ppermute | solution.py:23
  55.6 1.1 slice.136
  56.9 1.4 %fusion.54 = bf16[256,1024]{1,0:T(8,128)(2,1)S(1)} fusion(f32[256,1024]{1,0:T(8,128)S(1)} %fusion.69, bf16[256,2048]{1,0:T(8,128)(2,1)} %collective-permute-done.6, bf16[256,128]{1,0:T(8,128)(2,1)S(1)} %get-tuple-element.64, bf16[256,128]{1,0:T(8,128)(2,1)S(1)} %get-tuple-element.65), kind=kOutput, calls=%fused_computation.53 | convolution fusion | flops 135004160 | bytes 2228224 | tf_op jit(solution)/shard_map/dot_general | solution.py:315
  58.3 0.4 collective-permute-start.11
  58.6 0.3 fusion.53
  59.0 1.7 %collective-permute-start.10 = (bf16[256,1024]{1,0:T(8,128)(2,1)S(1)}, bf16[256,1024]{1,0:T(8,128)(2,1)S(1)}, u32[]{:S(2)}, u32[]{:S(2)}) collective-permute-start(bf16[256,1024]{1,0:T(8,128)(2,1)S(1)} %fusion.53), channel_id=1, source_target_pairs={{0,16},{8,24},{16,0},{24,8},{1,17},{9,25},{17,1},{25,9},{2,18},{10... | collective-permute-start | bytes 1572872 | tf_op jit(solution)/shard_map/ppermute | solution.py:23
  60.7 1.3 collective-permute-start.8
  62.0 5.2 %collective-permute-start.9 = (f32[28,8,128]{2,1,0:T(8,128)S(1)}, f32[28,8,128]{2,1,0:T(8,128)S(1)}, u32[]{:S(2)}, u32[]{:S(2)}) collective-permute-start(f32[28,8,128]{2,1,0:T(8,128)S(1)} %get-tuple-element.75), channel_id=1, source_target_pairs={{0,1},{1,2},{2,3},{4,5},{5,6},{6,7},{8,9},{9,10},{10,11},{12,13},{... | collective-permute-start | bytes 344072 | tf_op jit(solution)/shard_map/ppermute | solution.py:29
  67.2 2.1 %convolution_convert_fusion.g_ref = bf16[896,1024]{1,0:T(8,128)(2,1)S(1)} fusion(bf16[896,1024]{1,0:T(8,128)(2,1)S(1)} %bitcast.77, bf16[1024,4096]{1,0:T(8,128)(2,1)S(1)} %bitcast.81), kind=kOutput, calls=%fused_computation.14 | convolution fusion | flops 1879965696 | bytes 5767168 | tf_op jit(solution)/shard_map/dot_general | solution.py:117
  69.3 2.1 %fusion.10.q_ref = bf16[896,1024]{1,0:T(8,128)(2,1)S(1)} fusion(bf16[896,1024]{1,0:T(8,128)(2,1)S(1)} %bitcast.76, bf16[1024,4096]{1,0:T(8,128)(2,1)S(1)} %bitcast.81), kind=kOutput, calls=%fused_computation.11 | convolution fusion | flops 1879965696 | bytes 5767168 | tf_op jit(solution)/shard_map/dot_general | solution.py:113
  71.5 0.8 collective-permute-done.10
  72.3 0.3 fusion.32
  72.7 1.4 %fusion.31 = f32[256,1024]{1,0:T(8,128)S(1)} fusion(f32[256,1024]{1,0:T(8,128)S(1)} %fusion.67, bf16[256,1024]{1,0:T(8,128)(2,1)S(1)} %collective-permute-done.11, bf16[256,2048]{1,0:T(8,128)(2,1)} %collective-permute-done.6, bf16[256,128]{1,0:T(8,128)(2,1)S(1)} %get-tuple-element.63, bf16[256,128]{1,0:T(8,128)(2,1)S(1)} %get-tuple-element.62), kind=kOutput, calls=%fused_computation.40 | convolution fusion | flops 135266304 | bytes 3276800 | tf_op jit(solution)/shard_map/dot_general | solution.py:315
  74.0 7.2 %key_pass.1 = bf16[2,256,1024]{2,1,0:T(8,128)(2,1)S(1)} custom-call(s32[5]{0:T(128)S(1)} %stack.15.place_ref, bf16[896,1024]{1,0:T(8,128)(2,1)S(1)} %fusion.13.k_ref, bf16[896,1024]{1,0:T(8,128)(2,1)S(1)} %fusion.16.v_ref, bf16[896,1024]{1,0:T(8,128)(2,1)S(1)} %fusion.10.q_ref, bf16[896,1024]{1,0:T(8,128)(2,1)S(1)} %convolution_convert_fusion.g_ref, ...), custom_call_target="tpu_custom_call" | custom-call | flops 4294967296 | bytes 4194304 | tf_op jit(solution)/shard_map/key_pass/pallas_call | solution.py:297
  81.3 0.3 fusion.116
  81.7 0.3 fusion.110
  82.1 1.8 %collective-permute-start.13 = (bf16[128,1024]{1,0:T(8,128)(2,1)S(1)}, bf16[128,1024]{1,0:T(8,128)(2,1)S(1)}, u32[]{:S(2)}, u32[]{:S(2)}) collective-permute-start(bf16[128,1024]{1,0:T(8,128)(2,1)S(1)} %dynamic-slice_convert_fusion.3), channel_id=1, source_target_pairs={{0,4},{4,0},{1,5},{5,1},{2,6},{6,2},{3,7},{7,3},{8,12},{12,8},{9,1... | collective-permute-start | bytes 786440 | tf_op jit(solution)/shard_map/ppermute | solution.py:23
  84.0 1.6 %collective-permute-start.14 = (bf16[128,1024]{1,0:T(8,128)(2,1)S(1)}, bf16[128,1024]{1,0:T(8,128)(2,1)S(1)}, u32[]{:S(2)}, u32[]{:S(2)}) collective-permute-start(bf16[128,1024]{1,0:T(8,128)(2,1)S(1)} %dynamic-slice_convert_fusion.2), channel_id=1, source_target_pairs={{0,16},{8,24},{16,0},{24,8},{1,17},{9,25},{17,1},{25,9},{2,18},{10... | collective-permute-start | bytes 786440 | tf_op jit(solution)/shard_map/ppermute | solution.py:23
  86.2 4.7 %collective-permute-done.13 = bf16[128,1024]{1,0:T(8,128)(2,1)S(1)} collective-permute-done((bf16[128,1024]{1,0:T(8,128)(2,1)S(1)}, bf16[128,1024]{1,0:T(8,128)(2,1)S(1)}, u32[]{:S(2)}, u32[]{:S(2)}) %collective-permute-start.13) | collective-permute-done | bytes 262176 | tf_op jit(solution)/shard_map/ppermute | solution.py:23
  91.0 1.5 %collective-permute-done.14 = bf16[128,1024]{1,0:T(8,128)(2,1)S(1)} collective-permute-done((bf16[128,1024]{1,0:T(8,128)(2,1)S(1)}, bf16[128,1024]{1,0:T(8,128)(2,1)S(1)}, u32[]{:S(2)}, u32[]{:S(2)}) %collective-permute-start.14) | collective-permute-done | bytes 262176 | tf_op jit(solution)/shard_map/ppermute | solution.py:23
  92.6 0.3 fusion.56
  93.0 0.4 collective-permute-start.20
  93.3 0.3 fusion.55
  93.7 1.8 %collective-permute-start.18 = (bf16[256,1024]{1,0:T(8,128)(2,1)S(1)}, bf16[256,1024]{1,0:T(8,128)(2,1)S(1)}, u32[]{:S(2)}, u32[]{:S(2)}) collective-permute-start(bf16[256,1024]{1,0:T(8,128)(2,1)S(1)} %fusion.55), channel_id=1, source_target_pairs={{0,16},{8,24},{16,0},{24,8},{1,17},{9,25},{17,1},{25,9},{2,18},{10... | collective-permute-start | bytes 1572872 | tf_op jit(solution)/shard_map/ppermute | solution.py:23
  95.5 5.3 %collective-permute-start.15 = (bf16[32,2048]{1,0:T(8,128)(2,1)S(1)}, bf16[32,2048]{1,0:T(8,128)(2,1)S(1)}, u32[]{:S(2)}, u32[]{:S(2)}) collective-permute-start(bf16[32,2048]{1,0:T(8,128)(2,1)S(1)} %get-tuple-element.42), channel_id=1, source_target_pairs={{0,3},{1,2},{2,1},{3,0},{4,7},{5,6},{6,5},{7,4},{8,11},{9,10},{10,... | collective-permute-start | bytes 393224 | tf_op jit(solution)/shard_map/ppermute | solution.py:23
  100.8 0.6 collective-permute-start.17
  101.5 2.0 %fusion.138 = (f32[256]{0:T(256)S(1)}, f32[256]{0:T(256)S(1)}, f32[256,1024]{1,0:T(8,128)S(1)}) fusion(f32[256]{0:T(256)S(1)} %get-tuple-element.35, f32[256]{0:T(256)S(1)} %get-tuple-element.36, bf16[1,16,16,1024]{3,2,1,0:T(8,128)(2,1)S(1)} %copy-done.1, f32[1024]{0:T(1024)S(1)} %copy-done.5, bf16[1024,4096]{1,0:T(8,128)(2,1)S(1)} %bitcast.81, ...), kind=kOutput, calls=%fused_computation.188 | convolution fusion | flops 1617165824 | bytes 9445376 | tf_op jit(solution)/shard_map/dot_general | solution.py:117
  103.5 1.5 %fusion.50 = bf16[256,1024]{1,0:T(8,128)(2,1)} fusion(bf16[256,1024]{1,0:T(8,128)(2,1)S(1)} %get-tuple-element.26, bf16[1024,4096]{1,0:T(8,128)(2,1)S(1)} %bitcast.81, bf16[256,1024]{1,0:T(8,128)(2,1)S(1)} %bitcast.68, f32[256]{0:T(256)S(1)} %convert_element_type.134), kind=kOutput, calls=%fused_computation.51 | convolution fusion | flops 537919488 | bytes 3671040 | tf_op jit(solution)/shard_map/dot_general | solution.py:113
  105.1 1.2 collective-permute-done.20
  106.6 1.6 %collective-permute-start.21 = (bf16[128,1024]{1,0:T(8,128)(2,1)S(1)}, bf16[128,1024]{1,0:T(8,128)(2,1)S(1)}, u32[]{:S(2)}, u32[]{:S(2)}) collective-permute-start(bf16[128,1024]{1,0:T(8,128)(2,1)S(1)} %dynamic-slice_convert_fusion), channel_id=1, source_target_pairs={{0,16},{8,24},{16,0},{24,8},{1,17},{9,25},{17,1},{25,9},{2,18},{10... | collective-permute-start | bytes 786440 | tf_op jit(solution)/shard_map/ppermute | solution.py:23
  108.2 0.3 fusion.30
  108.6 0.6 collective-permute-start.19
  109.2 4.1 %collective-permute-done.21 = bf16[128,1024]{1,0:T(8,128)(2,1)S(1)} collective-permute-done((bf16[128,1024]{1,0:T(8,128)(2,1)S(1)}, bf16[128,1024]{1,0:T(8,128)(2,1)S(1)}, u32[]{:S(2)}, u32[]{:S(2)}) %collective-permute-start.21) | collective-permute-done | bytes 262176 | tf_op jit(solution)/shard_map/ppermute | solution.py:23
  113.4 1.6 %collective-permute-done.19 = bf16[128,1024]{1,0:T(8,128)(2,1)S(1)} collective-permute-done((bf16[128,1024]{1,0:T(8,128)(2,1)S(1)}, bf16[128,1024]{1,0:T(8,128)(2,1)S(1)}, u32[]{:S(2)}, u32[]{:S(2)}) %collective-permute-start.19) | collective-permute-done | bytes 262176 | tf_op jit(solution)/shard_map/ppermute | solution.py:23
  115.1 5.3 %collective-permute-start.22 = (bf16[32,2048]{1,0:T(8,128)(2,1)S(1)}, bf16[32,2048]{1,0:T(8,128)(2,1)S(1)}, u32[]{:S(2)}, u32[]{:S(2)}) collective-permute-start(bf16[32,2048]{1,0:T(8,128)(2,1)S(1)} %get-tuple-element.39), channel_id=1, source_target_pairs={{0,3},{1,2},{2,1},{3,0},{4,7},{5,6},{6,5},{7,4},{8,11},{9,10},{10,... | collective-permute-start | bytes 393224 | tf_op jit(solution)/shard_map/ppermute | solution.py:23
  120.5 0.6 collective-permute-start.24
  121.1 1.2 fusion.64
  122.4 2.3 %collective-permute-done.22 = bf16[32,2048]{1,0:T(8,128)(2,1)S(1)} collective-permute-done((bf16[32,2048]{1,0:T(8,128)(2,1)S(1)}, bf16[32,2048]{1,0:T(8,128)(2,1)S(1)}, u32[]{:S(2)}, u32[]{:S(2)}) %collective-permute-start.22) | collective-permute-done | bytes 131104 | tf_op jit(solution)/shard_map/ppermute | solution.py:23
  124.7 3.8 %collective-permute-done.23 = bf16[32,2048]{1,0:T(8,128)(2,1)S(1)} collective-permute-done((bf16[32,2048]{1,0:T(8,128)(2,1)S(1)}, bf16[32,2048]{1,0:T(8,128)(2,1)S(1)}, u32[]{:S(2)}, u32[]{:S(2)}) %collective-permute-start.23) | collective-permute-done | bytes 131104 | tf_op jit(solution)/shard_map/ppermute | solution.py:23
  128.6 0.8 maximum_multiply_fusion
  (73 shorter events, 4.2 us)
Async XLA Ops:
  1.5 1.0 copy-start
  2.6 1.0 copy-start.2
  3.6 0.7 copy-start.4
  6.0 16.0 %collective-permute-start = (bf16[6,16,2048]{2,1,0:T(8,128)(2,1)S(1)}, bf16[6,16,2048]{2,1,0:T(8,128)(2,1)S(1)}, u32[]{:S(2)}, u32[]{:S(2)}) collective-permute-start(bf16[6,16,2048]{2,1,0:T(8,128)(2,1)S(1)} %bitcast.73), channel_id=1, source_target_pairs={{0,4},{4,0},{1,5},{5,1},{2,6},{6,2},{3,7},{7,3},{8,12},{12,8},{9,1... | collective-permute-start | bytes 1179656 | tf_op jit(solution)/shard_map/ppermute | solution.py:23
  9.0 46.5 %collective-permute-start.6 = (bf16[256,2048]{1,0:T(8,128)(2,1)S(1)}, bf16[256,2048]{1,0:T(8,128)(2,1)}, u32[]{:S(2)}, u32[]{:S(2)}) collective-permute-start(bf16[256,2048]{1,0:T(8,128)(2,1)S(1)} %get-tuple-element.18), channel_id=1, source_target_pairs={{0,8},{8,0},{16,24},{24,16},{1,9},{9,1},{17,25},{25,17},{2,10},{10... | collective-permute-start | bytes 3145736 | tf_op jit(solution)/shard_map/ppermute | solution.py:23
  10.1 22.0 %collective-permute-start.3 = (bf16[16,8,2048]{2,1,0:T(8,128)(2,1)}, bf16[16,8,2048]{2,1,0:T(8,128)(2,1)}, u32[]{:S(2)}, u32[]{:S(2)}) collective-permute-start(bf16[16,8,2048]{2,1,0:T(8,128)(2,1)} %get-tuple-element.50), channel_id=1, source_target_pairs={{1,0},{2,1},{3,2},{5,4},{6,5},{7,6},{9,8},{10,9},{11,10},{13,12},{... | collective-permute-start | bytes 1572872 | tf_op jit(solution)/shard_map/ppermute | solution.py:29
  11.4 20.7 %collective-permute-start.4 = (bf16[16,8,2048]{2,1,0:T(8,128)(2,1)}, bf16[16,8,2048]{2,1,0:T(8,128)(2,1)}, u32[]{:S(2)}, u32[]{:S(2)}) collective-permute-start(bf16[16,8,2048]{2,1,0:T(8,128)(2,1)} %get-tuple-element.51), channel_id=1, source_target_pairs={{0,1},{1,2},{2,3},{4,5},{5,6},{6,7},{8,9},{9,10},{10,11},{12,13},{... | collective-permute-start | bytes 1572872 | tf_op jit(solution)/shard_map/ppermute | solution.py:29
  22.0 8.7 %collective-permute-start.1 = (bf16[6,8,2048]{2,1,0:T(8,128)(2,1)S(1)}, bf16[6,8,2048]{2,1,0:T(8,128)(2,1)S(1)}, u32[]{:S(2)}, u32[]{:S(2)}) collective-permute-start(bf16[6,8,2048]{2,1,0:T(8,128)(2,1)S(1)} %get-tuple-element.71), channel_id=1, source_target_pairs={{1,0},{2,1},{3,2},{5,4},{6,5},{7,6},{9,8},{10,9},{11,10},{13,12},{... | collective-permute-start | bytes 589832 | tf_op jit(solution)/shard_map/ppermute | solution.py:29
  23.3 8.6 %collective-permute-start.2 = (bf16[6,8,2048]{2,1,0:T(8,128)(2,1)S(1)}, bf16[6,8,2048]{2,1,0:T(8,128)(2,1)S(1)}, u32[]{:S(2)}, u32[]{:S(2)}) collective-permute-start(bf16[6,8,2048]{2,1,0:T(8,128)(2,1)S(1)} %get-tuple-element.70), channel_id=1, source_target_pairs={{0,1},{1,2},{2,3},{4,5},{5,6},{6,7},{8,9},{9,10},{10,11},{12,13},{... | collective-permute-start | bytes 589832 | tf_op jit(solution)/shard_map/ppermute | solution.py:29
  31.9 2.5 %slice-start = ((s8[8388608]{0:T(1024)(128)(4,1)}), s8[4194304]{0:T(1024)(128)(4,1)S(1)}, s32[]{:S(2)}) async-start(s8[8388608]{0:T(1024)(128)(4,1)} %bitcast.80), calls=%async_computation | async-start | bytes 8388608
  32.1 3.7 %slice-start.1 = ((s8[8388608]{0:T(1024)(128)(4,1)}), s8[4194304]{0:T(1024)(128)(4,1)S(1)}, s32[]{:S(2)}) async-start(s8[8388608]{0:T(1024)(128)(4,1)} %bitcast.80), calls=%async_computation.1 | async-start | bytes 8388608
  50.4 6.3 %collective-permute-start.7 = (bf16[2,256,1024]{2,1,0:T(8,128)(2,1)S(1)}, bf16[2,256,1024]{2,1,0:T(8,128)(2,1)S(1)}, u32[]{:S(2)}, u32[]{:S(2)}) collective-permute-start(bf16[2,256,1024]{2,1,0:T(8,128)(2,1)S(1)} %get-tuple-element.20), channel_id=1, source_target_pairs={{0,8},{8,0},{16,24},{24,16},{1,9},{9,1},{17,25},{25,17},{2,10},{10... | collective-permute-start | bytes 3145736 | tf_op jit(solution)/shard_map/ppermute | solution.py:23
  51.3 4.2 %collective-permute-start.5 = (f32[6,16,128]{2,1,0:T(8,128)S(1)}, f32[6,16,128]{2,1,0:T(8,128)S(1)}, u32[]{:S(2)}, u32[]{:S(2)}) collective-permute-start(f32[6,16,128]{2,1,0:T(8,128)S(1)} %bitcast.79), channel_id=1, source_target_pairs={{0,4},{4,0},{1,5},{5,1},{2,6},{6,2},{3,7},{7,3},{8,12},{12,8},{9,1... | collective-permute-start | bytes 147464 | tf_op jit(solution)/shard_map/ppermute | solution.py:23
  58.3 14.4 %collective-permute-start.11 = (bf16[256,1024]{1,0:T(8,128)(2,1)S(1)}, bf16[256,1024]{1,0:T(8,128)(2,1)S(1)}, u32[]{:S(2)}, u32[]{:S(2)}) collective-permute-start(bf16[256,1024]{1,0:T(8,128)(2,1)S(1)} %fusion.54), channel_id=1, source_target_pairs={{0,4},{4,0},{1,5},{5,1},{2,6},{6,2},{3,7},{7,3},{8,12},{12,8},{9,1... | collective-permute-start | bytes 1572872 | tf_op jit(solution)/shard_map/ppermute | solution.py:23
  59.0 13.3 %collective-permute-start.10 = (bf16[256,1024]{1,0:T(8,128)(2,1)S(1)}, bf16[256,1024]{1,0:T(8,128)(2,1)S(1)}, u32[]{:S(2)}, u32[]{:S(2)}) collective-permute-start(bf16[256,1024]{1,0:T(8,128)(2,1)S(1)} %fusion.53), channel_id=1, source_target_pairs={{0,16},{8,24},{16,0},{24,8},{1,17},{9,25},{17,1},{25,9},{2,18},{10... | collective-permute-start | bytes 1572872 | tf_op jit(solution)/shard_map/ppermute | solution.py:23
  60.7 10.7 %collective-permute-start.8 = (f32[28,8,128]{2,1,0:T(8,128)S(1)}, f32[28,8,128]{2,1,0:T(8,128)S(1)}, u32[]{:S(2)}, u32[]{:S(2)}) collective-permute-start(f32[28,8,128]{2,1,0:T(8,128)S(1)} %get-tuple-element.74), channel_id=1, source_target_pairs={{1,0},{2,1},{3,2},{5,4},{6,5},{7,6},{9,8},{10,9},{11,10},{13,12},{... | collective-permute-start | bytes 344072 | tf_op jit(solution)/shard_map/ppermute | solution.py:29
  62.0 9.4 %collective-permute-start.9 = (f32[28,8,128]{2,1,0:T(8,128)S(1)}, f32[28,8,128]{2,1,0:T(8,128)S(1)}, u32[]{:S(2)}, u32[]{:S(2)}) collective-permute-start(f32[28,8,128]{2,1,0:T(8,128)S(1)} %get-tuple-element.75), channel_id=1, source_target_pairs={{0,1},{1,2},{2,3},{4,5},{5,6},{6,7},{8,9},{9,10},{10,11},{12,13},{... | collective-permute-start | bytes 344072 | tf_op jit(solution)/shard_map/ppermute | solution.py:29
  81.3 11.4 %collective-permute-start.12 = (bf16[2,256,1024]{2,1,0:T(8,128)(2,1)S(1)}, bf16[2,256,1024]{2,1,0:T(8,128)(2,1)S(1)}, u32[]{:S(2)}, u32[]{:S(2)}) collective-permute-start(bf16[2,256,1024]{2,1,0:T(8,128)(2,1)S(1)} %key_pass.1), channel_id=1, source_target_pairs={{0,8},{8,0},{16,24},{24,16},{1,9},{9,1},{17,25},{25,17},{2,10},{10... | collective-permute-start | bytes 3145736 | tf_op jit(solution)/shard_map/ppermute | solution.py:23
  82.1 8.8 %collective-permute-start.13 = (bf16[128,1024]{1,0:T(8,128)(2,1)S(1)}, bf16[128,1024]{1,0:T(8,128)(2,1)S(1)}, u32[]{:S(2)}, u32[]{:S(2)}) collective-permute-start(bf16[128,1024]{1,0:T(8,128)(2,1)S(1)} %dynamic-slice_convert_fusion.3), channel_id=1, source_target_pairs={{0,4},{4,0},{1,5},{5,1},{2,6},{6,2},{3,7},{7,3},{8,12},{12,8},{9,1... | collective-permute-start | bytes 786440 | tf_op jit(solution)/shard_map/ppermute | solution.py:23
  84.0 8.5 %collective-permute-start.14 = (bf16[128,1024]{1,0:T(8,128)(2,1)S(1)}, bf16[128,1024]{1,0:T(8,128)(2,1)S(1)}, u32[]{:S(2)}, u32[]{:S(2)}) collective-permute-start(bf16[128,1024]{1,0:T(8,128)(2,1)S(1)} %dynamic-slice_convert_fusion.2), channel_id=1, source_target_pairs={{0,16},{8,24},{16,0},{24,8},{1,17},{9,25},{17,1},{25,9},{2,18},{10... | collective-permute-start | bytes 786440 | tf_op jit(solution)/shard_map/ppermute | solution.py:23
  92.6 8.9 %copy-start.1 = (bf16[1,16,16,1024]{3,2,1,0:T(8,128)(2,1)S(1)}, bf16[1,16,16,1024]{3,2,1,0:T(8,128)(2,1)}, u32[]{:S(2)}) copy-start(bf16[1,16,16,1024]{3,2,1,0:T(8,128)(2,1)} %param.5) | copy-start | bytes 1572868
  92.6 8.9 %copy-start.5 = (f32[1024]{0:T(1024)S(1)}, f32[1024]{0:T(1024)}, u32[]{:S(2)}) copy-start(f32[1024]{0:T(1024)} %param.7) | copy-start | bytes 12292
  93.0 13.3 %collective-permute-start.20 = (bf16[256,1024]{1,0:T(8,128)(2,1)S(1)}, bf16[256,1024]{1,0:T(8,128)(2,1)S(1)}, u32[]{:S(2)}, u32[]{:S(2)}) collective-permute-start(bf16[256,1024]{1,0:T(8,128)(2,1)S(1)} %fusion.56), channel_id=1, source_target_pairs={{0,4},{4,0},{1,5},{5,1},{2,6},{6,2},{3,7},{7,3},{8,12},{12,8},{9,1... | collective-permute-start | bytes 1572872 | tf_op jit(solution)/shard_map/ppermute | solution.py:23
  93.7 14.5 %collective-permute-start.18 = (bf16[256,1024]{1,0:T(8,128)(2,1)S(1)}, bf16[256,1024]{1,0:T(8,128)(2,1)S(1)}, u32[]{:S(2)}, u32[]{:S(2)}) collective-permute-start(bf16[256,1024]{1,0:T(8,128)(2,1)S(1)} %fusion.55), channel_id=1, source_target_pairs={{0,16},{8,24},{16,0},{24,8},{1,17},{9,25},{17,1},{25,9},{2,18},{10... | collective-permute-start | bytes 1572872 | tf_op jit(solution)/shard_map/ppermute | solution.py:23
  95.5 25.0 %collective-permute-start.15 = (bf16[32,2048]{1,0:T(8,128)(2,1)S(1)}, bf16[32,2048]{1,0:T(8,128)(2,1)S(1)}, u32[]{:S(2)}, u32[]{:S(2)}) collective-permute-start(bf16[32,2048]{1,0:T(8,128)(2,1)S(1)} %get-tuple-element.42), channel_id=1, source_target_pairs={{0,3},{1,2},{2,1},{3,0},{4,7},{5,6},{6,5},{7,4},{8,11},{9,10},{10,... | collective-permute-start | bytes 393224 | tf_op jit(solution)/shard_map/ppermute | solution.py:23
  100.8 21.5 %collective-permute-start.16 = (bf16[32,2048]{1,0:T(8,128)(2,1)S(1)}, bf16[32,2048]{1,0:T(8,128)(2,1)S(1)}, u32[]{:S(2)}, u32[]{:S(2)}) collective-permute-start(bf16[32,2048]{1,0:T(8,128)(2,1)S(1)} %get-tuple-element.44), channel_id=1, source_target_pairs={{0,2},{1,3},{2,0},{3,1},{4,6},{5,7},{6,4},{7,5},{8,10},{9,11},{10,... | collective-permute-start | bytes 393224 | tf_op jit(solution)/shard_map/ppermute | solution.py:23
  100.8 21.5 %collective-permute-start.17 = (bf16[32,2048]{1,0:T(8,128)(2,1)S(1)}, bf16[32,2048]{1,0:T(8,128)(2,1)S(1)}, u32[]{:S(2)}, u32[]{:S(2)}) collective-permute-start(bf16[32,2048]{1,0:T(8,128)(2,1)S(1)} %get-tuple-element.43), channel_id=1, source_target_pairs={{0,1},{1,0},{2,3},{3,2},{4,5},{5,4},{6,7},{7,6},{8,9},{9,8},{10,11... | collective-permute-start | bytes 393224 | tf_op jit(solution)/shard_map/ppermute | solution.py:23
  106.6 14.5 %copy-start.3 = (bf16[1,16,16,1024]{3,2,1,0:T(8,128)(2,1)S(1)}, bf16[1,16,16,1024]{3,2,1,0:T(8,128)(2,1)}, u32[]{:S(2)}) copy-start(bf16[1,16,16,1024]{3,2,1,0:T(8,128)(2,1)} %param.9) | copy-start | bytes 1572868
  106.6 6.7 %collective-permute-start.21 = (bf16[128,1024]{1,0:T(8,128)(2,1)S(1)}, bf16[128,1024]{1,0:T(8,128)(2,1)S(1)}, u32[]{:S(2)}, u32[]{:S(2)}) collective-permute-start(bf16[128,1024]{1,0:T(8,128)(2,1)S(1)} %dynamic-slice_convert_fusion), channel_id=1, source_target_pairs={{0,16},{8,24},{16,0},{24,8},{1,17},{9,25},{17,1},{25,9},{2,18},{10... | collective-permute-start | bytes 786440 | tf_op jit(solution)/shard_map/ppermute | solution.py:23
  108.6 6.4 %collective-permute-start.19 = (bf16[128,1024]{1,0:T(8,128)(2,1)S(1)}, bf16[128,1024]{1,0:T(8,128)(2,1)S(1)}, u32[]{:S(2)}, u32[]{:S(2)}) collective-permute-start(bf16[128,1024]{1,0:T(8,128)(2,1)S(1)} %dynamic-slice_convert_fusion.1), channel_id=1, source_target_pairs={{0,4},{4,0},{1,5},{5,1},{2,6},{6,2},{3,7},{7,3},{8,12},{12,8},{9,1... | collective-permute-start | bytes 786440 | tf_op jit(solution)/shard_map/ppermute | solution.py:23
  115.1 9.5 %collective-permute-start.22 = (bf16[32,2048]{1,0:T(8,128)(2,1)S(1)}, bf16[32,2048]{1,0:T(8,128)(2,1)S(1)}, u32[]{:S(2)}, u32[]{:S(2)}) collective-permute-start(bf16[32,2048]{1,0:T(8,128)(2,1)S(1)} %get-tuple-element.39), channel_id=1, source_target_pairs={{0,3},{1,2},{2,1},{3,0},{4,7},{5,6},{6,5},{7,4},{8,11},{9,10},{10,... | collective-permute-start | bytes 393224 | tf_op jit(solution)/shard_map/ppermute | solution.py:23
  120.5 8.0 %collective-permute-start.23 = (bf16[32,2048]{1,0:T(8,128)(2,1)S(1)}, bf16[32,2048]{1,0:T(8,128)(2,1)S(1)}, u32[]{:S(2)}, u32[]{:S(2)}) collective-permute-start(bf16[32,2048]{1,0:T(8,128)(2,1)S(1)} %get-tuple-element.40), channel_id=1, source_target_pairs={{0,2},{1,3},{2,0},{3,1},{4,6},{5,7},{6,4},{7,5},{8,10},{9,11},{10,... | collective-permute-start | bytes 393224 | tf_op jit(solution)/shard_map/ppermute | solution.py:23
  120.5 8.0 %collective-permute-start.24 = (bf16[32,2048]{1,0:T(8,128)(2,1)S(1)}, bf16[32,2048]{1,0:T(8,128)(2,1)S(1)}, u32[]{:S(2)}, u32[]{:S(2)}) collective-permute-start(bf16[32,2048]{1,0:T(8,128)(2,1)S(1)} %get-tuple-element.41), channel_id=1, source_target_pairs={{0,1},{1,0},{2,3},{3,2},{4,5},{5,4},{6,7},{7,6},{8,9},{9,8},{10,11... | collective-permute-start | bytes 393224 | tf_op jit(solution)/shard_map/ppermute | solution.py:23

commit v3 on v2

--- a/solution.py
+++ b/solution.py
@@ -48,8 +48,16 @@
 
 
 def column_halo(block):
-    right = moved(block[:, :SIDE], "gx", -1)
-    left = moved(block[:, -SIDE:], "gx", 1)
+    count = lax.axis_size("gx")
+    even = lax.axis_index("gx") % 2 == 0
+    first, last = block[:, :SIDE], block[:, -SIDE:]
+    pairs = []
+    for start in range(2):
+        for low in range(start, count - 1, 2):
+            pairs += [(start, low, low + 1), (start, low + 1, low)]
+    one = lax.ppermute(jnp.where(even, last, first), "gx", [p[1:] for p in pairs if p[0] == 0])
+    two = lax.ppermute(jnp.where(even, first, last), "gx", [p[1:] for p in pairs if p[0] == 1])
+    right, left = jnp.where(even, one, two), jnp.where(even, two, one)
     return jnp.concatenate([block, right, left], axis=1)
 
 
@@ -137,7 +145,19 @@
 
 
 def query_pass(
-    head_dim, tile, place_ref, q_ref, g_ref, k_ref, v_ref, out_ref, stat_ref, bias_ref
+    head_dim,
+    tile,
+    place_ref,
+    q_ref,
+    g_ref,
+    normed_ref,
+    key_w_ref,
+    value_w_ref,
+    out_ref,
+    stat_ref,
+    k_ref,
+    v_ref,
+    bias_ref,
 ):
     scaling = 1.0 / math.sqrt(head_dim)
     strips, count, window = bias_ref.shape
@@ -149,16 +169,24 @@
         fill_bias(place_ref, bias_ref, *tile)
         stat_ref[...] = jnp.zeros_like(stat_ref)
 
+    k_ref[...] = times(normed_ref[...], key_w_ref[...]).astype(BF)
+    v_ref[...] = times(normed_ref[...], value_w_ref[...]).astype(BF)
     lane = lax.broadcasted_iota(jnp.int32, (count, 128), 1) - group * (2 * GROUP)
-    for strip in range(strips):
+
+    def dots(strip):
         own = pl.ds(strip * count, count)
         near = pl.ds(strip * step, window)
         queries = spread_heads(q_ref[own, :] * jnp.asarray(scaling, BF), head_dim)
         grads = spread_heads(g_ref[own, :], head_dim)
-        keys = k_ref[near, :]
-        values = v_ref[near, :]
-        scores = times_t(queries, keys)
-        grad_probs = times_t(grads, values)
+        return times_t(queries, k_ref[near, :]), times_t(grads, v_ref[near, :])
+
+    ahead = dots(0)
+    for strip in range(strips):
+        own = pl.ds(strip * count, count)
+        near = pl.ds(strip * step, window)
+        scores, grad_probs = ahead
+        if strip + 1 < strips:
+            ahead = dots(strip + 1)
         stats = stat_ref[own, :]
         probs_parts, grad_parts = [], []
         for head in range(GROUP):
@@ -175,8 +203,8 @@
             grad_parts.append((probs * (grad_part - delta)).astype(BF))
             stats = jnp.where(lane == 2 * head, row_max + jnp.log(total), stats)
             stats = jnp.where(lane == 2 * head + 1, delta, stats)
-        attended = times(jnp.concatenate(probs_parts, axis=0), values)
-        grad_queries = times(jnp.concatenate(grad_parts, axis=0), keys)
+        attended = times(jnp.concatenate(probs_parts, axis=0), v_ref[near, :])
+        grad_queries = times(jnp.concatenate(grad_parts, axis=0), k_ref[near, :])
         out_ref[0, own, :] = gather_heads(attended, count, head_dim).astype(BF)
         out_ref[1, own, :] = (gather_heads(grad_queries, count, head_dim) * scaling).astype(BF)
         stat_ref[own, :] = stats
@@ -207,21 +235,36 @@
         fill_bias(place_ref, bias_ref, *tile)
         turned[...] = stat_ref[...].T
 
+    part_width = q_ref.shape[1]
+    keys_at = pl.multiple_of(group * part_width, part_width)
+    values_at = pl.multiple_of((group + pl.num_programs(0)) * part_width, part_width)
     rows = pl.ds(pl.multiple_of((group + first) * (2 * GROUP), 2 * GROUP), 2 * GROUP)
 
     def own_tokens(ref, strip):
         starts = [(RADIUS + strip * STRIP + row) * slots for row in range(STRIP)]
         return jnp.concatenate([ref[pl.ds(start, tile[1]), :] for start in starts], axis=0)
 
-    for strip in range(strips):
-        own = pl.ds(strip * count, count)
+    def dots(strip):
         near = pl.ds(strip * step, window)
         keys = spread_heads(own_tokens(k_ref, strip) * jnp.asarray(scaling, BF), head_dim)
         values = spread_heads(own_tokens(v_ref, strip), head_dim)
-        queries = q_ref[near, :]
-        grads = g_ref[near, :]
-        scores = times_t(keys, queries)
-        grad_probs = times_t(values, grads)
+        return times_t(keys, q_ref[near, :]), times_t(values, g_ref[near, :])
+
+    def finish(strip, probs, grads):
+        own = pl.ds(strip * count, count)
+        near = pl.ds(strip * step, window)
+        grad_values = gather_heads(times(probs, g_ref[near, :]), count, head_dim)
+        grad_keys = gather_heads(times(grads, q_ref[near, :]), count, head_dim) * scaling
+        out_ref[own, pl.ds(values_at, part_width)] = grad_values.astype(BF)
+        out_ref[own, pl.ds(keys_at, part_width)] = grad_keys.astype(BF)
+
+    ahead = dots(0)
+    behind = None
+    for strip in range(strips):
+        near = pl.ds(strip * step, window)
+        scores, grad_probs = ahead
+        if strip + 1 < strips:
+            ahead = dots(strip + 1)
         stats = turned[rows, near]
         probs_parts, grad_parts = [], []
         for head in range(GROUP):
@@ -231,10 +274,10 @@
             centred = grad_probs[part] - stats[2 * head + 1 : 2 * head + 2]
             probs_parts.append(probs.astype(BF))
             grad_parts.append((probs * centred).astype(BF))
-        grad_values = times(jnp.concatenate(probs_parts, axis=0), grads)
-        grad_keys = times(jnp.concatenate(grad_parts, axis=0), queries)
-        out_ref[1, own, :] = gather_heads(grad_values, count, head_dim).astype(BF)
-        out_ref[0, own, :] = (gather_heads(grad_keys, count, head_dim) * scaling).astype(BF)
+        if strip > 0:
+            finish(strip - 1, *behind)
+        behind = (jnp.concatenate(probs_parts, axis=0), jnp.concatenate(grad_parts, axis=0))
+    finish(strips - 1, *behind)
 
 
 def whole(shape):
@@ -263,9 +306,9 @@
     return pl.CostEstimate(flops=flops, bytes_accessed=4 * 1024 * 1024, transcendentals=0)
 
 
-def run_queries(place, queries, grads, keys, values, head_dim, tile):
+def run_queries(place, queries, grads, normed_ext, weights, head_dim, tile):
     tokens, width = queries.shape
-    ext = keys.shape[0]
+    ext = normed_ext.shape[0]
     part = GROUP * head_dim
     groups = width // part
     return pl.pallas_call(
@@ -275,19 +318,27 @@
             SCALARS,
             columns(tokens, part),
             columns(tokens, part),
+            whole(normed_ext.shape),
+            columns(width, part, groups),
+            columns(width, part, 2 * groups),
+        ],
+        out_specs=[
+            pair_columns(tokens, part),
+            whole((tokens, 128)),
             columns(ext, part),
             columns(ext, part),
         ],
-        out_specs=[pair_columns(tokens, part), whole((tokens, 128))],
         out_shape=[
             jax.ShapeDtypeStruct((2, tokens, width), BF),
             jax.ShapeDtypeStruct((tokens, 128), F32),
+            jax.ShapeDtypeStruct((ext, width), BF),
+            jax.ShapeDtypeStruct((ext, width), BF),
         ],
         scratch_shapes=[pltpu.VMEM(window_shape(tile), F32)],
         compiler_params=pltpu.CompilerParams(**PARAMS),
         cost_estimate=attention_cost(tile, groups, part),
         name="query_pass",
-    )(place, queries, grads, keys, values)
+    )(place, queries, grads, normed_ext, weights, weights)
 
 
 def run_keys(place, keys, values, queries, grads, stats, head_dim, tile, first, groups):
@@ -298,8 +349,8 @@
         functools.partial(key_pass, head_dim, tile, first),
         grid=(groups,),
         in_specs=[SCALARS] + [columns(ext, part, first)] * 4 + [whole(stats.shape)],
-        out_specs=pair_columns(tokens, part),
-        out_shape=jax.ShapeDtypeStruct((2, tokens, groups * part), BF),
+        out_specs=whole((tokens, 2 * groups * part)),
+        out_shape=jax.ShapeDtypeStruct((tokens, 2 * groups * part), BF),
         scratch_shapes=[pltpu.VMEM(window_shape(tile), F32), pltpu.VMEM((128, ext), F32)],
         compiler_params=pltpu.CompilerParams(**PARAMS),
         cost_estimate=attention_cost(tile, groups, part),
@@ -331,8 +382,8 @@
     return slide_swap(block, True) if across_slides else swapped(block, "gy", by)
 
 
-def pick_rows(array, index, across_slides):
-    rows = array.shape[1] // lax.axis_size("slide")
+def pick_rows(array, index, across_slides, width):
+    rows = width // lax.axis_size("slide")
     core = lax.axis_index("slide") % 2
     if across_slides:
         return lax.dynamic_slice_in_dim(array, (2 * index + core) * rows, rows, axis=1)
@@ -347,7 +398,7 @@
 def pair_product(lefts, rights, index, across_slides):
     total = None
     for left, right in zip(lefts, rights):
-        term = product_t(pick_rows(left, index, across_slides), right)
+        term = product_t(pick_rows(left, index, across_slides, right.shape[1]), right)
         total = term if total is None else total + term
     return total
 
@@ -442,14 +493,14 @@
 
     normed, branch_flat = both[:, :model_width], both[:, model_width:]
     both_other = slide_swap(both, False)
-    normed_pair = (normed, both_other[:, :model_width])
+    normed_pair = (both, both_other)
     branch_pair = (branch_flat, both_other[:, model_width:])
     grad_attn = times_t(branch_flat, weight_out).astype(BF)
     queries = times(normed, weight_in[:, :model_width]).astype(BF)
-    key_ext = times(normed_ext, weight_in[:, model_width : 2 * model_width]).astype(BF)
-    value_ext = times(normed_ext, weight_in[:, 2 * model_width :]).astype(BF)
-
-    found, stats = run_queries(place, queries, grad_attn, key_ext, value_ext, head_dim, tile)
+
+    found, stats, key_ext, value_ext = run_queries(
+        place, queries, grad_attn, normed_ext, weights, head_dim, tile
+    )
     attended, grad_queries = found[0], found[1]
 
     found_other = slide_swap(found, False)
@@ -470,28 +521,31 @@
     grad_ext = times_t(branch_late, weight_out).astype(BF)
 
     stats_ext, one, two = lax.optimization_barrier((stats_ext, one, two))
-    groups = HEADS // GROUP
-    owed = run_keys(
-        place, key_ext, value_ext, query_ext, grad_ext, stats_ext, head_dim, tile, 0, groups
-    )
-    grad_keys, grad_values = owed[0], owed[1]
-    owed_other = slide_swap(owed, False)
-    grad_key_pair = (grad_keys, owed_other[0])
-    grad_value_pair = (grad_values, owed_other[1])
-    third_sent = first_blocks(normed_pair, grad_key_pair, True)
-    fourth_sent = first_blocks(normed_pair, grad_value_pair, False)
-    first_part = second_halvings(one, two)
-    three = first_halving(third_sent, normed_pair, grad_key_pair, True)
-    four = first_halving(fourth_sent, normed_pair, grad_value_pair, False)
+    half = HEADS // GROUP // 2
+    held = (key_ext, value_ext, query_ext, grad_ext)
+    owed_low = run_keys(place, *held, stats_ext, head_dim, tile, 0, half)
+    first_part, stats_late = lax.optimization_barrier((second_halvings(one, two), stats_ext))
+    owed_high = run_keys(place, *held, stats_late, head_dim, tile, half, half)
+    low_other = slide_swap(owed_low, False)
+    low_pair = lax.optimization_barrier((owed_low, low_other, owed_high))[:2]
+    high_pair = (owed_high, slide_swap(owed_high, False))
+    third_sent = first_blocks(normed_pair, low_pair, True)
+    fourth_sent = first_blocks(normed_pair, high_pair, False)
+    three = first_halving(third_sent, normed_pair, low_pair, True)
+    four = first_halving(fourth_sent, normed_pair, high_pair, False)
     first_sums = reduce_columns(after(first_part, *third_sent, *fourth_sent))
     second_sums = reduce_columns(second_halvings(three, four))
 
-    late = lax.optimization_barrier((attended, grad_keys, grad_values, third_sent, fourth_sent))
-    attended_late, keys_late, values_late = late[:3]
+    late = lax.optimization_barrier((attended, owed_low, owed_high, third_sent, fourth_sent))
+    attended_late, low_late, high_late = late[:3]
     projection = times(attended_late, weight_out)
     block_output = (tokens_flat.astype(F32) + tissue_mask * projection).astype(BF)
 
-    grad_projected = jnp.concatenate([grad_queries, keys_late, values_late], axis=-1)
+    cut = model_width // 2
+    grad_projected = jnp.concatenate(
+        [grad_queries, low_late[:, :cut], high_late[:, :cut], low_late[:, cut:], high_late[:, cut:]],
+        axis=-1,
+    )
     scaled = times_t(grad_projected, weight_in) * norm_gain
     inverse = moments[:, 1:2]
     normalized = (tokens_flat.astype(F32) - moments[:, :1]) * inverse
@@ -503,7 +557,15 @@
     inv_root = 1.0 / math.sqrt(slides * rows_count * cols_count * token_count)
     width = model_width
     weight_grads = jnp.concatenate(
-        [first_sums[:, :width], second_sums, first_sums[:, width:]], axis=1
+        [
+            first_sums[:, :width],
+            second_sums[:, :cut],
+            second_sums[:, width : width + cut],
+            second_sums[:, cut:width],
+            second_sums[:, width + cut :],
+            first_sums[:, width:],
+        ],
+        axis=1,
     )
     return (
         block_output.reshape((1,) + grid),

time: 130 us -> 120 us (0.923)
  matrix products: 24 us -> 17.7 us
  starting transfers between devices: 44.3 us -> 38.2 us
  Pallas kernels: 19.2 us -> 21.8 us
  local copies, waits for them, and re-layouts: 8.38 us -> 6.75 us
  other arithmetic: 5.06 us -> 6.6 us
    ppermute x6, starting transfers between devices: 19 us -> 12.9 us  [the longest x3 9.94 us: column_halo(): lax.ppermute(jnp.where(even, last, first), 'gx', [p[1:] for p in pairs if...]
    dot_general x5 -> x3, matrix products: 10.1 us -> 5.92 us  [times(): return jnp.dot(left, right, preferred_element_type=F32)]
    select_n x0 -> x6, other arithmetic: none -> 2.41 us  [the longest x3 1.32 us: column_halo(): right, left = (jnp.where(even, one, two), jnp.where(even, two, one))]
    slice x6 -> x1, local copies, waits for them, and re-layouts: 2.25 us -> 0.07 us  [local(): attended, grad_queries = (found[0], found[1])]
    dot_general x16, matrix products: 7.36 us -> 5.28 us  [product_t(): lax.dot_general(left, right, (((0,), (0,)), ((), ())), preferred_element_...]
    pallas_call x1, Pallas kernels: 10.3 us -> 12.4 us  [run_queries(): pl.pallas_call(functools.partial(query_pass, head_dim, tile), grid=(group...]
    ppermute x19 -> x20, waiting for transfers between devices: 23.2 us -> 22 us  [swapped(): return lax.ppermute(array, axis, [(i, i ^ by) for i in range(count)])]
    unnamed x18 -> x25, local copies, waits for them, and re-layouts: 4.44 us -> 5.2 us
  transfers between devices with their start and end apart: 25 -> 26, of which waited for: 11 -> 12; matrix products, arithmetic and copies ran while one was open for 22% -> 19% of each run, Pallas kernels for 8% -> 17%
where the time goes in v3:
time: 120 us; the launch traced here: 119 us
  starting transfers between devices  38.2 us (32%)
  waiting for transfers between devices  26.9 us (22%)
  Pallas kernels  21.8 us (18%)
  matrix products  17.7 us (15%)
  local copies, waits for them, and re-layouts  6.75 us (6%)
  other arithmetic  6.6 us (6%)
  between operations  1.31 us (1%)
    ppermute x20, starting transfers between devices, swapped(): return lax.ppermute(array, axis, [(i, i ^ by) for i in range(count)])  25.2 us
    ppermute x20, waiting for transfers between devices, swapped(): return lax.ppermute(array, axis, [(i, i ^ by) for i in range(count)])  22 us
    pallas_call x1, Pallas kernels, run_queries(): pl.pallas_call(functools.partial(query_pass, head_dim, tile), grid=(group...  12.4 us
    ppermute x3, starting transfers between devices, column_halo(): lax.ppermute(jnp.where(even, last, first), 'gx', [p[1:] for p in pairs if...  9.94 us
    pallas_call x2, Pallas kernels, run_keys(): pl.pallas_call(functools.partial(key_pass, head_dim, tile, first), grid=(...  7.69 us
    dot_general x3, matrix products, times_t(): lax.dot_general(left, right, (((1,), (1,)), ((), ())), preferred_element_...  6.49 us
    dot_general x3, matrix products, times(): return jnp.dot(left, right, preferred_element_type=F32)  5.92 us
    dot_general x16, matrix products, product_t(): lax.dot_general(left, right, (((0,), (0,)), ((), ())), preferred_element_...  5.28 us
  transfers between devices with their start and end apart: 26, of which 12 were waited for; matrix products, arithmetic and copies ran while one was open for 19% of the time, Pallas kernels for 17%

profile of v3, /device:TPU:0, one launch (start us, length us, event | category | flops | bytes accessed | tf_op | source)
XLA Modules:
  0.0 119.2 jit_solution(8013899889426284978)
XLA Ops:
  0.6 0.7 convert_element_type.127
  1.5 1.0 copy-done
  2.6 1.0 copy-done.2
  3.6 0.7 copy-done.4
  4.3 1.7 %prepare.1 = (bf16[256,2048]{1,0:T(8,128)(2,1)S(1)}, bf16[96,2048]{1,0:T(8,128)(2,1)S(1)}, f32[256,128]{1,0:T(8,128)S(1)}) custom-call(s32[5]{0:T(128)S(1)} %stack.15.place_ref, bf16[256,1024]{1,0:T(8,128)(2,1)S(1)} %bitcast.66, bf16[256,1024]{1,0:T(8,128)(2,1)S(1)} %bitcast.68, f32[256,1]{1,0:T(8,128)S(1)} %convert_element_type.165.t_ref, ...), custom_call_target="tpu_custom_call" | custom-call | bytes 3145728 | tf_op jit(solution)/shard_map/prepare/pallas_call | solution.py:88
  6.0 3.0 %collective-permute-start = (bf16[6,16,2048]{2,1,0:T(8,128)(2,1)S(1)}, bf16[6,16,2048]{2,1,0:T(8,128)(2,1)S(1)}, u32[]{:S(2)}, u32[]{:S(2)}) collective-permute-start(bf16[6,16,2048]{2,1,0:T(8,128)(2,1)S(1)} %bitcast.71), channel_id=1, source_target_pairs={{0,4},{4,0},{1,5},{5,1},{2,6},{6,2},{3,7},{7,3},{8,12},{12,8},{9,1... | collective-permute-start | bytes 1179656 | tf_op jit(solution)/shard_map/ppermute | solution.py:23
  9.0 1.0 broadcast_select_fusion.5
  10.1 1.6 %collective-permute-start.3 = (bf16[16,8,2048]{2,1,0:T(8,128)(2,1)}, bf16[16,8,2048]{2,1,0:T(8,128)(2,1)}, u32[]{:S(2)}, u32[]{:S(2)}) collective-permute-start(bf16[16,8,2048]{2,1,0:T(8,128)(2,1)} %get-tuple-element.69), channel_id=1, source_target_pairs={{0,1},{1,0},{2,3},{3,2},{4,5},{5,4},{6,7},{7,6},{8,9},{9,8},{10,11... | collective-permute-start | bytes 1572872 | tf_op jit(solution)/shard_map/ppermute | solution.py:58
  11.6 1.5 %collective-permute-start.4 = (bf16[16,8,2048]{2,1,0:T(8,128)(2,1)}, bf16[16,8,2048]{2,1,0:T(8,128)(2,1)}, u32[]{:S(2)}, u32[]{:S(2)}) collective-permute-start(bf16[16,8,2048]{2,1,0:T(8,128)(2,1)} %get-tuple-element.70), channel_id=1, source_target_pairs={{1,2},{2,1},{5,6},{6,5},{9,10},{10,9},{13,14},{14,13},{17,18},{18,... | collective-permute-start | bytes 1572872 | tf_op jit(solution)/shard_map/ppermute | solution.py:59
  13.2 2.3 %fusion.30.q_ref = bf16[256,1024]{1,0:T(8,128)(2,1)S(1)} fusion(bf16[1024,4096]{1,0:T(8,128)(2,1)} %value_w_ref.1, bf16[256,2048]{1,0:T(8,128)(2,1)S(1)} %get-tuple-element.24), kind=kOutput, calls=%fused_computation.39 | convolution fusion | flops 537133056 | bytes 3145728 | tf_op jit(solution)/shard_map/dot_general | solution.py:121
  15.7 2.3 %fusion.27.g_ref = bf16[256,1024]{1,0:T(8,128)(2,1)S(1)} fusion(bf16[1024,4096]{1,0:T(8,128)(2,1)} %value_w_ref.1, bf16[256,2048]{1,0:T(8,128)(2,1)S(1)} %get-tuple-element.24), kind=kOutput, calls=%fused_computation.38 | convolution fusion | flops 537133056 | bytes 3145728 | tf_op jit(solution)/shard_map/dot_general | solution.py:125
  18.3 3.7 %collective-permute-start.1 = (bf16[6,8,2048]{2,1,0:T(8,128)(2,1)S(1)}, bf16[6,8,2048]{2,1,0:T(8,128)(2,1)S(1)}, u32[]{:S(2)}, u32[]{:S(2)}) collective-permute-start(bf16[6,8,2048]{2,1,0:T(8,128)(2,1)S(1)} %get-tuple-element.83), channel_id=1, source_target_pairs={{0,1},{1,0},{2,3},{3,2},{4,5},{5,4},{6,7},{7,6},{8,9},{9,8},{10,11... | collective-permute-start | bytes 589832 | tf_op jit(solution)/shard_map/ppermute | solution.py:58
  22.0 0.7 collective-permute-start.2
  22.7 2.4 %collective-permute-done.3 = bf16[16,8,2048]{2,1,0:T(8,128)(2,1)} collective-permute-done((bf16[16,8,2048]{2,1,0:T(8,128)(2,1)}, bf16[16,8,2048]{2,1,0:T(8,128)(2,1)}, u32[]{:S(2)}, u32[]{:S(2)}) %collective-permute-start.3) | collective-permute-done | bytes 524320 | tf_op jit(solution)/shard_map/ppermute | solution.py:58
  25.1 1.3 %broadcast_select_fusion.3 = (bf16[16,8,2048]{2,1,0:T(8,128)(2,1)S(1)}, bf16[16,8,2048]{2,1,0:T(8,128)(2,1)S(1)}) fusion(bf16[16,8,2048]{2,1,0:T(8,128)(2,1)} %collective-permute-done.3, bf16[16,8,2048]{2,1,0:T(8,128)(2,1)} %collective-permute-done.4, pred[]{:T(512)S(6)} %eq.32), kind=kLoop, calls=%fused_computation.73 | loop fusion | flops 524288 | bytes 2097153 | tf_op jit(solution)/shard_map/jit(_where)/select_n | solution.py:60
  26.4 2.4 %collective-permute-done.1 = bf16[6,8,2048]{2,1,0:T(8,128)(2,1)S(1)} collective-permute-done((bf16[6,8,2048]{2,1,0:T(8,128)(2,1)S(1)}, bf16[6,8,2048]{2,1,0:T(8,128)(2,1)S(1)}, u32[]{:S(2)}, u32[]{:S(2)}) %collective-permute-start.1) | collective-permute-done | bytes 196640 | tf_op jit(solution)/shard_map/ppermute | solution.py:58
  28.9 0.3 broadcast_select_fusion.1
  29.2 0.5 pad_maximum_fusion
  29.7 0.4 fusion.125
  30.1 0.9 slice-done
  31.1 1.4 %slice-done.1 = s8[4194304]{0:T(1024)(128)(4,1)S(1)} async-done(((s8[8388608]{0:T(1024)(128)(4,1)}), s8[4194304]{0:T(1024)(128)(4,1)S(1)}, s32[]{:S(2)}) %slice-start.1) | async-done | bytes 4194328
  32.4 12.4 %query_pass.1 = (bf16[2,256,1024]{2,1,0:T(8,128)(2,1)S(1)}, f32[256,128]{1,0:T(8,128)S(1)}, bf16[896,1024]{1,0:T(8,128)(2,1)S(1)}, bf16[896,1024]{1,0:T(8,128)(2,1)S(1)}) custom-call(s32[5]{0:T(128)S(1)} %stack.15.place_ref, bf16[256,1024]{1,0:T(8,128)(2,1)S(1)} %fusion.30.q_ref, bf16[256,1024]{1,0:T(8,128)(2,1)S(1)} %fusion.27.g_ref, ...), custom_call_target="tpu_custom_call" | custom-call | flops 4294967296 | bytes 4194304 | tf_op jit(solution)/shard_map/query_pass/pallas_call | solution.py:314
  45.0 0.4 collective-permute-start.5
  45.7 0.3 fusion.48
  46.9 2.3 %collective-permute-done.5 = f32[6,16,128]{2,1,0:T(8,128)S(1)} collective-permute-done((f32[6,16,128]{2,1,0:T(8,128)S(1)}, f32[6,16,128]{2,1,0:T(8,128)S(1)}, u32[]{:S(2)}, u32[]{:S(2)}) %collective-permute-start.5) | collective-permute-done | bytes 49184 | tf_op jit(solution)/shard_map/ppermute | solution.py:23
  49.4 0.3 fusion.36
  49.8 1.6 %collective-permute-start.10 = (bf16[256,1024]{1,0:T(8,128)(2,1)S(1)}, bf16[256,1024]{1,0:T(8,128)(2,1)S(1)}, u32[]{:S(2)}, u32[]{:S(2)}) collective-permute-start(bf16[256,1024]{1,0:T(8,128)(2,1)S(1)} %fusion.36), channel_id=1, source_target_pairs={{0,16},{8,24},{16,0},{24,8},{1,17},{9,25},{17,1},{25,9},{2,18},{10... | collective-permute-start | bytes 1572872 | tf_op jit(solution)/shard_map/ppermute | solution.py:23
  51.7 0.6 collective-permute-start.11
  52.3 2.1 %fusion.6.q_ref = bf16[896,1024]{1,0:T(8,128)(2,1)S(1)} fusion(bf16[896,1024]{1,0:T(8,128)(2,1)S(1)} %bitcast.63, bf16[1024,4096]{1,0:T(8,128)(2,1)S(1)} %bitcast.59), kind=kOutput, calls=%fused_computation.7 | convolution fusion | flops 1879965696 | bytes 5767168 | tf_op jit(solution)/shard_map/dot_general | solution.py:121
  54.4 4.7 %collective-permute-start.8 = (f32[28,8,128]{2,1,0:T(8,128)S(1)}, f32[28,8,128]{2,1,0:T(8,128)S(1)}, u32[]{:S(2)}, u32[]{:S(2)}) collective-permute-start(f32[28,8,128]{2,1,0:T(8,128)S(1)} %get-tuple-element.87), channel_id=1, source_target_pairs={{0,1},{1,0},{2,3},{3,2},{4,5},{5,4},{6,7},{7,6},{8,9},{9,8},{10,11... | collective-permute-start | bytes 344072 | tf_op jit(solution)/shard_map/ppermute | solution.py:58
  59.0 0.8 collective-permute-start.9
  59.9 2.1 %convolution_convert_fusion.g_ref = bf16[896,1024]{1,0:T(8,128)(2,1)S(1)} fusion(bf16[896,1024]{1,0:T(8,128)(2,1)S(1)} %bitcast.72, bf16[1024,4096]{1,0:T(8,128)(2,1)S(1)} %bitcast.59), kind=kOutput, calls=%fused_computation.8 | convolution fusion | flops 1879965696 | bytes 5767168 | tf_op jit(solution)/shard_map/dot_general | solution.py:125
  62.1 0.9 collective-permute-done.10
  63.0 0.3 fusion.17
  63.3 1.2 %collective-permute-done.11 = bf16[256,1024]{1,0:T(8,128)(2,1)S(1)} collective-permute-done((bf16[256,1024]{1,0:T(8,128)(2,1)S(1)}, bf16[256,1024]{1,0:T(8,128)(2,1)S(1)}, u32[]{:S(2)}, u32[]{:S(2)}) %collective-permute-start.11) | collective-permute-done | bytes 524320 | tf_op jit(solution)/shard_map/ppermute | solution.py:23
  64.9 0.6 collective-permute-start.13
  65.6 0.4 collective-permute-start.12
  66.0 3.8 %key_pass.2 = bf16[256,1024]{1,0:T(8,128)(2,1)S(1)} custom-call(s32[5]{0:T(128)S(1)} %stack.15.place_ref, bf16[896,1024]{1,0:T(8,128)(2,1)S(1)} %get-tuple-element.27.k_ref, bf16[896,1024]{1,0:T(8,128)(2,1)S(1)} %get-tuple-element.28.v_ref, bf16[896,1024]{1,0:T(8,128)(2,1)S(1)} %fusion.6.q_ref, bf16[896,1024]{1,0:T(8,128)(2,1)S(1)} %convolution_convert_fusion.g_ref, ...), custom_call_target="tpu_custom_call" | custom-call | flops 2147483648 | bytes 4194304 | tf_op jit(solution)/shard_map/key_pass/pallas_call | solution.py:348
  69.9 1.5 %collective-permute-done.13 = bf16[128,1024]{1,0:T(8,128)(2,1)S(1)} collective-permute-done((bf16[128,1024]{1,0:T(8,128)(2,1)S(1)}, bf16[128,1024]{1,0:T(8,128)(2,1)S(1)}, u32[]{:S(2)}, u32[]{:S(2)}) %collective-permute-start.13) | collective-permute-done | bytes 262176 | tf_op jit(solution)/shard_map/ppermute | solution.py:23
  71.4 0.6 collective-permute-done.12
  72.2 3.9 %key_pass.3 = bf16[256,1024]{1,0:T(8,128)(2,1)S(1)} custom-call(s32[5]{0:T(128)S(1)} %stack.15.place_ref, bf16[896,1024]{1,0:T(8,128)(2,1)S(1)} %get-tuple-element.27.k_ref, bf16[896,1024]{1,0:T(8,128)(2,1)S(1)} %get-tuple-element.28.v_ref, bf16[896,1024]{1,0:T(8,128)(2,1)S(1)} %fusion.6.q_ref, bf16[896,1024]{1,0:T(8,128)(2,1)S(1)} %convolution_convert_fusion.g_ref, ...), custom_call_target="tpu_custom_call" | custom-call | flops 2147483648 | bytes 4194304 | tf_op jit(solution)/shard_map/key_pass/pallas_call | solution.py:348
  76.8 0.3 fusion.103
  77.1 0.3 fusion.38
  77.5 1.6 %collective-permute-start.19 = (bf16[256,1024]{1,0:T(8,128)(2,1)S(1)}, bf16[256,1024]{1,0:T(8,128)(2,1)S(1)}, u32[]{:S(2)}, u32[]{:S(2)}) collective-permute-start(bf16[256,1024]{1,0:T(8,128)(2,1)S(1)} %fusion.38), channel_id=1, source_target_pairs={{0,16},{8,24},{16,0},{24,8},{1,17},{9,25},{17,1},{25,9},{2,18},{10... | collective-permute-start | bytes 1572872 | tf_op jit(solution)/shard_map/ppermute | solution.py:23
  79.0 0.3 fusion.98
  79.7 0.6 collective-permute-start.21
  80.5 4.7 %collective-permute-start.18 = (bf16[32,2048]{1,0:T(8,128)(2,1)S(1)}, bf16[32,2048]{1,0:T(8,128)(2,1)S(1)}, u32[]{:S(2)}, u32[]{:S(2)}) collective-permute-start(bf16[32,2048]{1,0:T(8,128)(2,1)S(1)} %get-tuple-element.63), channel_id=1, source_target_pairs={{0,1},{1,0},{2,3},{3,2},{4,5},{5,4},{6,7},{7,6},{8,9},{9,8},{10,11... | collective-permute-start | bytes 393224 | tf_op jit(solution)/shard_map/ppermute | solution.py:23
  85.1 1.2 %collective-permute-start.17 = (bf16[32,2048]{1,0:T(8,128)(2,1)S(1)}, bf16[32,2048]{1,0:T(8,128)(2,1)S(1)}, u32[]{:S(2)}, u32[]{:S(2)}) collective-permute-start(bf16[32,2048]{1,0:T(8,128)(2,1)S(1)} %get-tuple-element.64), channel_id=1, source_target_pairs={{0,2},{1,3},{2,0},{3,1},{4,6},{5,7},{6,4},{7,5},{8,10},{9,11},{10,... | collective-permute-start | bytes 393224 | tf_op jit(solution)/shard_map/ppermute | solution.py:23
  86.4 1.4 %collective-permute-start.16 = (bf16[32,2048]{1,0:T(8,128)(2,1)S(1)}, bf16[32,2048]{1,0:T(8,128)(2,1)S(1)}, u32[]{:S(2)}, u32[]{:S(2)}) collective-permute-start(bf16[32,2048]{1,0:T(8,128)(2,1)S(1)} %get-tuple-element.62), channel_id=1, source_target_pairs={{0,3},{1,2},{2,1},{3,0},{4,7},{5,6},{6,5},{7,4},{8,11},{9,10},{10,... | collective-permute-start | bytes 393224 | tf_op jit(solution)/shard_map/ppermute | solution.py:23
  87.8 2.0 %fusion.124 = (f32[256]{0:T(256)S(1)}, f32[256]{0:T(256)S(1)}, f32[256,1024]{1,0:T(8,128)S(1)}) fusion(f32[256]{0:T(256)S(1)} %get-tuple-element.47, f32[256]{0:T(256)S(1)} %get-tuple-element.48, bf16[1,16,16,1024]{3,2,1,0:T(8,128)(2,1)S(1)} %copy-done.1, f32[1024]{0:T(1024)S(1)} %copy-done.5, bf16[256,3072]{1,0:T(8,128)(2,1)S(1)} %slice_dynamic-update-slice_fusion, ...), kind=kOutput, calls=%fused_computation.196 | convolution fusion | flops 1612447232 | bytes 9445376 | tf_op jit(solution)/shard_map/dot_general | solution.py:125
  89.8 1.5 %fusion.33 = bf16[256,1024]{1,0:T(8,128)(2,1)} fusion(bf16[256,1024]{1,0:T(8,128)(2,1)S(1)} %get-tuple-element.39, bf16[1024,4096]{1,0:T(8,128)(2,1)S(1)} %bitcast.59, bf16[256,1024]{1,0:T(8,128)(2,1)S(1)} %bitcast.67, f32[256]{0:T(256)S(1)} %convert_element_type.128), kind=kOutput, calls=%fused_computation.40 | convolution fusion | flops 537919488 | bytes 3671040 | tf_op jit(solution)/shard_map/dot_general | solution.py:121
  91.4 1.2 %fusion.47 = bf16[256,1024]{1,0:T(8,128)(2,1)} fusion(f32[256,1024]{1,0:T(8,128)S(1)} %get-tuple-element.91, f32[256]{0:T(256)S(1)} %get-tuple-element.92, f32[256]{0:T(256)S(1)} %get-tuple-element.48, f32[256]{0:T(256)S(1)} %get-tuple-element.93, f32[256]{0:T(256)S(1)} %get-tuple-element.47, bf16[1,16,16,1024]{3,2,1,0:T(8,128)(2,1)S(1)} %copy-done.3, ...), kind=kLoop, calls=%fused_computation.52 | loop fusion | flops 2621440 | bytes 2625536 | tf_op jit(solution)/shard_map/convert_element_type | solution.py:555
  92.6 0.3 fusion.15
  93.0 1.6 %collective-permute-start.20 = (bf16[128,1024]{1,0:T(8,128)(2,1)S(1)}, bf16[128,1024]{1,0:T(8,128)(2,1)S(1)}, u32[]{:S(2)}, u32[]{:S(2)}) collective-permute-start(bf16[128,1024]{1,0:T(8,128)(2,1)S(1)} %dynamic-slice_convert_fusion.1), channel_id=1, source_target_pairs={{0,4},{4,0},{1,5},{5,1},{2,6},{6,2},{3,7},{7,3},{8,12},{12,8},{9,1... | collective-permute-start | bytes 786440 | tf_op jit(solution)/shard_map/ppermute | solution.py:23
  95.0 0.6 collective-permute-start.22
  95.6 2.5 %collective-permute-done.17 = bf16[32,2048]{1,0:T(8,128)(2,1)S(1)} collective-permute-done((bf16[32,2048]{1,0:T(8,128)(2,1)S(1)}, bf16[32,2048]{1,0:T(8,128)(2,1)S(1)}, u32[]{:S(2)}, u32[]{:S(2)}) %collective-permute-start.17) | collective-permute-done | bytes 131104 | tf_op jit(solution)/shard_map/ppermute | solution.py:23
  98.1 2.5 %collective-permute-done.20 = bf16[128,1024]{1,0:T(8,128)(2,1)S(1)} collective-permute-done((bf16[128,1024]{1,0:T(8,128)(2,1)S(1)}, bf16[128,1024]{1,0:T(8,128)(2,1)S(1)}, u32[]{:S(2)}, u32[]{:S(2)}) %collective-permute-start.20) | collective-permute-done | bytes 262176 | tf_op jit(solution)/shard_map/ppermute | solution.py:23
  100.7 1.6 %collective-permute-done.22 = bf16[128,1024]{1,0:T(8,128)(2,1)S(1)} collective-permute-done((bf16[128,1024]{1,0:T(8,128)(2,1)S(1)}, bf16[128,1024]{1,0:T(8,128)(2,1)S(1)}, u32[]{:S(2)}, u32[]{:S(2)}) %collective-permute-start.22) | collective-permute-done | bytes 262176 | tf_op jit(solution)/shard_map/ppermute | solution.py:23
  102.4 4.2 %collective-permute-start.25 = (bf16[32,2048]{1,0:T(8,128)(2,1)S(1)}, bf16[32,2048]{1,0:T(8,128)(2,1)S(1)}, u32[]{:S(2)}, u32[]{:S(2)}) collective-permute-start(bf16[32,2048]{1,0:T(8,128)(2,1)S(1)} %get-tuple-element.53), channel_id=1, source_target_pairs={{0,1},{1,0},{2,3},{3,2},{4,5},{5,4},{6,7},{7,6},{8,9},{9,8},{10,11... | collective-permute-start | bytes 393224 | tf_op jit(solution)/shard_map/ppermute | solution.py:23
  106.6 1.2 %collective-permute-start.24 = (bf16[32,2048]{1,0:T(8,128)(2,1)S(1)}, bf16[32,2048]{1,0:T(8,128)(2,1)S(1)}, u32[]{:S(2)}, u32[]{:S(2)}) collective-permute-start(bf16[32,2048]{1,0:T(8,128)(2,1)S(1)} %get-tuple-element.52), channel_id=1, source_target_pairs={{0,2},{1,3},{2,0},{3,1},{4,6},{5,7},{6,4},{7,5},{8,10},{9,11},{10,... | collective-permute-start | bytes 393224 | tf_op jit(solution)/shard_map/ppermute | solution.py:23
  107.9 1.4 %collective-permute-start.23 = (bf16[32,2048]{1,0:T(8,128)(2,1)S(1)}, bf16[32,2048]{1,0:T(8,128)(2,1)S(1)}, u32[]{:S(2)}, u32[]{:S(2)}) collective-permute-start(bf16[32,2048]{1,0:T(8,128)(2,1)S(1)} %get-tuple-element.51), channel_id=1, source_target_pairs={{0,3},{1,2},{2,1},{3,0},{4,7},{5,6},{6,5},{7,4},{8,11},{9,10},{10,... | collective-permute-start | bytes 393224 | tf_op jit(solution)/shard_map/ppermute | solution.py:23
  109.3 1.7 %collective-permute-done.25 = bf16[32,2048]{1,0:T(8,128)(2,1)S(1)} collective-permute-done((bf16[32,2048]{1,0:T(8,128)(2,1)S(1)}, bf16[32,2048]{1,0:T(8,128)(2,1)S(1)}, u32[]{:S(2)}, u32[]{:S(2)}) %collective-permute-start.25) | collective-permute-done | bytes 131104 | tf_op jit(solution)/shard_map/ppermute | solution.py:23
  111.0 7.2 %collective-permute-done.24 = bf16[32,2048]{1,0:T(8,128)(2,1)S(1)} collective-permute-done((bf16[32,2048]{1,0:T(8,128)(2,1)S(1)}, bf16[32,2048]{1,0:T(8,128)(2,1)S(1)}, u32[]{:S(2)}, u32[]{:S(2)}) %collective-permute-start.24) | collective-permute-done | bytes 131104 | tf_op jit(solution)/shard_map/ppermute | solution.py:23
  118.3 0.8 broadcast_multiply_fusion
  (82 shorter events, 5.1 us)
Async XLA Ops:
  1.5 1.0 copy-start
  2.6 1.0 copy-start.2
  3.6 0.7 copy-start.4
  6.0 12.3 %collective-permute-start = (bf16[6,16,2048]{2,1,0:T(8,128)(2,1)S(1)}, bf16[6,16,2048]{2,1,0:T(8,128)(2,1)S(1)}, u32[]{:S(2)}, u32[]{:S(2)}) collective-permute-start(bf16[6,16,2048]{2,1,0:T(8,128)(2,1)S(1)} %bitcast.71), channel_id=1, source_target_pairs={{0,4},{4,0},{1,5},{5,1},{2,6},{6,2},{3,7},{7,3},{8,12},{12,8},{9,1... | collective-permute-start | bytes 1179656 | tf_op jit(solution)/shard_map/ppermute | solution.py:23
  9.0 40.2 %collective-permute-start.6 = (bf16[256,2048]{1,0:T(8,128)(2,1)S(1)}, bf16[256,2048]{1,0:T(8,128)(2,1)S(1)}, u32[]{:S(2)}, u32[]{:S(2)}) collective-permute-start(bf16[256,2048]{1,0:T(8,128)(2,1)S(1)} %get-tuple-element.24), channel_id=1, source_target_pairs={{0,8},{8,0},{16,24},{24,16},{1,9},{9,1},{17,25},{25,17},{2,10},{10... | collective-permute-start | bytes 3145736 | tf_op jit(solution)/shard_map/ppermute | solution.py:23
  10.1 15.0 %collective-permute-start.3 = (bf16[16,8,2048]{2,1,0:T(8,128)(2,1)}, bf16[16,8,2048]{2,1,0:T(8,128)(2,1)}, u32[]{:S(2)}, u32[]{:S(2)}) collective-permute-start(bf16[16,8,2048]{2,1,0:T(8,128)(2,1)} %get-tuple-element.69), channel_id=1, source_target_pairs={{0,1},{1,0},{2,3},{3,2},{4,5},{5,4},{6,7},{7,6},{8,9},{9,8},{10,11... | collective-permute-start | bytes 1572872 | tf_op jit(solution)/shard_map/ppermute | solution.py:58
  11.6 13.5 %collective-permute-start.4 = (bf16[16,8,2048]{2,1,0:T(8,128)(2,1)}, bf16[16,8,2048]{2,1,0:T(8,128)(2,1)}, u32[]{:S(2)}, u32[]{:S(2)}) collective-permute-start(bf16[16,8,2048]{2,1,0:T(8,128)(2,1)} %get-tuple-element.70), channel_id=1, source_target_pairs={{1,2},{2,1},{5,6},{6,5},{9,10},{10,9},{13,14},{14,13},{17,18},{18,... | collective-permute-start | bytes 1572872 | tf_op jit(solution)/shard_map/ppermute | solution.py:59
  18.3 10.5 %collective-permute-start.1 = (bf16[6,8,2048]{2,1,0:T(8,128)(2,1)S(1)}, bf16[6,8,2048]{2,1,0:T(8,128)(2,1)S(1)}, u32[]{:S(2)}, u32[]{:S(2)}) collective-permute-start(bf16[6,8,2048]{2,1,0:T(8,128)(2,1)S(1)} %get-tuple-element.83), channel_id=1, source_target_pairs={{0,1},{1,0},{2,3},{3,2},{4,5},{5,4},{6,7},{7,6},{8,9},{9,8},{10,11... | collective-permute-start | bytes 589832 | tf_op jit(solution)/shard_map/ppermute | solution.py:58
  22.0 6.8 %collective-permute-start.2 = (bf16[6,8,2048]{2,1,0:T(8,128)(2,1)S(1)}, bf16[6,8,2048]{2,1,0:T(8,128)(2,1)S(1)}, u32[]{:S(2)}, u32[]{:S(2)}) collective-permute-start(bf16[6,8,2048]{2,1,0:T(8,128)(2,1)S(1)} %get-tuple-element.84), channel_id=1, source_target_pairs={{1,2},{2,1},{5,6},{6,5},{9,10},{10,9},{13,14},{14,13},{17,18},{18,... | collective-permute-start | bytes 589832 | tf_op jit(solution)/shard_map/ppermute | solution.py:59
  28.9 2.2 %slice-start = ((s8[8388608]{0:T(1024)(128)(4,1)}), s8[4194304]{0:T(1024)(128)(4,1)S(1)}, s32[]{:S(2)}) async-start(s8[8388608]{0:T(1024)(128)(4,1)} %bitcast.58), calls=%async_computation | async-start | bytes 8388608
  29.2 3.2 %slice-start.1 = ((s8[8388608]{0:T(1024)(128)(4,1)}), s8[4194304]{0:T(1024)(128)(4,1)S(1)}, s32[]{:S(2)}) async-start(s8[8388608]{0:T(1024)(128)(4,1)} %bitcast.58), calls=%async_computation.1 | async-start | bytes 8388608
  44.9 4.4 %collective-permute-start.7 = (bf16[2,256,1024]{2,1,0:T(8,128)(2,1)S(1)}, bf16[2,256,1024]{2,1,0:T(8,128)(2,1)S(1)}, u32[]{:S(2)}, u32[]{:S(2)}) collective-permute-start(bf16[2,256,1024]{2,1,0:T(8,128)(2,1)S(1)} %get-tuple-element.26), channel_id=1, source_target_pairs={{0,8},{8,0},{16,24},{24,16},{1,9},{9,1},{17,25},{25,17},{2,10},{10... | collective-permute-start | bytes 3145736 | tf_op jit(solution)/shard_map/ppermute | solution.py:23
  45.0 4.2 %collective-permute-start.5 = (f32[6,16,128]{2,1,0:T(8,128)S(1)}, f32[6,16,128]{2,1,0:T(8,128)S(1)}, u32[]{:S(2)}, u32[]{:S(2)}) collective-permute-start(f32[6,16,128]{2,1,0:T(8,128)S(1)} %bitcast.74), channel_id=1, source_target_pairs={{0,4},{4,0},{1,5},{5,1},{2,6},{6,2},{3,7},{7,3},{8,12},{12,8},{9,1... | collective-permute-start | bytes 147464 | tf_op jit(solution)/shard_map/ppermute | solution.py:23
  49.8 13.2 %collective-permute-start.10 = (bf16[256,1024]{1,0:T(8,128)(2,1)S(1)}, bf16[256,1024]{1,0:T(8,128)(2,1)S(1)}, u32[]{:S(2)}, u32[]{:S(2)}) collective-permute-start(bf16[256,1024]{1,0:T(8,128)(2,1)S(1)} %fusion.36), channel_id=1, source_target_pairs={{0,16},{8,24},{16,0},{24,8},{1,17},{9,25},{17,1},{25,9},{2,18},{10... | collective-permute-start | bytes 1572872 | tf_op jit(solution)/shard_map/ppermute | solution.py:23
  51.7 12.9 %collective-permute-start.11 = (bf16[256,1024]{1,0:T(8,128)(2,1)S(1)}, bf16[256,1024]{1,0:T(8,128)(2,1)S(1)}, u32[]{:S(2)}, u32[]{:S(2)}) collective-permute-start(bf16[256,1024]{1,0:T(8,128)(2,1)S(1)} %fusion.37), channel_id=1, source_target_pairs={{0,4},{4,0},{1,5},{5,1},{2,6},{6,2},{3,7},{7,3},{8,12},{12,8},{9,1... | collective-permute-start | bytes 1572872 | tf_op jit(solution)/shard_map/ppermute | solution.py:23
  54.4 7.6 %collective-permute-start.8 = (f32[28,8,128]{2,1,0:T(8,128)S(1)}, f32[28,8,128]{2,1,0:T(8,128)S(1)}, u32[]{:S(2)}, u32[]{:S(2)}) collective-permute-start(f32[28,8,128]{2,1,0:T(8,128)S(1)} %get-tuple-element.87), channel_id=1, source_target_pairs={{0,1},{1,0},{2,3},{3,2},{4,5},{5,4},{6,7},{7,6},{8,9},{9,8},{10,11... | collective-permute-start | bytes 344072 | tf_op jit(solution)/shard_map/ppermute | solution.py:58
  59.0 3.0 %collective-permute-start.9 = (f32[28,8,128]{2,1,0:T(8,128)S(1)}, f32[28,8,128]{2,1,0:T(8,128)S(1)}, u32[]{:S(2)}, u32[]{:S(2)}) collective-permute-start(f32[28,8,128]{2,1,0:T(8,128)S(1)} %get-tuple-element.88), channel_id=1, source_target_pairs={{1,2},{2,1},{5,6},{6,5},{9,10},{10,9},{13,14},{14,13},{17,18},{18,... | collective-permute-start | bytes 344072 | tf_op jit(solution)/shard_map/ppermute | solution.py:59
  64.9 6.4 %collective-permute-start.13 = (bf16[128,1024]{1,0:T(8,128)(2,1)S(1)}, bf16[128,1024]{1,0:T(8,128)(2,1)S(1)}, u32[]{:S(2)}, u32[]{:S(2)}) collective-permute-start(bf16[128,1024]{1,0:T(8,128)(2,1)S(1)} %dynamic-slice_convert_fusion.2), channel_id=1, source_target_pairs={{0,16},{8,24},{16,0},{24,8},{1,17},{9,25},{17,1},{25,9},{2,18},{10... | collective-permute-start | bytes 786440 | tf_op jit(solution)/shard_map/ppermute | solution.py:23
  65.6 6.4 %collective-permute-start.12 = (bf16[128,1024]{1,0:T(8,128)(2,1)S(1)}, bf16[128,1024]{1,0:T(8,128)(2,1)S(1)}, u32[]{:S(2)}, u32[]{:S(2)}) collective-permute-start(bf16[128,1024]{1,0:T(8,128)(2,1)S(1)} %dynamic-slice_convert_fusion.3), channel_id=1, source_target_pairs={{0,4},{4,0},{1,5},{5,1},{2,6},{6,2},{3,7},{7,3},{8,12},{12,8},{9,1... | collective-permute-start | bytes 786440 | tf_op jit(solution)/shard_map/ppermute | solution.py:23
  69.8 7.0 %collective-permute-start.14 = (bf16[256,1024]{1,0:T(8,128)(2,1)S(1)}, bf16[256,1024]{1,0:T(8,128)(2,1)S(1)}, u32[]{:S(2)}, u32[]{:S(2)}) collective-permute-start(bf16[256,1024]{1,0:T(8,128)(2,1)S(1)} %key_pass.2), channel_id=1, source_target_pairs={{0,8},{8,0},{16,24},{24,16},{1,9},{9,1},{17,25},{25,17},{2,10},{10... | collective-permute-start | bytes 1572872 | tf_op jit(solution)/shard_map/ppermute | solution.py:23
  76.0 3.3 %collective-permute-start.15 = (bf16[256,1024]{1,0:T(8,128)(2,1)S(1)}, bf16[256,1024]{1,0:T(8,128)(2,1)S(1)}, u32[]{:S(2)}, u32[]{:S(2)}) collective-permute-start(bf16[256,1024]{1,0:T(8,128)(2,1)S(1)} %key_pass.3), channel_id=1, source_target_pairs={{0,8},{8,0},{16,24},{24,16},{1,9},{9,1},{17,25},{25,17},{2,10},{10... | collective-permute-start | bytes 1572872 | tf_op jit(solution)/shard_map/ppermute | solution.py:23
  77.5 15.1 %collective-permute-start.19 = (bf16[256,1024]{1,0:T(8,128)(2,1)S(1)}, bf16[256,1024]{1,0:T(8,128)(2,1)S(1)}, u32[]{:S(2)}, u32[]{:S(2)}) collective-permute-start(bf16[256,1024]{1,0:T(8,128)(2,1)S(1)} %fusion.38), channel_id=1, source_target_pairs={{0,16},{8,24},{16,0},{24,8},{1,17},{9,25},{17,1},{25,9},{2,18},{10... | collective-permute-start | bytes 1572872 | tf_op jit(solution)/shard_map/ppermute | solution.py:23
  79.4 8.4 %copy-start.1 = (bf16[1,16,16,1024]{3,2,1,0:T(8,128)(2,1)S(1)}, bf16[1,16,16,1024]{3,2,1,0:T(8,128)(2,1)}, u32[]{:S(2)}) copy-start(bf16[1,16,16,1024]{3,2,1,0:T(8,128)(2,1)} %param.5) | copy-start | bytes 1572868
  79.4 8.4 %copy-start.5 = (f32[1024]{0:T(1024)S(1)}, f32[1024]{0:T(1024)}, u32[]{:S(2)}) copy-start(f32[1024]{0:T(1024)} %param.7) | copy-start | bytes 12292
  79.7 14.9 %collective-permute-start.21 = (bf16[256,1024]{1,0:T(8,128)(2,1)S(1)}, bf16[256,1024]{1,0:T(8,128)(2,1)S(1)}, u32[]{:S(2)}, u32[]{:S(2)}) collective-permute-start(bf16[256,1024]{1,0:T(8,128)(2,1)S(1)} %fusion.39), channel_id=1, source_target_pairs={{0,4},{4,0},{1,5},{5,1},{2,6},{6,2},{3,7},{7,3},{8,12},{12,8},{9,1... | collective-permute-start | bytes 1572872 | tf_op jit(solution)/shard_map/ppermute | solution.py:23
  80.5 15.1 %collective-permute-start.18 = (bf16[32,2048]{1,0:T(8,128)(2,1)S(1)}, bf16[32,2048]{1,0:T(8,128)(2,1)S(1)}, u32[]{:S(2)}, u32[]{:S(2)}) collective-permute-start(bf16[32,2048]{1,0:T(8,128)(2,1)S(1)} %get-tuple-element.63), channel_id=1, source_target_pairs={{0,1},{1,0},{2,3},{3,2},{4,5},{5,4},{6,7},{7,6},{8,9},{9,8},{10,11... | collective-permute-start | bytes 393224 | tf_op jit(solution)/shard_map/ppermute | solution.py:23
  85.1 12.9 %collective-permute-start.17 = (bf16[32,2048]{1,0:T(8,128)(2,1)S(1)}, bf16[32,2048]{1,0:T(8,128)(2,1)S(1)}, u32[]{:S(2)}, u32[]{:S(2)}) collective-permute-start(bf16[32,2048]{1,0:T(8,128)(2,1)S(1)} %get-tuple-element.64), channel_id=1, source_target_pairs={{0,2},{1,3},{2,0},{3,1},{4,6},{5,7},{6,4},{7,5},{8,10},{9,11},{10,... | collective-permute-start | bytes 393224 | tf_op jit(solution)/shard_map/ppermute | solution.py:23
  86.4 11.7 %collective-permute-start.16 = (bf16[32,2048]{1,0:T(8,128)(2,1)S(1)}, bf16[32,2048]{1,0:T(8,128)(2,1)S(1)}, u32[]{:S(2)}, u32[]{:S(2)}) collective-permute-start(bf16[32,2048]{1,0:T(8,128)(2,1)S(1)} %get-tuple-element.62), channel_id=1, source_target_pairs={{0,3},{1,2},{2,1},{3,0},{4,7},{5,6},{6,5},{7,4},{8,11},{9,10},{10,... | collective-permute-start | bytes 393224 | tf_op jit(solution)/shard_map/ppermute | solution.py:23
  89.8 1.5 %copy-start.3 = (bf16[1,16,16,1024]{3,2,1,0:T(8,128)(2,1)S(1)}, bf16[1,16,16,1024]{3,2,1,0:T(8,128)(2,1)}, u32[]{:S(2)}) copy-start(bf16[1,16,16,1024]{3,2,1,0:T(8,128)(2,1)} %param.9) | copy-start | bytes 1572868
  93.0 7.6 %collective-permute-start.20 = (bf16[128,1024]{1,0:T(8,128)(2,1)S(1)}, bf16[128,1024]{1,0:T(8,128)(2,1)S(1)}, u32[]{:S(2)}, u32[]{:S(2)}) collective-permute-start(bf16[128,1024]{1,0:T(8,128)(2,1)S(1)} %dynamic-slice_convert_fusion.1), channel_id=1, source_target_pairs={{0,4},{4,0},{1,5},{5,1},{2,6},{6,2},{3,7},{7,3},{8,12},{12,8},{9,1... | collective-permute-start | bytes 786440 | tf_op jit(solution)/shard_map/ppermute | solution.py:23
  95.0 7.3 %collective-permute-start.22 = (bf16[128,1024]{1,0:T(8,128)(2,1)S(1)}, bf16[128,1024]{1,0:T(8,128)(2,1)S(1)}, u32[]{:S(2)}, u32[]{:S(2)}) collective-permute-start(bf16[128,1024]{1,0:T(8,128)(2,1)S(1)} %dynamic-slice_convert_fusion), channel_id=1, source_target_pairs={{0,16},{8,24},{16,0},{24,8},{1,17},{9,25},{17,1},{25,9},{2,18},{10... | collective-permute-start | bytes 786440 | tf_op jit(solution)/shard_map/ppermute | solution.py:23
  102.4 8.6 %collective-permute-start.25 = (bf16[32,2048]{1,0:T(8,128)(2,1)S(1)}, bf16[32,2048]{1,0:T(8,128)(2,1)S(1)}, u32[]{:S(2)}, u32[]{:S(2)}) collective-permute-start(bf16[32,2048]{1,0:T(8,128)(2,1)S(1)} %get-tuple-element.53), channel_id=1, source_target_pairs={{0,1},{1,0},{2,3},{3,2},{4,5},{5,4},{6,7},{7,6},{8,9},{9,8},{10,11... | collective-permute-start | bytes 393224 | tf_op jit(solution)/shard_map/ppermute | solution.py:23
  106.6 11.5 %collective-permute-start.24 = (bf16[32,2048]{1,0:T(8,128)(2,1)S(1)}, bf16[32,2048]{1,0:T(8,128)(2,1)S(1)}, u32[]{:S(2)}, u32[]{:S(2)}) collective-permute-start(bf16[32,2048]{1,0:T(8,128)(2,1)S(1)} %get-tuple-element.52), channel_id=1, source_target_pairs={{0,2},{1,3},{2,0},{3,1},{4,6},{5,7},{6,4},{7,5},{8,10},{9,11},{10,... | collective-permute-start | bytes 393224 | tf_op jit(solution)/shard_map/ppermute | solution.py:23
  107.9 10.3 %collective-permute-start.23 = (bf16[32,2048]{1,0:T(8,128)(2,1)S(1)}, bf16[32,2048]{1,0:T(8,128)(2,1)S(1)}, u32[]{:S(2)}, u32[]{:S(2)}) collective-permute-start(bf16[32,2048]{1,0:T(8,128)(2,1)S(1)} %get-tuple-element.51), channel_id=1, source_target_pairs={{0,3},{1,2},{2,1},{3,0},{4,7},{5,6},{6,5},{7,4},{8,11},{9,10},{10,... | collective-permute-start | bytes 393224 | tf_op jit(solution)/shard_map/ppermute | solution.py:23

commit v4 on v3

--- a/solution.py
+++ b/solution.py
@@ -59,6 +59,10 @@
     two = lax.ppermute(jnp.where(even, first, last), "gx", [p[1:] for p in pairs if p[0] == 1])
     right, left = jnp.where(even, one, two), jnp.where(even, two, one)
     return jnp.concatenate([block, right, left], axis=1)
+
+
+def in_hbm(array):
+    return pltpu.with_memory_space_constraint(array, pltpu.HBM)
 
 
 def prepare(place_ref, x_ref, c_ref, t_ref, gain_ref, both_ref, face_ref, moment_ref):
@@ -98,7 +102,7 @@
         compiler_params=pltpu.CompilerParams(**PARAMS),
         cost_estimate=pl.CostEstimate(flops=0, bytes_accessed=3 * 1024 * 1024, transcendentals=0),
         name="prepare",
-    )(place, tokens, cotangent, tissue, gain)
+    )(place, in_hbm(tokens), in_hbm(cotangent), tissue, in_hbm(gain))
 
 
 def spread_heads(block, head_dim):
@@ -338,7 +342,7 @@
         compiler_params=pltpu.CompilerParams(**PARAMS),
         cost_estimate=attention_cost(tile, groups, part),
         name="query_pass",
-    )(place, queries, grads, normed_ext, weights, weights)
+    )(place, queries, grads, normed_ext, in_hbm(weights), in_hbm(weights))
 
 
 def run_keys(place, keys, values, queries, grads, stats, head_dim, tile, first, groups):

time: 120 us -> 116 us (0.967)
  local copies, waits for them, and re-layouts: 6.75 us -> 1.69 us
  Pallas kernels: 21.8 us -> 23.3 us
    unnamed x25 -> x19, local copies, waits for them, and re-layouts: 5.2 us -> 0.16 us
  transfers between devices with their start and end apart: 26 -> 26, of which waited for: 12 -> 12; matrix products, arithmetic and copies ran while one was open for 19% -> 20% of each run, Pallas kernels for 17% -> 18%
where the time goes in v4:
time: 116 us
  starting transfers between devices  38.2 us (33%)
  waiting for transfers between devices  26.9 us (23%)
  Pallas kernels  23.3 us (20%)
  matrix products  17.7 us (15%)
  other arithmetic  6.69 us (6%)
  local copies, waits for them, and re-layouts  1.69 us (1%)
  between operations  1.32 us (1%)
    ppermute x20, starting transfers between devices, swapped(): return lax.ppermute(array, axis, [(i, i ^ by) for i in range(count)])  25.2 us
    ppermute x20, waiting for transfers between devices, swapped(): return lax.ppermute(array, axis, [(i, i ^ by) for i in range(count)])  22 us
    pallas_call x1, Pallas kernels, run_queries(): pl.pallas_call(functools.partial(query_pass, head_dim, tile), grid=(group...  12.7 us
    ppermute x3, starting transfers between devices, column_halo(): lax.ppermute(jnp.where(even, last, first), 'gx', [p[1:] for p in pairs if...  9.93 us
    pallas_call x2, Pallas kernels, run_keys(): pl.pallas_call(functools.partial(key_pass, head_dim, tile, first), grid=(...  7.69 us
    dot_general x3, matrix products, times_t(): lax.dot_general(left, right, (((1,), (1,)), ((), ())), preferred_element_...  6.49 us
    dot_general x3, matrix products, times(): return jnp.dot(left, right, preferred_element_type=F32)  5.91 us
    dot_general x16, matrix products, product_t(): lax.dot_general(left, right, (((0,), (0,)), ((), ())), preferred_element_...  5.27 us
  transfers between devices with their start and end apart: 26, of which 12 were waited for; matrix products, arithmetic and copies ran while one was open for 20% of the time, Pallas kernels for 18%

profile of v4, /device:TPU:0, one launch (start us, length us, event | category | flops | bytes accessed | tf_op | source)
XLA Modules:
  0.0 115.7 jit_solution(61492949789244644)
XLA Ops:
  0.6 0.7 convert_element_type.127
  1.5 2.8 %prepare.1 = (bf16[256,2048]{1,0:T(8,128)(2,1)S(1)}, bf16[96,2048]{1,0:T(8,128)(2,1)S(1)}, f32[256,128]{1,0:T(8,128)S(1)}) custom-call(s32[5]{0:T(128)S(1)} %stack.15.place_ref, bf16[256,1024]{1,0:T(8,128)(2,1)} %bitcast.68, bf16[256,1024]{1,0:T(8,128)(2,1)} %bitcast.70, f32[256,1]{1,0:T(8,128)S(1)} %convert_element_type.165.t_ref, f32[1,1024]{1,0:T(1,128)} %bitcast.74), custom_call_target="tpu_custom_call" | custom-call | bytes 3145728 | tf_op jit(solution)/shard_map/prepare/pallas_call | solution.py:92
  4.4 3.0 %collective-permute-start = (bf16[6,16,2048]{2,1,0:T(8,128)(2,1)S(1)}, bf16[6,16,2048]{2,1,0:T(8,128)(2,1)S(1)}, u32[]{:S(2)}, u32[]{:S(2)}) collective-permute-start(bf16[6,16,2048]{2,1,0:T(8,128)(2,1)S(1)} %bitcast.65), channel_id=1, source_target_pairs={{0,4},{4,0},{1,5},{5,1},{2,6},{6,2},{3,7},{7,3},{8,12},{12,8},{9,1... | collective-permute-start | bytes 1179656 | tf_op jit(solution)/shard_map/ppermute | solution.py:23
  7.4 1.0 broadcast_select_fusion.5
  8.5 1.6 %collective-permute-start.3 = (bf16[16,8,2048]{2,1,0:T(8,128)(2,1)}, bf16[16,8,2048]{2,1,0:T(8,128)(2,1)}, u32[]{:S(2)}, u32[]{:S(2)}) collective-permute-start(bf16[16,8,2048]{2,1,0:T(8,128)(2,1)} %get-tuple-element.69), channel_id=1, source_target_pairs={{0,1},{1,0},{2,3},{3,2},{4,5},{5,4},{6,7},{7,6},{8,9},{9,8},{10,11... | collective-permute-start | bytes 1572872 | tf_op jit(solution)/shard_map/ppermute | solution.py:58
  10.0 1.5 %collective-permute-start.4 = (bf16[16,8,2048]{2,1,0:T(8,128)(2,1)}, bf16[16,8,2048]{2,1,0:T(8,128)(2,1)}, u32[]{:S(2)}, u32[]{:S(2)}) collective-permute-start(bf16[16,8,2048]{2,1,0:T(8,128)(2,1)} %get-tuple-element.70), channel_id=1, source_target_pairs={{1,2},{2,1},{5,6},{6,5},{9,10},{10,9},{13,14},{14,13},{17,18},{18,... | collective-permute-start | bytes 1572872 | tf_op jit(solution)/shard_map/ppermute | solution.py:59
  11.6 2.3 %fusion.30.q_ref = bf16[256,1024]{1,0:T(8,128)(2,1)S(1)} fusion(bf16[1024,4096]{1,0:T(8,128)(2,1)} %value_w_ref.1, bf16[256,2048]{1,0:T(8,128)(2,1)S(1)} %get-tuple-element.24), kind=kOutput, calls=%fused_computation.39 | convolution fusion | flops 537133056 | bytes 3145728 | tf_op jit(solution)/shard_map/dot_general | solution.py:125
  14.1 2.3 %fusion.27.g_ref = bf16[256,1024]{1,0:T(8,128)(2,1)S(1)} fusion(bf16[1024,4096]{1,0:T(8,128)(2,1)} %value_w_ref.1, bf16[256,2048]{1,0:T(8,128)(2,1)S(1)} %get-tuple-element.24), kind=kOutput, calls=%fused_computation.38 | convolution fusion | flops 537133056 | bytes 3145728 | tf_op jit(solution)/shard_map/dot_general | solution.py:129
  16.7 3.7 %collective-permute-start.1 = (bf16[6,8,2048]{2,1,0:T(8,128)(2,1)S(1)}, bf16[6,8,2048]{2,1,0:T(8,128)(2,1)S(1)}, u32[]{:S(2)}, u32[]{:S(2)}) collective-permute-start(bf16[6,8,2048]{2,1,0:T(8,128)(2,1)S(1)} %get-tuple-element.83), channel_id=1, source_target_pairs={{0,1},{1,0},{2,3},{3,2},{4,5},{5,4},{6,7},{7,6},{8,9},{9,8},{10,11... | collective-permute-start | bytes 589832 | tf_op jit(solution)/shard_map/ppermute | solution.py:58
  20.4 0.7 collective-permute-start.2
  21.1 2.4 %collective-permute-done.3 = bf16[16,8,2048]{2,1,0:T(8,128)(2,1)} collective-permute-done((bf16[16,8,2048]{2,1,0:T(8,128)(2,1)}, bf16[16,8,2048]{2,1,0:T(8,128)(2,1)}, u32[]{:S(2)}, u32[]{:S(2)}) %collective-permute-start.3) | collective-permute-done | bytes 524320 | tf_op jit(solution)/shard_map/ppermute | solution.py:58
  23.5 1.3 %broadcast_select_fusion.3 = (bf16[16,8,2048]{2,1,0:T(8,128)(2,1)S(1)}, bf16[16,8,2048]{2,1,0:T(8,128)(2,1)S(1)}) fusion(bf16[16,8,2048]{2,1,0:T(8,128)(2,1)} %collective-permute-done.3, bf16[16,8,2048]{2,1,0:T(8,128)(2,1)} %collective-permute-done.4, pred[]{:T(512)S(6)} %eq.32), kind=kLoop, calls=%fused_computation.73 | loop fusion | flops 524288 | bytes 2097153 | tf_op jit(solution)/shard_map/jit(_where)/select_n | solution.py:60
  24.8 2.4 %collective-permute-done.1 = bf16[6,8,2048]{2,1,0:T(8,128)(2,1)S(1)} collective-permute-done((bf16[6,8,2048]{2,1,0:T(8,128)(2,1)S(1)}, bf16[6,8,2048]{2,1,0:T(8,128)(2,1)S(1)}, u32[]{:S(2)}, u32[]{:S(2)}) %collective-permute-start.1) | collective-permute-done | bytes 196640 | tf_op jit(solution)/shard_map/ppermute | solution.py:58
  27.3 0.3 broadcast_select_fusion.1
  27.6 0.6 pad_maximum_fusion
  28.2 0.4 fusion.125
  28.6 12.7 %query_pass.1 = (bf16[2,256,1024]{2,1,0:T(8,128)(2,1)S(1)}, f32[256,128]{1,0:T(8,128)S(1)}, bf16[896,1024]{1,0:T(8,128)(2,1)S(1)}, bf16[896,1024]{1,0:T(8,128)(2,1)S(1)}) custom-call(s32[5]{0:T(128)S(1)} %stack.15.place_ref, bf16[256,1024]{1,0:T(8,128)(2,1)S(1)} %fusion.30.q_ref, bf16[256,1024]{1,0:T(8,128)(2,1)S(1)} %fusion.27.g_ref, ...), custom_call_target="tpu_custom_call" | custom-call | flops 4294967296 | bytes 4194304 | tf_op jit(solution)/shard_map/query_pass/pallas_call | solution.py:318
  41.5 0.4 collective-permute-start.5
  41.9 0.3 fusion.50
  42.2 0.3 fusion.48
  42.7 0.3 fusion.59
  43.0 0.3 fusion.57
  43.4 2.3 %collective-permute-done.5 = f32[6,16,128]{2,1,0:T(8,128)S(1)} collective-permute-done((f32[6,16,128]{2,1,0:T(8,128)S(1)}, f32[6,16,128]{2,1,0:T(8,128)S(1)}, u32[]{:S(2)}, u32[]{:S(2)}) %collective-permute-start.5) | collective-permute-done | bytes 49184 | tf_op jit(solution)/shard_map/ppermute | solution.py:23
  45.9 0.3 fusion.36
  46.3 1.6 %collective-permute-start.10 = (bf16[256,1024]{1,0:T(8,128)(2,1)S(1)}, bf16[256,1024]{1,0:T(8,128)(2,1)S(1)}, u32[]{:S(2)}, u32[]{:S(2)}) collective-permute-start(bf16[256,1024]{1,0:T(8,128)(2,1)S(1)} %fusion.36), channel_id=1, source_target_pairs={{0,16},{8,24},{16,0},{24,8},{1,17},{9,25},{17,1},{25,9},{2,18},{10... | collective-permute-start | bytes 1572872 | tf_op jit(solution)/shard_map/ppermute | solution.py:23
  48.2 0.6 collective-permute-start.11
  48.8 2.1 %fusion.6.q_ref = bf16[896,1024]{1,0:T(8,128)(2,1)S(1)} fusion(bf16[896,1024]{1,0:T(8,128)(2,1)S(1)} %bitcast.61, bf16[1024,4096]{1,0:T(8,128)(2,1)S(1)} %bitcast.67), kind=kOutput, calls=%fused_computation.7 | convolution fusion | flops 1879965696 | bytes 5767168 | tf_op jit(solution)/shard_map/dot_general | solution.py:125
  50.9 4.7 %collective-permute-start.8 = (f32[28,8,128]{2,1,0:T(8,128)S(1)}, f32[28,8,128]{2,1,0:T(8,128)S(1)}, u32[]{:S(2)}, u32[]{:S(2)}) collective-permute-start(f32[28,8,128]{2,1,0:T(8,128)S(1)} %get-tuple-element.87), channel_id=1, source_target_pairs={{0,1},{1,0},{2,3},{3,2},{4,5},{5,4},{6,7},{7,6},{8,9},{9,8},{10,11... | collective-permute-start | bytes 344072 | tf_op jit(solution)/shard_map/ppermute | solution.py:58
  55.5 0.8 collective-permute-start.9
  56.4 2.1 %convolution_convert_fusion.g_ref = bf16[896,1024]{1,0:T(8,128)(2,1)S(1)} fusion(bf16[896,1024]{1,0:T(8,128)(2,1)S(1)} %bitcast.71, bf16[1024,4096]{1,0:T(8,128)(2,1)S(1)} %bitcast.67), kind=kOutput, calls=%fused_computation.8 | convolution fusion | flops 1879965696 | bytes 5767168 | tf_op jit(solution)/shard_map/dot_general | solution.py:129
  58.6 0.9 collective-permute-done.10
  59.5 0.3 fusion.17
  59.8 1.3 %collective-permute-done.11 = bf16[256,1024]{1,0:T(8,128)(2,1)S(1)} collective-permute-done((bf16[256,1024]{1,0:T(8,128)(2,1)S(1)}, bf16[256,1024]{1,0:T(8,128)(2,1)S(1)}, u32[]{:S(2)}, u32[]{:S(2)}) %collective-permute-start.11) | collective-permute-done | bytes 524320 | tf_op jit(solution)/shard_map/ppermute | solution.py:23
  61.4 0.6 collective-permute-start.13
  62.1 0.4 collective-permute-start.12
  62.5 3.8 %key_pass.2 = bf16[256,1024]{1,0:T(8,128)(2,1)S(1)} custom-call(s32[5]{0:T(128)S(1)} %stack.15.place_ref, bf16[896,1024]{1,0:T(8,128)(2,1)S(1)} %get-tuple-element.27.k_ref, bf16[896,1024]{1,0:T(8,128)(2,1)S(1)} %get-tuple-element.28.v_ref, bf16[896,1024]{1,0:T(8,128)(2,1)S(1)} %fusion.6.q_ref, bf16[896,1024]{1,0:T(8,128)(2,1)S(1)} %convolution_convert_fusion.g_ref, ...), custom_call_target="tpu_custom_call" | custom-call | flops 2147483648 | bytes 4194304 | tf_op jit(solution)/shard_map/key_pass/pallas_call | solution.py:352
  66.4 1.5 %collective-permute-done.13 = bf16[128,1024]{1,0:T(8,128)(2,1)S(1)} collective-permute-done((bf16[128,1024]{1,0:T(8,128)(2,1)S(1)}, bf16[128,1024]{1,0:T(8,128)(2,1)S(1)}, u32[]{:S(2)}, u32[]{:S(2)}) %collective-permute-start.13) | collective-permute-done | bytes 262176 | tf_op jit(solution)/shard_map/ppermute | solution.py:23
  67.9 0.6 collective-permute-done.12
  68.7 3.9 %key_pass.3 = bf16[256,1024]{1,0:T(8,128)(2,1)S(1)} custom-call(s32[5]{0:T(128)S(1)} %stack.15.place_ref, bf16[896,1024]{1,0:T(8,128)(2,1)S(1)} %get-tuple-element.27.k_ref, bf16[896,1024]{1,0:T(8,128)(2,1)S(1)} %get-tuple-element.28.v_ref, bf16[896,1024]{1,0:T(8,128)(2,1)S(1)} %fusion.6.q_ref, bf16[896,1024]{1,0:T(8,128)(2,1)S(1)} %convolution_convert_fusion.g_ref, ...), custom_call_target="tpu_custom_call" | custom-call | flops 2147483648 | bytes 4194304 | tf_op jit(solution)/shard_map/key_pass/pallas_call | solution.py:352
  72.6 0.3 fusion.84
  72.9 0.3 fusion.91
  73.3 0.3 fusion.103
  73.6 0.3 fusion.38
  74.0 1.6 %collective-permute-start.19 = (bf16[256,1024]{1,0:T(8,128)(2,1)S(1)}, bf16[256,1024]{1,0:T(8,128)(2,1)S(1)}, u32[]{:S(2)}, u32[]{:S(2)}) collective-permute-start(bf16[256,1024]{1,0:T(8,128)(2,1)S(1)} %fusion.38), channel_id=1, source_target_pairs={{0,16},{8,24},{16,0},{24,8},{1,17},{9,25},{17,1},{25,9},{2,18},{10... | collective-permute-start | bytes 1572872 | tf_op jit(solution)/shard_map/ppermute | solution.py:23
  75.5 0.3 fusion.98
  76.2 0.6 collective-permute-start.21
  76.9 4.7 %collective-permute-start.18 = (bf16[32,2048]{1,0:T(8,128)(2,1)S(1)}, bf16[32,2048]{1,0:T(8,128)(2,1)S(1)}, u32[]{:S(2)}, u32[]{:S(2)}) collective-permute-start(bf16[32,2048]{1,0:T(8,128)(2,1)S(1)} %get-tuple-element.63), channel_id=1, source_target_pairs={{0,1},{1,0},{2,3},{3,2},{4,5},{5,4},{6,7},{7,6},{8,9},{9,8},{10,11... | collective-permute-start | bytes 393224 | tf_op jit(solution)/shard_map/ppermute | solution.py:23
  81.6 1.2 %collective-permute-start.17 = (bf16[32,2048]{1,0:T(8,128)(2,1)S(1)}, bf16[32,2048]{1,0:T(8,128)(2,1)S(1)}, u32[]{:S(2)}, u32[]{:S(2)}) collective-permute-start(bf16[32,2048]{1,0:T(8,128)(2,1)S(1)} %get-tuple-element.64), channel_id=1, source_target_pairs={{0,2},{1,3},{2,0},{3,1},{4,6},{5,7},{6,4},{7,5},{8,10},{9,11},{10,... | collective-permute-start | bytes 393224 | tf_op jit(solution)/shard_map/ppermute | solution.py:23
  82.9 1.4 %collective-permute-start.16 = (bf16[32,2048]{1,0:T(8,128)(2,1)S(1)}, bf16[32,2048]{1,0:T(8,128)(2,1)S(1)}, u32[]{:S(2)}, u32[]{:S(2)}) collective-permute-start(bf16[32,2048]{1,0:T(8,128)(2,1)S(1)} %get-tuple-element.62), channel_id=1, source_target_pairs={{0,3},{1,2},{2,1},{3,0},{4,7},{5,6},{6,5},{7,4},{8,11},{9,10},{10,... | collective-permute-start | bytes 393224 | tf_op jit(solution)/shard_map/ppermute | solution.py:23
  84.2 2.0 %fusion.124 = (f32[256]{0:T(256)S(1)}, f32[256]{0:T(256)S(1)}, f32[256,1024]{1,0:T(8,128)S(1)}) fusion(f32[256]{0:T(256)S(1)} %get-tuple-element.47, f32[256]{0:T(256)S(1)} %get-tuple-element.48, bf16[1,16,16,1024]{3,2,1,0:T(8,128)(2,1)S(1)} %copy-done, f32[1024]{0:T(1024)S(1)} %copy-done.2, bf16[256,3072]{1,0:T(8,128)(2,1)S(1)} %slice_dynamic-update-slice_fusion, ...), kind=kOutput, calls=%fused_computation.196 | convolution fusion | flops 1612447232 | bytes 9445376 | tf_op jit(solution)/shard_map/dot_general | solution.py:129
  86.3 1.5 %fusion.33 = bf16[256,1024]{1,0:T(8,128)(2,1)} fusion(bf16[256,1024]{1,0:T(8,128)(2,1)S(1)} %get-tuple-element.39, bf16[1024,4096]{1,0:T(8,128)(2,1)S(1)} %bitcast.67, bf16[256,1024]{1,0:T(8,128)(2,1)S(1)} %bitcast.69, f32[256]{0:T(256)S(1)} %convert_element_type.128), kind=kOutput, calls=%fused_computation.40 | convolution fusion | flops 537919488 | bytes 3671040 | tf_op jit(solution)/shard_map/dot_general | solution.py:125
  87.8 1.2 %fusion.47 = bf16[256,1024]{1,0:T(8,128)(2,1)} fusion(f32[256,1024]{1,0:T(8,128)S(1)} %get-tuple-element.91, f32[256]{0:T(256)S(1)} %get-tuple-element.92, f32[256]{0:T(256)S(1)} %get-tuple-element.48, f32[256]{0:T(256)S(1)} %get-tuple-element.93, f32[256]{0:T(256)S(1)} %get-tuple-element.47, bf16[1,16,16,1024]{3,2,1,0:T(8,128)(2,1)S(1)} %copy-done.1, ...), kind=kLoop, calls=%fused_computation.52 | loop fusion | flops 2621440 | bytes 2625536 | tf_op jit(solution)/shard_map/convert_element_type | solution.py:559
  89.1 0.3 fusion.15
  89.5 1.6 %collective-permute-start.20 = (bf16[128,1024]{1,0:T(8,128)(2,1)S(1)}, bf16[128,1024]{1,0:T(8,128)(2,1)S(1)}, u32[]{:S(2)}, u32[]{:S(2)}) collective-permute-start(bf16[128,1024]{1,0:T(8,128)(2,1)S(1)} %dynamic-slice_convert_fusion.1), channel_id=1, source_target_pairs={{0,4},{4,0},{1,5},{5,1},{2,6},{6,2},{3,7},{7,3},{8,12},{12,8},{9,1... | collective-permute-start | bytes 786440 | tf_op jit(solution)/shard_map/ppermute | solution.py:23
  91.5 0.6 collective-permute-start.22
  92.1 2.5 %collective-permute-done.17 = bf16[32,2048]{1,0:T(8,128)(2,1)S(1)} collective-permute-done((bf16[32,2048]{1,0:T(8,128)(2,1)S(1)}, bf16[32,2048]{1,0:T(8,128)(2,1)S(1)}, u32[]{:S(2)}, u32[]{:S(2)}) %collective-permute-start.17) | collective-permute-done | bytes 131104 | tf_op jit(solution)/shard_map/ppermute | solution.py:23
  94.6 2.5 %collective-permute-done.20 = bf16[128,1024]{1,0:T(8,128)(2,1)S(1)} collective-permute-done((bf16[128,1024]{1,0:T(8,128)(2,1)S(1)}, bf16[128,1024]{1,0:T(8,128)(2,1)S(1)}, u32[]{:S(2)}, u32[]{:S(2)}) %collective-permute-start.20) | collective-permute-done | bytes 262176 | tf_op jit(solution)/shard_map/ppermute | solution.py:23
  97.2 1.6 %collective-permute-done.22 = bf16[128,1024]{1,0:T(8,128)(2,1)S(1)} collective-permute-done((bf16[128,1024]{1,0:T(8,128)(2,1)S(1)}, bf16[128,1024]{1,0:T(8,128)(2,1)S(1)}, u32[]{:S(2)}, u32[]{:S(2)}) %collective-permute-start.22) | collective-permute-done | bytes 262176 | tf_op jit(solution)/shard_map/ppermute | solution.py:23
  99.0 4.2 %collective-permute-start.25 = (bf16[32,2048]{1,0:T(8,128)(2,1)S(1)}, bf16[32,2048]{1,0:T(8,128)(2,1)S(1)}, u32[]{:S(2)}, u32[]{:S(2)}) collective-permute-start(bf16[32,2048]{1,0:T(8,128)(2,1)S(1)} %get-tuple-element.53), channel_id=1, source_target_pairs={{0,1},{1,0},{2,3},{3,2},{4,5},{5,4},{6,7},{7,6},{8,9},{9,8},{10,11... | collective-permute-start | bytes 393224 | tf_op jit(solution)/shard_map/ppermute | solution.py:23
  103.2 1.3 %collective-permute-start.24 = (bf16[32,2048]{1,0:T(8,128)(2,1)S(1)}, bf16[32,2048]{1,0:T(8,128)(2,1)S(1)}, u32[]{:S(2)}, u32[]{:S(2)}) collective-permute-start(bf16[32,2048]{1,0:T(8,128)(2,1)S(1)} %get-tuple-element.52), channel_id=1, source_target_pairs={{0,2},{1,3},{2,0},{3,1},{4,6},{5,7},{6,4},{7,5},{8,10},{9,11},{10,... | collective-permute-start | bytes 393224 | tf_op jit(solution)/shard_map/ppermute | solution.py:23
  104.4 1.4 %collective-permute-start.23 = (bf16[32,2048]{1,0:T(8,128)(2,1)S(1)}, bf16[32,2048]{1,0:T(8,128)(2,1)S(1)}, u32[]{:S(2)}, u32[]{:S(2)}) collective-permute-start(bf16[32,2048]{1,0:T(8,128)(2,1)S(1)} %get-tuple-element.51), channel_id=1, source_target_pairs={{0,3},{1,2},{2,1},{3,0},{4,7},{5,6},{6,5},{7,4},{8,11},{9,10},{10,... | collective-permute-start | bytes 393224 | tf_op jit(solution)/shard_map/ppermute | solution.py:23
  105.8 1.7 %collective-permute-done.25 = bf16[32,2048]{1,0:T(8,128)(2,1)S(1)} collective-permute-done((bf16[32,2048]{1,0:T(8,128)(2,1)S(1)}, bf16[32,2048]{1,0:T(8,128)(2,1)S(1)}, u32[]{:S(2)}, u32[]{:S(2)}) %collective-permute-start.25) | collective-permute-done | bytes 131104 | tf_op jit(solution)/shard_map/ppermute | solution.py:23
  107.5 7.2 %collective-permute-done.24 = bf16[32,2048]{1,0:T(8,128)(2,1)S(1)} collective-permute-done((bf16[32,2048]{1,0:T(8,128)(2,1)S(1)}, bf16[32,2048]{1,0:T(8,128)(2,1)S(1)}, u32[]{:S(2)}, u32[]{:S(2)}) %collective-permute-start.24) | collective-permute-done | bytes 131104 | tf_op jit(solution)/shard_map/ppermute | solution.py:23
  114.9 0.8 broadcast_multiply_fusion
  (76 shorter events, 3.5 us)
Async XLA Ops:
  4.4 12.3 %collective-permute-start = (bf16[6,16,2048]{2,1,0:T(8,128)(2,1)S(1)}, bf16[6,16,2048]{2,1,0:T(8,128)(2,1)S(1)}, u32[]{:S(2)}, u32[]{:S(2)}) collective-permute-start(bf16[6,16,2048]{2,1,0:T(8,128)(2,1)S(1)} %bitcast.65), channel_id=1, source_target_pairs={{0,4},{4,0},{1,5},{5,1},{2,6},{6,2},{3,7},{7,3},{8,12},{12,8},{9,1... | collective-permute-start | bytes 1179656 | tf_op jit(solution)/shard_map/ppermute | solution.py:23
  7.4 38.3 %collective-permute-start.6 = (bf16[256,2048]{1,0:T(8,128)(2,1)S(1)}, bf16[256,2048]{1,0:T(8,128)(2,1)S(1)}, u32[]{:S(2)}, u32[]{:S(2)}) collective-permute-start(bf16[256,2048]{1,0:T(8,128)(2,1)S(1)} %get-tuple-element.24), channel_id=1, source_target_pairs={{0,8},{8,0},{16,24},{24,16},{1,9},{9,1},{17,25},{25,17},{2,10},{10... | collective-permute-start | bytes 3145736 | tf_op jit(solution)/shard_map/ppermute | solution.py:23
  8.5 15.0 %collective-permute-start.3 = (bf16[16,8,2048]{2,1,0:T(8,128)(2,1)}, bf16[16,8,2048]{2,1,0:T(8,128)(2,1)}, u32[]{:S(2)}, u32[]{:S(2)}) collective-permute-start(bf16[16,8,2048]{2,1,0:T(8,128)(2,1)} %get-tuple-element.69), channel_id=1, source_target_pairs={{0,1},{1,0},{2,3},{3,2},{4,5},{5,4},{6,7},{7,6},{8,9},{9,8},{10,11... | collective-permute-start | bytes 1572872 | tf_op jit(solution)/shard_map/ppermute | solution.py:58
  10.0 13.5 %collective-permute-start.4 = (bf16[16,8,2048]{2,1,0:T(8,128)(2,1)}, bf16[16,8,2048]{2,1,0:T(8,128)(2,1)}, u32[]{:S(2)}, u32[]{:S(2)}) collective-permute-start(bf16[16,8,2048]{2,1,0:T(8,128)(2,1)} %get-tuple-element.70), channel_id=1, source_target_pairs={{1,2},{2,1},{5,6},{6,5},{9,10},{10,9},{13,14},{14,13},{17,18},{18,... | collective-permute-start | bytes 1572872 | tf_op jit(solution)/shard_map/ppermute | solution.py:59
  16.7 10.5 %collective-permute-start.1 = (bf16[6,8,2048]{2,1,0:T(8,128)(2,1)S(1)}, bf16[6,8,2048]{2,1,0:T(8,128)(2,1)S(1)}, u32[]{:S(2)}, u32[]{:S(2)}) collective-permute-start(bf16[6,8,2048]{2,1,0:T(8,128)(2,1)S(1)} %get-tuple-element.83), channel_id=1, source_target_pairs={{0,1},{1,0},{2,3},{3,2},{4,5},{5,4},{6,7},{7,6},{8,9},{9,8},{10,11... | collective-permute-start | bytes 589832 | tf_op jit(solution)/shard_map/ppermute | solution.py:58
  20.4 6.8 %collective-permute-start.2 = (bf16[6,8,2048]{2,1,0:T(8,128)(2,1)S(1)}, bf16[6,8,2048]{2,1,0:T(8,128)(2,1)S(1)}, u32[]{:S(2)}, u32[]{:S(2)}) collective-permute-start(bf16[6,8,2048]{2,1,0:T(8,128)(2,1)S(1)} %get-tuple-element.84), channel_id=1, source_target_pairs={{1,2},{2,1},{5,6},{6,5},{9,10},{10,9},{13,14},{14,13},{17,18},{18,... | collective-permute-start | bytes 589832 | tf_op jit(solution)/shard_map/ppermute | solution.py:59
  41.4 4.4 %collective-permute-start.7 = (bf16[2,256,1024]{2,1,0:T(8,128)(2,1)S(1)}, bf16[2,256,1024]{2,1,0:T(8,128)(2,1)S(1)}, u32[]{:S(2)}, u32[]{:S(2)}) collective-permute-start(bf16[2,256,1024]{2,1,0:T(8,128)(2,1)S(1)} %get-tuple-element.26), channel_id=1, source_target_pairs={{0,8},{8,0},{16,24},{24,16},{1,9},{9,1},{17,25},{25,17},{2,10},{10... | collective-permute-start | bytes 3145736 | tf_op jit(solution)/shard_map/ppermute | solution.py:23
  41.5 4.2 %collective-permute-start.5 = (f32[6,16,128]{2,1,0:T(8,128)S(1)}, f32[6,16,128]{2,1,0:T(8,128)S(1)}, u32[]{:S(2)}, u32[]{:S(2)}) collective-permute-start(f32[6,16,128]{2,1,0:T(8,128)S(1)} %bitcast.73), channel_id=1, source_target_pairs={{0,4},{4,0},{1,5},{5,1},{2,6},{6,2},{3,7},{7,3},{8,12},{12,8},{9,1... | collective-permute-start | bytes 147464 | tf_op jit(solution)/shard_map/ppermute | solution.py:23
  41.9 6.9 %slice-start = ((s8[8388608]{0:T(1024)(128)(4,1)}), s8[4194304]{0:T(1024)(128)(4,1)S(1)}, s32[]{:S(2)}) async-start(s8[8388608]{0:T(1024)(128)(4,1)} %bitcast.66), calls=%async_computation | async-start | bytes 8388608
  43.3 5.5 %slice-start.1 = ((s8[8388608]{0:T(1024)(128)(4,1)}), s8[4194304]{0:T(1024)(128)(4,1)S(1)}, s32[]{:S(2)}) async-start(s8[8388608]{0:T(1024)(128)(4,1)} %bitcast.66), calls=%async_computation.1 | async-start | bytes 8388608
  46.3 13.2 %collective-permute-start.10 = (bf16[256,1024]{1,0:T(8,128)(2,1)S(1)}, bf16[256,1024]{1,0:T(8,128)(2,1)S(1)}, u32[]{:S(2)}, u32[]{:S(2)}) collective-permute-start(bf16[256,1024]{1,0:T(8,128)(2,1)S(1)} %fusion.36), channel_id=1, source_target_pairs={{0,16},{8,24},{16,0},{24,8},{1,17},{9,25},{17,1},{25,9},{2,18},{10... | collective-permute-start | bytes 1572872 | tf_op jit(solution)/shard_map/ppermute | solution.py:23
  48.2 12.9 %collective-permute-start.11 = (bf16[256,1024]{1,0:T(8,128)(2,1)S(1)}, bf16[256,1024]{1,0:T(8,128)(2,1)S(1)}, u32[]{:S(2)}, u32[]{:S(2)}) collective-permute-start(bf16[256,1024]{1,0:T(8,128)(2,1)S(1)} %fusion.37), channel_id=1, source_target_pairs={{0,4},{4,0},{1,5},{5,1},{2,6},{6,2},{3,7},{7,3},{8,12},{12,8},{9,1... | collective-permute-start | bytes 1572872 | tf_op jit(solution)/shard_map/ppermute | solution.py:23
  50.9 7.6 %collective-permute-start.8 = (f32[28,8,128]{2,1,0:T(8,128)S(1)}, f32[28,8,128]{2,1,0:T(8,128)S(1)}, u32[]{:S(2)}, u32[]{:S(2)}) collective-permute-start(f32[28,8,128]{2,1,0:T(8,128)S(1)} %get-tuple-element.87), channel_id=1, source_target_pairs={{0,1},{1,0},{2,3},{3,2},{4,5},{5,4},{6,7},{7,6},{8,9},{9,8},{10,11... | collective-permute-start | bytes 344072 | tf_op jit(solution)/shard_map/ppermute | solution.py:58
  55.5 3.0 %collective-permute-start.9 = (f32[28,8,128]{2,1,0:T(8,128)S(1)}, f32[28,8,128]{2,1,0:T(8,128)S(1)}, u32[]{:S(2)}, u32[]{:S(2)}) collective-permute-start(f32[28,8,128]{2,1,0:T(8,128)S(1)} %get-tuple-element.88), channel_id=1, source_target_pairs={{1,2},{2,1},{5,6},{6,5},{9,10},{10,9},{13,14},{14,13},{17,18},{18,... | collective-permute-start | bytes 344072 | tf_op jit(solution)/shard_map/ppermute | solution.py:59
  61.4 6.4 %collective-permute-start.13 = (bf16[128,1024]{1,0:T(8,128)(2,1)S(1)}, bf16[128,1024]{1,0:T(8,128)(2,1)S(1)}, u32[]{:S(2)}, u32[]{:S(2)}) collective-permute-start(bf16[128,1024]{1,0:T(8,128)(2,1)S(1)} %dynamic-slice_convert_fusion.2), channel_id=1, source_target_pairs={{0,16},{8,24},{16,0},{24,8},{1,17},{9,25},{17,1},{25,9},{2,18},{10... | collective-permute-start | bytes 786440 | tf_op jit(solution)/shard_map/ppermute | solution.py:23
  62.1 6.4 %collective-permute-start.12 = (bf16[128,1024]{1,0:T(8,128)(2,1)S(1)}, bf16[128,1024]{1,0:T(8,128)(2,1)S(1)}, u32[]{:S(2)}, u32[]{:S(2)}) collective-permute-start(bf16[128,1024]{1,0:T(8,128)(2,1)S(1)} %dynamic-slice_convert_fusion.3), channel_id=1, source_target_pairs={{0,4},{4,0},{1,5},{5,1},{2,6},{6,2},{3,7},{7,3},{8,12},{12,8},{9,1... | collective-permute-start | bytes 786440 | tf_op jit(solution)/shard_map/ppermute | solution.py:23
  66.3 7.0 %collective-permute-start.14 = (bf16[256,1024]{1,0:T(8,128)(2,1)S(1)}, bf16[256,1024]{1,0:T(8,128)(2,1)S(1)}, u32[]{:S(2)}, u32[]{:S(2)}) collective-permute-start(bf16[256,1024]{1,0:T(8,128)(2,1)S(1)} %key_pass.2), channel_id=1, source_target_pairs={{0,8},{8,0},{16,24},{24,16},{1,9},{9,1},{17,25},{25,17},{2,10},{10... | collective-permute-start | bytes 1572872 | tf_op jit(solution)/shard_map/ppermute | solution.py:23
  72.5 3.3 %collective-permute-start.15 = (bf16[256,1024]{1,0:T(8,128)(2,1)S(1)}, bf16[256,1024]{1,0:T(8,128)(2,1)S(1)}, u32[]{:S(2)}, u32[]{:S(2)}) collective-permute-start(bf16[256,1024]{1,0:T(8,128)(2,1)S(1)} %key_pass.3), channel_id=1, source_target_pairs={{0,8},{8,0},{16,24},{24,16},{1,9},{9,1},{17,25},{25,17},{2,10},{10... | collective-permute-start | bytes 1572872 | tf_op jit(solution)/shard_map/ppermute | solution.py:23
  74.0 15.1 %collective-permute-start.19 = (bf16[256,1024]{1,0:T(8,128)(2,1)S(1)}, bf16[256,1024]{1,0:T(8,128)(2,1)S(1)}, u32[]{:S(2)}, u32[]{:S(2)}) collective-permute-start(bf16[256,1024]{1,0:T(8,128)(2,1)S(1)} %fusion.38), channel_id=1, source_target_pairs={{0,16},{8,24},{16,0},{24,8},{1,17},{9,25},{17,1},{25,9},{2,18},{10... | collective-permute-start | bytes 1572872 | tf_op jit(solution)/shard_map/ppermute | solution.py:23
  75.9 8.4 %copy-start = (bf16[1,16,16,1024]{3,2,1,0:T(8,128)(2,1)S(1)}, bf16[1,16,16,1024]{3,2,1,0:T(8,128)(2,1)}, u32[]{:S(2)}) copy-start(bf16[1,16,16,1024]{3,2,1,0:T(8,128)(2,1)} %param.5) | copy-start | bytes 1572868
  75.9 8.4 %copy-start.2 = (f32[1024]{0:T(1024)S(1)}, f32[1024]{0:T(1024)}, u32[]{:S(2)}) copy-start(f32[1024]{0:T(1024)} %param.7) | copy-start | bytes 12292
  76.2 14.9 %collective-permute-start.21 = (bf16[256,1024]{1,0:T(8,128)(2,1)S(1)}, bf16[256,1024]{1,0:T(8,128)(2,1)S(1)}, u32[]{:S(2)}, u32[]{:S(2)}) collective-permute-start(bf16[256,1024]{1,0:T(8,128)(2,1)S(1)} %fusion.39), channel_id=1, source_target_pairs={{0,4},{4,0},{1,5},{5,1},{2,6},{6,2},{3,7},{7,3},{8,12},{12,8},{9,1... | collective-permute-start | bytes 1572872 | tf_op jit(solution)/shard_map/ppermute | solution.py:23
  76.9 15.1 %collective-permute-start.18 = (bf16[32,2048]{1,0:T(8,128)(2,1)S(1)}, bf16[32,2048]{1,0:T(8,128)(2,1)S(1)}, u32[]{:S(2)}, u32[]{:S(2)}) collective-permute-start(bf16[32,2048]{1,0:T(8,128)(2,1)S(1)} %get-tuple-element.63), channel_id=1, source_target_pairs={{0,1},{1,0},{2,3},{3,2},{4,5},{5,4},{6,7},{7,6},{8,9},{9,8},{10,11... | collective-permute-start | bytes 393224 | tf_op jit(solution)/shard_map/ppermute | solution.py:23
  81.6 12.9 %collective-permute-start.17 = (bf16[32,2048]{1,0:T(8,128)(2,1)S(1)}, bf16[32,2048]{1,0:T(8,128)(2,1)S(1)}, u32[]{:S(2)}, u32[]{:S(2)}) collective-permute-start(bf16[32,2048]{1,0:T(8,128)(2,1)S(1)} %get-tuple-element.64), channel_id=1, source_target_pairs={{0,2},{1,3},{2,0},{3,1},{4,6},{5,7},{6,4},{7,5},{8,10},{9,11},{10,... | collective-permute-start | bytes 393224 | tf_op jit(solution)/shard_map/ppermute | solution.py:23
  82.9 11.7 %collective-permute-start.16 = (bf16[32,2048]{1,0:T(8,128)(2,1)S(1)}, bf16[32,2048]{1,0:T(8,128)(2,1)S(1)}, u32[]{:S(2)}, u32[]{:S(2)}) collective-permute-start(bf16[32,2048]{1,0:T(8,128)(2,1)S(1)} %get-tuple-element.62), channel_id=1, source_target_pairs={{0,3},{1,2},{2,1},{3,0},{4,7},{5,6},{6,5},{7,4},{8,11},{9,10},{10,... | collective-permute-start | bytes 393224 | tf_op jit(solution)/shard_map/ppermute | solution.py:23
  86.3 1.5 %copy-start.1 = (bf16[1,16,16,1024]{3,2,1,0:T(8,128)(2,1)S(1)}, bf16[1,16,16,1024]{3,2,1,0:T(8,128)(2,1)}, u32[]{:S(2)}) copy-start(bf16[1,16,16,1024]{3,2,1,0:T(8,128)(2,1)} %param.9) | copy-start | bytes 1572868
  89.5 7.6 %collective-permute-start.20 = (bf16[128,1024]{1,0:T(8,128)(2,1)S(1)}, bf16[128,1024]{1,0:T(8,128)(2,1)S(1)}, u32[]{:S(2)}, u32[]{:S(2)}) collective-permute-start(bf16[128,1024]{1,0:T(8,128)(2,1)S(1)} %dynamic-slice_convert_fusion.1), channel_id=1, source_target_pairs={{0,4},{4,0},{1,5},{5,1},{2,6},{6,2},{3,7},{7,3},{8,12},{12,8},{9,1... | collective-permute-start | bytes 786440 | tf_op jit(solution)/shard_map/ppermute | solution.py:23
  91.5 7.4 %collective-permute-start.22 = (bf16[128,1024]{1,0:T(8,128)(2,1)S(1)}, bf16[128,1024]{1,0:T(8,128)(2,1)S(1)}, u32[]{:S(2)}, u32[]{:S(2)}) collective-permute-start(bf16[128,1024]{1,0:T(8,128)(2,1)S(1)} %dynamic-slice_convert_fusion), channel_id=1, source_target_pairs={{0,16},{8,24},{16,0},{24,8},{1,17},{9,25},{17,1},{25,9},{2,18},{10... | collective-permute-start | bytes 786440 | tf_op jit(solution)/shard_map/ppermute | solution.py:23
  99.0 8.6 %collective-permute-start.25 = (bf16[32,2048]{1,0:T(8,128)(2,1)S(1)}, bf16[32,2048]{1,0:T(8,128)(2,1)S(1)}, u32[]{:S(2)}, u32[]{:S(2)}) collective-permute-start(bf16[32,2048]{1,0:T(8,128)(2,1)S(1)} %get-tuple-element.53), channel_id=1, source_target_pairs={{0,1},{1,0},{2,3},{3,2},{4,5},{5,4},{6,7},{7,6},{8,9},{9,8},{10,11... | collective-permute-start | bytes 393224 | tf_op jit(solution)/shard_map/ppermute | solution.py:23
  103.2 11.6 %collective-permute-start.24 = (bf16[32,2048]{1,0:T(8,128)(2,1)S(1)}, bf16[32,2048]{1,0:T(8,128)(2,1)S(1)}, u32[]{:S(2)}, u32[]{:S(2)}) collective-permute-start(bf16[32,2048]{1,0:T(8,128)(2,1)S(1)} %get-tuple-element.52), channel_id=1, source_target_pairs={{0,2},{1,3},{2,0},{3,1},{4,6},{5,7},{6,4},{7,5},{8,10},{9,11},{10,... | collective-permute-start | bytes 393224 | tf_op jit(solution)/shard_map/ppermute | solution.py:23
  104.4 10.3 %collective-permute-start.23 = (bf16[32,2048]{1,0:T(8,128)(2,1)S(1)}, bf16[32,2048]{1,0:T(8,128)(2,1)S(1)}, u32[]{:S(2)}, u32[]{:S(2)}) collective-permute-start(bf16[32,2048]{1,0:T(8,128)(2,1)S(1)} %get-tuple-element.51), channel_id=1, source_target_pairs={{0,3},{1,2},{2,1},{3,0},{4,7},{5,6},{6,5},{7,4},{8,11},{9,10},{10,... | collective-permute-start | bytes 393224 | tf_op jit(solution)/shard_map/ppermute | solution.py:23

commit v5 on v4

v5 whole, which is shorter than its diff:
```python
import functools
import math

import jax
import jax.numpy as jnp
from jax import lax
from jax.experimental import pallas as pl
from jax.experimental.pallas import tpu as pltpu
from jax.sharding import PartitionSpec as P

HEADS = 16
RADIUS = 6
EPSILON = 1e-06
STRIP = 4
GROUP = 4
SIDE = 8
BF = jnp.bfloat16
F32 = jnp.float32


def swapped(array, axis, by):
    count = lax.axis_size(axis)
    return lax.ppermute(array, axis, [(i, i ^ by) for i in range(count)])


def moved(array, axis, by):
    count = lax.axis_size(axis)
    pairs = [(i, i + by) for i in range(count) if 0 <= i + by < count]
    return lax.ppermute(array, axis, pairs)


def rows_around(block, facing=None):
    rows_count = lax.axis_size("gy")
    if rows_count == 2:
        at_top = lax.axis_index("gy") == 0
        if facing is None:
            facing = jnp.where(at_top, block[-RADIUS:], block[:RADIUS])
        return (swapped(facing, "gy", 1),)
    return (moved(block[-RADIUS:], "gy", 1), moved(block[:RADIUS], "gy", -1))


def with_rows(block, rows):
    if len(rows) == 1:
        at_top = lax.axis_index("gy") == 0
        zero = jnp.zeros((), block.dtype)
        rows = (jnp.where(at_top, zero, rows[0]), jnp.where(at_top, rows[0], zero))
    return jnp.concatenate([rows[0], block, rows[1]], axis=0)


def facing_columns(to_right, to_left):
    even = lax.axis_index("gx") % 2 == 0
    return jnp.where(even, to_right, to_left), jnp.where(even, to_left, to_right)


def exchange_columns(out_one, out_two):
    count = lax.axis_size("gx")
    even = lax.axis_index("gx") % 2 == 0
    first, second = [], []
    for low in range(count - 1):
        pairs = second if low % 2 else first
        pairs += [(low, low + 1), (low + 1, low)]
    one = lax.ppermute(out_one, "gx", first)
    two = lax.ppermute(out_two, "gx", second)
    return jnp.where(even, two, one), jnp.where(even, one, two)


def column_halo(block):
    left, right = exchange_columns(*facing_columns(block[:, -SIDE:], block[:, :SIDE]))
    return jnp.concatenate([block, right, left], axis=1)


def owed_columns(grid):
    cols = grid.shape[2] - 2 * SIDE
    return facing_columns(grid[:, :, cols : cols + SIDE], grid[:, :, cols + SIDE :])


def return_columns(grid, out_one, out_two):
    cols = grid.shape[2] - 2 * SIDE
    from_left, from_right = exchange_columns(out_one, out_two)
    return grid[:, :, :cols].astype(F32) + jnp.concatenate([from_left, from_right], axis=2)


def owed_rows(grid):
    top, bottom = grid[:, :RADIUS].astype(BF), grid[:, -RADIUS:].astype(BF)
    if lax.axis_size("gy") == 2:
        return (jnp.where(lax.axis_index("gy") == 0, bottom, top),)
    return (top, bottom)


def return_rows(grid, outward):
    own = grid[:, RADIUS:-RADIUS]
    if len(outward) == 1:
        at_top = lax.axis_index("gy") == 0
        other = swapped(outward[0], "gy", 1)
        zero = jnp.zeros((), BF)
        above, below = jnp.where(at_top, zero, other), jnp.where(at_top, other, zero)
    else:
        above = moved(outward[1], "gy", 1)
        below = moved(outward[0], "gy", -1)
    rest = ((0, 0), (0, own.shape[1] - RADIUS), (0, 0), (0, 0))
    above = jnp.pad(above, rest)
    below = jnp.pad(below, (rest[0], rest[1][::-1], rest[2], rest[3]))
    return own + above.astype(F32) + below.astype(F32)


def in_hbm(array):
    return pltpu.with_memory_space_constraint(array, pltpu.HBM)


def prepare(
    place_ref, x_ref, c_ref, t_ref, gain_ref, normed_ref, branch_ref, face_ref, moment_ref
):
    block, width = x_ref.shape
    step = pl.program_id(0)
    rows = pl.ds(pl.multiple_of(step * block, block), block)
    x = x_ref[...].astype(F32)
    mean = jnp.sum(x, axis=1, keepdims=True) * (1.0 / width)
    centered = x - mean
    variance = jnp.sum(centered * centered, axis=1, keepdims=True) * (1.0 / width)
    inverse = lax.rsqrt(variance + EPSILON)
    normed_ref[rows, :] = (centered * inverse * gain_ref[...]).astype(BF)
    branch_ref[...] = (c_ref[...].astype(F32) * t_ref[...]).astype(BF)
    lane = lax.broadcasted_iota(jnp.int32, moment_ref.shape, 1)
    moment_ref[...] = jnp.where(lane == 0, mean, inverse)

    @pl.when(step == pl.num_programs(0) - 1)
    def _():
        first = pl.multiple_of(place_ref[4], 16)
        face_ref[...] = normed_ref[pl.ds(first, face_ref.shape[0]), :]


def run_prepare(place, tokens, cotangent, tissue, gain, face):
    count, width = tokens.shape
    block = min(count, 64)
    part = lambda columns: pl.BlockSpec((block, columns), lambda step: (step, 0))
    return pl.pallas_call(
        prepare,
        grid=(count // block,),
        in_specs=[SCALARS, part(width), part(width), part(1), whole((1, width))],
        out_specs=[whole((count, width)), part(width), whole((face, width)), part(128)],
        out_shape=[
            jax.ShapeDtypeStruct((count, width), BF),
            jax.ShapeDtypeStruct((count, width), BF),
            jax.ShapeDtypeStruct((face, width), BF),
            jax.ShapeDtypeStruct((count, 128), F32),
        ],
        compiler_params=pltpu.CompilerParams(**PARAMS),
        cost_estimate=pl.CostEstimate(flops=0, bytes_accessed=3 * 1024 * 1024, transcendentals=0),
        name="prepare",
    )(place, in_hbm(tokens), in_hbm(cotangent), tissue, in_hbm(gain))


def spread_heads(block, head_dim):
    lane_head = lax.broadcasted_iota(jnp.int32, block.shape, 1) // head_dim
    zero = jnp.zeros_like(block)
    return jnp.concatenate(
        [jnp.where(lane_head == head, block, zero) for head in range(GROUP)], axis=0
    )


def gather_heads(full, count, head_dim):
    lane_head = lax.broadcasted_iota(jnp.int32, (count, full.shape[1]), 1) // head_dim
    result = full[:count]
    for head in range(1, GROUP):
        result = jnp.where(lane_head == head, full[head * count : (head + 1) * count], result)
    return result


def times(left, right):
    return jnp.dot(left, right, preferred_element_type=F32)


def times_t(left, right):
    return lax.dot_general(left, right, (((1,), (1,)), ((), ())), preferred_element_type=F32)


def fill_bias(place_ref, bias_ref, tile_rows, tile_cols):
    strips, count, window = bias_ref.shape
    slots = tile_cols + 2 * SIDE
    own = lax.broadcasted_iota(jnp.int32, (count, window), 0)
    near = lax.broadcasted_iota(jnp.int32, (count, window), 1)
    own_row, own_col = own // tile_cols, own % tile_cols
    near_row, slot = near // slots, near % slots
    near_col = jnp.where(slot < tile_cols + SIDE, slot, slot - slots)
    row_gap = near_row - RADIUS - own_row
    col_gap = near_col - own_col
    col = place_ref[1] + near_col
    allowed = (jnp.abs(row_gap) <= RADIUS) & (jnp.abs(col_gap) <= RADIUS)
    allowed = allowed & (col >= 0) & (col < place_ref[3])
    for strip in range(strips):
        row = place_ref[0] + strip * STRIP + near_row - RADIUS
        kept = allowed & (row >= 0) & (row < place_ref[2])
        bias_ref[strip] = jnp.where(kept, 0.0, -1e30).astype(F32)


def query_pass(
    head_dim,
    tile,
    place_ref,
    q_ref,
    g_ref,
    normed_ref,
    key_w_ref,
    value_w_ref,
    out_ref,
    owed_ref,
    bias_ref,
    k_ref,
    v_ref,
    dk_ref,
    dv_ref,
):
    scaling = 1.0 / math.sqrt(head_dim)
    strips, count, window = bias_ref.shape
    step = (tile[1] + 2 * SIDE) * STRIP
    group = pl.program_id(0)

    @pl.when(group == 0)
    def _():
        fill_bias(place_ref, bias_ref, *tile)

    k_ref[...] = times(normed_ref[...], key_w_ref[...]).astype(BF)
    v_ref[...] = times(normed_ref[...], value_w_ref[...]).astype(BF)
    dk_ref[...] = jnp.zeros_like(dk_ref)
    dv_ref[...] = jnp.zeros_like(dv_ref)

    def dots(strip):
        own = pl.ds(strip * count, count)
        near = pl.ds(strip * step, window)
        queries = spread_heads(q_ref[own, :] * jnp.asarray(scaling, BF), head_dim)
        grads = spread_heads(g_ref[own, :], head_dim)
        scores = times_t(queries, k_ref[near, :])
        return queries, grads, scores, times_t(grads, v_ref[near, :])

    ahead = dots(0)
    for strip in range(strips):
        own = pl.ds(strip * count, count)
        near = pl.ds(strip * step, window)
        queries, grads, scores, grad_probs = ahead
        if strip + 1 < strips:
            ahead = dots(strip + 1)
        probs_parts, grad_parts = [], []
        for head in range(GROUP):
            part = slice(head * count, (head + 1) * count)
            masked = scores[part] + bias_ref[strip]
            row_max = jnp.max(masked, axis=1, keepdims=True)
            exponent = jnp.exp(masked - row_max)
            grad_part = grad_probs[part]
            total = jnp.sum(exponent, axis=1, keepdims=True)
            share = 1.0 / total
            delta = jnp.sum(exponent * grad_part, axis=1, keepdims=True) * share
            probs = exponent * share
            probs_parts.append(probs.astype(BF))
            grad_parts.append((probs * (grad_part - delta)).astype(BF))
        probs = jnp.concatenate(probs_parts, axis=0)
        grad_scores = jnp.concatenate(grad_parts, axis=0)
        attended = times(probs, v_ref[near, :])
        grad_queries = times(grad_scores, k_ref[near, :])
        out_ref[0, own, :] = gather_heads(attended, count, head_dim).astype(BF)
        out_ref[1, own, :] = (gather_heads(grad_queries, count, head_dim) * scaling).astype(BF)
        dk_ref[near, :] += product_t(grad_scores, queries)
        dv_ref[near, :] += product_t(probs, grads)
    owed_ref[0] = dk_ref[...].astype(BF)
    owed_ref[1] = dv_ref[...].astype(BF)


def whole(shape):
    return pl.BlockSpec(shape, lambda group: (0,) * len(shape))


def columns(rows, width, first=0):
    return pl.BlockSpec((rows, width), lambda group: (0, first + group))


def pair_columns(rows, width):
    return pl.BlockSpec((2, rows, width), lambda group: (0, 0, group))


SCALARS = pl.BlockSpec(memory_space=pltpu.SMEM)
PARAMS = dict(vmem_limit_bytes=24 * 1024 * 1024)


def window_shape(tile):
    return (tile[0] // STRIP, STRIP * tile[1], (STRIP + 2 * RADIUS) * (tile[1] + 2 * SIDE))


def attention_cost(tile, groups, part):
    strips, count, window = window_shape(tile)
    flops = 4 * 2 * groups * strips * GROUP * count * window * part
    return pl.CostEstimate(flops=flops, bytes_accessed=4 * 1024 * 1024, transcendentals=0)


def run_queries(place, queries, grads, normed_ext, weights, head_dim, tile):
    tokens, width = queries.shape
    ext = normed_ext.shape[0]
    part = GROUP * head_dim
    groups = width // part
    return pl.pallas_call(
        functools.partial(query_pass, head_dim, tile),
        grid=(groups,),
        in_specs=[
            SCALARS,
            columns(tokens, part),
            columns(tokens, part),
            whole(normed_ext.shape),
            columns(width, part, groups),
            columns(width, part, 2 * groups),
        ],
        out_specs=[pair_columns(tokens, part), pair_columns(ext, part)],
        out_shape=[
            jax.ShapeDtypeStruct((2, tokens, width), BF),
            jax.ShapeDtypeStruct((2, ext, width), BF),
        ],
        scratch_shapes=[pltpu.VMEM(window_shape(tile), F32)]
        + [pltpu.VMEM((ext, part), BF)] * 2
        + [pltpu.VMEM((ext, part), F32)] * 2,
        compiler_params=pltpu.CompilerParams(**PARAMS),
        cost_estimate=attention_cost(tile, groups, part),
        name="query_pass",
    )(place, queries, grads, normed_ext, in_hbm(weights), in_hbm(weights))


def own_part(array, index, axis):
    return lax.dynamic_index_in_dim(array, index, axis, keepdims=False)


def product_t(left, right):
    return lax.dot_general(left, right, (((0,), (0,)), ((), ())), preferred_element_type=F32)


def slide_swap(array, high):
    return swapped(array, "slide", lax.axis_size("slide") // 2 if high else 1)


def partners(across_slides):
    if across_slides:
        index = lax.axis_index("slide") // 2
        return index, [(1, 1 - index)]
    index = lax.axis_index("gy")
    return index, [(by, index ^ by) for by in range(1, lax.axis_size("gy"))]


def sent(block, across_slides, by):
    return slide_swap(block, True) if across_slides else swapped(block, "gy", by)


def pick_rows(array, index, across_slides, width):
    rows = width // lax.axis_size("slide")
    core = lax.axis_index("slide") % 2
    if across_slides:
        return lax.dynamic_slice_in_dim(array, (2 * index + core) * rows, rows, axis=1)
    rest = rows // lax.axis_size("gy")
    parts = [
        lax.dynamic_slice_in_dim(array, (2 * high + core) * rows + index * rest, rest, axis=1)
        for high in range(lax.axis_size("slide") // 2)
    ]
    return jnp.concatenate(parts, axis=1)


def pair_product(lefts, rights, index, across_slides):
    total = None
    for left, right in zip(lefts, rights):
        term = product_t(pick_rows(left, index, across_slides, right.shape[1]), right)
        total = term if total is None else total + term
    return total


def partner_half(left, right):
    rows = left.shape[1] // lax.axis_size("slide")
    other = 1 - lax.axis_index("slide") % 2
    parts = [
        lax.dynamic_slice_in_dim(left, (2 * high + other) * rows, rows, axis=1)
        for high in range(lax.axis_size("slide") // 2)
    ]
    return product_t(jnp.concatenate(parts, axis=1), right).astype(BF)


def halved_product(left, right, arrived, index, across_slides):
    rows = arrived.shape[0] // 2
    if across_slides:
        match = lax.dynamic_slice_in_dim(arrived, index * rows, rows, axis=0)
    else:
        rest = rows // lax.axis_size("gy")
        match = jnp.concatenate(
            [
                lax.dynamic_slice_in_dim(arrived, high * rows + index * rest, rest, axis=0)
                for high in range(2)
            ],
            axis=0,
        )
    return product_t(pick_rows(left, index, across_slides, left.shape[1]), right) + match.astype(F32)


def blocks_of(product, across_slides):
    index, others = partners(across_slides)
    return [product(target).astype(BF) for _, target in others], lambda: product(index)


def first_halving(blocks, mine, across_slides):
    others = partners(across_slides)[1]
    arrived = [sent(block, across_slides, by) for block, (by, _) in zip(blocks, others)]
    total = mine()
    for block in arrived:
        total = total + block.astype(F32)
    return total


def second_halving(part, across_slides):
    index, others = partners(across_slides)
    rows = part.shape[0] // (len(others) + 1)
    mine = lax.dynamic_slice_in_dim(part, index * rows, rows, axis=0)
    for by, target in others:
        block = lax.dynamic_slice_in_dim(part, target * rows, rows, axis=0).astype(BF)
        mine = mine + sent(block, across_slides, by).astype(F32)
    return mine


def reduce_columns(part):
    count = lax.axis_size("gx")
    index = lax.axis_index("gx")
    rows = part.shape[0] // count
    mine = lax.dynamic_slice_in_dim(part, index * rows, rows, axis=0)
    arrived = []
    for by in range(count - 1, 0, -1):
        block = lax.dynamic_slice_in_dim(part, (index ^ by) * rows, rows, axis=0)
        arrived.append(swapped(block.astype(BF), "gx", by))
    for block in arrived:
        mine = mine + block.astype(F32)
    return mine


def second_halvings(one, two):
    return jnp.concatenate([second_halving(one, False), second_halving(two, True)], axis=1)


def after(array, *earlier):
    return lax.optimization_barrier((array, *earlier))[0]


def local(tokens, weights, norm_gain, tissue, cotangent):
    tile_tokens = tokens[0]
    tile_rows, tile_cols, model_width = tile_tokens.shape
    tile = (tile_rows, tile_cols)
    head_dim = model_width // HEADS
    token_count = tile_rows * tile_cols
    slides = lax.axis_size("slide")
    rows_count = lax.axis_size("gy")
    cols_count = lax.axis_size("gx")
    weight_in = weights[:, : 3 * model_width]
    weight_out = weights[:, 3 * model_width :]
    face = RADIUS * tile_cols
    at_top = lax.axis_index("gy") == 0
    place = jnp.stack(
        [
            lax.axis_index("gy") * tile_rows,
            lax.axis_index("gx") * tile_cols,
            jnp.int32(tile_rows * rows_count),
            jnp.int32(tile_cols * cols_count),
            jnp.where(at_top, token_count - face, 0),
        ]
    ).astype(jnp.int32)

    flat = (token_count, model_width)
    grid = (tile_rows, tile_cols, model_width)
    tissue_mask = tissue[0].astype(F32).reshape(token_count, 1)
    tokens_flat = tile_tokens.reshape(flat)
    cot_flat = cotangent[0].reshape(flat)
    normed, branch_flat, facing, moments = run_prepare(
        place, tokens_flat, cot_flat, tissue_mask, norm_gain.reshape(1, model_width), face
    )
    normed_tile = normed.reshape(grid)
    rows = rows_around(normed_tile, facing.reshape(RADIUS, tile_cols, model_width))
    middle = column_halo(normed_tile)
    normed_ext = with_rows(middle, [column_halo(row) for row in rows])
    ext_rows, ext_cols = normed_ext.shape[:2]
    normed_ext = normed_ext.reshape(ext_rows * ext_cols, model_width)

    grad_attn = times_t(branch_flat, weight_out).astype(BF)
    queries = times(normed, weight_in[:, :model_width]).astype(BF)
    normed_pair = (normed, slide_swap(normed, False))
    branch_pair = (branch_flat, slide_swap(branch_flat, False))

    found, owed = run_queries(place, queries, grad_attn, normed_ext, weights, head_dim, tile)
    attended, grad_queries = found[0], found[1]

    found_other = slide_swap(found, False)
    key_half = partner_half(normed_ext, owed[0])
    value_half = partner_half(normed_ext, owed[1])
    key_arrived, value_arrived = slide_swap(key_half, False), slide_swap(value_half, False)
    found_other = after(found_other, key_half, value_half)
    query_sent, query_kept = blocks_of(
        lambda index: pair_product(normed_pair, (grad_queries, found_other[1]), index, True), True
    )
    out_sent, out_kept = blocks_of(
        lambda index: pair_product((attended, found_other[0]), branch_pair, index, False), False
    )

    owed_grid = after(owed, *query_sent, *out_sent)
    owed_grid = owed_grid.reshape(2, ext_rows, ext_cols, model_width)
    outward = owed_columns(owed_grid)
    key_sent, key_kept = blocks_of(
        lambda index: halved_product(normed_ext, owed[0], key_arrived, index, True), True
    )
    value_sent, value_kept = blocks_of(
        lambda index: halved_product(normed_ext, owed[1], value_arrived, index, False), False
    )

    first_kept = lax.optimization_barrier((query_kept(), out_kept(), key_sent, value_sent))[:2]
    one = first_halving(query_sent, lambda: first_kept[0], True)
    two = first_halving(out_sent, lambda: first_kept[1], False)
    second_kept = lax.optimization_barrier((key_kept(), value_kept(), one, two))[:2]
    three = first_halving(key_sent, lambda: second_kept[0], True)
    four = first_halving(value_sent, lambda: second_kept[1], False)
    owed_cols = return_columns(owed_grid, *outward)
    owed_up = owed_rows(owed_cols)
    second_sums = reduce_columns(after(second_halvings(three, four), *owed_up))
    first_sums = reduce_columns(second_halvings(one, two))
    owed_sum = return_rows(owed_cols, owed_up).astype(BF).reshape((2,) + flat)

    attended_late = after(attended, *key_sent, *value_sent)
    projection = times(attended_late, weight_out)
    block_output = (tokens_flat.astype(F32) + tissue_mask * projection).astype(BF)

    grad_projected = jnp.concatenate([grad_queries, owed_sum[0], owed_sum[1]], axis=-1)
    scaled = times_t(grad_projected, weight_in) * norm_gain
    inverse = moments[:, 1:2]
    normalized = (tokens_flat.astype(F32) - moments[:, :1]) * inverse
    first_mean = jnp.mean(scaled, axis=-1, keepdims=True)
    second_mean = jnp.mean(scaled * normalized, axis=-1, keepdims=True)
    input_grad = inverse * (scaled - first_mean - normalized * second_mean)
    input_grad = (cot_flat.astype(F32) + input_grad).astype(BF)

    inv_root = 1.0 / math.sqrt(slides * rows_count * cols_count * token_count)
    width = model_width
    weight_grads = jnp.concatenate(
        [first_sums[:, :width], second_sums, first_sums[:, width:]], axis=1
    )
    return (
        block_output.reshape((1,) + grid),
        input_grad.reshape((1,) + grid),
        weight_grads * inv_root,
    )


def solution(mesh):
    tile = P("slide", "gy", "gx", None)
    return jax.shard_map(
        local,
        mesh=mesh,
        in_specs=(tile, P(), P(), P("slide", "gy", "gx"), tile),
        out_specs=(tile, tile, P(("slide", "gy", "gx"), None)),
        check_vma=False,
    )
```

time: 116 us -> 111 us (0.957)
  Pallas kernels: 23.3 us -> 17.8 us
  starting transfers between devices: 38.2 us -> 34.4 us
  waiting for transfers between devices: 26.9 us -> 29.3 us
    pallas_call x2 -> x0, Pallas kernels: 7.69 us -> none  [run_keys(): pl.pallas_call(functools.partial(key_pass, head_dim, tile, first), grid=(...]
    ppermute x20 -> x21, waiting for transfers between devices: 22 us -> 27.5 us  [swapped(): return lax.ppermute(array, axis, [(i, i ^ by) for i in range(count)])]
    dot_general x16 -> x14, matrix products: 5.27 us -> 9.96 us  [product_t(): lax.dot_general(left, right, (((0,), (0,)), ((), ())), preferred_element_...]
    ppermute x6, waiting for transfers between devices: 4.89 us -> 1.79 us  [the longest x3 1.79 us: exchange_columns(): one = lax.ppermute(out_one, 'gx', first)]
    ppermute x20 -> x21, starting transfers between devices: 25.2 us -> 22.7 us  [swapped(): return lax.ppermute(array, axis, [(i, i ^ by) for i in range(count)])]
    pallas_call x1, Pallas kernels: 12.7 us -> 14.9 us  [run_queries(): pl.pallas_call(functools.partial(query_pass, head_dim, tile), grid=(group...]
    dot_general x3 -> x2, matrix products: 6.49 us -> 4.38 us  [times_t(): lax.dot_general(left, right, (((1,), (1,)), ((), ())), preferred_element_...]
    dot_general x3 -> x2, matrix products: 5.91 us -> 3.83 us  [times(): return jnp.dot(left, right, preferred_element_type=F32)]
  transfers between devices with their start and end apart: 26 -> 27, of which waited for: 12 -> 10; matrix products, arithmetic and copies ran while one was open for 20% -> 21% of each run, Pallas kernels for 18% -> 14%
where the time goes in v5:
time: 111 us
  starting transfers between devices  34.4 us (31%)
  waiting for transfers between devices  29.3 us (26%)
  matrix products  18.2 us (16%)
  Pallas kernels  17.8 us (16%)
  other arithmetic  7.74 us (7%)
  local copies, waits for them, and re-layouts  1.87 us (2%)
  between operations  1.31 us (1%)
    ppermute x21, waiting for transfers between devices, swapped(): return lax.ppermute(array, axis, [(i, i ^ by) for i in range(count)])  27.5 us
    ppermute x21, starting transfers between devices, swapped(): return lax.ppermute(array, axis, [(i, i ^ by) for i in range(count)])  22.7 us
    pallas_call x1, Pallas kernels, run_queries(): pl.pallas_call(functools.partial(query_pass, head_dim, tile), grid=(group...  14.9 us
    dot_general x14, matrix products, product_t(): lax.dot_general(left, right, (((0,), (0,)), ((), ())), preferred_element_...  9.96 us
    ppermute x3, starting transfers between devices, exchange_columns(): one = lax.ppermute(out_one, 'gx', first)  8.84 us
    dot_general x2, matrix products, times_t(): lax.dot_general(left, right, (((1,), (1,)), ((), ())), preferred_element_...  4.38 us
    dot_general x2, matrix products, times(): return jnp.dot(left, right, preferred_element_type=F32)  3.83 us
    ppermute x3, starting transfers between devices, exchange_columns(): two = lax.ppermute(out_two, 'gx', second)  2.93 us
  transfers between devices with their start and end apart: 27, of which 10 were waited for; matrix products, arithmetic and copies ran while one was open for 21% of the time, Pallas kernels for 14%

profile of v5, /device:TPU:0, one launch (start us, length us, event | category | flops | bytes accessed | tf_op | source)
XLA Modules:
  0.0 110.6 jit_solution(2316387202471508766)
XLA Ops:
  0.6 0.7 convert_element_type.160
  1.5 2.8 %prepare.1 = (bf16[256,1024]{1,0:T(8,128)(2,1)S(1)}, bf16[256,1024]{1,0:T(8,128)(2,1)S(1)}, bf16[96,1024]{1,0:T(8,128)(2,1)S(1)}, f32[256,128]{1,0:T(8,128)S(1)}) custom-call(s32[5]{0:T(128)S(1)} %stack.15.place_ref, bf16[256,1024]{1,0:T(8,128)(2,1)} %bitcast.91, bf16[256,1024]{1,0:T(8,128)(2,1)} %bitcast.93, f32[256,1]{1,0:T(8,128)S(1)} %convert_element_type.207.t_ref, ...), custom_call_target="tpu_custom_call" | custom-call | bytes 3145728 | tf_op jit(solution)/shard_map/prepare/pallas_call | solution.py:136
  4.4 3.0 %collective-permute-start = (bf16[6,16,1024]{2,1,0:T(8,128)(2,1)S(1)}, bf16[6,16,1024]{2,1,0:T(8,128)(2,1)S(1)}, u32[]{:S(2)}, u32[]{:S(2)}) collective-permute-start(bf16[6,16,1024]{2,1,0:T(8,128)(2,1)S(1)} %bitcast.88), channel_id=1, source_target_pairs={{0,4},{4,0},{1,5},{5,1},{2,6},{6,2},{3,7},{7,3},{8,12},{12,8},{9,1... | collective-permute-start | bytes 589832 | tf_op jit(solution)/shard_map/ppermute | solution.py:23
  7.4 0.8 broadcast_select_fusion.11
  8.3 1.6 %collective-permute-start.3 = (bf16[16,8,1024]{2,1,0:T(8,128)(2,1)}, bf16[16,8,1024]{2,1,0:T(8,128)(2,1)S(1)}, u32[]{:S(2)}, u32[]{:S(2)}) collective-permute-start(bf16[16,8,1024]{2,1,0:T(8,128)(2,1)} %get-tuple-element.72), channel_id=1, source_target_pairs={{0,1},{1,0},{2,3},{3,2},{4,5},{5,4},{6,7},{7,6},{8,9},{9,8},{10,11... | collective-permute-start | bytes 786440 | tf_op jit(solution)/shard_map/ppermute | solution.py:62
  9.8 1.4 %collective-permute-start.4 = (bf16[16,8,1024]{2,1,0:T(8,128)(2,1)}, bf16[16,8,1024]{2,1,0:T(8,128)(2,1)}, u32[]{:S(2)}, u32[]{:S(2)}) collective-permute-start(bf16[16,8,1024]{2,1,0:T(8,128)(2,1)} %get-tuple-element.73), channel_id=1, source_target_pairs={{1,2},{2,1},{5,6},{6,5},{9,10},{10,9},{13,14},{14,13},{17,18},{18,... | collective-permute-start | bytes 786440 | tf_op jit(solution)/shard_map/ppermute | solution.py:63
  11.2 0.2 collective-permute-start.9
  11.4 2.3 %fusion.59.g_ref = bf16[256,1024]{1,0:T(8,128)(2,1)S(1)} fusion(bf16[256,1024]{1,0:T(8,128)(2,1)S(1)} %get-tuple-element.18, bf16[1024,4096]{1,0:T(8,128)(2,1)} %value_w_ref.1), kind=kOutput, calls=%fused_computation.57 | convolution fusion | flops 537133056 | bytes 3145728 | tf_op jit(solution)/shard_map/dot_general | solution.py:174
  13.8 2.3 %fusion.62.q_ref = bf16[256,1024]{1,0:T(8,128)(2,1)S(1)} fusion(bf16[256,1024]{1,0:T(8,128)(2,1)S(1)} %get-tuple-element.17, bf16[1024,4096]{1,0:T(8,128)(2,1)} %value_w_ref.1), kind=kOutput, calls=%fused_computation.58 | convolution fusion | flops 537133056 | bytes 3145728 | tf_op jit(solution)/shard_map/dot_general | solution.py:170
  16.1 0.2 slice_reduce_fusion.1
  16.6 3.6 %collective-permute-start.1 = (bf16[6,8,1024]{2,1,0:T(8,128)(2,1)S(1)}, bf16[6,8,1024]{2,1,0:T(8,128)(2,1)S(1)}, u32[]{:S(2)}, u32[]{:S(2)}) collective-permute-start(bf16[6,8,1024]{2,1,0:T(8,128)(2,1)S(1)} %get-tuple-element.82), channel_id=1, source_target_pairs={{0,1},{1,0},{2,3},{3,2},{4,5},{5,4},{6,7},{7,6},{8,9},{9,8},{10,11... | collective-permute-start | bytes 294920 | tf_op jit(solution)/shard_map/ppermute | solution.py:62
  20.2 0.7 collective-permute-start.2
  20.8 1.0 broadcast_select_fusion.9
  21.8 1.8 %collective-permute-done.1 = bf16[6,8,1024]{2,1,0:T(8,128)(2,1)S(1)} collective-permute-done((bf16[6,8,1024]{2,1,0:T(8,128)(2,1)S(1)}, bf16[6,8,1024]{2,1,0:T(8,128)(2,1)S(1)}, u32[]{:S(2)}, u32[]{:S(2)}) %collective-permute-start.1) | collective-permute-done | bytes 98336 | tf_op jit(solution)/shard_map/ppermute | solution.py:62
  23.8 0.2 pad_maximum_fusion
  24.2 14.9 %query_pass.1 = (bf16[2,256,1024]{2,1,0:T(8,128)(2,1)S(1)}, bf16[2,896,1024]{2,1,0:T(8,128)(2,1)S(1)}) custom-call(s32[5]{0:T(128)S(1)} %stack.15.place_ref, bf16[256,1024]{1,0:T(8,128)(2,1)S(1)} %fusion.62.q_ref, bf16[256,1024]{1,0:T(8,128)(2,1)S(1)} %fusion.59.g_ref, bf16[896,1024]{1,0:T(8,128)(2,1)S(1)} %bitcast.80, bf16[1024,4096]{1,0:T(8,128)(2,1)} %value_w_ref.1, ...), custom_call_target="tpu_custom_call" | custom-call | flops 4294967296 | bytes 4194304 | tf_op jit(solution)/shard_map/query_pass/pallas_call | solution.py:298
  39.1 1.3 %fusion.27 = bf16[512,1024]{1,0:T(8,128)(2,1)S(1)} fusion(bf16[2,896,1024]{2,1,0:T(8,128)(2,1)S(1)} %get-tuple-element.25, bf16[896,256]{1,0:T(8,128)(2,1)S(1)} %get-tuple-element.46, bf16[896,256]{1,0:T(8,128)(2,1)S(1)} %get-tuple-element.45), kind=kOutput, calls=%fused_computation.38 | convolution fusion | flops 941883392 | bytes 3801088 | tf_op jit(solution)/shard_map/dot_general | solution.py:328
  40.4 1.3 %fusion.30 = bf16[512,1024]{1,0:T(8,128)(2,1)S(1)} fusion(bf16[2,896,1024]{2,1,0:T(8,128)(2,1)S(1)} %get-tuple-element.25, bf16[896,256]{1,0:T(8,128)(2,1)S(1)} %get-tuple-element.46, bf16[896,256]{1,0:T(8,128)(2,1)S(1)} %get-tuple-element.45), kind=kOutput, calls=%fused_computation.39 | convolution fusion | flops 941883392 | bytes 3801088 | tf_op jit(solution)/shard_map/dot_general | solution.py:328
  41.9 0.3 fusion.126
  42.3 0.5 collective-permute-start.6
  43.0 0.3 fusion.123
  43.3 0.3 fusion.115
  43.6 0.3 fusion.108
  43.9 0.2 constant_dynamic-slice_fusion.3
  44.2 0.2 collective-permute-done.8
  44.5 1.2 %fusion.68 = bf16[256,1024]{1,0:T(8,128)(2,1)S(1)} fusion(f32[256,1024]{1,0:T(8,128)S(1)} %fusion.126, bf16[2,256,1024]{2,1,0:T(8,128)(2,1)S(1)} %collective-permute-done.8, bf16[256,1024]{1,0:T(8,128)(2,1)} %collective-permute-done.7, s32[]{:T(128)S(6)} %select_n.257), kind=kOutput, calls=%fused_computation.60 | convolution fusion | flops 134742016 | bytes 2228228 | tf_op jit(solution)/shard_map/dot_general | solution.py:328
  45.7 1.6 %collective-permute-start.13 = (bf16[256,1024]{1,0:T(8,128)(2,1)S(1)}, bf16[256,1024]{1,0:T(8,128)(2,1)S(1)}, u32[]{:S(2)}, u32[]{:S(2)}) collective-permute-start(bf16[256,1024]{1,0:T(8,128)(2,1)S(1)} %fusion.68), channel_id=1, source_target_pairs={{0,16},{8,24},{16,0},{24,8},{1,17},{9,25},{17,1},{25,9},{2,18},{10... | collective-permute-start | bytes 1572872 | tf_op jit(solution)/shard_map/ppermute | solution.py:23
  47.3 0.3 fusion.69
  47.7 0.6 collective-permute-start.15
  48.3 0.7 add_convert_fusion
  49.1 1.6 %collective-permute-start.22 = (bf16[256,1024]{1,0:T(8,128)(2,1)S(1)}, bf16[256,1024]{1,0:T(8,128)(2,1)S(1)}, u32[]{:S(2)}, u32[]{:S(2)}) collective-permute-start(bf16[256,1024]{1,0:T(8,128)(2,1)S(1)} %add_convert_fusion), channel_id=1, source_target_pairs={{0,4},{4,0},{1,5},{5,1},{2,6},{6,2},{3,7},{7,3},{8,12},{12,8},{9,1... | collective-permute-start | bytes 1572872 | tf_op jit(solution)/shard_map/ppermute | solution.py:23
  50.7 0.8 fusion.56
  51.4 0.6 collective-permute-start.20
  52.0 1.2 %convolution_add_fusion.1 = f32[256,1024]{1,0:T(8,128)S(1)} fusion(f32[256,1024]{1,0:T(8,128)S(1)} %fusion.123, bf16[2,256,1024]{2,1,0:T(8,128)(2,1)S(1)} %collective-permute-done.8, bf16[256,1024]{1,0:T(8,128)(2,1)} %collective-permute-done.7, s32[]{:T(128)S(6)} %select_n.274), kind=kOutput, calls=%fused_computation.47 | convolution fusion | flops 134479872 | bytes 2752516 | tf_op jit(solution)/shard_map/dot_general | solution.py:328
  53.3 0.3 convolution_add_fusion
  53.7 0.9 collective-permute-start.10
  54.6 0.7 convert_add_fusion.3
  55.4 0.8 fusion.42
  56.1 4.4 %collective-permute-done.13 = bf16[256,1024]{1,0:T(8,128)(2,1)S(1)} collective-permute-done((bf16[256,1024]{1,0:T(8,128)(2,1)S(1)}, bf16[256,1024]{1,0:T(8,128)(2,1)S(1)}, u32[]{:S(2)}, u32[]{:S(2)}) %collective-permute-start.13) | collective-permute-done | bytes 524320 | tf_op jit(solution)/shard_map/ppermute | solution.py:23
  60.5 3.7 %collective-permute-start.11 = (bf16[2,28,8,1024]{3,2,1,0:T(8,128)(2,1)S(1)}, bf16[2,28,8,1024]{3,2,1,0:T(8,128)(2,1)S(1)}, u32[]{:S(2)}, u32[]{:S(2)}) collective-permute-start(bf16[2,28,8,1024]{3,2,1,0:T(8,128)(2,1)S(1)} %get-tuple-element.38), channel_id=1, source_target_pairs={{0,1},{1,0},{2,3},{3,2},{4,5},{5,4},{6,7},{7,6},{8,9},{9,8},{10,11... | collective-permute-start | bytes 2752520 | tf_op jit(solution)/shard_map/ppermute | solution.py:62
  64.4 0.6 collective-permute-start.14
  65.1 5.9 %collective-permute-done.20 = bf16[256,1024]{1,0:T(8,128)(2,1)S(1)} collective-permute-done((bf16[256,1024]{1,0:T(8,128)(2,1)S(1)}, bf16[256,1024]{1,0:T(8,128)(2,1)S(1)}, u32[]{:S(2)}, u32[]{:S(2)}) %collective-permute-start.20) | collective-permute-done | bytes 524320 | tf_op jit(solution)/shard_map/ppermute | solution.py:23
  71.1 1.5 %collective-permute-start.16 = (bf16[128,1024]{1,0:T(8,128)(2,1)S(1)}, bf16[128,1024]{1,0:T(8,128)(2,1)S(1)}, u32[]{:S(2)}, u32[]{:S(2)}) collective-permute-start(bf16[128,1024]{1,0:T(8,128)(2,1)S(1)} %dynamic-slice_convert_fusion.2), channel_id=1, source_target_pairs={{0,16},{8,24},{16,0},{24,8},{1,17},{9,25},{17,1},{25,9},{2,18},{10... | collective-permute-start | bytes 786440 | tf_op jit(solution)/shard_map/ppermute | solution.py:23
  72.7 1.0 collective-permute-done.22
  73.8 0.5 collective-permute-start.21
  74.5 4.9 %collective-permute-done.14 = bf16[128,1024]{1,0:T(8,128)(2,1)S(1)} collective-permute-done((bf16[128,1024]{1,0:T(8,128)(2,1)S(1)}, bf16[128,1024]{1,0:T(8,128)(2,1)S(1)}, u32[]{:S(2)}, u32[]{:S(2)}) %collective-permute-start.14) | collective-permute-done | bytes 262176 | tf_op jit(solution)/shard_map/ppermute | solution.py:23
  79.4 0.5 collective-permute-start.23
  80.1 1.0 collective-permute-start.17
  81.1 2.9 %collective-permute-done.21 = bf16[128,1024]{1,0:T(8,128)(2,1)S(1)} collective-permute-done((bf16[128,1024]{1,0:T(8,128)(2,1)S(1)}, bf16[128,1024]{1,0:T(8,128)(2,1)S(1)}, u32[]{:S(2)}, u32[]{:S(2)}) %collective-permute-start.21) | collective-permute-done | bytes 262176 | tf_op jit(solution)/shard_map/ppermute | solution.py:23
  84.0 3.4 %collective-permute-start.18 = (bf16[32,2048]{1,0:T(8,128)(2,1)S(1)}, bf16[32,2048]{1,0:T(8,128)(2,1)S(1)}, u32[]{:S(2)}, u32[]{:S(2)}) collective-permute-start(bf16[32,2048]{1,0:T(8,128)(2,1)S(1)} %get-tuple-element.55), channel_id=1, source_target_pairs={{0,2},{1,3},{2,0},{3,1},{4,6},{5,7},{6,4},{7,5},{8,10},{9,11},{10,... | collective-permute-start | bytes 393224 | tf_op jit(solution)/shard_map/ppermute | solution.py:23
  87.5 2.0 %collective-permute-start.19 = (bf16[32,2048]{1,0:T(8,128)(2,1)S(1)}, bf16[32,2048]{1,0:T(8,128)(2,1)S(1)}, u32[]{:S(2)}, u32[]{:S(2)}) collective-permute-start(bf16[32,2048]{1,0:T(8,128)(2,1)S(1)} %get-tuple-element.56), channel_id=1, source_target_pairs={{0,1},{1,0},{2,3},{3,2},{4,5},{5,4},{6,7},{7,6},{8,9},{9,8},{10,11... | collective-permute-start | bytes 393224 | tf_op jit(solution)/shard_map/ppermute | solution.py:23
  89.8 1.0 fusion.143
  90.9 1.3 %collective-permute-start.24 = (bf16[32,2048]{1,0:T(8,128)(2,1)S(1)}, bf16[32,2048]{1,0:T(8,128)(2,1)S(1)}, u32[]{:S(2)}, u32[]{:S(2)}) collective-permute-start(bf16[32,2048]{1,0:T(8,128)(2,1)S(1)} %get-tuple-element.47), channel_id=1, source_target_pairs={{0,3},{1,2},{2,1},{3,0},{4,7},{5,6},{6,5},{7,4},{8,11},{9,10},{10,... | collective-permute-start | bytes 393224 | tf_op jit(solution)/shard_map/ppermute | solution.py:23
  92.1 0.7 collective-permute-start.26
  92.8 2.5 %collective-permute-start.25 = (bf16[32,2048]{1,0:T(8,128)(2,1)S(1)}, bf16[32,2048]{1,0:T(8,128)(2,1)S(1)}, u32[]{:S(2)}, u32[]{:S(2)}) collective-permute-start(bf16[32,2048]{1,0:T(8,128)(2,1)S(1)} %get-tuple-element.49), channel_id=1, source_target_pairs={{0,2},{1,3},{2,0},{3,1},{4,6},{5,7},{6,4},{7,5},{8,10},{9,11},{10,... | collective-permute-start | bytes 393224 | tf_op jit(solution)/shard_map/ppermute | solution.py:23
  95.3 1.5 %fusion.65 = bf16[256,1024]{1,0:T(8,128)(2,1)} fusion(bf16[256,1024]{1,0:T(8,128)(2,1)S(1)} %get-tuple-element.22, bf16[1024,4096]{1,0:T(8,128)(2,1)S(1)} %bitcast.90, bf16[256,1024]{1,0:T(8,128)(2,1)S(1)} %bitcast.92, f32[256]{0:T(256)S(1)} %convert_element_type.161), kind=kOutput, calls=%fused_computation.59 | convolution fusion | flops 537919488 | bytes 3671040 | tf_op jit(solution)/shard_map/dot_general | solution.py:170
  96.9 0.5 collective-permute-start.12
  97.5 2.7 %collective-permute-done.24 = bf16[32,2048]{1,0:T(8,128)(2,1)S(1)} collective-permute-done((bf16[32,2048]{1,0:T(8,128)(2,1)S(1)}, bf16[32,2048]{1,0:T(8,128)(2,1)S(1)}, u32[]{:S(2)}, u32[]{:S(2)}) %collective-permute-start.24) | collective-permute-done | bytes 131104 | tf_op jit(solution)/shard_map/ppermute | solution.py:23
  100.2 5.4 %collective-permute-done.25 = bf16[32,2048]{1,0:T(8,128)(2,1)S(1)} collective-permute-done((bf16[32,2048]{1,0:T(8,128)(2,1)S(1)}, bf16[32,2048]{1,0:T(8,128)(2,1)S(1)}, u32[]{:S(2)}, u32[]{:S(2)}) %collective-permute-start.25) | collective-permute-done | bytes 131104 | tf_op jit(solution)/shard_map/ppermute | solution.py:23
  105.7 0.8 maximum_multiply_fusion
  106.6 0.3 fusion.3
  107.1 0.2 copy-done.2
  107.3 2.0 %fusion.144 = (f32[256]{0:T(256)S(1)}, f32[256]{0:T(256)S(1)}, f32[256,1024]{1,0:T(8,128)S(1)}) fusion(f32[256]{0:T(256)S(1)} %get-tuple-element.33, f32[256]{0:T(256)S(1)} %get-tuple-element.34, bf16[1,16,16,1024]{3,2,1,0:T(8,128)(2,1)S(1)} %copy-done, f32[1024]{0:T(1024)S(1)} %copy-done.2, bf16[1024,4096]{1,0:T(8,128)(2,1)S(1)} %bitcast.90, ...), kind=kOutput, calls=%fused_computation.191 | convolution fusion | flops 1617165824 | bytes 9445376 | tf_op jit(solution)/shard_map/dot_general | solution.py:174
  109.4 1.2 %fusion.77 = bf16[256,1024]{1,0:T(8,128)(2,1)} fusion(f32[256,1024]{1,0:T(8,128)S(1)} %get-tuple-element.84, f32[256]{0:T(256)S(1)} %get-tuple-element.85, f32[256]{0:T(256)S(1)} %get-tuple-element.34, f32[256]{0:T(256)S(1)} %get-tuple-element.86, f32[256]{0:T(256)S(1)} %get-tuple-element.33, bf16[1,16,16,1024]{3,2,1,0:T(8,128)(2,1)S(1)} %copy-done.1, ...), kind=kLoop, calls=%fused_computation.69 | loop fusion | flops 2621440 | bytes 2625536 | tf_op jit(solution)/shard_map/convert_element_type | solution.py:531
  (66 shorter events, 3.0 us)
Async XLA Ops:
  4.4 12.1 %collective-permute-start = (bf16[6,16,1024]{2,1,0:T(8,128)(2,1)S(1)}, bf16[6,16,1024]{2,1,0:T(8,128)(2,1)S(1)}, u32[]{:S(2)}, u32[]{:S(2)}) collective-permute-start(bf16[6,16,1024]{2,1,0:T(8,128)(2,1)S(1)} %bitcast.88), channel_id=1, source_target_pairs={{0,4},{4,0},{1,5},{5,1},{2,6},{6,2},{3,7},{7,3},{8,12},{12,8},{9,1... | collective-permute-start | bytes 589832 | tf_op jit(solution)/shard_map/ppermute | solution.py:23
  7.4 37.0 %collective-permute-start.7 = (bf16[256,1024]{1,0:T(8,128)(2,1)S(1)}, bf16[256,1024]{1,0:T(8,128)(2,1)}, u32[]{:S(2)}, u32[]{:S(2)}) collective-permute-start(bf16[256,1024]{1,0:T(8,128)(2,1)S(1)} %get-tuple-element.17), channel_id=1, source_target_pairs={{0,8},{8,0},{16,24},{24,16},{1,9},{9,1},{17,25},{25,17},{2,10},{10... | collective-permute-start | bytes 1572872 | tf_op jit(solution)/shard_map/ppermute | solution.py:23
  8.3 11.9 %collective-permute-start.3 = (bf16[16,8,1024]{2,1,0:T(8,128)(2,1)}, bf16[16,8,1024]{2,1,0:T(8,128)(2,1)S(1)}, u32[]{:S(2)}, u32[]{:S(2)}) collective-permute-start(bf16[16,8,1024]{2,1,0:T(8,128)(2,1)} %get-tuple-element.72), channel_id=1, source_target_pairs={{0,1},{1,0},{2,3},{3,2},{4,5},{5,4},{6,7},{7,6},{8,9},{9,8},{10,11... | collective-permute-start | bytes 786440 | tf_op jit(solution)/shard_map/ppermute | solution.py:62
  9.8 11.0 %collective-permute-start.4 = (bf16[16,8,1024]{2,1,0:T(8,128)(2,1)}, bf16[16,8,1024]{2,1,0:T(8,128)(2,1)}, u32[]{:S(2)}, u32[]{:S(2)}) collective-permute-start(bf16[16,8,1024]{2,1,0:T(8,128)(2,1)} %get-tuple-element.73), channel_id=1, source_target_pairs={{1,2},{2,1},{5,6},{6,5},{9,10},{10,9},{13,14},{14,13},{17,18},{18,... | collective-permute-start | bytes 786440 | tf_op jit(solution)/shard_map/ppermute | solution.py:63
  11.2 36.1 %collective-permute-start.9 = (bf16[256,1024]{1,0:T(8,128)(2,1)S(1)}, bf16[256,1024]{1,0:T(8,128)(2,1)S(1)}, u32[]{:S(2)}, u32[]{:S(2)}) collective-permute-start(bf16[256,1024]{1,0:T(8,128)(2,1)S(1)} %get-tuple-element.18), channel_id=1, source_target_pairs={{0,8},{8,0},{16,24},{24,16},{1,9},{9,1},{17,25},{25,17},{2,10},{10... | collective-permute-start | bytes 1572872 | tf_op jit(solution)/shard_map/ppermute | solution.py:23
  16.6 7.1 %collective-permute-start.1 = (bf16[6,8,1024]{2,1,0:T(8,128)(2,1)S(1)}, bf16[6,8,1024]{2,1,0:T(8,128)(2,1)S(1)}, u32[]{:S(2)}, u32[]{:S(2)}) collective-permute-start(bf16[6,8,1024]{2,1,0:T(8,128)(2,1)S(1)} %get-tuple-element.82), channel_id=1, source_target_pairs={{0,1},{1,0},{2,3},{3,2},{4,5},{5,4},{6,7},{7,6},{8,9},{9,8},{10,11... | collective-permute-start | bytes 294920 | tf_op jit(solution)/shard_map/ppermute | solution.py:62
  20.2 3.5 %collective-permute-start.2 = (bf16[6,8,1024]{2,1,0:T(8,128)(2,1)S(1)}, bf16[6,8,1024]{2,1,0:T(8,128)(2,1)S(1)}, u32[]{:S(2)}, u32[]{:S(2)}) collective-permute-start(bf16[6,8,1024]{2,1,0:T(8,128)(2,1)S(1)} %get-tuple-element.83), channel_id=1, source_target_pairs={{1,2},{2,1},{5,6},{6,5},{9,10},{10,9},{13,14},{14,13},{17,18},{18,... | collective-permute-start | bytes 294920 | tf_op jit(solution)/shard_map/ppermute | solution.py:63
  41.7 2.7 %collective-permute-start.8 = (bf16[2,256,1024]{2,1,0:T(8,128)(2,1)S(1)}, bf16[2,256,1024]{2,1,0:T(8,128)(2,1)S(1)}, u32[]{:S(2)}, u32[]{:S(2)}) collective-permute-start(bf16[2,256,1024]{2,1,0:T(8,128)(2,1)S(1)} %get-tuple-element.20), channel_id=1, source_target_pairs={{0,8},{8,0},{16,24},{24,16},{1,9},{9,1},{17,25},{25,17},{2,10},{10... | collective-permute-start | bytes 3145736 | tf_op jit(solution)/shard_map/ppermute | solution.py:23
  42.3 6.0 %collective-permute-start.6 = (bf16[512,1024]{1,0:T(8,128)(2,1)S(1)}, bf16[512,1024]{1,0:T(8,128)(2,1)S(1)}, u32[]{:S(2)}, u32[]{:S(2)}) collective-permute-start(bf16[512,1024]{1,0:T(8,128)(2,1)S(1)} %fusion.30), channel_id=1, source_target_pairs={{0,8},{8,0},{16,24},{24,16},{1,9},{9,1},{17,25},{25,17},{2,10},{10... | collective-permute-start | bytes 3145736 | tf_op jit(solution)/shard_map/ppermute | solution.py:23
  42.8 7.8 %collective-permute-start.5 = (bf16[512,1024]{1,0:T(8,128)(2,1)S(1)}, bf16[512,1024]{1,0:T(8,128)(2,1)S(1)}, u32[]{:S(2)}, u32[]{:S(2)}) collective-permute-start(bf16[512,1024]{1,0:T(8,128)(2,1)S(1)} %fusion.27), channel_id=1, source_target_pairs={{0,8},{8,0},{16,24},{24,16},{1,9},{9,1},{17,25},{25,17},{2,10},{10... | collective-permute-start | bytes 3145736 | tf_op jit(solution)/shard_map/ppermute | solution.py:23
  45.7 14.8 %collective-permute-start.13 = (bf16[256,1024]{1,0:T(8,128)(2,1)S(1)}, bf16[256,1024]{1,0:T(8,128)(2,1)S(1)}, u32[]{:S(2)}, u32[]{:S(2)}) collective-permute-start(bf16[256,1024]{1,0:T(8,128)(2,1)S(1)} %fusion.68), channel_id=1, source_target_pairs={{0,16},{8,24},{16,0},{24,8},{1,17},{9,25},{17,1},{25,9},{2,18},{10... | collective-permute-start | bytes 1572872 | tf_op jit(solution)/shard_map/ppermute | solution.py:23
  47.7 16.7 %collective-permute-start.15 = (bf16[256,1024]{1,0:T(8,128)(2,1)S(1)}, bf16[256,1024]{1,0:T(8,128)(2,1)S(1)}, u32[]{:S(2)}, u32[]{:S(2)}) collective-permute-start(bf16[256,1024]{1,0:T(8,128)(2,1)S(1)} %fusion.69), channel_id=1, source_target_pairs={{0,4},{4,0},{1,5},{5,1},{2,6},{6,2},{3,7},{7,3},{8,12},{12,8},{9,1... | collective-permute-start | bytes 1572872 | tf_op jit(solution)/shard_map/ppermute | solution.py:23
  49.1 24.7 %collective-permute-start.22 = (bf16[256,1024]{1,0:T(8,128)(2,1)S(1)}, bf16[256,1024]{1,0:T(8,128)(2,1)S(1)}, u32[]{:S(2)}, u32[]{:S(2)}) collective-permute-start(bf16[256,1024]{1,0:T(8,128)(2,1)S(1)} %add_convert_fusion), channel_id=1, source_target_pairs={{0,4},{4,0},{1,5},{5,1},{2,6},{6,2},{3,7},{7,3},{8,12},{12,8},{9,1... | collective-permute-start | bytes 1572872 | tf_op jit(solution)/shard_map/ppermute | solution.py:23
  51.4 19.7 %collective-permute-start.20 = (bf16[256,1024]{1,0:T(8,128)(2,1)S(1)}, bf16[256,1024]{1,0:T(8,128)(2,1)S(1)}, u32[]{:S(2)}, u32[]{:S(2)}) collective-permute-start(bf16[256,1024]{1,0:T(8,128)(2,1)S(1)} %fusion.56), channel_id=1, source_target_pairs={{0,16},{8,24},{16,0},{24,8},{1,17},{9,25},{17,1},{25,9},{2,18},{10... | collective-permute-start | bytes 1572872 | tf_op jit(solution)/shard_map/ppermute | solution.py:23
  53.7 35.9 %collective-permute-start.10 = (bf16[2,28,8,1024]{3,2,1,0:T(8,128)(2,1)S(1)}, bf16[2,28,8,1024]{3,2,1,0:T(8,128)(2,1)S(1)}, u32[]{:S(2)}, u32[]{:S(2)}) collective-permute-start(bf16[2,28,8,1024]{3,2,1,0:T(8,128)(2,1)S(1)} %get-tuple-element.37), channel_id=1, source_target_pairs={{1,2},{2,1},{5,6},{6,5},{9,10},{10,9},{13,14},{14,13},{17,18},{18,... | collective-permute-start | bytes 2752520 | tf_op jit(solution)/shard_map/ppermute | solution.py:63
  60.5 29.1 %collective-permute-start.11 = (bf16[2,28,8,1024]{3,2,1,0:T(8,128)(2,1)S(1)}, bf16[2,28,8,1024]{3,2,1,0:T(8,128)(2,1)S(1)}, u32[]{:S(2)}, u32[]{:S(2)}) collective-permute-start(bf16[2,28,8,1024]{3,2,1,0:T(8,128)(2,1)S(1)} %get-tuple-element.38), channel_id=1, source_target_pairs={{0,1},{1,0},{2,3},{3,2},{4,5},{5,4},{6,7},{7,6},{8,9},{9,8},{10,11... | collective-permute-start | bytes 2752520 | tf_op jit(solution)/shard_map/ppermute | solution.py:62
  64.4 15.0 %collective-permute-start.14 = (bf16[128,1024]{1,0:T(8,128)(2,1)S(1)}, bf16[128,1024]{1,0:T(8,128)(2,1)S(1)}, u32[]{:S(2)}, u32[]{:S(2)}) collective-permute-start(bf16[128,1024]{1,0:T(8,128)(2,1)S(1)} %dynamic-slice_convert_fusion.3), channel_id=1, source_target_pairs={{0,4},{4,0},{1,5},{5,1},{2,6},{6,2},{3,7},{7,3},{8,12},{12,8},{9,1... | collective-permute-start | bytes 786440 | tf_op jit(solution)/shard_map/ppermute | solution.py:23
  71.1 8.9 %collective-permute-start.16 = (bf16[128,1024]{1,0:T(8,128)(2,1)S(1)}, bf16[128,1024]{1,0:T(8,128)(2,1)S(1)}, u32[]{:S(2)}, u32[]{:S(2)}) collective-permute-start(bf16[128,1024]{1,0:T(8,128)(2,1)S(1)} %dynamic-slice_convert_fusion.2), channel_id=1, source_target_pairs={{0,16},{8,24},{16,0},{24,8},{1,17},{9,25},{17,1},{25,9},{2,18},{10... | collective-permute-start | bytes 786440 | tf_op jit(solution)/shard_map/ppermute | solution.py:23
  73.8 10.2 %collective-permute-start.21 = (bf16[128,1024]{1,0:T(8,128)(2,1)S(1)}, bf16[128,1024]{1,0:T(8,128)(2,1)S(1)}, u32[]{:S(2)}, u32[]{:S(2)}) collective-permute-start(bf16[128,1024]{1,0:T(8,128)(2,1)S(1)} %dynamic-slice_convert_fusion.1), channel_id=1, source_target_pairs={{0,4},{4,0},{1,5},{5,1},{2,6},{6,2},{3,7},{7,3},{8,12},{12,8},{9,1... | collective-permute-start | bytes 786440 | tf_op jit(solution)/shard_map/ppermute | solution.py:23
  79.4 8.1 %collective-permute-start.23 = (bf16[128,1024]{1,0:T(8,128)(2,1)S(1)}, bf16[128,1024]{1,0:T(8,128)(2,1)S(1)}, u32[]{:S(2)}, u32[]{:S(2)}) collective-permute-start(bf16[128,1024]{1,0:T(8,128)(2,1)S(1)} %dynamic-slice_convert_fusion), channel_id=1, source_target_pairs={{0,16},{8,24},{16,0},{24,8},{1,17},{9,25},{17,1},{25,9},{2,18},{10... | collective-permute-start | bytes 786440 | tf_op jit(solution)/shard_map/ppermute | solution.py:23
  80.1 12.7 %collective-permute-start.17 = (bf16[32,2048]{1,0:T(8,128)(2,1)S(1)}, bf16[32,2048]{1,0:T(8,128)(2,1)S(1)}, u32[]{:S(2)}, u32[]{:S(2)}) collective-permute-start(bf16[32,2048]{1,0:T(8,128)(2,1)S(1)} %get-tuple-element.54), channel_id=1, source_target_pairs={{0,3},{1,2},{2,1},{3,0},{4,7},{5,6},{6,5},{7,4},{8,11},{9,10},{10,... | collective-permute-start | bytes 393224 | tf_op jit(solution)/shard_map/ppermute | solution.py:23
  84.0 12.9 %collective-permute-start.18 = (bf16[32,2048]{1,0:T(8,128)(2,1)S(1)}, bf16[32,2048]{1,0:T(8,128)(2,1)S(1)}, u32[]{:S(2)}, u32[]{:S(2)}) collective-permute-start(bf16[32,2048]{1,0:T(8,128)(2,1)S(1)} %get-tuple-element.55), channel_id=1, source_target_pairs={{0,2},{1,3},{2,0},{3,1},{4,6},{5,7},{6,4},{7,5},{8,10},{9,11},{10,... | collective-permute-start | bytes 393224 | tf_op jit(solution)/shard_map/ppermute | solution.py:23
  87.5 10.0 %collective-permute-start.19 = (bf16[32,2048]{1,0:T(8,128)(2,1)S(1)}, bf16[32,2048]{1,0:T(8,128)(2,1)S(1)}, u32[]{:S(2)}, u32[]{:S(2)}) collective-permute-start(bf16[32,2048]{1,0:T(8,128)(2,1)S(1)} %get-tuple-element.56), channel_id=1, source_target_pairs={{0,1},{1,0},{2,3},{3,2},{4,5},{5,4},{6,7},{7,6},{8,9},{9,8},{10,11... | collective-permute-start | bytes 393224 | tf_op jit(solution)/shard_map/ppermute | solution.py:23
  89.5 5.9 %slice-start = ((s8[8388608]{0:T(1024)(128)(4,1)}), s8[4194304]{0:T(1024)(128)(4,1)S(1)}, s32[]{:S(2)}) async-start(s8[8388608]{0:T(1024)(128)(4,1)} %bitcast.89), calls=%async_computation | async-start | bytes 8388608
  89.7 5.6 %slice-start.1 = ((s8[8388608]{0:T(1024)(128)(4,1)}), s8[4194304]{0:T(1024)(128)(4,1)S(1)}, s32[]{:S(2)}) async-start(s8[8388608]{0:T(1024)(128)(4,1)} %bitcast.89), calls=%async_computation.1 | async-start | bytes 8388608
  89.8 5.6 %copy-start = (bf16[1,16,16,1024]{3,2,1,0:T(8,128)(2,1)S(1)}, bf16[1,16,16,1024]{3,2,1,0:T(8,128)(2,1)}, u32[]{:S(2)}) copy-start(bf16[1,16,16,1024]{3,2,1,0:T(8,128)(2,1)} %param.5) | copy-start | bytes 1572868
  90.9 9.3 %collective-permute-start.24 = (bf16[32,2048]{1,0:T(8,128)(2,1)S(1)}, bf16[32,2048]{1,0:T(8,128)(2,1)S(1)}, u32[]{:S(2)}, u32[]{:S(2)}) collective-permute-start(bf16[32,2048]{1,0:T(8,128)(2,1)S(1)} %get-tuple-element.47), channel_id=1, source_target_pairs={{0,3},{1,2},{2,1},{3,0},{4,7},{5,6},{6,5},{7,4},{8,11},{9,10},{10,... | collective-permute-start | bytes 393224 | tf_op jit(solution)/shard_map/ppermute | solution.py:23
  92.1 8.0 %collective-permute-start.26 = (bf16[32,2048]{1,0:T(8,128)(2,1)S(1)}, bf16[32,2048]{1,0:T(8,128)(2,1)S(1)}, u32[]{:S(2)}, u32[]{:S(2)}) collective-permute-start(bf16[32,2048]{1,0:T(8,128)(2,1)S(1)} %get-tuple-element.48), channel_id=1, source_target_pairs={{0,1},{1,0},{2,3},{3,2},{4,5},{5,4},{6,7},{7,6},{8,9},{9,8},{10,11... | collective-permute-start | bytes 393224 | tf_op jit(solution)/shard_map/ppermute | solution.py:23
  92.8 12.7 %collective-permute-start.25 = (bf16[32,2048]{1,0:T(8,128)(2,1)S(1)}, bf16[32,2048]{1,0:T(8,128)(2,1)S(1)}, u32[]{:S(2)}, u32[]{:S(2)}) collective-permute-start(bf16[32,2048]{1,0:T(8,128)(2,1)S(1)} %get-tuple-element.49), channel_id=1, source_target_pairs={{0,2},{1,3},{2,0},{3,1},{4,6},{5,7},{6,4},{7,5},{8,10},{9,11},{10,... | collective-permute-start | bytes 393224 | tf_op jit(solution)/shard_map/ppermute | solution.py:23
  96.9 9.6 %collective-permute-start.12 = (bf16[2,6,16,1024]{3,2,1,0:T(8,128)(2,1)S(1)}, bf16[2,6,16,1024]{3,2,1,0:T(8,128)(2,1)S(1)}, u32[]{:S(2)}, u32[]{:S(2)}) collective-permute-start(bf16[2,6,16,1024]{3,2,1,0:T(8,128)(2,1)S(1)} %slice_select_fusion), channel_id=1, source_target_pairs={{0,4},{4,0},{1,5},{5,1},{2,6},{6,2},{3,7},{7,3},{8,12},{12,8},{9,1... | collective-permute-start | bytes 1179656 | tf_op jit(solution)/shard_map/ppermute | solution.py:23
  106.6 0.7 copy-start.2
  107.3 2.1 %copy-start.1 = (bf16[1,16,16,1024]{3,2,1,0:T(8,128)(2,1)S(1)}, bf16[1,16,16,1024]{3,2,1,0:T(8,128)(2,1)}, u32[]{:S(2)}) copy-start(bf16[1,16,16,1024]{3,2,1,0:T(8,128)(2,1)} %param.9) | copy-start | bytes 1572868

commit v6 on v5

--- a/solution.py
+++ b/solution.py
@@ -49,7 +49,7 @@
 
 def facing_columns(to_right, to_left):
     even = lax.axis_index("gx") % 2 == 0
-    return jnp.where(even, to_right, to_left), jnp.where(even, to_left, to_right)
+    return jnp.where(even, to_left, to_right), jnp.where(even, to_right, to_left)
 
 
 def exchange_columns(out_one, out_two):
@@ -57,11 +57,11 @@
     even = lax.axis_index("gx") % 2 == 0
     first, second = [], []
     for low in range(count - 1):
-        pairs = second if low % 2 else first
+        pairs = first if low % 2 else second
         pairs += [(low, low + 1), (low + 1, low)]
     one = lax.ppermute(out_one, "gx", first)
     two = lax.ppermute(out_two, "gx", second)
-    return jnp.where(even, two, one), jnp.where(even, one, two)
+    return jnp.where(even, one, two), jnp.where(even, two, one)
 
 
 def column_halo(block):
@@ -415,18 +415,41 @@
     return mine
 
 
-def reduce_columns(part):
+def column_blocks(part):
     count = lax.axis_size("gx")
     index = lax.axis_index("gx")
     rows = part.shape[0] // count
     mine = lax.dynamic_slice_in_dim(part, index * rows, rows, axis=0)
-    arrived = []
-    for by in range(count - 1, 0, -1):
-        block = lax.dynamic_slice_in_dim(part, (index ^ by) * rows, rows, axis=0)
-        arrived.append(swapped(block.astype(BF), "gx", by))
+    others = [
+        lax.dynamic_slice_in_dim(part, (index ^ by) * rows, rows, axis=0).astype(BF)
+        for by in range(count - 1, 0, -1)
+    ]
+    return mine, others
+
+
+def reduce_columns(mine, others):
+    count = lax.axis_size("gx")
+    arrived = [
+        swapped(block, "gx", by) for block, by in zip(others, range(count - 1, 0, -1))
+    ]
     for block in arrived:
         mine = mine + block.astype(F32)
     return mine
+
+
+def halve_columns(part):
+    count, width = lax.axis_size("gx"), part.shape[1]
+    index = lax.axis_index("gx")
+    rows = part.shape[0] // count
+    by = 1
+    while by < count:
+        bit = lax.rem(index // by, 2)
+        blocks = part.reshape(-1, 2, rows, width)
+        going = lax.dynamic_index_in_dim(blocks, 1 - bit, 1, keepdims=False).astype(BF)
+        kept = lax.dynamic_index_in_dim(blocks, bit, 1, keepdims=False)
+        part = (kept + swapped(going, "gx", by).astype(F32)).reshape(-1, width)
+        by *= 2
+    return part
 
 
 def second_halvings(one, two):
@@ -513,8 +536,8 @@
     four = first_halving(value_sent, lambda: second_kept[1], False)
     owed_cols = return_columns(owed_grid, *outward)
     owed_up = owed_rows(owed_cols)
-    second_sums = reduce_columns(after(second_halvings(three, four), *owed_up))
-    first_sums = reduce_columns(second_halvings(one, two))
+    mine, others = column_blocks(after(second_halvings(three, four), *owed_up))
+    first_sums = reduce_columns(*column_blocks(second_halvings(one, two)))
     owed_sum = return_rows(owed_cols, owed_up).astype(BF).reshape((2,) + flat)
 
     attended_late = after(attended, *key_sent, *value_sent)
@@ -530,6 +553,7 @@
     input_grad = inverse * (scaled - first_mean - normalized * second_mean)
     input_grad = (cot_flat.astype(F32) + input_grad).astype(BF)
 
+    second_sums = reduce_columns(after(mine, input_grad), others)
     inv_root = 1.0 / math.sqrt(slides * rows_count * cols_count * token_count)
     width = model_width
     weight_grads = jnp.concatenate(

time: 111 us -> 107 us (0.964)
  starting transfers between devices: 34.4 us -> 32 us
  waiting for transfers between devices: 29.3 us -> 27.6 us
    ppermute x3, starting transfers between devices: 8.84 us -> 2.94 us  [exchange_columns(): one = lax.ppermute(out_one, 'gx', first)]
    ppermute x3, starting transfers between devices: 2.93 us -> 8.83 us  [exchange_columns(): two = lax.ppermute(out_two, 'gx', second)]
    ppermute x21, starting transfers between devices: 22.7 us -> 20.2 us  [swapped(): return lax.ppermute(array, axis, [(i, i ^ by) for i in range(count)])]
    ppermute x3, waiting for transfers between devices: 0.01 us -> 1.79 us  [exchange_columns(): two = lax.ppermute(out_two, 'gx', second)]
    ppermute x3, waiting for transfers between devices: 1.79 us -> 0.01 us  [exchange_columns(): one = lax.ppermute(out_one, 'gx', first)]
    ppermute x21, waiting for transfers between devices: 27.5 us -> 25.8 us  [swapped(): return lax.ppermute(array, axis, [(i, i ^ by) for i in range(count)])]
  transfers between devices with their start and end apart: 27 -> 27, of which waited for: 10 -> 10; matrix products, arithmetic and copies ran while one was open for 21% -> 24% of each run, Pallas kernels for 14% -> 14%
where the time goes in v6:
time: 107 us
  starting transfers between devices  32 us (30%)
  waiting for transfers between devices  27.6 us (26%)
  matrix products  18.2 us (17%)
  Pallas kernels  17.8 us (17%)
  other arithmetic  7.88 us (7%)
  local copies, waits for them, and re-layouts  1.88 us (2%)
  between operations  1.33 us (1%)
    ppermute x21, waiting for transfers between devices, swapped(): return lax.ppermute(array, axis, [(i, i ^ by) for i in range(count)])  25.8 us
    ppermute x21, starting transfers between devices, swapped(): return lax.ppermute(array, axis, [(i, i ^ by) for i in range(count)])  20.2 us
    pallas_call x1, Pallas kernels, run_queries(): pl.pallas_call(functools.partial(query_pass, head_dim, tile), grid=(group...  14.9 us
    dot_general x14, matrix products, product_t(): lax.dot_general(left, right, (((0,), (0,)), ((), ())), preferred_element_...  9.95 us
    ppermute x3, starting transfers between devices, exchange_columns(): two = lax.ppermute(out_two, 'gx', second)  8.83 us
    dot_general x2, matrix products, times_t(): lax.dot_general(left, right, (((1,), (1,)), ((), ())), preferred_element_...  4.38 us
    dot_general x2, matrix products, times(): return jnp.dot(left, right, preferred_element_type=F32)  3.83 us
    ppermute x3, starting transfers between devices, exchange_columns(): one = lax.ppermute(out_one, 'gx', first)  2.94 us
  transfers between devices with their start and end apart: 27, of which 10 were waited for; matrix products, arithmetic and copies ran while one was open for 24% of the time, Pallas kernels for 14%

profile of v6, /device:TPU:0, one launch (start us, length us, event | category | flops | bytes accessed | tf_op | source)
XLA Modules:
  0.0 106.6 jit_solution(4639363878242300924)
XLA Ops:
  0.6 0.7 convert_element_type.160
  1.5 2.8 %prepare.1 = (bf16[256,1024]{1,0:T(8,128)(2,1)S(1)}, bf16[256,1024]{1,0:T(8,128)(2,1)S(1)}, bf16[96,1024]{1,0:T(8,128)(2,1)S(1)}, f32[256,128]{1,0:T(8,128)S(1)}) custom-call(s32[5]{0:T(128)S(1)} %stack.15.place_ref, bf16[256,1024]{1,0:T(8,128)(2,1)} %bitcast.91, bf16[256,1024]{1,0:T(8,128)(2,1)} %bitcast.93, f32[256,1]{1,0:T(8,128)S(1)} %convert_element_type.207.t_ref, ...), custom_call_target="tpu_custom_call" | custom-call | bytes 3145728 | tf_op jit(solution)/shard_map/prepare/pallas_call | solution.py:136
  4.4 3.0 %collective-permute-start = (bf16[6,16,1024]{2,1,0:T(8,128)(2,1)S(1)}, bf16[6,16,1024]{2,1,0:T(8,128)(2,1)S(1)}, u32[]{:S(2)}, u32[]{:S(2)}) collective-permute-start(bf16[6,16,1024]{2,1,0:T(8,128)(2,1)S(1)} %bitcast.88), channel_id=1, source_target_pairs={{0,4},{4,0},{1,5},{5,1},{2,6},{6,2},{3,7},{7,3},{8,12},{12,8},{9,1... | collective-permute-start | bytes 589832 | tf_op jit(solution)/shard_map/ppermute | solution.py:23
  7.4 0.8 broadcast_select_fusion.11
  8.3 1.6 %collective-permute-start.3 = (bf16[16,8,1024]{2,1,0:T(8,128)(2,1)}, bf16[16,8,1024]{2,1,0:T(8,128)(2,1)S(1)}, u32[]{:S(2)}, u32[]{:S(2)}) collective-permute-start(bf16[16,8,1024]{2,1,0:T(8,128)(2,1)} %get-tuple-element.74), channel_id=1, source_target_pairs={{0,1},{1,0},{2,3},{3,2},{4,5},{5,4},{6,7},{7,6},{8,9},{9,8},{10,11... | collective-permute-start | bytes 786440 | tf_op jit(solution)/shard_map/ppermute | solution.py:63
  9.8 1.4 %collective-permute-start.4 = (bf16[16,8,1024]{2,1,0:T(8,128)(2,1)}, bf16[16,8,1024]{2,1,0:T(8,128)(2,1)}, u32[]{:S(2)}, u32[]{:S(2)}) collective-permute-start(bf16[16,8,1024]{2,1,0:T(8,128)(2,1)} %get-tuple-element.75), channel_id=1, source_target_pairs={{1,2},{2,1},{5,6},{6,5},{9,10},{10,9},{13,14},{14,13},{17,18},{18,... | collective-permute-start | bytes 786440 | tf_op jit(solution)/shard_map/ppermute | solution.py:62
  11.2 0.2 collective-permute-start.9
  11.4 2.3 %fusion.59.g_ref = bf16[256,1024]{1,0:T(8,128)(2,1)S(1)} fusion(bf16[256,1024]{1,0:T(8,128)(2,1)S(1)} %get-tuple-element.19, bf16[1024,4096]{1,0:T(8,128)(2,1)} %value_w_ref.1), kind=kOutput, calls=%fused_computation.57 | convolution fusion | flops 537133056 | bytes 3145728 | tf_op jit(solution)/shard_map/dot_general | solution.py:174
  13.8 2.3 %fusion.62.q_ref = bf16[256,1024]{1,0:T(8,128)(2,1)S(1)} fusion(bf16[256,1024]{1,0:T(8,128)(2,1)S(1)} %get-tuple-element.18, bf16[1024,4096]{1,0:T(8,128)(2,1)} %value_w_ref.1), kind=kOutput, calls=%fused_computation.58 | convolution fusion | flops 537133056 | bytes 3145728 | tf_op jit(solution)/shard_map/dot_general | solution.py:170
  16.1 0.2 slice_reduce_fusion.1
  16.6 3.6 %collective-permute-start.1 = (bf16[6,8,1024]{2,1,0:T(8,128)(2,1)S(1)}, bf16[6,8,1024]{2,1,0:T(8,128)(2,1)S(1)}, u32[]{:S(2)}, u32[]{:S(2)}) collective-permute-start(bf16[6,8,1024]{2,1,0:T(8,128)(2,1)S(1)} %get-tuple-element.84), channel_id=1, source_target_pairs={{0,1},{1,0},{2,3},{3,2},{4,5},{5,4},{6,7},{7,6},{8,9},{9,8},{10,11... | collective-permute-start | bytes 294920 | tf_op jit(solution)/shard_map/ppermute | solution.py:63
  20.2 0.7 collective-permute-start.2
  20.8 1.0 broadcast_select_fusion.9
  21.8 1.8 %collective-permute-done.1 = bf16[6,8,1024]{2,1,0:T(8,128)(2,1)S(1)} collective-permute-done((bf16[6,8,1024]{2,1,0:T(8,128)(2,1)S(1)}, bf16[6,8,1024]{2,1,0:T(8,128)(2,1)S(1)}, u32[]{:S(2)}, u32[]{:S(2)}) %collective-permute-start.1) | collective-permute-done | bytes 98336 | tf_op jit(solution)/shard_map/ppermute | solution.py:63
  23.8 0.2 pad_maximum_fusion
  24.2 14.9 %query_pass.1 = (bf16[2,256,1024]{2,1,0:T(8,128)(2,1)S(1)}, bf16[2,896,1024]{2,1,0:T(8,128)(2,1)S(1)}) custom-call(s32[5]{0:T(128)S(1)} %stack.15.place_ref, bf16[256,1024]{1,0:T(8,128)(2,1)S(1)} %fusion.62.q_ref, bf16[256,1024]{1,0:T(8,128)(2,1)S(1)} %fusion.59.g_ref, bf16[896,1024]{1,0:T(8,128)(2,1)S(1)} %bitcast.80, bf16[1024,4096]{1,0:T(8,128)(2,1)} %value_w_ref.1, ...), custom_call_target="tpu_custom_call" | custom-call | flops 4294967296 | bytes 4194304 | tf_op jit(solution)/shard_map/query_pass/pallas_call | solution.py:298
  39.1 1.3 %fusion.27 = bf16[512,1024]{1,0:T(8,128)(2,1)S(1)} fusion(bf16[2,896,1024]{2,1,0:T(8,128)(2,1)S(1)} %get-tuple-element.26, bf16[896,256]{1,0:T(8,128)(2,1)S(1)} %get-tuple-element.48, bf16[896,256]{1,0:T(8,128)(2,1)S(1)} %get-tuple-element.47), kind=kOutput, calls=%fused_computation.38 | convolution fusion | flops 941883392 | bytes 3801088 | tf_op jit(solution)/shard_map/dot_general | solution.py:328
  40.4 1.3 %fusion.30 = bf16[512,1024]{1,0:T(8,128)(2,1)S(1)} fusion(bf16[2,896,1024]{2,1,0:T(8,128)(2,1)S(1)} %get-tuple-element.26, bf16[896,256]{1,0:T(8,128)(2,1)S(1)} %get-tuple-element.48, bf16[896,256]{1,0:T(8,128)(2,1)S(1)} %get-tuple-element.47), kind=kOutput, calls=%fused_computation.39 | convolution fusion | flops 941883392 | bytes 3801088 | tf_op jit(solution)/shard_map/dot_general | solution.py:328
  41.9 0.3 fusion.126
  42.3 0.5 collective-permute-start.6
  43.0 0.3 fusion.123
  43.3 0.3 fusion.115
  43.6 0.3 fusion.108
  43.9 0.2 constant_dynamic-slice_fusion.4
  44.2 0.2 collective-permute-done.8
  44.5 1.2 %fusion.68 = bf16[256,1024]{1,0:T(8,128)(2,1)S(1)} fusion(f32[256,1024]{1,0:T(8,128)S(1)} %fusion.126, bf16[2,256,1024]{2,1,0:T(8,128)(2,1)S(1)} %collective-permute-done.8, bf16[256,1024]{1,0:T(8,128)(2,1)} %collective-permute-done.7, s32[]{:T(128)S(6)} %select_n.257), kind=kOutput, calls=%fused_computation.60 | convolution fusion | flops 134742016 | bytes 2228228 | tf_op jit(solution)/shard_map/dot_general | solution.py:328
  45.7 1.6 %collective-permute-start.13 = (bf16[256,1024]{1,0:T(8,128)(2,1)S(1)}, bf16[256,1024]{1,0:T(8,128)(2,1)S(1)}, u32[]{:S(2)}, u32[]{:S(2)}) collective-permute-start(bf16[256,1024]{1,0:T(8,128)(2,1)S(1)} %fusion.68), channel_id=1, source_target_pairs={{0,16},{8,24},{16,0},{24,8},{1,17},{9,25},{17,1},{25,9},{2,18},{10... | collective-permute-start | bytes 1572872 | tf_op jit(solution)/shard_map/ppermute | solution.py:23
  47.3 0.3 fusion.69
  47.7 0.6 collective-permute-start.15
  48.3 0.7 add_convert_fusion
  49.1 1.6 %collective-permute-start.22 = (bf16[256,1024]{1,0:T(8,128)(2,1)S(1)}, bf16[256,1024]{1,0:T(8,128)(2,1)S(1)}, u32[]{:S(2)}, u32[]{:S(2)}) collective-permute-start(bf16[256,1024]{1,0:T(8,128)(2,1)S(1)} %add_convert_fusion), channel_id=1, source_target_pairs={{0,4},{4,0},{1,5},{5,1},{2,6},{6,2},{3,7},{7,3},{8,12},{12,8},{9,1... | collective-permute-start | bytes 1572872 | tf_op jit(solution)/shard_map/ppermute | solution.py:23
  50.7 0.7 fusion.56
  51.4 0.6 collective-permute-start.20
  52.2 0.9 collective-permute-start.10
  53.1 1.5 %fusion.65 = bf16[256,1024]{1,0:T(8,128)(2,1)} fusion(bf16[256,1024]{1,0:T(8,128)(2,1)S(1)} %get-tuple-element.23, bf16[1024,4096]{1,0:T(8,128)(2,1)S(1)} %bitcast.90, bf16[256,1024]{1,0:T(8,128)(2,1)S(1)} %bitcast.92, f32[256]{0:T(256)S(1)} %convert_element_type.161), kind=kOutput, calls=%fused_computation.59 | convolution fusion | flops 537919488 | bytes 3671040 | tf_op jit(solution)/shard_map/dot_general | solution.py:170
  54.6 0.7 convert_add_fusion.3
  55.4 0.8 fusion.42
  56.2 1.2 %convolution_add_fusion.1 = f32[256,1024]{1,0:T(8,128)S(1)} fusion(f32[256,1024]{1,0:T(8,128)S(1)} %fusion.123, bf16[2,256,1024]{2,1,0:T(8,128)(2,1)S(1)} %collective-permute-done.8, bf16[256,1024]{1,0:T(8,128)(2,1)} %collective-permute-done.7, s32[]{:T(128)S(6)} %select_n.274), kind=kOutput, calls=%fused_computation.47 | convolution fusion | flops 134479872 | bytes 2752516 | tf_op jit(solution)/shard_map/dot_general | solution.py:328
  57.4 0.3 convolution_add_fusion
  57.7 2.8 %collective-permute-done.13 = bf16[256,1024]{1,0:T(8,128)(2,1)S(1)} collective-permute-done((bf16[256,1024]{1,0:T(8,128)(2,1)S(1)}, bf16[256,1024]{1,0:T(8,128)(2,1)S(1)}, u32[]{:S(2)}, u32[]{:S(2)}) %collective-permute-start.13) | collective-permute-done | bytes 524320 | tf_op jit(solution)/shard_map/ppermute | solution.py:23
  60.5 3.7 %collective-permute-start.11 = (bf16[2,28,8,1024]{3,2,1,0:T(8,128)(2,1)S(1)}, bf16[2,28,8,1024]{3,2,1,0:T(8,128)(2,1)S(1)}, u32[]{:S(2)}, u32[]{:S(2)}) collective-permute-start(bf16[2,28,8,1024]{3,2,1,0:T(8,128)(2,1)S(1)} %get-tuple-element.40), channel_id=1, source_target_pairs={{0,1},{1,0},{2,3},{3,2},{4,5},{5,4},{6,7},{7,6},{8,9},{9,8},{10,11... | collective-permute-start | bytes 2752520 | tf_op jit(solution)/shard_map/ppermute | solution.py:63
  64.4 0.6 collective-permute-start.14
  65.2 5.9 %collective-permute-done.20 = bf16[256,1024]{1,0:T(8,128)(2,1)S(1)} collective-permute-done((bf16[256,1024]{1,0:T(8,128)(2,1)S(1)}, bf16[256,1024]{1,0:T(8,128)(2,1)S(1)}, u32[]{:S(2)}, u32[]{:S(2)}) %collective-permute-start.20) | collective-permute-done | bytes 524320 | tf_op jit(solution)/shard_map/ppermute | solution.py:23
  71.1 1.5 %collective-permute-start.16 = (bf16[128,1024]{1,0:T(8,128)(2,1)S(1)}, bf16[128,1024]{1,0:T(8,128)(2,1)S(1)}, u32[]{:S(2)}, u32[]{:S(2)}) collective-permute-start(bf16[128,1024]{1,0:T(8,128)(2,1)S(1)} %dynamic-slice_convert_fusion.2), channel_id=1, source_target_pairs={{0,16},{8,24},{16,0},{24,8},{1,17},{9,25},{17,1},{25,9},{2,18},{10... | collective-permute-start | bytes 786440 | tf_op jit(solution)/shard_map/ppermute | solution.py:23
  72.8 1.0 collective-permute-done.22
  73.8 0.5 collective-permute-start.21
  74.5 4.9 %collective-permute-done.14 = bf16[128,1024]{1,0:T(8,128)(2,1)S(1)} collective-permute-done((bf16[128,1024]{1,0:T(8,128)(2,1)S(1)}, bf16[128,1024]{1,0:T(8,128)(2,1)S(1)}, u32[]{:S(2)}, u32[]{:S(2)}) %collective-permute-start.14) | collective-permute-done | bytes 262176 | tf_op jit(solution)/shard_map/ppermute | solution.py:23
  79.4 0.5 collective-permute-start.23
  80.1 1.0 collective-permute-start.17
  81.1 2.9 %collective-permute-done.21 = bf16[128,1024]{1,0:T(8,128)(2,1)S(1)} collective-permute-done((bf16[128,1024]{1,0:T(8,128)(2,1)S(1)}, bf16[128,1024]{1,0:T(8,128)(2,1)S(1)}, u32[]{:S(2)}, u32[]{:S(2)}) %collective-permute-start.21) | collective-permute-done | bytes 262176 | tf_op jit(solution)/shard_map/ppermute | solution.py:23
  84.0 3.4 %collective-permute-start.18 = (bf16[32,2048]{1,0:T(8,128)(2,1)S(1)}, bf16[32,2048]{1,0:T(8,128)(2,1)S(1)}, u32[]{:S(2)}, u32[]{:S(2)}) collective-permute-start(bf16[32,2048]{1,0:T(8,128)(2,1)S(1)} %get-tuple-element.57), channel_id=1, source_target_pairs={{0,2},{1,3},{2,0},{3,1},{4,6},{5,7},{6,4},{7,5},{8,10},{9,11},{10,... | collective-permute-start | bytes 393224 | tf_op jit(solution)/shard_map/ppermute | solution.py:23
  87.5 1.9 %collective-permute-start.19 = (bf16[32,2048]{1,0:T(8,128)(2,1)S(1)}, bf16[32,2048]{1,0:T(8,128)(2,1)S(1)}, u32[]{:S(2)}, u32[]{:S(2)}) collective-permute-start(bf16[32,2048]{1,0:T(8,128)(2,1)S(1)} %get-tuple-element.58), channel_id=1, source_target_pairs={{0,1},{1,0},{2,3},{3,2},{4,5},{5,4},{6,7},{7,6},{8,9},{9,8},{10,11... | collective-permute-start | bytes 393224 | tf_op jit(solution)/shard_map/ppermute | solution.py:23
  89.7 1.0 fusion.143
  90.8 0.6 collective-permute-start.12
  91.4 1.3 %collective-permute-start.24 = (bf16[32,2048]{1,0:T(8,128)(2,1)S(1)}, bf16[32,2048]{1,0:T(8,128)(2,1)S(1)}, u32[]{:S(2)}, u32[]{:S(2)}) collective-permute-start(bf16[32,2048]{1,0:T(8,128)(2,1)S(1)} %get-tuple-element.49), channel_id=1, source_target_pairs={{0,3},{1,2},{2,1},{3,0},{4,7},{5,6},{6,5},{7,4},{8,11},{9,10},{10,... | collective-permute-start | bytes 393224 | tf_op jit(solution)/shard_map/ppermute | solution.py:23
  92.6 0.7 collective-permute-start.26
  93.3 3.7 %collective-permute-done.18 = bf16[32,2048]{1,0:T(8,128)(2,1)S(1)} collective-permute-done((bf16[32,2048]{1,0:T(8,128)(2,1)S(1)}, bf16[32,2048]{1,0:T(8,128)(2,1)S(1)}, u32[]{:S(2)}, u32[]{:S(2)}) %collective-permute-start.18) | collective-permute-done | bytes 131104 | tf_op jit(solution)/shard_map/ppermute | solution.py:23
  97.2 1.9 %collective-permute-done.12 = bf16[2,6,16,1024]{3,2,1,0:T(8,128)(2,1)S(1)} collective-permute-done((bf16[2,6,16,1024]{3,2,1,0:T(8,128)(2,1)S(1)}, bf16[2,6,16,1024]{3,2,1,0:T(8,128)(2,1)S(1)}, u32[]{:S(2)}, u32[]{:S(2)}) %collective-permute-start.12) | collective-permute-done | bytes 393248 | tf_op jit(solution)/shard_map/ppermute | solution.py:23
  99.2 0.3 fusion.3
  99.6 0.2 copy-done.2
  99.8 2.0 %fusion.144 = (f32[256]{0:T(256)S(1)}, f32[256]{0:T(256)S(1)}, f32[256,1024]{1,0:T(8,128)S(1)}) fusion(f32[256]{0:T(256)S(1)} %get-tuple-element.35, f32[256]{0:T(256)S(1)} %get-tuple-element.36, bf16[1,16,16,1024]{3,2,1,0:T(8,128)(2,1)S(1)} %copy-done, f32[1024]{0:T(1024)S(1)} %copy-done.2, bf16[1024,4096]{1,0:T(8,128)(2,1)S(1)} %bitcast.90, ...), kind=kOutput, calls=%fused_computation.192 | convolution fusion | flops 1617165824 | bytes 9445376 | tf_op jit(solution)/shard_map/dot_general | solution.py:174
  101.9 1.2 %fusion.77 = bf16[256,1024]{1,0:T(8,128)(2,1)} fusion(f32[256,1024]{1,0:T(8,128)S(1)} %get-tuple-element.86, f32[256]{0:T(256)S(1)} %get-tuple-element.87, f32[256]{0:T(256)S(1)} %get-tuple-element.36, f32[256]{0:T(256)S(1)} %get-tuple-element.88, f32[256]{0:T(256)S(1)} %get-tuple-element.35, bf16[1,16,16,1024]{3,2,1,0:T(8,128)(2,1)S(1)} %copy-done.1, ...), kind=kLoop, calls=%fused_computation.69 | loop fusion | flops 2621440 | bytes 2625536 | tf_op jit(solution)/shard_map/convert_element_type | solution.py:554
  103.2 2.5 %collective-permute-done.25 = bf16[32,2048]{1,0:T(8,128)(2,1)S(1)} collective-permute-done((bf16[32,2048]{1,0:T(8,128)(2,1)S(1)}, bf16[32,2048]{1,0:T(8,128)(2,1)S(1)}, u32[]{:S(2)}, u32[]{:S(2)}) %collective-permute-start.25) | collective-permute-done | bytes 131104 | tf_op jit(solution)/shard_map/ppermute | solution.py:23
  105.7 0.8 maximum_multiply_fusion
  (68 shorter events, 3.1 us)
Async XLA Ops:
  4.4 12.1 %collective-permute-start = (bf16[6,16,1024]{2,1,0:T(8,128)(2,1)S(1)}, bf16[6,16,1024]{2,1,0:T(8,128)(2,1)S(1)}, u32[]{:S(2)}, u32[]{:S(2)}) collective-permute-start(bf16[6,16,1024]{2,1,0:T(8,128)(2,1)S(1)} %bitcast.88), channel_id=1, source_target_pairs={{0,4},{4,0},{1,5},{5,1},{2,6},{6,2},{3,7},{7,3},{8,12},{12,8},{9,1... | collective-permute-start | bytes 589832 | tf_op jit(solution)/shard_map/ppermute | solution.py:23
  7.4 37.0 %collective-permute-start.7 = (bf16[256,1024]{1,0:T(8,128)(2,1)S(1)}, bf16[256,1024]{1,0:T(8,128)(2,1)}, u32[]{:S(2)}, u32[]{:S(2)}) collective-permute-start(bf16[256,1024]{1,0:T(8,128)(2,1)S(1)} %get-tuple-element.18), channel_id=1, source_target_pairs={{0,8},{8,0},{16,24},{24,16},{1,9},{9,1},{17,25},{25,17},{2,10},{10... | collective-permute-start | bytes 1572872 | tf_op jit(solution)/shard_map/ppermute | solution.py:23
  8.3 11.9 %collective-permute-start.3 = (bf16[16,8,1024]{2,1,0:T(8,128)(2,1)}, bf16[16,8,1024]{2,1,0:T(8,128)(2,1)S(1)}, u32[]{:S(2)}, u32[]{:S(2)}) collective-permute-start(bf16[16,8,1024]{2,1,0:T(8,128)(2,1)} %get-tuple-element.74), channel_id=1, source_target_pairs={{0,1},{1,0},{2,3},{3,2},{4,5},{5,4},{6,7},{7,6},{8,9},{9,8},{10,11... | collective-permute-start | bytes 786440 | tf_op jit(solution)/shard_map/ppermute | solution.py:63
  9.8 11.0 %collective-permute-start.4 = (bf16[16,8,1024]{2,1,0:T(8,128)(2,1)}, bf16[16,8,1024]{2,1,0:T(8,128)(2,1)}, u32[]{:S(2)}, u32[]{:S(2)}) collective-permute-start(bf16[16,8,1024]{2,1,0:T(8,128)(2,1)} %get-tuple-element.75), channel_id=1, source_target_pairs={{1,2},{2,1},{5,6},{6,5},{9,10},{10,9},{13,14},{14,13},{17,18},{18,... | collective-permute-start | bytes 786440 | tf_op jit(solution)/shard_map/ppermute | solution.py:62
  11.2 36.1 %collective-permute-start.9 = (bf16[256,1024]{1,0:T(8,128)(2,1)S(1)}, bf16[256,1024]{1,0:T(8,128)(2,1)S(1)}, u32[]{:S(2)}, u32[]{:S(2)}) collective-permute-start(bf16[256,1024]{1,0:T(8,128)(2,1)S(1)} %get-tuple-element.19), channel_id=1, source_target_pairs={{0,8},{8,0},{16,24},{24,16},{1,9},{9,1},{17,25},{25,17},{2,10},{10... | collective-permute-start | bytes 1572872 | tf_op jit(solution)/shard_map/ppermute | solution.py:23
  16.6 7.0 %collective-permute-start.1 = (bf16[6,8,1024]{2,1,0:T(8,128)(2,1)S(1)}, bf16[6,8,1024]{2,1,0:T(8,128)(2,1)S(1)}, u32[]{:S(2)}, u32[]{:S(2)}) collective-permute-start(bf16[6,8,1024]{2,1,0:T(8,128)(2,1)S(1)} %get-tuple-element.84), channel_id=1, source_target_pairs={{0,1},{1,0},{2,3},{3,2},{4,5},{5,4},{6,7},{7,6},{8,9},{9,8},{10,11... | collective-permute-start | bytes 294920 | tf_op jit(solution)/shard_map/ppermute | solution.py:63
  20.2 3.5 %collective-permute-start.2 = (bf16[6,8,1024]{2,1,0:T(8,128)(2,1)S(1)}, bf16[6,8,1024]{2,1,0:T(8,128)(2,1)S(1)}, u32[]{:S(2)}, u32[]{:S(2)}) collective-permute-start(bf16[6,8,1024]{2,1,0:T(8,128)(2,1)S(1)} %get-tuple-element.85), channel_id=1, source_target_pairs={{1,2},{2,1},{5,6},{6,5},{9,10},{10,9},{13,14},{14,13},{17,18},{18,... | collective-permute-start | bytes 294920 | tf_op jit(solution)/shard_map/ppermute | solution.py:62
  41.7 2.7 %collective-permute-start.8 = (bf16[2,256,1024]{2,1,0:T(8,128)(2,1)S(1)}, bf16[2,256,1024]{2,1,0:T(8,128)(2,1)S(1)}, u32[]{:S(2)}, u32[]{:S(2)}) collective-permute-start(bf16[2,256,1024]{2,1,0:T(8,128)(2,1)S(1)} %get-tuple-element.21), channel_id=1, source_target_pairs={{0,8},{8,0},{16,24},{24,16},{1,9},{9,1},{17,25},{25,17},{2,10},{10... | collective-permute-start | bytes 3145736 | tf_op jit(solution)/shard_map/ppermute | solution.py:23
  42.3 6.0 %collective-permute-start.6 = (bf16[512,1024]{1,0:T(8,128)(2,1)S(1)}, bf16[512,1024]{1,0:T(8,128)(2,1)S(1)}, u32[]{:S(2)}, u32[]{:S(2)}) collective-permute-start(bf16[512,1024]{1,0:T(8,128)(2,1)S(1)} %fusion.30), channel_id=1, source_target_pairs={{0,8},{8,0},{16,24},{24,16},{1,9},{9,1},{17,25},{25,17},{2,10},{10... | collective-permute-start | bytes 3145736 | tf_op jit(solution)/shard_map/ppermute | solution.py:23
  42.8 7.8 %collective-permute-start.5 = (bf16[512,1024]{1,0:T(8,128)(2,1)S(1)}, bf16[512,1024]{1,0:T(8,128)(2,1)S(1)}, u32[]{:S(2)}, u32[]{:S(2)}) collective-permute-start(bf16[512,1024]{1,0:T(8,128)(2,1)S(1)} %fusion.27), channel_id=1, source_target_pairs={{0,8},{8,0},{16,24},{24,16},{1,9},{9,1},{17,25},{25,17},{2,10},{10... | collective-permute-start | bytes 3145736 | tf_op jit(solution)/shard_map/ppermute | solution.py:23
  45.7 14.8 %collective-permute-start.13 = (bf16[256,1024]{1,0:T(8,128)(2,1)S(1)}, bf16[256,1024]{1,0:T(8,128)(2,1)S(1)}, u32[]{:S(2)}, u32[]{:S(2)}) collective-permute-start(bf16[256,1024]{1,0:T(8,128)(2,1)S(1)} %fusion.68), channel_id=1, source_target_pairs={{0,16},{8,24},{16,0},{24,8},{1,17},{9,25},{17,1},{25,9},{2,18},{10... | collective-permute-start | bytes 1572872 | tf_op jit(solution)/shard_map/ppermute | solution.py:23
  47.7 16.8 %collective-permute-start.15 = (bf16[256,1024]{1,0:T(8,128)(2,1)S(1)}, bf16[256,1024]{1,0:T(8,128)(2,1)S(1)}, u32[]{:S(2)}, u32[]{:S(2)}) collective-permute-start(bf16[256,1024]{1,0:T(8,128)(2,1)S(1)} %fusion.69), channel_id=1, source_target_pairs={{0,4},{4,0},{1,5},{5,1},{2,6},{6,2},{3,7},{7,3},{8,12},{12,8},{9,1... | collective-permute-start | bytes 1572872 | tf_op jit(solution)/shard_map/ppermute | solution.py:23
  48.2 4.8 %slice-start = ((s8[8388608]{0:T(1024)(128)(4,1)}), s8[4194304]{0:T(1024)(128)(4,1)S(1)}, s32[]{:S(2)}) async-start(s8[8388608]{0:T(1024)(128)(4,1)} %bitcast.89), calls=%async_computation | async-start | bytes 8388608
  49.1 4.0 %slice-start.1 = ((s8[8388608]{0:T(1024)(128)(4,1)}), s8[4194304]{0:T(1024)(128)(4,1)S(1)}, s32[]{:S(2)}) async-start(s8[8388608]{0:T(1024)(128)(4,1)} %bitcast.89), calls=%async_computation.1 | async-start | bytes 8388608
  49.1 24.7 %collective-permute-start.22 = (bf16[256,1024]{1,0:T(8,128)(2,1)S(1)}, bf16[256,1024]{1,0:T(8,128)(2,1)S(1)}, u32[]{:S(2)}, u32[]{:S(2)}) collective-permute-start(bf16[256,1024]{1,0:T(8,128)(2,1)S(1)} %add_convert_fusion), channel_id=1, source_target_pairs={{0,4},{4,0},{1,5},{5,1},{2,6},{6,2},{3,7},{7,3},{8,12},{12,8},{9,1... | collective-permute-start | bytes 1572872 | tf_op jit(solution)/shard_map/ppermute | solution.py:23
  51.4 1.7 %copy-start = (bf16[1,16,16,1024]{3,2,1,0:T(8,128)(2,1)S(1)}, bf16[1,16,16,1024]{3,2,1,0:T(8,128)(2,1)}, u32[]{:S(2)}) copy-start(bf16[1,16,16,1024]{3,2,1,0:T(8,128)(2,1)} %param.5) | copy-start | bytes 1572868
  51.4 19.7 %collective-permute-start.20 = (bf16[256,1024]{1,0:T(8,128)(2,1)S(1)}, bf16[256,1024]{1,0:T(8,128)(2,1)S(1)}, u32[]{:S(2)}, u32[]{:S(2)}) collective-permute-start(bf16[256,1024]{1,0:T(8,128)(2,1)S(1)} %fusion.56), channel_id=1, source_target_pairs={{0,16},{8,24},{16,0},{24,8},{1,17},{9,25},{17,1},{25,9},{2,18},{10... | collective-permute-start | bytes 1572872 | tf_op jit(solution)/shard_map/ppermute | solution.py:23
  52.2 37.4 %collective-permute-start.10 = (bf16[2,28,8,1024]{3,2,1,0:T(8,128)(2,1)S(1)}, bf16[2,28,8,1024]{3,2,1,0:T(8,128)(2,1)S(1)}, u32[]{:S(2)}, u32[]{:S(2)}) collective-permute-start(bf16[2,28,8,1024]{3,2,1,0:T(8,128)(2,1)S(1)} %get-tuple-element.39), channel_id=1, source_target_pairs={{1,2},{2,1},{5,6},{6,5},{9,10},{10,9},{13,14},{14,13},{17,18},{18,... | collective-permute-start | bytes 2752520 | tf_op jit(solution)/shard_map/ppermute | solution.py:62
  60.5 29.1 %collective-permute-start.11 = (bf16[2,28,8,1024]{3,2,1,0:T(8,128)(2,1)S(1)}, bf16[2,28,8,1024]{3,2,1,0:T(8,128)(2,1)S(1)}, u32[]{:S(2)}, u32[]{:S(2)}) collective-permute-start(bf16[2,28,8,1024]{3,2,1,0:T(8,128)(2,1)S(1)} %get-tuple-element.40), channel_id=1, source_target_pairs={{0,1},{1,0},{2,3},{3,2},{4,5},{5,4},{6,7},{7,6},{8,9},{9,8},{10,11... | collective-permute-start | bytes 2752520 | tf_op jit(solution)/shard_map/ppermute | solution.py:63
  64.4 14.9 %collective-permute-start.14 = (bf16[128,1024]{1,0:T(8,128)(2,1)S(1)}, bf16[128,1024]{1,0:T(8,128)(2,1)S(1)}, u32[]{:S(2)}, u32[]{:S(2)}) collective-permute-start(bf16[128,1024]{1,0:T(8,128)(2,1)S(1)} %dynamic-slice_convert_fusion.3), channel_id=1, source_target_pairs={{0,4},{4,0},{1,5},{5,1},{2,6},{6,2},{3,7},{7,3},{8,12},{12,8},{9,1... | collective-permute-start | bytes 786440 | tf_op jit(solution)/shard_map/ppermute | solution.py:23
  71.1 8.9 %collective-permute-start.16 = (bf16[128,1024]{1,0:T(8,128)(2,1)S(1)}, bf16[128,1024]{1,0:T(8,128)(2,1)S(1)}, u32[]{:S(2)}, u32[]{:S(2)}) collective-permute-start(bf16[128,1024]{1,0:T(8,128)(2,1)S(1)} %dynamic-slice_convert_fusion.2), channel_id=1, source_target_pairs={{0,16},{8,24},{16,0},{24,8},{1,17},{9,25},{17,1},{25,9},{2,18},{10... | collective-permute-start | bytes 786440 | tf_op jit(solution)/shard_map/ppermute | solution.py:23
  73.8 10.2 %collective-permute-start.21 = (bf16[128,1024]{1,0:T(8,128)(2,1)S(1)}, bf16[128,1024]{1,0:T(8,128)(2,1)S(1)}, u32[]{:S(2)}, u32[]{:S(2)}) collective-permute-start(bf16[128,1024]{1,0:T(8,128)(2,1)S(1)} %dynamic-slice_convert_fusion.1), channel_id=1, source_target_pairs={{0,4},{4,0},{1,5},{5,1},{2,6},{6,2},{3,7},{7,3},{8,12},{12,8},{9,1... | collective-permute-start | bytes 786440 | tf_op jit(solution)/shard_map/ppermute | solution.py:23
  79.4 8.1 %collective-permute-start.23 = (bf16[128,1024]{1,0:T(8,128)(2,1)S(1)}, bf16[128,1024]{1,0:T(8,128)(2,1)S(1)}, u32[]{:S(2)}, u32[]{:S(2)}) collective-permute-start(bf16[128,1024]{1,0:T(8,128)(2,1)S(1)} %dynamic-slice_convert_fusion), channel_id=1, source_target_pairs={{0,16},{8,24},{16,0},{24,8},{1,17},{9,25},{17,1},{25,9},{2,18},{10... | collective-permute-start | bytes 786440 | tf_op jit(solution)/shard_map/ppermute | solution.py:23
  80.1 12.5 %collective-permute-start.17 = (bf16[32,2048]{1,0:T(8,128)(2,1)S(1)}, bf16[32,2048]{1,0:T(8,128)(2,1)S(1)}, u32[]{:S(2)}, u32[]{:S(2)}) collective-permute-start(bf16[32,2048]{1,0:T(8,128)(2,1)S(1)} %get-tuple-element.56), channel_id=1, source_target_pairs={{0,3},{1,2},{2,1},{3,0},{4,7},{5,6},{6,5},{7,4},{8,11},{9,10},{10,... | collective-permute-start | bytes 393224 | tf_op jit(solution)/shard_map/ppermute | solution.py:23
  84.0 13.1 %collective-permute-start.18 = (bf16[32,2048]{1,0:T(8,128)(2,1)S(1)}, bf16[32,2048]{1,0:T(8,128)(2,1)S(1)}, u32[]{:S(2)}, u32[]{:S(2)}) collective-permute-start(bf16[32,2048]{1,0:T(8,128)(2,1)S(1)} %get-tuple-element.57), channel_id=1, source_target_pairs={{0,2},{1,3},{2,0},{3,1},{4,6},{5,7},{6,4},{7,5},{8,10},{9,11},{10,... | collective-permute-start | bytes 393224 | tf_op jit(solution)/shard_map/ppermute | solution.py:23
  87.5 9.6 %collective-permute-start.19 = (bf16[32,2048]{1,0:T(8,128)(2,1)S(1)}, bf16[32,2048]{1,0:T(8,128)(2,1)S(1)}, u32[]{:S(2)}, u32[]{:S(2)}) collective-permute-start(bf16[32,2048]{1,0:T(8,128)(2,1)S(1)} %get-tuple-element.58), channel_id=1, source_target_pairs={{0,1},{1,0},{2,3},{3,2},{4,5},{5,4},{6,7},{7,6},{8,9},{9,8},{10,11... | collective-permute-start | bytes 393224 | tf_op jit(solution)/shard_map/ppermute | solution.py:23
  90.8 8.3 %collective-permute-start.12 = (bf16[2,6,16,1024]{3,2,1,0:T(8,128)(2,1)S(1)}, bf16[2,6,16,1024]{3,2,1,0:T(8,128)(2,1)S(1)}, u32[]{:S(2)}, u32[]{:S(2)}) collective-permute-start(bf16[2,6,16,1024]{3,2,1,0:T(8,128)(2,1)S(1)} %slice_select_fusion), channel_id=1, source_target_pairs={{0,4},{4,0},{1,5},{5,1},{2,6},{6,2},{3,7},{7,3},{8,12},{12,8},{9,1... | collective-permute-start | bytes 1179656 | tf_op jit(solution)/shard_map/ppermute | solution.py:23
  91.4 11.8 %collective-permute-start.24 = (bf16[32,2048]{1,0:T(8,128)(2,1)S(1)}, bf16[32,2048]{1,0:T(8,128)(2,1)S(1)}, u32[]{:S(2)}, u32[]{:S(2)}) collective-permute-start(bf16[32,2048]{1,0:T(8,128)(2,1)S(1)} %get-tuple-element.49), channel_id=1, source_target_pairs={{0,3},{1,2},{2,1},{3,0},{4,7},{5,6},{6,5},{7,4},{8,11},{9,10},{10,... | collective-permute-start | bytes 393224 | tf_op jit(solution)/shard_map/ppermute | solution.py:23
  92.6 10.5 %collective-permute-start.26 = (bf16[32,2048]{1,0:T(8,128)(2,1)S(1)}, bf16[32,2048]{1,0:T(8,128)(2,1)S(1)}, u32[]{:S(2)}, u32[]{:S(2)}) collective-permute-start(bf16[32,2048]{1,0:T(8,128)(2,1)S(1)} %get-tuple-element.50), channel_id=1, source_target_pairs={{0,1},{1,0},{2,3},{3,2},{4,5},{5,4},{6,7},{7,6},{8,9},{9,8},{10,11... | collective-permute-start | bytes 393224 | tf_op jit(solution)/shard_map/ppermute | solution.py:23
  97.1 8.6 %collective-permute-start.25 = (bf16[32,2048]{1,0:T(8,128)(2,1)S(1)}, bf16[32,2048]{1,0:T(8,128)(2,1)S(1)}, u32[]{:S(2)}, u32[]{:S(2)}) collective-permute-start(bf16[32,2048]{1,0:T(8,128)(2,1)S(1)} %get-tuple-element.51), channel_id=1, source_target_pairs={{0,2},{1,3},{2,0},{3,1},{4,6},{5,7},{6,4},{7,5},{8,10},{9,11},{10,... | collective-permute-start | bytes 393224 | tf_op jit(solution)/shard_map/ppermute | solution.py:23
  99.1 0.7 copy-start.2
  99.8 2.1 %copy-start.1 = (bf16[1,16,16,1024]{3,2,1,0:T(8,128)(2,1)S(1)}, bf16[1,16,16,1024]{3,2,1,0:T(8,128)(2,1)}, u32[]{:S(2)}) copy-start(bf16[1,16,16,1024]{3,2,1,0:T(8,128)(2,1)} %param.9) | copy-start | bytes 1572868

commit v7 on v6

--- a/solution.py
+++ b/solution.py
@@ -499,9 +499,10 @@
     normed_ext = normed_ext.reshape(ext_rows * ext_cols, model_width)
 
     grad_attn = times_t(branch_flat, weight_out).astype(BF)
-    queries = times(normed, weight_in[:, :model_width]).astype(BF)
-    normed_pair = (normed, slide_swap(normed, False))
-    branch_pair = (branch_flat, slide_swap(branch_flat, False))
+    queries = times(after(normed, *rows), weight_in[:, :model_width]).astype(BF)
+    normed_late, branch_late, queries = lax.optimization_barrier((normed, branch_flat, queries))
+    normed_pair = (normed, slide_swap(normed_late, False))
+    branch_pair = (branch_flat, slide_swap(branch_late, False))
 
     found, owed = run_queries(place, queries, grad_attn, normed_ext, weights, head_dim, tile)
     attended, grad_queries = found[0], found[1]

time: 107 us -> 103 us (0.963)
  matrix products: 18.2 us -> 16.4 us
  other arithmetic: 7.88 us -> 6.15 us
    dot_general x14, matrix products: 9.95 us -> 8.17 us  [product_t(): lax.dot_general(left, right, (((0,), (0,)), ((), ())), preferred_element_...]
    ppermute x3, waiting for transfers between devices: 1.79 us -> 0.01 us  [exchange_columns(): two = lax.ppermute(out_two, 'gx', second)]
    ppermute x21, waiting for transfers between devices: 25.8 us -> 27.4 us  [swapped(): return lax.ppermute(array, axis, [(i, i ^ by) for i in range(count)])]
  transfers between devices with their start and end apart: 27 -> 27, of which waited for: 10 -> 9; matrix products, arithmetic and copies ran while one was open for 24% -> 22% of each run, Pallas kernels for 14% -> 15%
where the time goes in v7:
time: 103 us; the launch traced here: 102 us
  starting transfers between devices  31.3 us (30%)
  waiting for transfers between devices  27.4 us (27%)
  Pallas kernels  17.8 us (17%)
  matrix products  16.4 us (16%)
  other arithmetic  6.15 us (6%)
  local copies, waits for them, and re-layouts  1.87 us (2%)
  between operations  1.35 us (1%)
    ppermute x21, waiting for transfers between devices, swapped(): return lax.ppermute(array, axis, [(i, i ^ by) for i in range(count)])  27.4 us
    ppermute x21, starting transfers between devices, swapped(): return lax.ppermute(array, axis, [(i, i ^ by) for i in range(count)])  20.1 us
    pallas_call x1, Pallas kernels, run_queries(): pl.pallas_call(functools.partial(query_pass, head_dim, tile), grid=(group...  14.9 us
    ppermute x3, starting transfers between devices, exchange_columns(): two = lax.ppermute(out_two, 'gx', second)  9 us
    dot_general x14, matrix products, product_t(): lax.dot_general(left, right, (((0,), (0,)), ((), ())), preferred_element_...  8.17 us
    dot_general x2, matrix products, times_t(): lax.dot_general(left, right, (((1,), (1,)), ((), ())), preferred_element_...  4.38 us
    dot_general x2, matrix products, times(): return jnp.dot(left, right, preferred_element_type=F32)  3.83 us
    pallas_call x1, Pallas kernels, run_prepare(): pl.pallas_call(prepare, grid=(count // block,), in_specs=[SCALARS, part(w...  2.85 us
  transfers between devices with their start and end apart: 27, of which 9 were waited for; matrix products, arithmetic and copies ran while one was open for 22% of the time, Pallas kernels for 15%

profile of v7, /device:TPU:0, one launch (start us, length us, event | category | flops | bytes accessed | tf_op | source)
XLA Modules:
  0.0 102.3 jit_solution(6595684983641676026)
XLA Ops:
  0.6 0.7 convert_element_type.160
  1.5 2.8 %prepare.1 = (bf16[256,1024]{1,0:T(8,128)(2,1)S(1)}, bf16[256,1024]{1,0:T(8,128)(2,1)S(1)}, bf16[96,1024]{1,0:T(8,128)(2,1)S(1)}, f32[256,128]{1,0:T(8,128)S(1)}) custom-call(s32[5]{0:T(128)S(1)} %stack.15.place_ref, bf16[256,1024]{1,0:T(8,128)(2,1)} %bitcast.91, bf16[256,1024]{1,0:T(8,128)(2,1)} %bitcast.93, f32[256,1]{1,0:T(8,128)S(1)} %convert_element_type.207.t_ref, ...), custom_call_target="tpu_custom_call" | custom-call | bytes 3145728 | tf_op jit(solution)/shard_map/prepare/pallas_call | solution.py:136
  4.4 3.0 %collective-permute-start = (bf16[6,16,1024]{2,1,0:T(8,128)(2,1)S(1)}, bf16[6,16,1024]{2,1,0:T(8,128)(2,1)S(1)}, u32[]{:S(2)}, u32[]{:S(2)}) collective-permute-start(bf16[6,16,1024]{2,1,0:T(8,128)(2,1)S(1)} %bitcast.88), channel_id=1, source_target_pairs={{0,4},{4,0},{1,5},{5,1},{2,6},{6,2},{3,7},{7,3},{8,12},{12,8},{9,1... | collective-permute-start | bytes 589832 | tf_op jit(solution)/shard_map/ppermute | solution.py:23
  7.5 1.6 %collective-permute-start.3 = (bf16[16,8,1024]{2,1,0:T(8,128)(2,1)S(1)}, bf16[16,8,1024]{2,1,0:T(8,128)(2,1)S(1)}, u32[]{:S(2)}, u32[]{:S(2)}) collective-permute-start(bf16[16,8,1024]{2,1,0:T(8,128)(2,1)S(1)} %get-tuple-element.82), channel_id=1, source_target_pairs={{0,1},{1,0},{2,3},{3,2},{4,5},{5,4},{6,7},{7,6},{8,9},{9,8},{10,11... | collective-permute-start | bytes 786440 | tf_op jit(solution)/shard_map/ppermute | solution.py:63
  9.1 0.7 collective-permute-start.4
  9.8 2.3 %fusion.59.g_ref = bf16[256,1024]{1,0:T(8,128)(2,1)S(1)} fusion(bf16[256,1024]{1,0:T(8,128)(2,1)S(1)} %get-tuple-element.33, bf16[1024,4096]{1,0:T(8,128)(2,1)} %value_w_ref.1), kind=kOutput, calls=%fused_computation.57 | convolution fusion | flops 537133056 | bytes 3145728 | tf_op jit(solution)/shard_map/dot_general | solution.py:174
  12.3 0.2 slice_reduce_fusion.1
  12.6 4.5 %collective-permute-start.1 = (bf16[6,8,1024]{2,1,0:T(8,128)(2,1)S(1)}, bf16[6,8,1024]{2,1,0:T(8,128)(2,1)S(1)}, u32[]{:S(2)}, u32[]{:S(2)}) collective-permute-start(bf16[6,8,1024]{2,1,0:T(8,128)(2,1)S(1)} %get-tuple-element.92), channel_id=1, source_target_pairs={{0,1},{1,0},{2,3},{3,2},{4,5},{5,4},{6,7},{7,6},{8,9},{9,8},{10,11... | collective-permute-start | bytes 294920 | tf_op jit(solution)/shard_map/ppermute | solution.py:63
  17.0 0.7 collective-permute-start.2
  17.7 2.3 %fusion.62.q_ref = bf16[256,1024]{1,0:T(8,128)(2,1)S(1)} fusion(bf16[256,1024]{1,0:T(8,128)(2,1)S(1)} %get-tuple-element.31, bf16[1024,4096]{1,0:T(8,128)(2,1)} %value_w_ref.1), kind=kOutput, calls=%fused_computation.58 | convolution fusion | flops 537133056 | bytes 3145728 | tf_op jit(solution)/shard_map/dot_general | solution.py:170
  20.1 0.5 collective-permute-start.9
  20.7 0.2 broadcast_select_fusion.7
  20.9 0.2 pad_maximum_fusion
  21.3 14.9 %query_pass.1 = (bf16[2,256,1024]{2,1,0:T(8,128)(2,1)S(1)}, bf16[2,896,1024]{2,1,0:T(8,128)(2,1)S(1)}) custom-call(s32[5]{0:T(128)S(1)} %stack.15.place_ref, bf16[256,1024]{1,0:T(8,128)(2,1)S(1)} %fusion.62.q_ref, bf16[256,1024]{1,0:T(8,128)(2,1)S(1)} %fusion.59.g_ref, bf16[896,1024]{1,0:T(8,128)(2,1)S(1)} %bitcast.80, bf16[1024,4096]{1,0:T(8,128)(2,1)} %value_w_ref.1, ...), custom_call_target="tpu_custom_call" | custom-call | flops 4294967296 | bytes 4194304 | tf_op jit(solution)/shard_map/query_pass/pallas_call | solution.py:298
  36.2 1.3 %fusion.27 = bf16[512,1024]{1,0:T(8,128)(2,1)S(1)} fusion(bf16[2,896,1024]{2,1,0:T(8,128)(2,1)S(1)} %get-tuple-element.34, bf16[896,256]{1,0:T(8,128)(2,1)S(1)} %get-tuple-element.56, bf16[896,256]{1,0:T(8,128)(2,1)S(1)} %get-tuple-element.55), kind=kOutput, calls=%fused_computation.38 | convolution fusion | flops 941883392 | bytes 3801088 | tf_op jit(solution)/shard_map/dot_general | solution.py:328
  37.5 1.3 %fusion.30 = bf16[512,1024]{1,0:T(8,128)(2,1)S(1)} fusion(bf16[2,896,1024]{2,1,0:T(8,128)(2,1)S(1)} %get-tuple-element.34, bf16[896,256]{1,0:T(8,128)(2,1)S(1)} %get-tuple-element.56, bf16[896,256]{1,0:T(8,128)(2,1)S(1)} %get-tuple-element.55), kind=kOutput, calls=%fused_computation.39 | convolution fusion | flops 941883392 | bytes 3801088 | tf_op jit(solution)/shard_map/dot_general | solution.py:328
  38.7 0.2 collective-permute-start.8
  39.0 0.3 fusion.126
  39.4 0.5 collective-permute-start.6
  40.0 0.3 fusion.123
  40.4 0.3 fusion.115
  40.7 0.3 fusion.108
  41.0 0.2 constant_dynamic-slice_fusion.4
  41.3 0.2 collective-permute-done.8
  41.5 0.3 fusion.68
  41.9 1.6 %collective-permute-start.13 = (bf16[256,1024]{1,0:T(8,128)(2,1)S(1)}, bf16[256,1024]{1,0:T(8,128)(2,1)S(1)}, u32[]{:S(2)}, u32[]{:S(2)}) collective-permute-start(bf16[256,1024]{1,0:T(8,128)(2,1)S(1)} %fusion.68), channel_id=1, source_target_pairs={{0,16},{8,24},{16,0},{24,8},{1,17},{9,25},{17,1},{25,9},{2,18},{10... | collective-permute-start | bytes 1572872 | tf_op jit(solution)/shard_map/ppermute | solution.py:23
  43.5 0.3 fusion.69
  43.8 0.6 collective-permute-start.15
  44.5 0.7 add_convert_fusion
  45.2 1.6 %collective-permute-start.22 = (bf16[256,1024]{1,0:T(8,128)(2,1)S(1)}, bf16[256,1024]{1,0:T(8,128)(2,1)S(1)}, u32[]{:S(2)}, u32[]{:S(2)}) collective-permute-start(bf16[256,1024]{1,0:T(8,128)(2,1)S(1)} %add_convert_fusion), channel_id=1, source_target_pairs={{0,4},{4,0},{1,5},{5,1},{2,6},{6,2},{3,7},{7,3},{8,12},{12,8},{9,1... | collective-permute-start | bytes 1572872 | tf_op jit(solution)/shard_map/ppermute | solution.py:23
  46.8 0.8 fusion.56
  47.6 0.6 collective-permute-start.20
  48.3 0.9 collective-permute-start.10
  49.3 1.5 %fusion.65 = bf16[256,1024]{1,0:T(8,128)(2,1)} fusion(bf16[256,1024]{1,0:T(8,128)(2,1)S(1)} %get-tuple-element.29, bf16[1024,4096]{1,0:T(8,128)(2,1)S(1)} %bitcast.90, bf16[256,1024]{1,0:T(8,128)(2,1)S(1)} %bitcast.92, f32[256]{0:T(256)S(1)} %convert_element_type.161), kind=kOutput, calls=%fused_computation.59 | convolution fusion | flops 537919488 | bytes 3671040 | tf_op jit(solution)/shard_map/dot_general | solution.py:170
  50.8 0.7 convert_add_fusion.3
  51.5 0.8 fusion.42
  52.3 0.3 convolution_add_fusion.1
  52.7 0.3 convolution_add_fusion
  53.0 3.7 %collective-permute-done.13 = bf16[256,1024]{1,0:T(8,128)(2,1)S(1)} collective-permute-done((bf16[256,1024]{1,0:T(8,128)(2,1)S(1)}, bf16[256,1024]{1,0:T(8,128)(2,1)S(1)}, u32[]{:S(2)}, u32[]{:S(2)}) %collective-permute-start.13) | collective-permute-done | bytes 524320 | tf_op jit(solution)/shard_map/ppermute | solution.py:23
  56.7 2.9 %collective-permute-start.11 = (bf16[2,28,8,1024]{3,2,1,0:T(8,128)(2,1)S(1)}, bf16[2,28,8,1024]{3,2,1,0:T(8,128)(2,1)S(1)}, u32[]{:S(2)}, u32[]{:S(2)}) collective-permute-start(bf16[2,28,8,1024]{3,2,1,0:T(8,128)(2,1)S(1)} %get-tuple-element.48), channel_id=1, source_target_pairs={{0,1},{1,0},{2,3},{3,2},{4,5},{5,4},{6,7},{7,6},{8,9},{9,8},{10,11... | collective-permute-start | bytes 2752520 | tf_op jit(solution)/shard_map/ppermute | solution.py:63
  59.6 0.2 convert_add_fusion.5
  59.8 0.6 collective-permute-start.14
  60.6 6.7 %collective-permute-done.20 = bf16[256,1024]{1,0:T(8,128)(2,1)S(1)} collective-permute-done((bf16[256,1024]{1,0:T(8,128)(2,1)S(1)}, bf16[256,1024]{1,0:T(8,128)(2,1)S(1)}, u32[]{:S(2)}, u32[]{:S(2)}) %collective-permute-start.20) | collective-permute-done | bytes 524320 | tf_op jit(solution)/shard_map/ppermute | solution.py:23
  67.2 1.5 %collective-permute-start.16 = (bf16[128,1024]{1,0:T(8,128)(2,1)S(1)}, bf16[128,1024]{1,0:T(8,128)(2,1)S(1)}, u32[]{:S(2)}, u32[]{:S(2)}) collective-permute-start(bf16[128,1024]{1,0:T(8,128)(2,1)S(1)} %dynamic-slice_convert_fusion.2), channel_id=1, source_target_pairs={{0,16},{8,24},{16,0},{24,8},{1,17},{9,25},{17,1},{25,9},{2,18},{10... | collective-permute-start | bytes 786440 | tf_op jit(solution)/shard_map/ppermute | solution.py:23
  68.7 0.2 convert_add_fusion.2
  69.0 1.0 collective-permute-done.22
  69.9 0.5 collective-permute-start.21
  70.6 4.9 %collective-permute-done.14 = bf16[128,1024]{1,0:T(8,128)(2,1)S(1)} collective-permute-done((bf16[128,1024]{1,0:T(8,128)(2,1)S(1)}, bf16[128,1024]{1,0:T(8,128)(2,1)S(1)}, u32[]{:S(2)}, u32[]{:S(2)}) %collective-permute-start.14) | collective-permute-done | bytes 262176 | tf_op jit(solution)/shard_map/ppermute | solution.py:23
  75.5 0.5 collective-permute-start.23
  76.3 1.0 collective-permute-start.17
  77.3 2.9 %collective-permute-done.21 = bf16[128,1024]{1,0:T(8,128)(2,1)S(1)} collective-permute-done((bf16[128,1024]{1,0:T(8,128)(2,1)S(1)}, bf16[128,1024]{1,0:T(8,128)(2,1)S(1)}, u32[]{:S(2)}, u32[]{:S(2)}) %collective-permute-start.21) | collective-permute-done | bytes 262176 | tf_op jit(solution)/shard_map/ppermute | solution.py:23
  80.2 2.7 %collective-permute-start.18 = (bf16[32,2048]{1,0:T(8,128)(2,1)S(1)}, bf16[32,2048]{1,0:T(8,128)(2,1)S(1)}, u32[]{:S(2)}, u32[]{:S(2)}) collective-permute-start(bf16[32,2048]{1,0:T(8,128)(2,1)S(1)} %get-tuple-element.65), channel_id=1, source_target_pairs={{0,2},{1,3},{2,0},{3,1},{4,6},{5,7},{6,4},{7,5},{8,10},{9,11},{10,... | collective-permute-start | bytes 393224 | tf_op jit(solution)/shard_map/ppermute | solution.py:23
  83.0 1.8 %collective-permute-start.19 = (bf16[32,2048]{1,0:T(8,128)(2,1)S(1)}, bf16[32,2048]{1,0:T(8,128)(2,1)S(1)}, u32[]{:S(2)}, u32[]{:S(2)}) collective-permute-start(bf16[32,2048]{1,0:T(8,128)(2,1)S(1)} %get-tuple-element.66), channel_id=1, source_target_pairs={{0,1},{1,0},{2,3},{3,2},{4,5},{5,4},{6,7},{7,6},{8,9},{9,8},{10,11... | collective-permute-start | bytes 393224 | tf_op jit(solution)/shard_map/ppermute | solution.py:23
  85.1 1.0 fusion.143
  86.2 0.6 collective-permute-start.12
  86.8 2.3 %collective-permute-start.24 = (bf16[32,2048]{1,0:T(8,128)(2,1)S(1)}, bf16[32,2048]{1,0:T(8,128)(2,1)S(1)}, u32[]{:S(2)}, u32[]{:S(2)}) collective-permute-start(bf16[32,2048]{1,0:T(8,128)(2,1)S(1)} %get-tuple-element.57), channel_id=1, source_target_pairs={{0,3},{1,2},{2,1},{3,0},{4,7},{5,6},{6,5},{7,4},{8,11},{9,10},{10,... | collective-permute-start | bytes 393224 | tf_op jit(solution)/shard_map/ppermute | solution.py:23
  89.1 3.6 %collective-permute-done.18 = bf16[32,2048]{1,0:T(8,128)(2,1)S(1)} collective-permute-done((bf16[32,2048]{1,0:T(8,128)(2,1)S(1)}, bf16[32,2048]{1,0:T(8,128)(2,1)S(1)}, u32[]{:S(2)}, u32[]{:S(2)}) %collective-permute-start.18) | collective-permute-done | bytes 131104 | tf_op jit(solution)/shard_map/ppermute | solution.py:23
  92.8 1.7 %collective-permute-done.12 = bf16[2,6,16,1024]{3,2,1,0:T(8,128)(2,1)S(1)} collective-permute-done((bf16[2,6,16,1024]{3,2,1,0:T(8,128)(2,1)S(1)}, bf16[2,6,16,1024]{3,2,1,0:T(8,128)(2,1)S(1)}, u32[]{:S(2)}, u32[]{:S(2)}) %collective-permute-start.12) | collective-permute-done | bytes 393248 | tf_op jit(solution)/shard_map/ppermute | solution.py:23
  94.5 0.3 fusion.3
  95.0 0.2 copy-done.2
  95.2 2.0 %fusion.144 = (f32[256]{0:T(256)S(1)}, f32[256]{0:T(256)S(1)}, f32[256,1024]{1,0:T(8,128)S(1)}) fusion(f32[256]{0:T(256)S(1)} %get-tuple-element.43, f32[256]{0:T(256)S(1)} %get-tuple-element.44, bf16[1,16,16,1024]{3,2,1,0:T(8,128)(2,1)S(1)} %copy-done, f32[1024]{0:T(1024)S(1)} %copy-done.2, bf16[1024,4096]{1,0:T(8,128)(2,1)S(1)} %bitcast.90, ...), kind=kOutput, calls=%fused_computation.192 | convolution fusion | flops 1617165824 | bytes 9445376 | tf_op jit(solution)/shard_map/dot_general | solution.py:174
  97.3 1.2 %fusion.77 = bf16[256,1024]{1,0:T(8,128)(2,1)} fusion(f32[256,1024]{1,0:T(8,128)S(1)} %get-tuple-element.94, f32[256]{0:T(256)S(1)} %get-tuple-element.95, f32[256]{0:T(256)S(1)} %get-tuple-element.44, f32[256]{0:T(256)S(1)} %get-tuple-element.96, f32[256]{0:T(256)S(1)} %get-tuple-element.43, bf16[1,16,16,1024]{3,2,1,0:T(8,128)(2,1)S(1)} %copy-done.1, ...), kind=kLoop, calls=%fused_computation.69 | loop fusion | flops 2621440 | bytes 2625536 | tf_op jit(solution)/shard_map/convert_element_type | solution.py:555
  98.5 2.8 %collective-permute-done.25 = bf16[32,2048]{1,0:T(8,128)(2,1)S(1)} collective-permute-done((bf16[32,2048]{1,0:T(8,128)(2,1)S(1)}, bf16[32,2048]{1,0:T(8,128)(2,1)S(1)}, u32[]{:S(2)}, u32[]{:S(2)}) %collective-permute-start.25) | collective-permute-done | bytes 131104 | tf_op jit(solution)/shard_map/ppermute | solution.py:23
  101.4 0.8 maximum_multiply_fusion
  (68 shorter events, 2.7 us)
Async XLA Ops:
  4.4 8.2 %collective-permute-start = (bf16[6,16,1024]{2,1,0:T(8,128)(2,1)S(1)}, bf16[6,16,1024]{2,1,0:T(8,128)(2,1)S(1)}, u32[]{:S(2)}, u32[]{:S(2)}) collective-permute-start(bf16[6,16,1024]{2,1,0:T(8,128)(2,1)S(1)} %bitcast.88), channel_id=1, source_target_pairs={{0,4},{4,0},{1,5},{5,1},{2,6},{6,2},{3,7},{7,3},{8,12},{12,8},{9,1... | collective-permute-start | bytes 589832 | tf_op jit(solution)/shard_map/ppermute | solution.py:23
  7.5 12.6 %collective-permute-start.3 = (bf16[16,8,1024]{2,1,0:T(8,128)(2,1)S(1)}, bf16[16,8,1024]{2,1,0:T(8,128)(2,1)S(1)}, u32[]{:S(2)}, u32[]{:S(2)}) collective-permute-start(bf16[16,8,1024]{2,1,0:T(8,128)(2,1)S(1)} %get-tuple-element.82), channel_id=1, source_target_pairs={{0,1},{1,0},{2,3},{3,2},{4,5},{5,4},{6,7},{7,6},{8,9},{9,8},{10,11... | collective-permute-start | bytes 786440 | tf_op jit(solution)/shard_map/ppermute | solution.py:63
  9.1 11.5 %collective-permute-start.4 = (bf16[16,8,1024]{2,1,0:T(8,128)(2,1)S(1)}, bf16[16,8,1024]{2,1,0:T(8,128)(2,1)S(1)}, u32[]{:S(2)}, u32[]{:S(2)}) collective-permute-start(bf16[16,8,1024]{2,1,0:T(8,128)(2,1)S(1)} %get-tuple-element.83), channel_id=1, source_target_pairs={{1,2},{2,1},{5,6},{6,5},{9,10},{10,9},{13,14},{14,13},{17,18},{18,... | collective-permute-start | bytes 786440 | tf_op jit(solution)/shard_map/ppermute | solution.py:62
  12.6 8.1 %collective-permute-start.1 = (bf16[6,8,1024]{2,1,0:T(8,128)(2,1)S(1)}, bf16[6,8,1024]{2,1,0:T(8,128)(2,1)S(1)}, u32[]{:S(2)}, u32[]{:S(2)}) collective-permute-start(bf16[6,8,1024]{2,1,0:T(8,128)(2,1)S(1)} %get-tuple-element.92), channel_id=1, source_target_pairs={{0,1},{1,0},{2,3},{3,2},{4,5},{5,4},{6,7},{7,6},{8,9},{9,8},{10,11... | collective-permute-start | bytes 294920 | tf_op jit(solution)/shard_map/ppermute | solution.py:63
  17.0 3.6 %collective-permute-start.2 = (bf16[6,8,1024]{2,1,0:T(8,128)(2,1)S(1)}, bf16[6,8,1024]{2,1,0:T(8,128)(2,1)S(1)}, u32[]{:S(2)}, u32[]{:S(2)}) collective-permute-start(bf16[6,8,1024]{2,1,0:T(8,128)(2,1)S(1)} %get-tuple-element.93), channel_id=1, source_target_pairs={{1,2},{2,1},{5,6},{6,5},{9,10},{10,9},{13,14},{14,13},{17,18},{18,... | collective-permute-start | bytes 294920 | tf_op jit(solution)/shard_map/ppermute | solution.py:62
  20.0 21.5 %collective-permute-start.7 = (bf16[256,1024]{1,0:T(8,128)(2,1)S(1)}, bf16[256,1024]{1,0:T(8,128)(2,1)S(1)}, u32[]{:S(2)}, u32[]{:S(2)}) collective-permute-start(bf16[256,1024]{1,0:T(8,128)(2,1)S(1)} %get-tuple-element.31), channel_id=1, source_target_pairs={{0,8},{8,0},{16,24},{24,16},{1,9},{9,1},{17,25},{25,17},{2,10},{10... | collective-permute-start | bytes 1572872 | tf_op jit(solution)/shard_map/ppermute | solution.py:23
  20.1 23.4 %collective-permute-start.9 = (bf16[256,1024]{1,0:T(8,128)(2,1)S(1)}, bf16[256,1024]{1,0:T(8,128)(2,1)S(1)}, u32[]{:S(2)}, u32[]{:S(2)}) collective-permute-start(bf16[256,1024]{1,0:T(8,128)(2,1)S(1)} %get-tuple-element.33), channel_id=1, source_target_pairs={{0,8},{8,0},{16,24},{24,16},{1,9},{9,1},{17,25},{25,17},{2,10},{10... | collective-permute-start | bytes 1572872 | tf_op jit(solution)/shard_map/ppermute | solution.py:23
  38.7 2.7 %collective-permute-start.8 = (bf16[2,256,1024]{2,1,0:T(8,128)(2,1)S(1)}, bf16[2,256,1024]{2,1,0:T(8,128)(2,1)S(1)}, u32[]{:S(2)}, u32[]{:S(2)}) collective-permute-start(bf16[2,256,1024]{2,1,0:T(8,128)(2,1)S(1)} %get-tuple-element.27), channel_id=1, source_target_pairs={{0,8},{8,0},{16,24},{24,16},{1,9},{9,1},{17,25},{25,17},{2,10},{10... | collective-permute-start | bytes 3145736 | tf_op jit(solution)/shard_map/ppermute | solution.py:23
  39.4 5.0 %collective-permute-start.6 = (bf16[512,1024]{1,0:T(8,128)(2,1)S(1)}, bf16[512,1024]{1,0:T(8,128)(2,1)S(1)}, u32[]{:S(2)}, u32[]{:S(2)}) collective-permute-start(bf16[512,1024]{1,0:T(8,128)(2,1)S(1)} %fusion.30), channel_id=1, source_target_pairs={{0,8},{8,0},{16,24},{24,16},{1,9},{9,1},{17,25},{25,17},{2,10},{10... | collective-permute-start | bytes 3145736 | tf_op jit(solution)/shard_map/ppermute | solution.py:23
  39.9 6.9 %collective-permute-start.5 = (bf16[512,1024]{1,0:T(8,128)(2,1)S(1)}, bf16[512,1024]{1,0:T(8,128)(2,1)S(1)}, u32[]{:S(2)}, u32[]{:S(2)}) collective-permute-start(bf16[512,1024]{1,0:T(8,128)(2,1)S(1)} %fusion.27), channel_id=1, source_target_pairs={{0,8},{8,0},{16,24},{24,16},{1,9},{9,1},{17,25},{25,17},{2,10},{10... | collective-permute-start | bytes 3145736 | tf_op jit(solution)/shard_map/ppermute | solution.py:23
  41.9 14.8 %collective-permute-start.13 = (bf16[256,1024]{1,0:T(8,128)(2,1)S(1)}, bf16[256,1024]{1,0:T(8,128)(2,1)S(1)}, u32[]{:S(2)}, u32[]{:S(2)}) collective-permute-start(bf16[256,1024]{1,0:T(8,128)(2,1)S(1)} %fusion.68), channel_id=1, source_target_pairs={{0,16},{8,24},{16,0},{24,8},{1,17},{9,25},{17,1},{25,9},{2,18},{10... | collective-permute-start | bytes 1572872 | tf_op jit(solution)/shard_map/ppermute | solution.py:23
  43.8 16.0 %collective-permute-start.15 = (bf16[256,1024]{1,0:T(8,128)(2,1)S(1)}, bf16[256,1024]{1,0:T(8,128)(2,1)S(1)}, u32[]{:S(2)}, u32[]{:S(2)}) collective-permute-start(bf16[256,1024]{1,0:T(8,128)(2,1)S(1)} %fusion.69), channel_id=1, source_target_pairs={{0,4},{4,0},{1,5},{5,1},{2,6},{6,2},{3,7},{7,3},{8,12},{12,8},{9,1... | collective-permute-start | bytes 1572872 | tf_op jit(solution)/shard_map/ppermute | solution.py:23
  44.4 4.8 %slice-start = ((s8[8388608]{0:T(1024)(128)(4,1)}), s8[4194304]{0:T(1024)(128)(4,1)S(1)}, s32[]{:S(2)}) async-start(s8[8388608]{0:T(1024)(128)(4,1)} %bitcast.89), calls=%async_computation | async-start | bytes 8388608
  45.2 4.0 %slice-start.1 = ((s8[8388608]{0:T(1024)(128)(4,1)}), s8[4194304]{0:T(1024)(128)(4,1)S(1)}, s32[]{:S(2)}) async-start(s8[8388608]{0:T(1024)(128)(4,1)} %bitcast.89), calls=%async_computation.1 | async-start | bytes 8388608
  45.2 24.7 %collective-permute-start.22 = (bf16[256,1024]{1,0:T(8,128)(2,1)S(1)}, bf16[256,1024]{1,0:T(8,128)(2,1)S(1)}, u32[]{:S(2)}, u32[]{:S(2)}) collective-permute-start(bf16[256,1024]{1,0:T(8,128)(2,1)S(1)} %add_convert_fusion), channel_id=1, source_target_pairs={{0,4},{4,0},{1,5},{5,1},{2,6},{6,2},{3,7},{7,3},{8,12},{12,8},{9,1... | collective-permute-start | bytes 1572872 | tf_op jit(solution)/shard_map/ppermute | solution.py:23
  47.6 1.7 %copy-start = (bf16[1,16,16,1024]{3,2,1,0:T(8,128)(2,1)S(1)}, bf16[1,16,16,1024]{3,2,1,0:T(8,128)(2,1)}, u32[]{:S(2)}) copy-start(bf16[1,16,16,1024]{3,2,1,0:T(8,128)(2,1)} %param.5) | copy-start | bytes 1572868
  47.6 19.6 %collective-permute-start.20 = (bf16[256,1024]{1,0:T(8,128)(2,1)S(1)}, bf16[256,1024]{1,0:T(8,128)(2,1)S(1)}, u32[]{:S(2)}, u32[]{:S(2)}) collective-permute-start(bf16[256,1024]{1,0:T(8,128)(2,1)S(1)} %fusion.56), channel_id=1, source_target_pairs={{0,16},{8,24},{16,0},{24,8},{1,17},{9,25},{17,1},{25,9},{2,18},{10... | collective-permute-start | bytes 1572872 | tf_op jit(solution)/shard_map/ppermute | solution.py:23
  48.3 36.6 %collective-permute-start.10 = (bf16[2,28,8,1024]{3,2,1,0:T(8,128)(2,1)S(1)}, bf16[2,28,8,1024]{3,2,1,0:T(8,128)(2,1)S(1)}, u32[]{:S(2)}, u32[]{:S(2)}) collective-permute-start(bf16[2,28,8,1024]{3,2,1,0:T(8,128)(2,1)S(1)} %get-tuple-element.47), channel_id=1, source_target_pairs={{1,2},{2,1},{5,6},{6,5},{9,10},{10,9},{13,14},{14,13},{17,18},{18,... | collective-permute-start | bytes 2752520 | tf_op jit(solution)/shard_map/ppermute | solution.py:62
  56.7 28.3 %collective-permute-start.11 = (bf16[2,28,8,1024]{3,2,1,0:T(8,128)(2,1)S(1)}, bf16[2,28,8,1024]{3,2,1,0:T(8,128)(2,1)S(1)}, u32[]{:S(2)}, u32[]{:S(2)}) collective-permute-start(bf16[2,28,8,1024]{3,2,1,0:T(8,128)(2,1)S(1)} %get-tuple-element.48), channel_id=1, source_target_pairs={{0,1},{1,0},{2,3},{3,2},{4,5},{5,4},{6,7},{7,6},{8,9},{9,8},{10,11... | collective-permute-start | bytes 2752520 | tf_op jit(solution)/shard_map/ppermute | solution.py:63
  59.8 15.7 %collective-permute-start.14 = (bf16[128,1024]{1,0:T(8,128)(2,1)S(1)}, bf16[128,1024]{1,0:T(8,128)(2,1)S(1)}, u32[]{:S(2)}, u32[]{:S(2)}) collective-permute-start(bf16[128,1024]{1,0:T(8,128)(2,1)S(1)} %dynamic-slice_convert_fusion.3), channel_id=1, source_target_pairs={{0,4},{4,0},{1,5},{5,1},{2,6},{6,2},{3,7},{7,3},{8,12},{12,8},{9,1... | collective-permute-start | bytes 786440 | tf_op jit(solution)/shard_map/ppermute | solution.py:23
  67.2 8.9 %collective-permute-start.16 = (bf16[128,1024]{1,0:T(8,128)(2,1)S(1)}, bf16[128,1024]{1,0:T(8,128)(2,1)S(1)}, u32[]{:S(2)}, u32[]{:S(2)}) collective-permute-start(bf16[128,1024]{1,0:T(8,128)(2,1)S(1)} %dynamic-slice_convert_fusion.2), channel_id=1, source_target_pairs={{0,16},{8,24},{16,0},{24,8},{1,17},{9,25},{17,1},{25,9},{2,18},{10... | collective-permute-start | bytes 786440 | tf_op jit(solution)/shard_map/ppermute | solution.py:23
  69.9 10.2 %collective-permute-start.21 = (bf16[128,1024]{1,0:T(8,128)(2,1)S(1)}, bf16[128,1024]{1,0:T(8,128)(2,1)S(1)}, u32[]{:S(2)}, u32[]{:S(2)}) collective-permute-start(bf16[128,1024]{1,0:T(8,128)(2,1)S(1)} %dynamic-slice_convert_fusion.1), channel_id=1, source_target_pairs={{0,4},{4,0},{1,5},{5,1},{2,6},{6,2},{3,7},{7,3},{8,12},{12,8},{9,1... | collective-permute-start | bytes 786440 | tf_op jit(solution)/shard_map/ppermute | solution.py:23
  75.5 7.4 %collective-permute-start.23 = (bf16[128,1024]{1,0:T(8,128)(2,1)S(1)}, bf16[128,1024]{1,0:T(8,128)(2,1)S(1)}, u32[]{:S(2)}, u32[]{:S(2)}) collective-permute-start(bf16[128,1024]{1,0:T(8,128)(2,1)S(1)} %dynamic-slice_convert_fusion), channel_id=1, source_target_pairs={{0,16},{8,24},{16,0},{24,8},{1,17},{9,25},{17,1},{25,9},{2,18},{10... | collective-permute-start | bytes 786440 | tf_op jit(solution)/shard_map/ppermute | solution.py:23
  76.3 12.8 %collective-permute-start.17 = (bf16[32,2048]{1,0:T(8,128)(2,1)S(1)}, bf16[32,2048]{1,0:T(8,128)(2,1)S(1)}, u32[]{:S(2)}, u32[]{:S(2)}) collective-permute-start(bf16[32,2048]{1,0:T(8,128)(2,1)S(1)} %get-tuple-element.64), channel_id=1, source_target_pairs={{0,3},{1,2},{2,1},{3,0},{4,7},{5,6},{6,5},{7,4},{8,11},{9,10},{10,... | collective-permute-start | bytes 393224 | tf_op jit(solution)/shard_map/ppermute | solution.py:23
  80.2 12.5 %collective-permute-start.18 = (bf16[32,2048]{1,0:T(8,128)(2,1)S(1)}, bf16[32,2048]{1,0:T(8,128)(2,1)S(1)}, u32[]{:S(2)}, u32[]{:S(2)}) collective-permute-start(bf16[32,2048]{1,0:T(8,128)(2,1)S(1)} %get-tuple-element.65), channel_id=1, source_target_pairs={{0,2},{1,3},{2,0},{3,1},{4,6},{5,7},{6,4},{7,5},{8,10},{9,11},{10,... | collective-permute-start | bytes 393224 | tf_op jit(solution)/shard_map/ppermute | solution.py:23
  83.0 9.7 %collective-permute-start.19 = (bf16[32,2048]{1,0:T(8,128)(2,1)S(1)}, bf16[32,2048]{1,0:T(8,128)(2,1)S(1)}, u32[]{:S(2)}, u32[]{:S(2)}) collective-permute-start(bf16[32,2048]{1,0:T(8,128)(2,1)S(1)} %get-tuple-element.66), channel_id=1, source_target_pairs={{0,1},{1,0},{2,3},{3,2},{4,5},{5,4},{6,7},{7,6},{8,9},{9,8},{10,11... | collective-permute-start | bytes 393224 | tf_op jit(solution)/shard_map/ppermute | solution.py:23
  86.2 8.3 %collective-permute-start.12 = (bf16[2,6,16,1024]{3,2,1,0:T(8,128)(2,1)S(1)}, bf16[2,6,16,1024]{3,2,1,0:T(8,128)(2,1)S(1)}, u32[]{:S(2)}, u32[]{:S(2)}) collective-permute-start(bf16[2,6,16,1024]{3,2,1,0:T(8,128)(2,1)S(1)} %slice_select_fusion), channel_id=1, source_target_pairs={{0,4},{4,0},{1,5},{5,1},{2,6},{6,2},{3,7},{7,3},{8,12},{12,8},{9,1... | collective-permute-start | bytes 1179656 | tf_op jit(solution)/shard_map/ppermute | solution.py:23
  86.8 11.7 %collective-permute-start.24 = (bf16[32,2048]{1,0:T(8,128)(2,1)S(1)}, bf16[32,2048]{1,0:T(8,128)(2,1)S(1)}, u32[]{:S(2)}, u32[]{:S(2)}) collective-permute-start(bf16[32,2048]{1,0:T(8,128)(2,1)S(1)} %get-tuple-element.57), channel_id=1, source_target_pairs={{0,3},{1,2},{2,1},{3,0},{4,7},{5,6},{6,5},{7,4},{8,11},{9,10},{10,... | collective-permute-start | bytes 393224 | tf_op jit(solution)/shard_map/ppermute | solution.py:23
  89.1 9.5 %collective-permute-start.26 = (bf16[32,2048]{1,0:T(8,128)(2,1)S(1)}, bf16[32,2048]{1,0:T(8,128)(2,1)S(1)}, u32[]{:S(2)}, u32[]{:S(2)}) collective-permute-start(bf16[32,2048]{1,0:T(8,128)(2,1)S(1)} %get-tuple-element.58), channel_id=1, source_target_pairs={{0,1},{1,0},{2,3},{3,2},{4,5},{5,4},{6,7},{7,6},{8,9},{9,8},{10,11... | collective-permute-start | bytes 393224 | tf_op jit(solution)/shard_map/ppermute | solution.py:23
  92.6 8.7 %collective-permute-start.25 = (bf16[32,2048]{1,0:T(8,128)(2,1)S(1)}, bf16[32,2048]{1,0:T(8,128)(2,1)S(1)}, u32[]{:S(2)}, u32[]{:S(2)}) collective-permute-start(bf16[32,2048]{1,0:T(8,128)(2,1)S(1)} %get-tuple-element.59), channel_id=1, source_target_pairs={{0,2},{1,3},{2,0},{3,1},{4,6},{5,7},{6,4},{7,5},{8,10},{9,11},{10,... | collective-permute-start | bytes 393224 | tf_op jit(solution)/shard_map/ppermute | solution.py:23
  94.5 0.7 copy-start.2
  95.2 2.1 %copy-start.1 = (bf16[1,16,16,1024]{3,2,1,0:T(8,128)(2,1)S(1)}, bf16[1,16,16,1024]{3,2,1,0:T(8,128)(2,1)}, u32[]{:S(2)}) copy-start(bf16[1,16,16,1024]{3,2,1,0:T(8,128)(2,1)} %param.9) | copy-start | bytes 1572868

commit v8 on v7

--- a/solution.py
+++ b/solution.py
@@ -131,7 +131,7 @@
 
 def run_prepare(place, tokens, cotangent, tissue, gain, face):
     count, width = tokens.shape
-    block = min(count, 64)
+    block = min(count, 128)
     part = lambda columns: pl.BlockSpec((block, columns), lambda step: (step, 0))
     return pl.pallas_call(
         prepare,
@@ -302,7 +302,7 @@
             SCALARS,
             columns(tokens, part),
             columns(tokens, part),
-            whole(normed_ext.shape),
+            pl.BlockSpec(normed_ext.shape, lambda group: (0, 0), pipeline_mode=pl.Buffered(1)),
             columns(width, part, groups),
             columns(width, part, 2 * groups),
         ],

time: 103 us -> 101 us (0.981)
  Pallas kernels: 17.8 us -> 16.6 us
    pallas_call x1, Pallas kernels: 2.85 us -> 1.68 us  [run_prepare(): pl.pallas_call(prepare, grid=(count // block,), in_specs=[SCALARS, part(w...]
where the time goes in v8:
time: 101 us
  starting transfers between devices  31.3 us (31%)
  waiting for transfers between devices  27.4 us (27%)
  Pallas kernels  16.6 us (16%)
  matrix products  16.4 us (16%)
  other arithmetic  6.15 us (6%)
  local copies, waits for them, and re-layouts  1.87 us (2%)
  between operations  1.35 us (1%)
    ppermute x21, waiting for transfers between devices, swapped(): return lax.ppermute(array, axis, [(i, i ^ by) for i in range(count)])  27.4 us
    ppermute x21, starting transfers between devices, swapped(): return lax.ppermute(array, axis, [(i, i ^ by) for i in range(count)])  20.1 us
    pallas_call x1, Pallas kernels, run_queries(): pl.pallas_call(functools.partial(query_pass, head_dim, tile), grid=(group...  14.9 us
    ppermute x3, starting transfers between devices, exchange_columns(): two = lax.ppermute(out_two, 'gx', second)  8.99 us
    dot_general x14, matrix products, product_t(): lax.dot_general(left, right, (((0,), (0,)), ((), ())), preferred_element_...  8.17 us
    dot_general x2, matrix products, times_t(): lax.dot_general(left, right, (((1,), (1,)), ((), ())), preferred_element_...  4.38 us
    dot_general x2, matrix products, times(): return jnp.dot(left, right, preferred_element_type=F32)  3.83 us
    ppermute x3, starting transfers between devices, exchange_columns(): one = lax.ppermute(out_one, 'gx', first)  2.22 us
  transfers between devices with their start and end apart: 27, of which 9 were waited for; matrix products, arithmetic and copies ran while one was open for 22% of the time, Pallas kernels for 15%

profile of v8, /device:TPU:0, one launch (start us, length us, event | category | flops | bytes accessed | tf_op | source)
XLA Modules:
  0.0 101.1 jit_solution(1374504892047465315)
XLA Ops:
  0.6 0.7 convert_element_type.160
  1.5 1.7 %prepare.1 = (bf16[256,1024]{1,0:T(8,128)(2,1)S(1)}, bf16[256,1024]{1,0:T(8,128)(2,1)S(1)}, bf16[96,1024]{1,0:T(8,128)(2,1)S(1)}, f32[256,128]{1,0:T(8,128)S(1)}) custom-call(s32[5]{0:T(128)S(1)} %stack.15.place_ref, bf16[256,1024]{1,0:T(8,128)(2,1)} %bitcast.91, bf16[256,1024]{1,0:T(8,128)(2,1)} %bitcast.93, f32[256,1]{1,0:T(8,128)S(1)} %convert_element_type.207.t_ref, ...), custom_call_target="tpu_custom_call" | custom-call | bytes 3145728 | tf_op jit(solution)/shard_map/prepare/pallas_call | solution.py:136
  3.2 3.0 %collective-permute-start = (bf16[6,16,1024]{2,1,0:T(8,128)(2,1)S(1)}, bf16[6,16,1024]{2,1,0:T(8,128)(2,1)S(1)}, u32[]{:S(2)}, u32[]{:S(2)}) collective-permute-start(bf16[6,16,1024]{2,1,0:T(8,128)(2,1)S(1)} %bitcast.88), channel_id=1, source_target_pairs={{0,4},{4,0},{1,5},{5,1},{2,6},{6,2},{3,7},{7,3},{8,12},{12,8},{9,1... | collective-permute-start | bytes 589832 | tf_op jit(solution)/shard_map/ppermute | solution.py:23
  6.3 1.6 %collective-permute-start.3 = (bf16[16,8,1024]{2,1,0:T(8,128)(2,1)S(1)}, bf16[16,8,1024]{2,1,0:T(8,128)(2,1)S(1)}, u32[]{:S(2)}, u32[]{:S(2)}) collective-permute-start(bf16[16,8,1024]{2,1,0:T(8,128)(2,1)S(1)} %get-tuple-element.82), channel_id=1, source_target_pairs={{0,1},{1,0},{2,3},{3,2},{4,5},{5,4},{6,7},{7,6},{8,9},{9,8},{10,11... | collective-permute-start | bytes 786440 | tf_op jit(solution)/shard_map/ppermute | solution.py:63
  7.9 0.7 collective-permute-start.4
  8.6 2.3 %fusion.59.g_ref = bf16[256,1024]{1,0:T(8,128)(2,1)S(1)} fusion(bf16[256,1024]{1,0:T(8,128)(2,1)S(1)} %get-tuple-element.33, bf16[1024,4096]{1,0:T(8,128)(2,1)} %value_w_ref.1), kind=kOutput, calls=%fused_computation.57 | convolution fusion | flops 537133056 | bytes 3145728 | tf_op jit(solution)/shard_map/dot_general | solution.py:174
  11.2 0.2 slice_reduce_fusion.1
  11.4 4.4 %collective-permute-start.1 = (bf16[6,8,1024]{2,1,0:T(8,128)(2,1)S(1)}, bf16[6,8,1024]{2,1,0:T(8,128)(2,1)S(1)}, u32[]{:S(2)}, u32[]{:S(2)}) collective-permute-start(bf16[6,8,1024]{2,1,0:T(8,128)(2,1)S(1)} %get-tuple-element.92), channel_id=1, source_target_pairs={{0,1},{1,0},{2,3},{3,2},{4,5},{5,4},{6,7},{7,6},{8,9},{9,8},{10,11... | collective-permute-start | bytes 294920 | tf_op jit(solution)/shard_map/ppermute | solution.py:63
  15.9 0.7 collective-permute-start.2
  16.5 2.3 %fusion.62.q_ref = bf16[256,1024]{1,0:T(8,128)(2,1)S(1)} fusion(bf16[256,1024]{1,0:T(8,128)(2,1)S(1)} %get-tuple-element.31, bf16[1024,4096]{1,0:T(8,128)(2,1)} %value_w_ref.1), kind=kOutput, calls=%fused_computation.58 | convolution fusion | flops 537133056 | bytes 3145728 | tf_op jit(solution)/shard_map/dot_general | solution.py:170
  18.9 0.5 collective-permute-start.9
  19.5 0.2 broadcast_select_fusion.7
  19.7 0.2 pad_maximum_fusion
  20.1 14.9 %query_pass.1 = (bf16[2,256,1024]{2,1,0:T(8,128)(2,1)S(1)}, bf16[2,896,1024]{2,1,0:T(8,128)(2,1)S(1)}) custom-call(s32[5]{0:T(128)S(1)} %stack.15.place_ref, bf16[256,1024]{1,0:T(8,128)(2,1)S(1)} %fusion.62.q_ref, bf16[256,1024]{1,0:T(8,128)(2,1)S(1)} %fusion.59.g_ref, bf16[896,1024]{1,0:T(8,128)(2,1)S(1)} %bitcast.80, bf16[1024,4096]{1,0:T(8,128)(2,1)} %value_w_ref.1, ...), custom_call_target="tpu_custom_call" | custom-call | flops 4294967296 | bytes 4194304 | tf_op jit(solution)/shard_map/query_pass/pallas_call | solution.py:298
  35.0 1.3 %fusion.27 = bf16[512,1024]{1,0:T(8,128)(2,1)S(1)} fusion(bf16[2,896,1024]{2,1,0:T(8,128)(2,1)S(1)} %get-tuple-element.34, bf16[896,256]{1,0:T(8,128)(2,1)S(1)} %get-tuple-element.56, bf16[896,256]{1,0:T(8,128)(2,1)S(1)} %get-tuple-element.55), kind=kOutput, calls=%fused_computation.38 | convolution fusion | flops 941883392 | bytes 3801088 | tf_op jit(solution)/shard_map/dot_general | solution.py:328
  36.3 1.3 %fusion.30 = bf16[512,1024]{1,0:T(8,128)(2,1)S(1)} fusion(bf16[2,896,1024]{2,1,0:T(8,128)(2,1)S(1)} %get-tuple-element.34, bf16[896,256]{1,0:T(8,128)(2,1)S(1)} %get-tuple-element.56, bf16[896,256]{1,0:T(8,128)(2,1)S(1)} %get-tuple-element.55), kind=kOutput, calls=%fused_computation.39 | convolution fusion | flops 941883392 | bytes 3801088 | tf_op jit(solution)/shard_map/dot_general | solution.py:328
  37.6 0.2 collective-permute-start.8
  37.9 0.3 fusion.126
  38.2 0.5 collective-permute-start.6
  38.9 0.3 fusion.123
  39.2 0.3 fusion.115
  39.5 0.3 fusion.108
  39.9 0.2 constant_dynamic-slice_fusion.4
  40.1 0.2 collective-permute-done.8
  40.3 0.3 fusion.68
  40.7 1.6 %collective-permute-start.13 = (bf16[256,1024]{1,0:T(8,128)(2,1)S(1)}, bf16[256,1024]{1,0:T(8,128)(2,1)S(1)}, u32[]{:S(2)}, u32[]{:S(2)}) collective-permute-start(bf16[256,1024]{1,0:T(8,128)(2,1)S(1)} %fusion.68), channel_id=1, source_target_pairs={{0,16},{8,24},{16,0},{24,8},{1,17},{9,25},{17,1},{25,9},{2,18},{10... | collective-permute-start | bytes 1572872 | tf_op jit(solution)/shard_map/ppermute | solution.py:23
  42.3 0.3 fusion.69
  42.7 0.6 collective-permute-start.15
  43.3 0.7 add_convert_fusion
  44.1 1.6 %collective-permute-start.22 = (bf16[256,1024]{1,0:T(8,128)(2,1)S(1)}, bf16[256,1024]{1,0:T(8,128)(2,1)S(1)}, u32[]{:S(2)}, u32[]{:S(2)}) collective-permute-start(bf16[256,1024]{1,0:T(8,128)(2,1)S(1)} %add_convert_fusion), channel_id=1, source_target_pairs={{0,4},{4,0},{1,5},{5,1},{2,6},{6,2},{3,7},{7,3},{8,12},{12,8},{9,1... | collective-permute-start | bytes 1572872 | tf_op jit(solution)/shard_map/ppermute | solution.py:23
  45.6 0.8 fusion.56
  46.4 0.6 collective-permute-start.20
  47.2 0.9 collective-permute-start.10
  48.1 1.5 %fusion.65 = bf16[256,1024]{1,0:T(8,128)(2,1)} fusion(bf16[256,1024]{1,0:T(8,128)(2,1)S(1)} %get-tuple-element.29, bf16[1024,4096]{1,0:T(8,128)(2,1)S(1)} %bitcast.90, bf16[256,1024]{1,0:T(8,128)(2,1)S(1)} %bitcast.92, f32[256]{0:T(256)S(1)} %convert_element_type.161), kind=kOutput, calls=%fused_computation.59 | convolution fusion | flops 537919488 | bytes 3671040 | tf_op jit(solution)/shard_map/dot_general | solution.py:170
  49.6 0.7 convert_add_fusion.3
  50.4 0.8 fusion.42
  51.2 0.3 convolution_add_fusion.1
  51.5 0.3 convolution_add_fusion
  51.8 3.7 %collective-permute-done.13 = bf16[256,1024]{1,0:T(8,128)(2,1)S(1)} collective-permute-done((bf16[256,1024]{1,0:T(8,128)(2,1)S(1)}, bf16[256,1024]{1,0:T(8,128)(2,1)S(1)}, u32[]{:S(2)}, u32[]{:S(2)}) %collective-permute-start.13) | collective-permute-done | bytes 524320 | tf_op jit(solution)/shard_map/ppermute | solution.py:23
  55.5 2.9 %collective-permute-start.11 = (bf16[2,28,8,1024]{3,2,1,0:T(8,128)(2,1)S(1)}, bf16[2,28,8,1024]{3,2,1,0:T(8,128)(2,1)S(1)}, u32[]{:S(2)}, u32[]{:S(2)}) collective-permute-start(bf16[2,28,8,1024]{3,2,1,0:T(8,128)(2,1)S(1)} %get-tuple-element.48), channel_id=1, source_target_pairs={{0,1},{1,0},{2,3},{3,2},{4,5},{5,4},{6,7},{7,6},{8,9},{9,8},{10,11... | collective-permute-start | bytes 2752520 | tf_op jit(solution)/shard_map/ppermute | solution.py:63
  58.4 0.2 convert_add_fusion.5
  58.7 0.6 collective-permute-start.14
  59.4 6.7 %collective-permute-done.20 = bf16[256,1024]{1,0:T(8,128)(2,1)S(1)} collective-permute-done((bf16[256,1024]{1,0:T(8,128)(2,1)S(1)}, bf16[256,1024]{1,0:T(8,128)(2,1)S(1)}, u32[]{:S(2)}, u32[]{:S(2)}) %collective-permute-start.20) | collective-permute-done | bytes 524320 | tf_op jit(solution)/shard_map/ppermute | solution.py:23
  66.1 1.5 %collective-permute-start.16 = (bf16[128,1024]{1,0:T(8,128)(2,1)S(1)}, bf16[128,1024]{1,0:T(8,128)(2,1)S(1)}, u32[]{:S(2)}, u32[]{:S(2)}) collective-permute-start(bf16[128,1024]{1,0:T(8,128)(2,1)S(1)} %dynamic-slice_convert_fusion.2), channel_id=1, source_target_pairs={{0,16},{8,24},{16,0},{24,8},{1,17},{9,25},{17,1},{25,9},{2,18},{10... | collective-permute-start | bytes 786440 | tf_op jit(solution)/shard_map/ppermute | solution.py:23
  67.6 0.2 convert_add_fusion.2
  67.8 1.0 collective-permute-done.22
  68.8 0.5 collective-permute-start.21
  69.5 4.9 %collective-permute-done.14 = bf16[128,1024]{1,0:T(8,128)(2,1)S(1)} collective-permute-done((bf16[128,1024]{1,0:T(8,128)(2,1)S(1)}, bf16[128,1024]{1,0:T(8,128)(2,1)S(1)}, u32[]{:S(2)}, u32[]{:S(2)}) %collective-permute-start.14) | collective-permute-done | bytes 262176 | tf_op jit(solution)/shard_map/ppermute | solution.py:23
  74.4 0.5 collective-permute-start.23
  75.1 1.0 collective-permute-start.17
  76.1 2.9 %collective-permute-done.21 = bf16[128,1024]{1,0:T(8,128)(2,1)S(1)} collective-permute-done((bf16[128,1024]{1,0:T(8,128)(2,1)S(1)}, bf16[128,1024]{1,0:T(8,128)(2,1)S(1)}, u32[]{:S(2)}, u32[]{:S(2)}) %collective-permute-start.21) | collective-permute-done | bytes 262176 | tf_op jit(solution)/shard_map/ppermute | solution.py:23
  79.0 2.7 %collective-permute-start.18 = (bf16[32,2048]{1,0:T(8,128)(2,1)S(1)}, bf16[32,2048]{1,0:T(8,128)(2,1)S(1)}, u32[]{:S(2)}, u32[]{:S(2)}) collective-permute-start(bf16[32,2048]{1,0:T(8,128)(2,1)S(1)} %get-tuple-element.65), channel_id=1, source_target_pairs={{0,2},{1,3},{2,0},{3,1},{4,6},{5,7},{6,4},{7,5},{8,10},{9,11},{10,... | collective-permute-start | bytes 393224 | tf_op jit(solution)/shard_map/ppermute | solution.py:23
  81.8 1.8 %collective-permute-start.19 = (bf16[32,2048]{1,0:T(8,128)(2,1)S(1)}, bf16[32,2048]{1,0:T(8,128)(2,1)S(1)}, u32[]{:S(2)}, u32[]{:S(2)}) collective-permute-start(bf16[32,2048]{1,0:T(8,128)(2,1)S(1)} %get-tuple-element.66), channel_id=1, source_target_pairs={{0,1},{1,0},{2,3},{3,2},{4,5},{5,4},{6,7},{7,6},{8,9},{9,8},{10,11... | collective-permute-start | bytes 393224 | tf_op jit(solution)/shard_map/ppermute | solution.py:23
  84.0 1.0 fusion.143
  85.0 0.6 collective-permute-start.12
  85.6 2.3 %collective-permute-start.24 = (bf16[32,2048]{1,0:T(8,128)(2,1)S(1)}, bf16[32,2048]{1,0:T(8,128)(2,1)S(1)}, u32[]{:S(2)}, u32[]{:S(2)}) collective-permute-start(bf16[32,2048]{1,0:T(8,128)(2,1)S(1)} %get-tuple-element.57), channel_id=1, source_target_pairs={{0,3},{1,2},{2,1},{3,0},{4,7},{5,6},{6,5},{7,4},{8,11},{9,10},{10,... | collective-permute-start | bytes 393224 | tf_op jit(solution)/shard_map/ppermute | solution.py:23
  87.9 3.5 %collective-permute-done.18 = bf16[32,2048]{1,0:T(8,128)(2,1)S(1)} collective-permute-done((bf16[32,2048]{1,0:T(8,128)(2,1)S(1)}, bf16[32,2048]{1,0:T(8,128)(2,1)S(1)}, u32[]{:S(2)}, u32[]{:S(2)}) %collective-permute-start.18) | collective-permute-done | bytes 131104 | tf_op jit(solution)/shard_map/ppermute | solution.py:23
  91.6 1.7 %collective-permute-done.12 = bf16[2,6,16,1024]{3,2,1,0:T(8,128)(2,1)S(1)} collective-permute-done((bf16[2,6,16,1024]{3,2,1,0:T(8,128)(2,1)S(1)}, bf16[2,6,16,1024]{3,2,1,0:T(8,128)(2,1)S(1)}, u32[]{:S(2)}, u32[]{:S(2)}) %collective-permute-start.12) | collective-permute-done | bytes 393248 | tf_op jit(solution)/shard_map/ppermute | solution.py:23
  93.4 0.3 fusion.3
  93.8 0.2 copy-done.2
  94.1 2.0 %fusion.144 = (f32[256]{0:T(256)S(1)}, f32[256]{0:T(256)S(1)}, f32[256,1024]{1,0:T(8,128)S(1)}) fusion(f32[256]{0:T(256)S(1)} %get-tuple-element.43, f32[256]{0:T(256)S(1)} %get-tuple-element.44, bf16[1,16,16,1024]{3,2,1,0:T(8,128)(2,1)S(1)} %copy-done, f32[1024]{0:T(1024)S(1)} %copy-done.2, bf16[1024,4096]{1,0:T(8,128)(2,1)S(1)} %bitcast.90, ...), kind=kOutput, calls=%fused_computation.192 | convolution fusion | flops 1617165824 | bytes 9445376 | tf_op jit(solution)/shard_map/dot_general | solution.py:174
  96.1 1.2 %fusion.77 = bf16[256,1024]{1,0:T(8,128)(2,1)} fusion(f32[256,1024]{1,0:T(8,128)S(1)} %get-tuple-element.94, f32[256]{0:T(256)S(1)} %get-tuple-element.95, f32[256]{0:T(256)S(1)} %get-tuple-element.44, f32[256]{0:T(256)S(1)} %get-tuple-element.96, f32[256]{0:T(256)S(1)} %get-tuple-element.43, bf16[1,16,16,1024]{3,2,1,0:T(8,128)(2,1)S(1)} %copy-done.1, ...), kind=kLoop, calls=%fused_computation.69 | loop fusion | flops 2621440 | bytes 2625536 | tf_op jit(solution)/shard_map/convert_element_type | solution.py:555
  97.4 2.8 %collective-permute-done.25 = bf16[32,2048]{1,0:T(8,128)(2,1)S(1)} collective-permute-done((bf16[32,2048]{1,0:T(8,128)(2,1)S(1)}, bf16[32,2048]{1,0:T(8,128)(2,1)S(1)}, u32[]{:S(2)}, u32[]{:S(2)}) %collective-permute-start.25) | collective-permute-done | bytes 131104 | tf_op jit(solution)/shard_map/ppermute | solution.py:23
  100.3 0.8 maximum_multiply_fusion
  (68 shorter events, 2.7 us)
Async XLA Ops:
  3.2 8.2 %collective-permute-start = (bf16[6,16,1024]{2,1,0:T(8,128)(2,1)S(1)}, bf16[6,16,1024]{2,1,0:T(8,128)(2,1)S(1)}, u32[]{:S(2)}, u32[]{:S(2)}) collective-permute-start(bf16[6,16,1024]{2,1,0:T(8,128)(2,1)S(1)} %bitcast.88), channel_id=1, source_target_pairs={{0,4},{4,0},{1,5},{5,1},{2,6},{6,2},{3,7},{7,3},{8,12},{12,8},{9,1... | collective-permute-start | bytes 589832 | tf_op jit(solution)/shard_map/ppermute | solution.py:23
  6.3 12.6 %collective-permute-start.3 = (bf16[16,8,1024]{2,1,0:T(8,128)(2,1)S(1)}, bf16[16,8,1024]{2,1,0:T(8,128)(2,1)S(1)}, u32[]{:S(2)}, u32[]{:S(2)}) collective-permute-start(bf16[16,8,1024]{2,1,0:T(8,128)(2,1)S(1)} %get-tuple-element.82), channel_id=1, source_target_pairs={{0,1},{1,0},{2,3},{3,2},{4,5},{5,4},{6,7},{7,6},{8,9},{9,8},{10,11... | collective-permute-start | bytes 786440 | tf_op jit(solution)/shard_map/ppermute | solution.py:63
  7.9 11.5 %collective-permute-start.4 = (bf16[16,8,1024]{2,1,0:T(8,128)(2,1)S(1)}, bf16[16,8,1024]{2,1,0:T(8,128)(2,1)S(1)}, u32[]{:S(2)}, u32[]{:S(2)}) collective-permute-start(bf16[16,8,1024]{2,1,0:T(8,128)(2,1)S(1)} %get-tuple-element.83), channel_id=1, source_target_pairs={{1,2},{2,1},{5,6},{6,5},{9,10},{10,9},{13,14},{14,13},{17,18},{18,... | collective-permute-start | bytes 786440 | tf_op jit(solution)/shard_map/ppermute | solution.py:62
  11.4 8.0 %collective-permute-start.1 = (bf16[6,8,1024]{2,1,0:T(8,128)(2,1)S(1)}, bf16[6,8,1024]{2,1,0:T(8,128)(2,1)S(1)}, u32[]{:S(2)}, u32[]{:S(2)}) collective-permute-start(bf16[6,8,1024]{2,1,0:T(8,128)(2,1)S(1)} %get-tuple-element.92), channel_id=1, source_target_pairs={{0,1},{1,0},{2,3},{3,2},{4,5},{5,4},{6,7},{7,6},{8,9},{9,8},{10,11... | collective-permute-start | bytes 294920 | tf_op jit(solution)/shard_map/ppermute | solution.py:63
  15.9 3.6 %collective-permute-start.2 = (bf16[6,8,1024]{2,1,0:T(8,128)(2,1)S(1)}, bf16[6,8,1024]{2,1,0:T(8,128)(2,1)S(1)}, u32[]{:S(2)}, u32[]{:S(2)}) collective-permute-start(bf16[6,8,1024]{2,1,0:T(8,128)(2,1)S(1)} %get-tuple-element.93), channel_id=1, source_target_pairs={{1,2},{2,1},{5,6},{6,5},{9,10},{10,9},{13,14},{14,13},{17,18},{18,... | collective-permute-start | bytes 294920 | tf_op jit(solution)/shard_map/ppermute | solution.py:62
  18.8 21.5 %collective-permute-start.7 = (bf16[256,1024]{1,0:T(8,128)(2,1)S(1)}, bf16[256,1024]{1,0:T(8,128)(2,1)S(1)}, u32[]{:S(2)}, u32[]{:S(2)}) collective-permute-start(bf16[256,1024]{1,0:T(8,128)(2,1)S(1)} %get-tuple-element.31), channel_id=1, source_target_pairs={{0,8},{8,0},{16,24},{24,16},{1,9},{9,1},{17,25},{25,17},{2,10},{10... | collective-permute-start | bytes 1572872 | tf_op jit(solution)/shard_map/ppermute | solution.py:23
  18.9 23.4 %collective-permute-start.9 = (bf16[256,1024]{1,0:T(8,128)(2,1)S(1)}, bf16[256,1024]{1,0:T(8,128)(2,1)S(1)}, u32[]{:S(2)}, u32[]{:S(2)}) collective-permute-start(bf16[256,1024]{1,0:T(8,128)(2,1)S(1)} %get-tuple-element.33), channel_id=1, source_target_pairs={{0,8},{8,0},{16,24},{24,16},{1,9},{9,1},{17,25},{25,17},{2,10},{10... | collective-permute-start | bytes 1572872 | tf_op jit(solution)/shard_map/ppermute | solution.py:23
  37.6 2.7 %collective-permute-start.8 = (bf16[2,256,1024]{2,1,0:T(8,128)(2,1)S(1)}, bf16[2,256,1024]{2,1,0:T(8,128)(2,1)S(1)}, u32[]{:S(2)}, u32[]{:S(2)}) collective-permute-start(bf16[2,256,1024]{2,1,0:T(8,128)(2,1)S(1)} %get-tuple-element.27), channel_id=1, source_target_pairs={{0,8},{8,0},{16,24},{24,16},{1,9},{9,1},{17,25},{25,17},{2,10},{10... | collective-permute-start | bytes 3145736 | tf_op jit(solution)/shard_map/ppermute | solution.py:23
  38.2 5.0 %collective-permute-start.6 = (bf16[512,1024]{1,0:T(8,128)(2,1)S(1)}, bf16[512,1024]{1,0:T(8,128)(2,1)S(1)}, u32[]{:S(2)}, u32[]{:S(2)}) collective-permute-start(bf16[512,1024]{1,0:T(8,128)(2,1)S(1)} %fusion.30), channel_id=1, source_target_pairs={{0,8},{8,0},{16,24},{24,16},{1,9},{9,1},{17,25},{25,17},{2,10},{10... | collective-permute-start | bytes 3145736 | tf_op jit(solution)/shard_map/ppermute | solution.py:23
  38.7 6.9 %collective-permute-start.5 = (bf16[512,1024]{1,0:T(8,128)(2,1)S(1)}, bf16[512,1024]{1,0:T(8,128)(2,1)S(1)}, u32[]{:S(2)}, u32[]{:S(2)}) collective-permute-start(bf16[512,1024]{1,0:T(8,128)(2,1)S(1)} %fusion.27), channel_id=1, source_target_pairs={{0,8},{8,0},{16,24},{24,16},{1,9},{9,1},{17,25},{25,17},{2,10},{10... | collective-permute-start | bytes 3145736 | tf_op jit(solution)/shard_map/ppermute | solution.py:23
  40.7 14.8 %collective-permute-start.13 = (bf16[256,1024]{1,0:T(8,128)(2,1)S(1)}, bf16[256,1024]{1,0:T(8,128)(2,1)S(1)}, u32[]{:S(2)}, u32[]{:S(2)}) collective-permute-start(bf16[256,1024]{1,0:T(8,128)(2,1)S(1)} %fusion.68), channel_id=1, source_target_pairs={{0,16},{8,24},{16,0},{24,8},{1,17},{9,25},{17,1},{25,9},{2,18},{10... | collective-permute-start | bytes 1572872 | tf_op jit(solution)/shard_map/ppermute | solution.py:23
  42.7 16.0 %collective-permute-start.15 = (bf16[256,1024]{1,0:T(8,128)(2,1)S(1)}, bf16[256,1024]{1,0:T(8,128)(2,1)S(1)}, u32[]{:S(2)}, u32[]{:S(2)}) collective-permute-start(bf16[256,1024]{1,0:T(8,128)(2,1)S(1)} %fusion.69), channel_id=1, source_target_pairs={{0,4},{4,0},{1,5},{5,1},{2,6},{6,2},{3,7},{7,3},{8,12},{12,8},{9,1... | collective-permute-start | bytes 1572872 | tf_op jit(solution)/shard_map/ppermute | solution.py:23
  43.2 4.8 %slice-start = ((s8[8388608]{0:T(1024)(128)(4,1)}), s8[4194304]{0:T(1024)(128)(4,1)S(1)}, s32[]{:S(2)}) async-start(s8[8388608]{0:T(1024)(128)(4,1)} %bitcast.89), calls=%async_computation | async-start | bytes 8388608
  44.0 4.0 %slice-start.1 = ((s8[8388608]{0:T(1024)(128)(4,1)}), s8[4194304]{0:T(1024)(128)(4,1)S(1)}, s32[]{:S(2)}) async-start(s8[8388608]{0:T(1024)(128)(4,1)} %bitcast.89), calls=%async_computation.1 | async-start | bytes 8388608
  44.1 24.7 %collective-permute-start.22 = (bf16[256,1024]{1,0:T(8,128)(2,1)S(1)}, bf16[256,1024]{1,0:T(8,128)(2,1)S(1)}, u32[]{:S(2)}, u32[]{:S(2)}) collective-permute-start(bf16[256,1024]{1,0:T(8,128)(2,1)S(1)} %add_convert_fusion), channel_id=1, source_target_pairs={{0,4},{4,0},{1,5},{5,1},{2,6},{6,2},{3,7},{7,3},{8,12},{12,8},{9,1... | collective-permute-start | bytes 1572872 | tf_op jit(solution)/shard_map/ppermute | solution.py:23
  46.4 1.7 %copy-start = (bf16[1,16,16,1024]{3,2,1,0:T(8,128)(2,1)S(1)}, bf16[1,16,16,1024]{3,2,1,0:T(8,128)(2,1)}, u32[]{:S(2)}) copy-start(bf16[1,16,16,1024]{3,2,1,0:T(8,128)(2,1)} %param.5) | copy-start | bytes 1572868
  46.4 19.6 %collective-permute-start.20 = (bf16[256,1024]{1,0:T(8,128)(2,1)S(1)}, bf16[256,1024]{1,0:T(8,128)(2,1)S(1)}, u32[]{:S(2)}, u32[]{:S(2)}) collective-permute-start(bf16[256,1024]{1,0:T(8,128)(2,1)S(1)} %fusion.56), channel_id=1, source_target_pairs={{0,16},{8,24},{16,0},{24,8},{1,17},{9,25},{17,1},{25,9},{2,18},{10... | collective-permute-start | bytes 1572872 | tf_op jit(solution)/shard_map/ppermute | solution.py:23
  47.2 36.6 %collective-permute-start.10 = (bf16[2,28,8,1024]{3,2,1,0:T(8,128)(2,1)S(1)}, bf16[2,28,8,1024]{3,2,1,0:T(8,128)(2,1)S(1)}, u32[]{:S(2)}, u32[]{:S(2)}) collective-permute-start(bf16[2,28,8,1024]{3,2,1,0:T(8,128)(2,1)S(1)} %get-tuple-element.47), channel_id=1, source_target_pairs={{1,2},{2,1},{5,6},{6,5},{9,10},{10,9},{13,14},{14,13},{17,18},{18,... | collective-permute-start | bytes 2752520 | tf_op jit(solution)/shard_map/ppermute | solution.py:62
  55.5 28.3 %collective-permute-start.11 = (bf16[2,28,8,1024]{3,2,1,0:T(8,128)(2,1)S(1)}, bf16[2,28,8,1024]{3,2,1,0:T(8,128)(2,1)S(1)}, u32[]{:S(2)}, u32[]{:S(2)}) collective-permute-start(bf16[2,28,8,1024]{3,2,1,0:T(8,128)(2,1)S(1)} %get-tuple-element.48), channel_id=1, source_target_pairs={{0,1},{1,0},{2,3},{3,2},{4,5},{5,4},{6,7},{7,6},{8,9},{9,8},{10,11... | collective-permute-start | bytes 2752520 | tf_op jit(solution)/shard_map/ppermute | solution.py:63
  58.7 15.7 %collective-permute-start.14 = (bf16[128,1024]{1,0:T(8,128)(2,1)S(1)}, bf16[128,1024]{1,0:T(8,128)(2,1)S(1)}, u32[]{:S(2)}, u32[]{:S(2)}) collective-permute-start(bf16[128,1024]{1,0:T(8,128)(2,1)S(1)} %dynamic-slice_convert_fusion.3), channel_id=1, source_target_pairs={{0,4},{4,0},{1,5},{5,1},{2,6},{6,2},{3,7},{7,3},{8,12},{12,8},{9,1... | collective-permute-start | bytes 786440 | tf_op jit(solution)/shard_map/ppermute | solution.py:23
  66.1 8.9 %collective-permute-start.16 = (bf16[128,1024]{1,0:T(8,128)(2,1)S(1)}, bf16[128,1024]{1,0:T(8,128)(2,1)S(1)}, u32[]{:S(2)}, u32[]{:S(2)}) collective-permute-start(bf16[128,1024]{1,0:T(8,128)(2,1)S(1)} %dynamic-slice_convert_fusion.2), channel_id=1, source_target_pairs={{0,16},{8,24},{16,0},{24,8},{1,17},{9,25},{17,1},{25,9},{2,18},{10... | collective-permute-start | bytes 786440 | tf_op jit(solution)/shard_map/ppermute | solution.py:23
  68.8 10.2 %collective-permute-start.21 = (bf16[128,1024]{1,0:T(8,128)(2,1)S(1)}, bf16[128,1024]{1,0:T(8,128)(2,1)S(1)}, u32[]{:S(2)}, u32[]{:S(2)}) collective-permute-start(bf16[128,1024]{1,0:T(8,128)(2,1)S(1)} %dynamic-slice_convert_fusion.1), channel_id=1, source_target_pairs={{0,4},{4,0},{1,5},{5,1},{2,6},{6,2},{3,7},{7,3},{8,12},{12,8},{9,1... | collective-permute-start | bytes 786440 | tf_op jit(solution)/shard_map/ppermute | solution.py:23
  74.4 7.4 %collective-permute-start.23 = (bf16[128,1024]{1,0:T(8,128)(2,1)S(1)}, bf16[128,1024]{1,0:T(8,128)(2,1)S(1)}, u32[]{:S(2)}, u32[]{:S(2)}) collective-permute-start(bf16[128,1024]{1,0:T(8,128)(2,1)S(1)} %dynamic-slice_convert_fusion), channel_id=1, source_target_pairs={{0,16},{8,24},{16,0},{24,8},{1,17},{9,25},{17,1},{25,9},{2,18},{10... | collective-permute-start | bytes 786440 | tf_op jit(solution)/shard_map/ppermute | solution.py:23
  75.1 12.8 %collective-permute-start.17 = (bf16[32,2048]{1,0:T(8,128)(2,1)S(1)}, bf16[32,2048]{1,0:T(8,128)(2,1)S(1)}, u32[]{:S(2)}, u32[]{:S(2)}) collective-permute-start(bf16[32,2048]{1,0:T(8,128)(2,1)S(1)} %get-tuple-element.64), channel_id=1, source_target_pairs={{0,3},{1,2},{2,1},{3,0},{4,7},{5,6},{6,5},{7,4},{8,11},{9,10},{10,... | collective-permute-start | bytes 393224 | tf_op jit(solution)/shard_map/ppermute | solution.py:23
  79.0 12.5 %collective-permute-start.18 = (bf16[32,2048]{1,0:T(8,128)(2,1)S(1)}, bf16[32,2048]{1,0:T(8,128)(2,1)S(1)}, u32[]{:S(2)}, u32[]{:S(2)}) collective-permute-start(bf16[32,2048]{1,0:T(8,128)(2,1)S(1)} %get-tuple-element.65), channel_id=1, source_target_pairs={{0,2},{1,3},{2,0},{3,1},{4,6},{5,7},{6,4},{7,5},{8,10},{9,11},{10,... | collective-permute-start | bytes 393224 | tf_op jit(solution)/shard_map/ppermute | solution.py:23
  81.8 9.6 %collective-permute-start.19 = (bf16[32,2048]{1,0:T(8,128)(2,1)S(1)}, bf16[32,2048]{1,0:T(8,128)(2,1)S(1)}, u32[]{:S(2)}, u32[]{:S(2)}) collective-permute-start(bf16[32,2048]{1,0:T(8,128)(2,1)S(1)} %get-tuple-element.66), channel_id=1, source_target_pairs={{0,1},{1,0},{2,3},{3,2},{4,5},{5,4},{6,7},{7,6},{8,9},{9,8},{10,11... | collective-permute-start | bytes 393224 | tf_op jit(solution)/shard_map/ppermute | solution.py:23
  85.0 8.3 %collective-permute-start.12 = (bf16[2,6,16,1024]{3,2,1,0:T(8,128)(2,1)S(1)}, bf16[2,6,16,1024]{3,2,1,0:T(8,128)(2,1)S(1)}, u32[]{:S(2)}, u32[]{:S(2)}) collective-permute-start(bf16[2,6,16,1024]{3,2,1,0:T(8,128)(2,1)S(1)} %slice_select_fusion), channel_id=1, source_target_pairs={{0,4},{4,0},{1,5},{5,1},{2,6},{6,2},{3,7},{7,3},{8,12},{12,8},{9,1... | collective-permute-start | bytes 1179656 | tf_op jit(solution)/shard_map/ppermute | solution.py:23
  85.6 11.8 %collective-permute-start.24 = (bf16[32,2048]{1,0:T(8,128)(2,1)S(1)}, bf16[32,2048]{1,0:T(8,128)(2,1)S(1)}, u32[]{:S(2)}, u32[]{:S(2)}) collective-permute-start(bf16[32,2048]{1,0:T(8,128)(2,1)S(1)} %get-tuple-element.57), channel_id=1, source_target_pairs={{0,3},{1,2},{2,1},{3,0},{4,7},{5,6},{6,5},{7,4},{8,11},{9,10},{10,... | collective-permute-start | bytes 393224 | tf_op jit(solution)/shard_map/ppermute | solution.py:23
  87.9 9.5 %collective-permute-start.26 = (bf16[32,2048]{1,0:T(8,128)(2,1)S(1)}, bf16[32,2048]{1,0:T(8,128)(2,1)S(1)}, u32[]{:S(2)}, u32[]{:S(2)}) collective-permute-start(bf16[32,2048]{1,0:T(8,128)(2,1)S(1)} %get-tuple-element.58), channel_id=1, source_target_pairs={{0,1},{1,0},{2,3},{3,2},{4,5},{5,4},{6,7},{7,6},{8,9},{9,8},{10,11... | collective-permute-start | bytes 393224 | tf_op jit(solution)/shard_map/ppermute | solution.py:23
  91.4 8.8 %collective-permute-start.25 = (bf16[32,2048]{1,0:T(8,128)(2,1)S(1)}, bf16[32,2048]{1,0:T(8,128)(2,1)S(1)}, u32[]{:S(2)}, u32[]{:S(2)}) collective-permute-start(bf16[32,2048]{1,0:T(8,128)(2,1)S(1)} %get-tuple-element.59), channel_id=1, source_target_pairs={{0,2},{1,3},{2,0},{3,1},{4,6},{5,7},{6,4},{7,5},{8,10},{9,11},{10,... | collective-permute-start | bytes 393224 | tf_op jit(solution)/shard_map/ppermute | solution.py:23
  93.4 0.7 copy-start.2
  94.1 2.1 %copy-start.1 = (bf16[1,16,16,1024]{3,2,1,0:T(8,128)(2,1)S(1)}, bf16[1,16,16,1024]{3,2,1,0:T(8,128)(2,1)}, u32[]{:S(2)}) copy-start(bf16[1,16,16,1024]{3,2,1,0:T(8,128)(2,1)} %param.9) | copy-start | bytes 1572868

commit v9 on v8

--- a/solution.py
+++ b/solution.py
@@ -108,7 +108,7 @@
 
 
 def prepare(
-    place_ref, x_ref, c_ref, t_ref, gain_ref, normed_ref, branch_ref, face_ref, moment_ref
+    place_ref, x_ref, gain_ref, normed_ref, face_ref, moment_ref
 ):
     block, width = x_ref.shape
     step = pl.program_id(0)
@@ -119,7 +119,6 @@
     variance = jnp.sum(centered * centered, axis=1, keepdims=True) * (1.0 / width)
     inverse = lax.rsqrt(variance + EPSILON)
     normed_ref[rows, :] = (centered * inverse * gain_ref[...]).astype(BF)
-    branch_ref[...] = (c_ref[...].astype(F32) * t_ref[...]).astype(BF)
     lane = lax.broadcasted_iota(jnp.int32, moment_ref.shape, 1)
     moment_ref[...] = jnp.where(lane == 0, mean, inverse)
 
@@ -129,17 +128,16 @@
         face_ref[...] = normed_ref[pl.ds(first, face_ref.shape[0]), :]
 
 
-def run_prepare(place, tokens, cotangent, tissue, gain, face):
+def run_prepare(place, tokens, gain, face):
     count, width = tokens.shape
     block = min(count, 128)
     part = lambda columns: pl.BlockSpec((block, columns), lambda step: (step, 0))
     return pl.pallas_call(
         prepare,
         grid=(count // block,),
-        in_specs=[SCALARS, part(width), part(width), part(1), whole((1, width))],
-        out_specs=[whole((count, width)), part(width), whole((face, width)), part(128)],
+        in_specs=[SCALARS, part(width), whole((1, width))],
+        out_specs=[whole((count, width)), whole((face, width)), part(128)],
         out_shape=[
-            jax.ShapeDtypeStruct((count, width), BF),
             jax.ShapeDtypeStruct((count, width), BF),
             jax.ShapeDtypeStruct((face, width), BF),
             jax.ShapeDtypeStruct((count, 128), F32),
@@ -147,7 +145,7 @@
         compiler_params=pltpu.CompilerParams(**PARAMS),
         cost_estimate=pl.CostEstimate(flops=0, bytes_accessed=3 * 1024 * 1024, transcendentals=0),
         name="prepare",
-    )(place, in_hbm(tokens), in_hbm(cotangent), tissue, in_hbm(gain))
+    )(place, in_hbm(tokens), in_hbm(gain))
 
 
 def spread_heads(block, head_dim):
@@ -488,8 +486,8 @@
     tissue_mask = tissue[0].astype(F32).reshape(token_count, 1)
     tokens_flat = tile_tokens.reshape(flat)
     cot_flat = cotangent[0].reshape(flat)
-    normed, branch_flat, facing, moments = run_prepare(
-        place, tokens_flat, cot_flat, tissue_mask, norm_gain.reshape(1, model_width), face
+    normed, facing, moments = run_prepare(
+        place, tokens_flat, norm_gain.reshape(1, model_width), face
     )
     normed_tile = normed.reshape(grid)
     rows = rows_around(normed_tile, facing.reshape(RADIUS, tile_cols, model_width))
@@ -498,9 +496,13 @@
     ext_rows, ext_cols = normed_ext.shape[:2]
     normed_ext = normed_ext.reshape(ext_rows * ext_cols, model_width)
 
+    queries = times(normed, weight_in[:, :model_width]).astype(BF)
+    mask_late = after(tissue_mask, *rows)
+    branch_flat = (mask_late * cot_flat.astype(F32)).astype(BF)
     grad_attn = times_t(branch_flat, weight_out).astype(BF)
-    queries = times(after(normed, *rows), weight_in[:, :model_width]).astype(BF)
-    normed_late, branch_late, queries = lax.optimization_barrier((normed, branch_flat, queries))
+    normed_late, branch_late, grad_attn = lax.optimization_barrier(
+        (normed, branch_flat, grad_attn)
+    )
     normed_pair = (normed, slide_swap(normed_late, False))
     branch_pair = (branch_flat, slide_swap(branch_late, False))
 

time: 101 us -> 101 us (level)
  no operation moved by 1% of the time
where the time goes in v9:
time: 101 us
  starting transfers between devices  30.9 us (31%)
  waiting for transfers between devices  28 us (28%)
  Pallas kernels  16.5 us (16%)
  matrix products  16.4 us (16%)
  other arithmetic  5.6 us (6%)
  local copies, waits for them, and re-layouts  1.87 us (2%)
  between operations  1.37 us (1%)
    ppermute x21, waiting for transfers between devices, swapped(): return lax.ppermute(array, axis, [(i, i ^ by) for i in range(count)])  28 us
    ppermute x21, starting transfers between devices, swapped(): return lax.ppermute(array, axis, [(i, i ^ by) for i in range(count)])  19.7 us
    pallas_call x1, Pallas kernels, run_queries(): pl.pallas_call(functools.partial(query_pass, head_dim, tile), grid=(group...  14.9 us
    ppermute x3, starting transfers between devices, exchange_columns(): two = lax.ppermute(out_two, 'gx', second)  8.78 us
    dot_general x14, matrix products, product_t(): lax.dot_general(left, right, (((0,), (0,)), ((), ())), preferred_element_...  8.16 us
    dot_general x2, matrix products, times_t(): lax.dot_general(left, right, (((1,), (1,)), ((), ())), preferred_element_...  4.38 us
    dot_general x2, matrix products, times(): return jnp.dot(left, right, preferred_element_type=F32)  3.83 us
    ppermute x3, starting transfers between devices, exchange_columns(): one = lax.ppermute(out_one, 'gx', first)  2.35 us
  transfers between devices with their start and end apart: 27, of which 9 were waited for; matrix products, arithmetic and copies ran while one was open for 22% of the time, Pallas kernels for 15%

profile of v9, /device:TPU:0, one launch (start us, length us, event | category | flops | bytes accessed | tf_op | source)
XLA Modules:
  0.0 100.6 jit_solution(14469761531199634031)
XLA Ops:
  0.7 1.5 %prepare.1 = (bf16[256,1024]{1,0:T(8,128)(2,1)S(1)}, bf16[96,1024]{1,0:T(8,128)(2,1)S(1)}, f32[256,128]{1,0:T(8,128)S(1)}) custom-call(s32[5]{0:T(128)S(1)} %stack.15.place_ref, bf16[256,1024]{1,0:T(8,128)(2,1)} %bitcast.94, f32[1,1024]{1,0:T(1,128)} %bitcast.99), custom_call_target="tpu_custom_call" | custom-call | bytes 3145728 | tf_op jit(solution)/shard_map/prepare/pallas_call | solution.py:135
  2.3 3.0 %collective-permute-start = (bf16[6,16,1024]{2,1,0:T(8,128)(2,1)S(1)}, bf16[6,16,1024]{2,1,0:T(8,128)(2,1)S(1)}, u32[]{:S(2)}, u32[]{:S(2)}) collective-permute-start(bf16[6,16,1024]{2,1,0:T(8,128)(2,1)S(1)} %bitcast.91), channel_id=1, source_target_pairs={{0,4},{4,0},{1,5},{5,1},{2,6},{6,2},{3,7},{7,3},{8,12},{12,8},{9,1... | collective-permute-start | bytes 589832 | tf_op jit(solution)/shard_map/ppermute | solution.py:23
  5.3 1.6 %collective-permute-start.3 = (bf16[16,8,1024]{2,1,0:T(8,128)(2,1)S(1)}, bf16[16,8,1024]{2,1,0:T(8,128)(2,1)S(1)}, u32[]{:S(2)}, u32[]{:S(2)}) collective-permute-start(bf16[16,8,1024]{2,1,0:T(8,128)(2,1)S(1)} %get-tuple-element.80), channel_id=1, source_target_pairs={{0,1},{1,0},{2,3},{3,2},{4,5},{5,4},{6,7},{7,6},{8,9},{9,8},{10,11... | collective-permute-start | bytes 786440 | tf_op jit(solution)/shard_map/ppermute | solution.py:63
  7.0 0.8 collective-permute-start.4
  7.8 2.3 %fusion.62.q_ref = bf16[256,1024]{1,0:T(8,128)(2,1)S(1)} fusion(bf16[256,1024]{1,0:T(8,128)(2,1)S(1)} %get-tuple-element.29, bf16[1024,4096]{1,0:T(8,128)(2,1)} %value_w_ref.1), kind=kOutput, calls=%fused_computation.60 | convolution fusion | flops 537133056 | bytes 3145728 | tf_op jit(solution)/shard_map/dot_general | solution.py:168
  10.4 0.2 slice_reduce_fusion.1
  10.7 4.4 %collective-permute-start.1 = (bf16[6,8,1024]{2,1,0:T(8,128)(2,1)S(1)}, bf16[6,8,1024]{2,1,0:T(8,128)(2,1)S(1)}, u32[]{:S(2)}, u32[]{:S(2)}) collective-permute-start(bf16[6,8,1024]{2,1,0:T(8,128)(2,1)S(1)} %get-tuple-element.90), channel_id=1, source_target_pairs={{0,1},{1,0},{2,3},{3,2},{4,5},{5,4},{6,7},{7,6},{8,9},{9,8},{10,11... | collective-permute-start | bytes 294920 | tf_op jit(solution)/shard_map/ppermute | solution.py:63
  15.1 0.7 collective-permute-start.2
  15.8 0.2 fusion.76
  16.0 2.3 %fusion.59.g_ref = bf16[256,1024]{1,0:T(8,128)(2,1)S(1)} fusion(bf16[256,1024]{1,0:T(8,128)(2,1)S(1)} %fusion.76, bf16[1024,4096]{1,0:T(8,128)(2,1)} %value_w_ref.1), kind=kOutput, calls=%fused_computation.59 | convolution fusion | flops 537133056 | bytes 3145728 | tf_op jit(solution)/shard_map/dot_general | solution.py:172
  18.4 0.5 collective-permute-start.9
  19.0 0.2 broadcast_select_fusion.7
  19.1 0.2 pad_maximum_fusion
  19.5 14.9 %query_pass.1 = (bf16[2,256,1024]{2,1,0:T(8,128)(2,1)S(1)}, bf16[2,896,1024]{2,1,0:T(8,128)(2,1)S(1)}) custom-call(s32[5]{0:T(128)S(1)} %stack.15.place_ref, bf16[256,1024]{1,0:T(8,128)(2,1)S(1)} %fusion.62.q_ref, bf16[256,1024]{1,0:T(8,128)(2,1)S(1)} %fusion.59.g_ref, bf16[896,1024]{1,0:T(8,128)(2,1)S(1)} %bitcast.83, bf16[1024,4096]{1,0:T(8,128)(2,1)} %value_w_ref.1, ...), custom_call_target="tpu_custom_call" | custom-call | flops 4294967296 | bytes 4194304 | tf_op jit(solution)/shard_map/query_pass/pallas_call | solution.py:296
  34.5 1.3 %fusion.27 = bf16[512,1024]{1,0:T(8,128)(2,1)S(1)} fusion(bf16[2,896,1024]{2,1,0:T(8,128)(2,1)S(1)} %get-tuple-element.32, bf16[896,256]{1,0:T(8,128)(2,1)S(1)} %get-tuple-element.54, bf16[896,256]{1,0:T(8,128)(2,1)S(1)} %get-tuple-element.53), kind=kOutput, calls=%fused_computation.38 | convolution fusion | flops 941883392 | bytes 3801088 | tf_op jit(solution)/shard_map/dot_general | solution.py:326
  35.8 1.3 %fusion.30 = bf16[512,1024]{1,0:T(8,128)(2,1)S(1)} fusion(bf16[2,896,1024]{2,1,0:T(8,128)(2,1)S(1)} %get-tuple-element.32, bf16[896,256]{1,0:T(8,128)(2,1)S(1)} %get-tuple-element.54, bf16[896,256]{1,0:T(8,128)(2,1)S(1)} %get-tuple-element.53), kind=kOutput, calls=%fused_computation.39 | convolution fusion | flops 941883392 | bytes 3801088 | tf_op jit(solution)/shard_map/dot_general | solution.py:326
  37.3 0.3 fusion.126
  37.7 0.5 collective-permute-start.6
  38.3 0.3 fusion.123
  38.7 0.3 fusion.115
  39.0 0.3 fusion.108
  39.3 0.2 constant_dynamic-slice_fusion.4
  39.6 0.2 collective-permute-done.8
  39.8 0.3 fusion.68
  40.1 1.6 %collective-permute-start.13 = (bf16[256,1024]{1,0:T(8,128)(2,1)S(1)}, bf16[256,1024]{1,0:T(8,128)(2,1)S(1)}, u32[]{:S(2)}, u32[]{:S(2)}) collective-permute-start(bf16[256,1024]{1,0:T(8,128)(2,1)S(1)} %fusion.68), channel_id=1, source_target_pairs={{0,16},{8,24},{16,0},{24,8},{1,17},{9,25},{17,1},{25,9},{2,18},{10... | collective-permute-start | bytes 1572872 | tf_op jit(solution)/shard_map/ppermute | solution.py:23
  41.8 0.3 fusion.69
  42.1 0.6 collective-permute-start.15
  42.8 0.7 add_convert_fusion
  43.5 1.6 %collective-permute-start.22 = (bf16[256,1024]{1,0:T(8,128)(2,1)S(1)}, bf16[256,1024]{1,0:T(8,128)(2,1)S(1)}, u32[]{:S(2)}, u32[]{:S(2)}) collective-permute-start(bf16[256,1024]{1,0:T(8,128)(2,1)S(1)} %add_convert_fusion), channel_id=1, source_target_pairs={{0,4},{4,0},{1,5},{5,1},{2,6},{6,2},{3,7},{7,3},{8,12},{12,8},{9,1... | collective-permute-start | bytes 1572872 | tf_op jit(solution)/shard_map/ppermute | solution.py:23
  45.1 0.7 fusion.56
  45.9 0.6 collective-permute-start.20
  46.6 0.9 collective-permute-start.10
  47.6 1.5 %fusion.65 = bf16[256,1024]{1,0:T(8,128)(2,1)} fusion(bf16[256,1024]{1,0:T(8,128)(2,1)S(1)} %get-tuple-element.27, bf16[1024,4096]{1,0:T(8,128)(2,1)S(1)} %bitcast.93, bf16[256,1024]{1,0:T(8,128)(2,1)S(1)} %bitcast.95, f32[256]{0:T(256)S(1)} %convert_element_type.168), kind=kOutput, calls=%fused_computation.61 | convolution fusion | flops 537919488 | bytes 3671040 | tf_op jit(solution)/shard_map/dot_general | solution.py:168
  49.1 0.7 convert_add_fusion.4
  49.8 0.8 fusion.42
  50.6 0.3 convolution_add_fusion.1
  51.0 0.3 convolution_add_fusion
  51.3 3.7 %collective-permute-done.13 = bf16[256,1024]{1,0:T(8,128)(2,1)S(1)} collective-permute-done((bf16[256,1024]{1,0:T(8,128)(2,1)S(1)}, bf16[256,1024]{1,0:T(8,128)(2,1)S(1)}, u32[]{:S(2)}, u32[]{:S(2)}) %collective-permute-start.13) | collective-permute-done | bytes 524320 | tf_op jit(solution)/shard_map/ppermute | solution.py:23
  55.0 2.7 %collective-permute-start.11 = (bf16[2,28,8,1024]{3,2,1,0:T(8,128)(2,1)S(1)}, bf16[2,28,8,1024]{3,2,1,0:T(8,128)(2,1)S(1)}, u32[]{:S(2)}, u32[]{:S(2)}) collective-permute-start(bf16[2,28,8,1024]{3,2,1,0:T(8,128)(2,1)S(1)} %get-tuple-element.46), channel_id=1, source_target_pairs={{0,1},{1,0},{2,3},{3,2},{4,5},{5,4},{6,7},{7,6},{8,9},{9,8},{10,11... | collective-permute-start | bytes 2752520 | tf_op jit(solution)/shard_map/ppermute | solution.py:63
  57.6 0.2 convert_add_fusion.6
  57.9 0.6 collective-permute-start.14
  58.5 0.2 convert_add_fusion.5
  58.7 6.8 %collective-permute-done.20 = bf16[256,1024]{1,0:T(8,128)(2,1)S(1)} collective-permute-done((bf16[256,1024]{1,0:T(8,128)(2,1)S(1)}, bf16[256,1024]{1,0:T(8,128)(2,1)S(1)}, u32[]{:S(2)}, u32[]{:S(2)}) %collective-permute-start.20) | collective-permute-done | bytes 524320 | tf_op jit(solution)/shard_map/ppermute | solution.py:23
  65.5 1.5 %collective-permute-start.16 = (bf16[128,1024]{1,0:T(8,128)(2,1)S(1)}, bf16[128,1024]{1,0:T(8,128)(2,1)S(1)}, u32[]{:S(2)}, u32[]{:S(2)}) collective-permute-start(bf16[128,1024]{1,0:T(8,128)(2,1)S(1)} %dynamic-slice_convert_fusion.2), channel_id=1, source_target_pairs={{0,16},{8,24},{16,0},{24,8},{1,17},{9,25},{17,1},{25,9},{2,18},{10... | collective-permute-start | bytes 786440 | tf_op jit(solution)/shard_map/ppermute | solution.py:23
  67.2 1.0 collective-permute-done.22
  68.2 0.5 collective-permute-start.21
  68.7 0.2 convert_add_fusion.2
  68.9 4.9 %collective-permute-done.14 = bf16[128,1024]{1,0:T(8,128)(2,1)S(1)} collective-permute-done((bf16[128,1024]{1,0:T(8,128)(2,1)S(1)}, bf16[128,1024]{1,0:T(8,128)(2,1)S(1)}, u32[]{:S(2)}, u32[]{:S(2)}) %collective-permute-start.14) | collective-permute-done | bytes 262176 | tf_op jit(solution)/shard_map/ppermute | solution.py:23
  73.8 0.5 collective-permute-start.23
  74.6 1.0 collective-permute-start.17
  75.5 2.9 %collective-permute-done.21 = bf16[128,1024]{1,0:T(8,128)(2,1)S(1)} collective-permute-done((bf16[128,1024]{1,0:T(8,128)(2,1)S(1)}, bf16[128,1024]{1,0:T(8,128)(2,1)S(1)}, u32[]{:S(2)}, u32[]{:S(2)}) %collective-permute-start.21) | collective-permute-done | bytes 262176 | tf_op jit(solution)/shard_map/ppermute | solution.py:23
  78.4 2.7 %collective-permute-start.18 = (bf16[32,2048]{1,0:T(8,128)(2,1)S(1)}, bf16[32,2048]{1,0:T(8,128)(2,1)S(1)}, u32[]{:S(2)}, u32[]{:S(2)}) collective-permute-start(bf16[32,2048]{1,0:T(8,128)(2,1)S(1)} %get-tuple-element.63), channel_id=1, source_target_pairs={{0,2},{1,3},{2,0},{3,1},{4,6},{5,7},{6,4},{7,5},{8,10},{9,11},{10,... | collective-permute-start | bytes 393224 | tf_op jit(solution)/shard_map/ppermute | solution.py:23
  81.2 1.6 %collective-permute-start.19 = (bf16[32,2048]{1,0:T(8,128)(2,1)S(1)}, bf16[32,2048]{1,0:T(8,128)(2,1)S(1)}, u32[]{:S(2)}, u32[]{:S(2)}) collective-permute-start(bf16[32,2048]{1,0:T(8,128)(2,1)S(1)} %get-tuple-element.64), channel_id=1, source_target_pairs={{0,1},{1,0},{2,3},{3,2},{4,5},{5,4},{6,7},{7,6},{8,9},{9,8},{10,11... | collective-permute-start | bytes 393224 | tf_op jit(solution)/shard_map/ppermute | solution.py:23
  83.2 1.0 fusion.143
  84.3 0.6 collective-permute-start.12
  84.9 2.1 %collective-permute-start.24 = (bf16[32,2048]{1,0:T(8,128)(2,1)S(1)}, bf16[32,2048]{1,0:T(8,128)(2,1)S(1)}, u32[]{:S(2)}, u32[]{:S(2)}) collective-permute-start(bf16[32,2048]{1,0:T(8,128)(2,1)S(1)} %get-tuple-element.55), channel_id=1, source_target_pairs={{0,3},{1,2},{2,1},{3,0},{4,7},{5,6},{6,5},{7,4},{8,11},{9,10},{10,... | collective-permute-start | bytes 393224 | tf_op jit(solution)/shard_map/ppermute | solution.py:23
  87.0 4.7 %collective-permute-done.18 = bf16[32,2048]{1,0:T(8,128)(2,1)S(1)} collective-permute-done((bf16[32,2048]{1,0:T(8,128)(2,1)S(1)}, bf16[32,2048]{1,0:T(8,128)(2,1)S(1)}, u32[]{:S(2)}, u32[]{:S(2)}) %collective-permute-start.18) | collective-permute-done | bytes 131104 | tf_op jit(solution)/shard_map/ppermute | solution.py:23
  91.8 0.8 collective-permute-done.12
  92.7 0.3 fusion.3
  93.1 0.3 copy-done.3
  93.4 2.0 %fusion.144 = (f32[256]{0:T(256)S(1)}, f32[256]{0:T(256)S(1)}, f32[256,1024]{1,0:T(8,128)S(1)}) fusion(f32[256]{0:T(256)S(1)} %get-tuple-element.41, f32[256]{0:T(256)S(1)} %get-tuple-element.42, bf16[1,16,16,1024]{3,2,1,0:T(8,128)(2,1)S(1)} %copy-done.1, f32[1024]{0:T(1024)S(1)} %copy-done.3, bf16[1024,4096]{1,0:T(8,128)(2,1)S(1)} %bitcast.93, ...), kind=kOutput, calls=%fused_computation.194 | convolution fusion | flops 1617165824 | bytes 9445376 | tf_op jit(solution)/shard_map/dot_general | solution.py:172
  95.4 1.2 %fusion.77 = bf16[256,1024]{1,0:T(8,128)(2,1)} fusion(f32[256,1024]{1,0:T(8,128)S(1)} %get-tuple-element.92, bf16[1,16,16,1024]{3,2,1,0:T(8,128)(2,1)S(1)} %copy-done, f32[256]{0:T(256)S(1)} %get-tuple-element.93, f32[256]{0:T(256)S(1)} %get-tuple-element.42, f32[256]{0:T(256)S(1)} %get-tuple-element.94, f32[256]{0:T(256)S(1)} %get-tuple-element.41, ...), kind=kLoop, calls=%fused_computation.71 | loop fusion | flops 2621440 | bytes 2625536 | tf_op jit(solution)/shard_map/convert_element_type | solution.py:557
  96.7 3.0 %collective-permute-done.25 = bf16[32,2048]{1,0:T(8,128)(2,1)S(1)} collective-permute-done((bf16[32,2048]{1,0:T(8,128)(2,1)S(1)}, bf16[32,2048]{1,0:T(8,128)(2,1)S(1)}, u32[]{:S(2)}, u32[]{:S(2)}) %collective-permute-start.25) | collective-permute-done | bytes 131104 | tf_op jit(solution)/shard_map/ppermute | solution.py:23
  99.7 0.8 maximum_multiply_fusion
  (71 shorter events, 2.6 us)
Async XLA Ops:
  2.3 8.4 %collective-permute-start = (bf16[6,16,1024]{2,1,0:T(8,128)(2,1)S(1)}, bf16[6,16,1024]{2,1,0:T(8,128)(2,1)S(1)}, u32[]{:S(2)}, u32[]{:S(2)}) collective-permute-start(bf16[6,16,1024]{2,1,0:T(8,128)(2,1)S(1)} %bitcast.91), channel_id=1, source_target_pairs={{0,4},{4,0},{1,5},{5,1},{2,6},{6,2},{3,7},{7,3},{8,12},{12,8},{9,1... | collective-permute-start | bytes 589832 | tf_op jit(solution)/shard_map/ppermute | solution.py:23
  5.3 13.0 %collective-permute-start.3 = (bf16[16,8,1024]{2,1,0:T(8,128)(2,1)S(1)}, bf16[16,8,1024]{2,1,0:T(8,128)(2,1)S(1)}, u32[]{:S(2)}, u32[]{:S(2)}) collective-permute-start(bf16[16,8,1024]{2,1,0:T(8,128)(2,1)S(1)} %get-tuple-element.80), channel_id=1, source_target_pairs={{0,1},{1,0},{2,3},{3,2},{4,5},{5,4},{6,7},{7,6},{8,9},{9,8},{10,11... | collective-permute-start | bytes 786440 | tf_op jit(solution)/shard_map/ppermute | solution.py:63
  7.0 3.2 %copy-start.2 = (s32[1,16,16]{2,1,0:T(8,128)S(1)}, s32[1,16,16]{2,1,0:T(8,128)}, u32[]{:S(2)}) copy-start(s32[1,16,16]{2,1,0:T(8,128)} %param.8) | copy-start | bytes 3076
  7.0 8.8 %copy-start = (bf16[1,16,16,1024]{3,2,1,0:T(8,128)(2,1)S(1)}, bf16[1,16,16,1024]{3,2,1,0:T(8,128)(2,1)}, u32[]{:S(2)}) copy-start(bf16[1,16,16,1024]{3,2,1,0:T(8,128)(2,1)} %param.9) | copy-start | bytes 1572868
  7.0 11.9 %collective-permute-start.4 = (bf16[16,8,1024]{2,1,0:T(8,128)(2,1)S(1)}, bf16[16,8,1024]{2,1,0:T(8,128)(2,1)S(1)}, u32[]{:S(2)}, u32[]{:S(2)}) collective-permute-start(bf16[16,8,1024]{2,1,0:T(8,128)(2,1)S(1)} %get-tuple-element.81), channel_id=1, source_target_pairs={{1,2},{2,1},{5,6},{6,5},{9,10},{10,9},{13,14},{14,13},{17,18},{18,... | collective-permute-start | bytes 786440 | tf_op jit(solution)/shard_map/ppermute | solution.py:62
  10.7 8.3 %collective-permute-start.1 = (bf16[6,8,1024]{2,1,0:T(8,128)(2,1)S(1)}, bf16[6,8,1024]{2,1,0:T(8,128)(2,1)S(1)}, u32[]{:S(2)}, u32[]{:S(2)}) collective-permute-start(bf16[6,8,1024]{2,1,0:T(8,128)(2,1)S(1)} %get-tuple-element.90), channel_id=1, source_target_pairs={{0,1},{1,0},{2,3},{3,2},{4,5},{5,4},{6,7},{7,6},{8,9},{9,8},{10,11... | collective-permute-start | bytes 294920 | tf_op jit(solution)/shard_map/ppermute | solution.py:63
  15.1 3.8 %collective-permute-start.2 = (bf16[6,8,1024]{2,1,0:T(8,128)(2,1)S(1)}, bf16[6,8,1024]{2,1,0:T(8,128)(2,1)S(1)}, u32[]{:S(2)}, u32[]{:S(2)}) collective-permute-start(bf16[6,8,1024]{2,1,0:T(8,128)(2,1)S(1)} %get-tuple-element.91), channel_id=1, source_target_pairs={{1,2},{2,1},{5,6},{6,5},{9,10},{10,9},{13,14},{14,13},{17,18},{18,... | collective-permute-start | bytes 294920 | tf_op jit(solution)/shard_map/ppermute | solution.py:62
  18.3 21.5 %collective-permute-start.7 = (bf16[256,1024]{1,0:T(8,128)(2,1)S(1)}, bf16[256,1024]{1,0:T(8,128)(2,1)S(1)}, u32[]{:S(2)}, u32[]{:S(2)}) collective-permute-start(bf16[256,1024]{1,0:T(8,128)(2,1)S(1)} %get-tuple-element.29), channel_id=1, source_target_pairs={{0,8},{8,0},{16,24},{24,16},{1,9},{9,1},{17,25},{25,17},{2,10},{10... | collective-permute-start | bytes 1572872 | tf_op jit(solution)/shard_map/ppermute | solution.py:23
  18.4 23.4 %collective-permute-start.9 = (bf16[256,1024]{1,0:T(8,128)(2,1)S(1)}, bf16[256,1024]{1,0:T(8,128)(2,1)S(1)}, u32[]{:S(2)}, u32[]{:S(2)}) collective-permute-start(bf16[256,1024]{1,0:T(8,128)(2,1)S(1)} %fusion.76), channel_id=1, source_target_pairs={{0,8},{8,0},{16,24},{24,16},{1,9},{9,1},{17,25},{25,17},{2,10},{10... | collective-permute-start | bytes 1572872 | tf_op jit(solution)/shard_map/ppermute | solution.py:23
  37.0 2.7 %collective-permute-start.8 = (bf16[2,256,1024]{2,1,0:T(8,128)(2,1)S(1)}, bf16[2,256,1024]{2,1,0:T(8,128)(2,1)S(1)}, u32[]{:S(2)}, u32[]{:S(2)}) collective-permute-start(bf16[2,256,1024]{2,1,0:T(8,128)(2,1)S(1)} %get-tuple-element.25), channel_id=1, source_target_pairs={{0,8},{8,0},{16,24},{24,16},{1,9},{9,1},{17,25},{25,17},{2,10},{10... | collective-permute-start | bytes 3145736 | tf_op jit(solution)/shard_map/ppermute | solution.py:23
  37.7 5.0 %collective-permute-start.6 = (bf16[512,1024]{1,0:T(8,128)(2,1)S(1)}, bf16[512,1024]{1,0:T(8,128)(2,1)S(1)}, u32[]{:S(2)}, u32[]{:S(2)}) collective-permute-start(bf16[512,1024]{1,0:T(8,128)(2,1)S(1)} %fusion.30), channel_id=1, source_target_pairs={{0,8},{8,0},{16,24},{24,16},{1,9},{9,1},{17,25},{25,17},{2,10},{10... | collective-permute-start | bytes 3145736 | tf_op jit(solution)/shard_map/ppermute | solution.py:23
  38.2 7.0 %collective-permute-start.5 = (bf16[512,1024]{1,0:T(8,128)(2,1)S(1)}, bf16[512,1024]{1,0:T(8,128)(2,1)S(1)}, u32[]{:S(2)}, u32[]{:S(2)}) collective-permute-start(bf16[512,1024]{1,0:T(8,128)(2,1)S(1)} %fusion.27), channel_id=1, source_target_pairs={{0,8},{8,0},{16,24},{24,16},{1,9},{9,1},{17,25},{25,17},{2,10},{10... | collective-permute-start | bytes 3145736 | tf_op jit(solution)/shard_map/ppermute | solution.py:23
  40.1 14.8 %collective-permute-start.13 = (bf16[256,1024]{1,0:T(8,128)(2,1)S(1)}, bf16[256,1024]{1,0:T(8,128)(2,1)S(1)}, u32[]{:S(2)}, u32[]{:S(2)}) collective-permute-start(bf16[256,1024]{1,0:T(8,128)(2,1)S(1)} %fusion.68), channel_id=1, source_target_pairs={{0,16},{8,24},{16,0},{24,8},{1,17},{9,25},{17,1},{25,9},{2,18},{10... | collective-permute-start | bytes 1572872 | tf_op jit(solution)/shard_map/ppermute | solution.py:23
  42.1 15.8 %collective-permute-start.15 = (bf16[256,1024]{1,0:T(8,128)(2,1)S(1)}, bf16[256,1024]{1,0:T(8,128)(2,1)S(1)}, u32[]{:S(2)}, u32[]{:S(2)}) collective-permute-start(bf16[256,1024]{1,0:T(8,128)(2,1)S(1)} %fusion.69), channel_id=1, source_target_pairs={{0,4},{4,0},{1,5},{5,1},{2,6},{6,2},{3,7},{7,3},{8,12},{12,8},{9,1... | collective-permute-start | bytes 1572872 | tf_op jit(solution)/shard_map/ppermute | solution.py:23
  42.7 4.9 %slice-start = ((s8[8388608]{0:T(1024)(128)(4,1)}), s8[4194304]{0:T(1024)(128)(4,1)S(1)}, s32[]{:S(2)}) async-start(s8[8388608]{0:T(1024)(128)(4,1)} %bitcast.92), calls=%async_computation | async-start | bytes 8388608
  43.5 4.0 %slice-start.1 = ((s8[8388608]{0:T(1024)(128)(4,1)}), s8[4194304]{0:T(1024)(128)(4,1)S(1)}, s32[]{:S(2)}) async-start(s8[8388608]{0:T(1024)(128)(4,1)} %bitcast.92), calls=%async_computation.1 | async-start | bytes 8388608
  43.5 24.7 %collective-permute-start.22 = (bf16[256,1024]{1,0:T(8,128)(2,1)S(1)}, bf16[256,1024]{1,0:T(8,128)(2,1)S(1)}, u32[]{:S(2)}, u32[]{:S(2)}) collective-permute-start(bf16[256,1024]{1,0:T(8,128)(2,1)S(1)} %add_convert_fusion), channel_id=1, source_target_pairs={{0,4},{4,0},{1,5},{5,1},{2,6},{6,2},{3,7},{7,3},{8,12},{12,8},{9,1... | collective-permute-start | bytes 1572872 | tf_op jit(solution)/shard_map/ppermute | solution.py:23
  45.9 1.7 %copy-start.1 = (bf16[1,16,16,1024]{3,2,1,0:T(8,128)(2,1)S(1)}, bf16[1,16,16,1024]{3,2,1,0:T(8,128)(2,1)}, u32[]{:S(2)}) copy-start(bf16[1,16,16,1024]{3,2,1,0:T(8,128)(2,1)} %param.5) | copy-start | bytes 1572868
  45.9 19.7 %collective-permute-start.20 = (bf16[256,1024]{1,0:T(8,128)(2,1)S(1)}, bf16[256,1024]{1,0:T(8,128)(2,1)S(1)}, u32[]{:S(2)}, u32[]{:S(2)}) collective-permute-start(bf16[256,1024]{1,0:T(8,128)(2,1)S(1)} %fusion.56), channel_id=1, source_target_pairs={{0,16},{8,24},{16,0},{24,8},{1,17},{9,25},{17,1},{25,9},{2,18},{10... | collective-permute-start | bytes 1572872 | tf_op jit(solution)/shard_map/ppermute | solution.py:23
  46.6 36.4 %collective-permute-start.10 = (bf16[2,28,8,1024]{3,2,1,0:T(8,128)(2,1)S(1)}, bf16[2,28,8,1024]{3,2,1,0:T(8,128)(2,1)S(1)}, u32[]{:S(2)}, u32[]{:S(2)}) collective-permute-start(bf16[2,28,8,1024]{3,2,1,0:T(8,128)(2,1)S(1)} %get-tuple-element.45), channel_id=1, source_target_pairs={{1,2},{2,1},{5,6},{6,5},{9,10},{10,9},{13,14},{14,13},{17,18},{18,... | collective-permute-start | bytes 2752520 | tf_op jit(solution)/shard_map/ppermute | solution.py:62
  55.0 28.1 %collective-permute-start.11 = (bf16[2,28,8,1024]{3,2,1,0:T(8,128)(2,1)S(1)}, bf16[2,28,8,1024]{3,2,1,0:T(8,128)(2,1)S(1)}, u32[]{:S(2)}, u32[]{:S(2)}) collective-permute-start(bf16[2,28,8,1024]{3,2,1,0:T(8,128)(2,1)S(1)} %get-tuple-element.46), channel_id=1, source_target_pairs={{0,1},{1,0},{2,3},{3,2},{4,5},{5,4},{6,7},{7,6},{8,9},{9,8},{10,11... | collective-permute-start | bytes 2752520 | tf_op jit(solution)/shard_map/ppermute | solution.py:63
  57.9 15.9 %collective-permute-start.14 = (bf16[128,1024]{1,0:T(8,128)(2,1)S(1)}, bf16[128,1024]{1,0:T(8,128)(2,1)S(1)}, u32[]{:S(2)}, u32[]{:S(2)}) collective-permute-start(bf16[128,1024]{1,0:T(8,128)(2,1)S(1)} %dynamic-slice_convert_fusion.3), channel_id=1, source_target_pairs={{0,4},{4,0},{1,5},{5,1},{2,6},{6,2},{3,7},{7,3},{8,12},{12,8},{9,1... | collective-permute-start | bytes 786440 | tf_op jit(solution)/shard_map/ppermute | solution.py:23
  65.5 8.9 %collective-permute-start.16 = (bf16[128,1024]{1,0:T(8,128)(2,1)S(1)}, bf16[128,1024]{1,0:T(8,128)(2,1)S(1)}, u32[]{:S(2)}, u32[]{:S(2)}) collective-permute-start(bf16[128,1024]{1,0:T(8,128)(2,1)S(1)} %dynamic-slice_convert_fusion.2), channel_id=1, source_target_pairs={{0,16},{8,24},{16,0},{24,8},{1,17},{9,25},{17,1},{25,9},{2,18},{10... | collective-permute-start | bytes 786440 | tf_op jit(solution)/shard_map/ppermute | solution.py:23
  68.2 10.2 %collective-permute-start.21 = (bf16[128,1024]{1,0:T(8,128)(2,1)S(1)}, bf16[128,1024]{1,0:T(8,128)(2,1)S(1)}, u32[]{:S(2)}, u32[]{:S(2)}) collective-permute-start(bf16[128,1024]{1,0:T(8,128)(2,1)S(1)} %dynamic-slice_convert_fusion.1), channel_id=1, source_target_pairs={{0,4},{4,0},{1,5},{5,1},{2,6},{6,2},{3,7},{7,3},{8,12},{12,8},{9,1... | collective-permute-start | bytes 786440 | tf_op jit(solution)/shard_map/ppermute | solution.py:23
  73.8 7.4 %collective-permute-start.23 = (bf16[128,1024]{1,0:T(8,128)(2,1)S(1)}, bf16[128,1024]{1,0:T(8,128)(2,1)S(1)}, u32[]{:S(2)}, u32[]{:S(2)}) collective-permute-start(bf16[128,1024]{1,0:T(8,128)(2,1)S(1)} %dynamic-slice_convert_fusion), channel_id=1, source_target_pairs={{0,16},{8,24},{16,0},{24,8},{1,17},{9,25},{17,1},{25,9},{2,18},{10... | collective-permute-start | bytes 786440 | tf_op jit(solution)/shard_map/ppermute | solution.py:23
  74.6 12.4 %collective-permute-start.17 = (bf16[32,2048]{1,0:T(8,128)(2,1)S(1)}, bf16[32,2048]{1,0:T(8,128)(2,1)S(1)}, u32[]{:S(2)}, u32[]{:S(2)}) collective-permute-start(bf16[32,2048]{1,0:T(8,128)(2,1)S(1)} %get-tuple-element.62), channel_id=1, source_target_pairs={{0,3},{1,2},{2,1},{3,0},{4,7},{5,6},{6,5},{7,4},{8,11},{9,10},{10,... | collective-permute-start | bytes 393224 | tf_op jit(solution)/shard_map/ppermute | solution.py:23
  78.4 13.2 %collective-permute-start.18 = (bf16[32,2048]{1,0:T(8,128)(2,1)S(1)}, bf16[32,2048]{1,0:T(8,128)(2,1)S(1)}, u32[]{:S(2)}, u32[]{:S(2)}) collective-permute-start(bf16[32,2048]{1,0:T(8,128)(2,1)S(1)} %get-tuple-element.63), channel_id=1, source_target_pairs={{0,2},{1,3},{2,0},{3,1},{4,6},{5,7},{6,4},{7,5},{8,10},{9,11},{10,... | collective-permute-start | bytes 393224 | tf_op jit(solution)/shard_map/ppermute | solution.py:23
  81.2 10.4 %collective-permute-start.19 = (bf16[32,2048]{1,0:T(8,128)(2,1)S(1)}, bf16[32,2048]{1,0:T(8,128)(2,1)S(1)}, u32[]{:S(2)}, u32[]{:S(2)}) collective-permute-start(bf16[32,2048]{1,0:T(8,128)(2,1)S(1)} %get-tuple-element.64), channel_id=1, source_target_pairs={{0,1},{1,0},{2,3},{3,2},{4,5},{5,4},{6,7},{7,6},{8,9},{9,8},{10,11... | collective-permute-start | bytes 393224 | tf_op jit(solution)/shard_map/ppermute | solution.py:23
  84.3 8.4 %collective-permute-start.12 = (bf16[2,6,16,1024]{3,2,1,0:T(8,128)(2,1)S(1)}, bf16[2,6,16,1024]{3,2,1,0:T(8,128)(2,1)S(1)}, u32[]{:S(2)}, u32[]{:S(2)}) collective-permute-start(bf16[2,6,16,1024]{3,2,1,0:T(8,128)(2,1)S(1)} %slice_select_fusion), channel_id=1, source_target_pairs={{0,4},{4,0},{1,5},{5,1},{2,6},{6,2},{3,7},{7,3},{8,12},{12,8},{9,1... | collective-permute-start | bytes 1179656 | tf_op jit(solution)/shard_map/ppermute | solution.py:23
  84.9 11.8 %collective-permute-start.24 = (bf16[32,2048]{1,0:T(8,128)(2,1)S(1)}, bf16[32,2048]{1,0:T(8,128)(2,1)S(1)}, u32[]{:S(2)}, u32[]{:S(2)}) collective-permute-start(bf16[32,2048]{1,0:T(8,128)(2,1)S(1)} %get-tuple-element.55), channel_id=1, source_target_pairs={{0,3},{1,2},{2,1},{3,0},{4,7},{5,6},{6,5},{7,4},{8,11},{9,10},{10,... | collective-permute-start | bytes 393224 | tf_op jit(solution)/shard_map/ppermute | solution.py:23
  87.0 9.7 %collective-permute-start.26 = (bf16[32,2048]{1,0:T(8,128)(2,1)S(1)}, bf16[32,2048]{1,0:T(8,128)(2,1)S(1)}, u32[]{:S(2)}, u32[]{:S(2)}) collective-permute-start(bf16[32,2048]{1,0:T(8,128)(2,1)S(1)} %get-tuple-element.56), channel_id=1, source_target_pairs={{0,1},{1,0},{2,3},{3,2},{4,5},{5,4},{6,7},{7,6},{8,9},{9,8},{10,11... | collective-permute-start | bytes 393224 | tf_op jit(solution)/shard_map/ppermute | solution.py:23
  91.6 8.0 %collective-permute-start.25 = (bf16[32,2048]{1,0:T(8,128)(2,1)S(1)}, bf16[32,2048]{1,0:T(8,128)(2,1)S(1)}, u32[]{:S(2)}, u32[]{:S(2)}) collective-permute-start(bf16[32,2048]{1,0:T(8,128)(2,1)S(1)} %get-tuple-element.57), channel_id=1, source_target_pairs={{0,2},{1,3},{2,0},{3,1},{4,6},{5,7},{6,4},{7,5},{8,10},{9,11},{10,... | collective-permute-start | bytes 393224 | tf_op jit(solution)/shard_map/ppermute | solution.py:23
  92.7 0.7 copy-start.3
